TPU v7x, 32 devices: a whole 2x2x4 slice. The times are simulated.
32 devices in a mesh: section: 2 (over core), dp: 16 (over z, y, x).
Axes of the slice: x: 2, y: 2, z: 4, core: 2. Of those that a mesh axis runs over, the one named last changes fastest.
Arguments:
- images: bfloat16 [2, 16, 16, 16, 512], P(None, 'dp'), may hold values from -6 to 6
- cotangent: bfloat16 [2, 16, 16, 16, 512], P(None, 'dp'), may hold values from -6 to 6
- crop_class: int32 [2, 16], P(None, 'dp'), may hold values from 0 to 2
- norm1_gain: bfloat16 [2, 512], P('section'), may hold values from 0.5 to 1.5
- norm1_shift: bfloat16 [2, 512], P('section'), may hold values from -1.796875 to 1.796875
- input_weight: bfloat16 [2, 512, 1024], P('section'), may hold values from -0.25 to 0.25
- input_bias: bfloat16 [2, 1024], P('section'), may hold values from -1.796875 to 1.796875
- conv_kernel: bfloat16 [2, 49, 960], P('section'), may hold values from -2.59375 to 2.59375
- conv_bias: bfloat16 [2, 960], P('section'), may hold values from -1.796875 to 1.796875
- gate1_weight: bfloat16 [2, 64, 128], P('section'), may hold values from -0.75 to 0.75
- gate1_bias: bfloat16 [2, 128], P('section'), may hold values from -1.796875 to 1.796875
- gate2_weight: bfloat16 [2, 128, 256], P('section'), may hold values from -0.5 to 0.5
- gate2_bias: bfloat16 [2, 256], P('section'), may hold values from -1.796875 to 1.796875
- gate3_weight: bfloat16 [2, 256, 512], P('section'), may hold values from -0.375 to 0.375
- gate3_bias: bfloat16 [2, 512], P('section'), may hold values from -1.796875 to 1.796875
- output_weight: bfloat16 [2, 512, 512], P('section'), may hold values from -0.25 to 0.25
- output_bias: bfloat16 [2, 512], P('section'), may hold values from -1.796875 to 1.796875
- branch_scale: bfloat16 [2, 512], P('section'), may hold values from 0.5 to 2
- norm2_gain: bfloat16 [2, 512], P('section'), may hold values from 0.5 to 1.5
- norm2_shift: bfloat16 [2, 512], P('section'), may hold values from -1.796875 to 1.796875
- expand_weight: bfloat16 [2, 512, 2048], P('section'), may hold values from -0.25 to 0.25
- expand_bias: bfloat16 [2, 2048], P('section'), may hold values from -1.796875 to 1.796875
- reduce_weight: bfloat16 [2, 2048, 512], P('section'), may hold values from -0.125 to 0.125
- reduce_bias: bfloat16 [2, 512], P('section'), may hold values from -1.796875 to 1.796875
- mlp_scale: bfloat16 [2, 512], P('section'), may hold values from 0.5 to 2
Outputs:
- block_outputs: bfloat16 [2, 2, 16, 16, 16, 512], P('section', None, 'dp')
- input_grads: float32 [2, 2, 16, 16, 16, 512], P('section', None, 'dp')
- norm1_gain_grad: float32 [2, 512], P('section')
- norm1_shift_grad: float32 [2, 512], P('section')
- input_weight_grad: float32 [2, 512, 1024], P('section')
- input_bias_grad: float32 [2, 1024], P('section')
- conv_kernel_grad: float32 [2, 49, 960], P('section')
- conv_bias_grad: float32 [2, 960], P('section')
- gate1_weight_grad: float32 [2, 64, 128], P('section')
- gate1_bias_grad: float32 [2, 128], P('section')
- gate2_weight_grad: float32 [2, 128, 256], P('section')
- gate2_bias_grad: float32 [2, 256], P('section')
- gate3_weight_grad: float32 [2, 256, 512], P('section')
- gate3_bias_grad: float32 [2, 512], P('section')
- output_weight_grad: float32 [2, 512, 512], P('section')
- output_bias_grad: float32 [2, 512], P('section')
- branch_scale_grad: float32 [2, 512], P('section')
- norm2_gain_grad: float32 [2, 512], P('section')
- norm2_shift_grad: float32 [2, 512], P('section')
- expand_weight_grad: float32 [2, 512, 2048], P('section')
- expand_bias_grad: float32 [2, 2048], P('section')
- reduce_weight_grad: float32 [2, 2048, 512], P('section')
- reduce_bias_grad: float32 [2, 512], P('section')
- mlp_scale_grad: float32 [2, 512], P('section')
Inputs may be any that keep to these rules, and one draw needn't show every extreme that they name: `crop_class`: 0 stands for a crop of 8 pixels a side, 1 for 12, 2 for 16; an image's pixels outside its crop are ignored.
All inputs are finite; a program needn't handle non-finite values.
Results may differ from a plain program's by a relative error of at most 0.025.
Values may be sent and summed in bfloat16 or wider, within the bound.
No kernel may reach another device: no remote copies, remote signals or barrier semaphores. Data moves between devices by JAX's collectives and lax.ppermute only.
A program may use at most 192 MiB of HBM per device.

v0:
```python
import jax
import jax.numpy as jnp
from jax import lax
from jax.sharding import PartitionSpec as P

SIDE_S = 8
SIDE_M = 12


eps_norm = 1e-06
conv_scale = 1.0 / 3.0
kernel_side = 7
matrix_slots = (2, 6, 8, 10, 12, 17, 19)


def shifted(x, axis, by):
    length = lax.axis_size(axis)
    pairs = [(i, i + by) for i in range(length) if 0 <= i + by < length]
    return lax.ppermute(x, axis, pairs)


def project(left, weight):
    return jnp.einsum("ihwk,kn->ihwn", left, weight, preferred_element_type=jnp.float32)


def project_back(upward, weight):
    return jnp.einsum("ihwn,kn->ihwk", upward, weight, preferred_element_type=jnp.float32)


def outer_total(left, upward):
    return jnp.einsum("ihwk,ihwn->kn", left, upward, preferred_element_type=jnp.float32)


def row_total(values):
    return jnp.sum(values.astype(jnp.float32), axis=(0, 1, 2))


def norm_forward(values, gain, shift):
    average = jnp.mean(values, axis=-1, keepdims=True)
    centered = values - average
    inv_std = lax.rsqrt(jnp.mean(centered * centered, axis=-1, keepdims=True) + eps_norm)
    normed = centered * inv_std
    return (normed * gain + shift, normed, inv_std)


def norm_backward(upward, normed, inv_std, gain):
    scaled = upward * gain
    inner = (
        scaled
        - jnp.mean(scaled, axis=-1, keepdims=True)
        - normed * jnp.mean(scaled * normed, axis=-1, keepdims=True)
    )
    return (inv_std * inner, row_total(upward * normed), row_total(upward))


def gelu_slope(values):
    cumulative = 0.5 * (1.0 + jax.scipy.special.erf(values * 0.7071067811865476))
    return cumulative + values * jnp.exp(-0.5 * values * values) * 0.3989422804014327


def conv_forward(source, kernel):
    channels = source.shape[-1]
    taps = kernel.reshape(kernel_side, kernel_side, 1, channels)
    return lax.conv_general_dilated(
        source,
        taps,
        (1, 1),
        ((3, 3), (3, 3)),
        dimension_numbers=("NHWC", "HWIO", "NHWC"),
        feature_group_count=channels,
        precision=lax.Precision.HIGHEST,
    )


def conv_backward(upward, source, kernel):
    unused_value, pull = jax.vjp(conv_forward, source, kernel)
    dsource, dkernel = pull(upward)
    return (dsource, dkernel)


def block_forward(start, region, weights):
    (
        norm1_gain,
        norm1_shift,
        input_weight,
        input_bias,
        conv_kernel,
        conv_bias,
        gate1_weight,
        gate1_bias,
        gate2_weight,
        gate2_bias,
        gate3_weight,
        gate3_bias,
        output_weight,
        output_bias,
        branch_scale,
        norm2_gain,
        norm2_shift,
        expand_weight,
        expand_bias,
        reduce_weight,
        reduce_bias,
        mlp_scale,
    ) = weights
    normed_out, normed1, inv_std1 = norm_forward(start, norm1_gain, norm1_shift)
    normed_low = normed_out.astype(jnp.bfloat16)
    merged = project(normed_low, input_weight) + input_bias
    leading = gate1_weight.shape[0]
    conv_in = merged[..., leading:] * region
    mixed = (conv_forward(conv_in, conv_kernel) + conv_bias) * conv_scale
    gated = merged[..., :leading] * mixed[..., :leading]
    gated_lows = []
    projections = []
    offset = leading
    for weight, bias in (
        (gate1_weight, gate1_bias),
        (gate2_weight, gate2_bias),
        (gate3_weight, gate3_bias),
    ):
        gated_low = gated.astype(jnp.bfloat16)
        gated_lows.append(gated_low)
        projected = project(gated_low, weight) + bias
        projections.append(projected)
        width = weight.shape[1]
        gated = projected * mixed[..., offset : offset + width]
        offset = offset + width
    last_low = gated.astype(jnp.bfloat16)
    branch = project(last_low, output_weight) + output_bias
    middle = start + branch_scale * branch
    second_out, normed2, inv_std2 = norm_forward(middle, norm2_gain, norm2_shift)
    second_low = second_out.astype(jnp.bfloat16)
    before = project(second_low, expand_weight) + expand_bias
    active_low = jax.nn.gelu(before, approximate=False).astype(jnp.bfloat16)
    output = project(active_low, reduce_weight) + reduce_bias
    result = region * (middle + mlp_scale * output)
    kept_values = (
        normed1,
        inv_std1,
        normed_low,
        merged,
        conv_in,
        mixed,
        gated_lows[0],
        gated_lows[1],
        gated_lows[2],
        projections[0],
        projections[1],
        projections[2],
        last_low,
        branch,
        normed2,
        inv_std2,
        second_low,
        before,
        active_low,
        output,
    )
    return (result, kept_values)


def mlp_backward(incoming, region, weights, kept_values):
    (
        norm1_gain,
        norm1_shift,
        input_weight,
        input_bias,
        conv_kernel,
        conv_bias,
        gate1_weight,
        gate1_bias,
        gate2_weight,
        gate2_bias,
        gate3_weight,
        gate3_bias,
        output_weight,
        output_bias,
        branch_scale,
        norm2_gain,
        norm2_shift,
        expand_weight,
        expand_bias,
        reduce_weight,
        reduce_bias,
        mlp_scale,
    ) = weights
    (
        normed1,
        inv_std1,
        normed_low,
        merged,
        conv_in,
        mixed,
        low_one,
        low_two,
        low_three,
        proj_one,
        proj_two,
        proj_three,
        last_low,
        branch,
        normed2,
        inv_std2,
        second_low,
        before,
        active_low,
        output,
    ) = kept_values
    residual_grad = region * incoming
    mlp_scale_grad = row_total(residual_grad * output)
    output_grad = (mlp_scale * residual_grad).astype(jnp.bfloat16)
    reduce_weight_grad = outer_total(active_low, output_grad)
    reduce_bias_grad = row_total(output_grad)
    active_grad = project_back(output_grad, reduce_weight)
    before_grad = (active_grad * gelu_slope(before)).astype(jnp.bfloat16)
    expand_weight_grad = outer_total(second_low, before_grad)
    expand_bias_grad = row_total(before_grad)
    second_grad = project_back(before_grad, expand_weight)
    middle_norm, norm2_gain_grad, norm2_shift_grad = norm_backward(
        second_grad, normed2, inv_std2, norm2_gain
    )
    middle_grad = residual_grad + middle_norm
    return (
        middle_grad,
        (
            norm2_gain_grad,
            norm2_shift_grad,
            expand_weight_grad,
            expand_bias_grad,
            reduce_weight_grad,
            reduce_bias_grad,
            mlp_scale_grad,
        ),
    )


def gn_backward(middle_grad, region, weights, kept_values):
    (
        norm1_gain,
        norm1_shift,
        input_weight,
        input_bias,
        conv_kernel,
        conv_bias,
        gate1_weight,
        gate1_bias,
        gate2_weight,
        gate2_bias,
        gate3_weight,
        gate3_bias,
        output_weight,
        output_bias,
        branch_scale,
        norm2_gain,
        norm2_shift,
        expand_weight,
        expand_bias,
        reduce_weight,
        reduce_bias,
        mlp_scale,
    ) = weights
    (
        normed1,
        inv_std1,
        normed_low,
        merged,
        conv_in,
        mixed,
        low_one,
        low_two,
        low_three,
        proj_one,
        proj_two,
        proj_three,
        last_low,
        branch,
        normed2,
        inv_std2,
        second_low,
        before,
        active_low,
        output,
    ) = kept_values
    branch_scale_grad = row_total(middle_grad * branch)
    branch_grad = (branch_scale * middle_grad).astype(jnp.bfloat16)
    output_weight_grad = outer_total(last_low, branch_grad)
    output_bias_grad = row_total(branch_grad)
    gated_grad = project_back(branch_grad, output_weight)
    gate_weights = (gate1_weight, gate2_weight, gate3_weight)
    gated_lows = (low_one, low_two, low_three)
    projections = (proj_one, proj_two, proj_three)
    leading = gate1_weight.shape[0]
    offsets = (
        leading,
        leading + gate1_weight.shape[1],
        leading + gate1_weight.shape[1] + gate2_weight.shape[1],
    )
    mixed_parts = [None, None, None, None]
    weight_grads = [None, None, None]
    bias_grads = [None, None, None]
    for level in (2, 1, 0):
        width = gate_weights[level].shape[1]
        lower = offsets[level]
        proj_grad = (gated_grad * mixed[..., lower : lower + width]).astype(jnp.bfloat16)
        mixed_parts[level + 1] = gated_grad * projections[level]
        weight_grads[level] = outer_total(gated_lows[level], proj_grad)
        bias_grads[level] = row_total(proj_grad)
        gated_grad = project_back(proj_grad, gate_weights[level])
    mixed_parts[0] = gated_grad * merged[..., :leading]
    head_grad = gated_grad * mixed[..., :leading]
    conv_grad = jnp.concatenate(mixed_parts, axis=-1) * conv_scale
    conv_bias_grad = row_total(conv_grad)
    conv_in_grad, conv_kernel_grad = conv_backward(conv_grad, conv_in, conv_kernel)
    merged_grad = jnp.concatenate([head_grad, conv_in_grad * region], axis=-1).astype(jnp.bfloat16)
    input_weight_grad = outer_total(normed_low, merged_grad)
    input_bias_grad = row_total(merged_grad)
    normed_grad = project_back(merged_grad, input_weight)
    start_norm, norm1_gain_grad, norm1_shift_grad = norm_backward(
        normed_grad, normed1, inv_std1, norm1_gain
    )
    field_grad = region * (middle_grad + start_norm)
    return (
        field_grad,
        (
            norm1_gain_grad,
            norm1_shift_grad,
            input_weight_grad,
            input_bias_grad,
            conv_kernel_grad,
            conv_bias_grad,
            weight_grads[0],
            bias_grads[0],
            weight_grads[1],
            bias_grads[1],
            weight_grads[2],
            bias_grads[2],
            output_weight_grad,
            output_bias_grad,
            branch_scale_grad,
        ),
    )


def keep_slot(buffer, values, slot_index, is_valid):
    current = lax.dynamic_index_in_dim(buffer, slot_index, 0, keepdims=False)
    return lax.dynamic_update_index_in_dim(
        buffer, jnp.where(is_valid, values, current), slot_index, 0
    )


def on_device(
    images,
    cotangent,
    crop_class,
    norm1_gain,
    norm1_shift,
    input_weight,
    input_bias,
    conv_kernel,
    conv_bias,
    gate1_weight,
    gate1_bias,
    gate2_weight,
    gate2_bias,
    gate3_weight,
    gate3_bias,
    output_weight,
    output_bias,
    branch_scale,
    norm2_gain,
    norm2_shift,
    expand_weight,
    expand_bias,
    reduce_weight,
    reduce_bias,
    mlp_scale,
):
    section_index = lax.axis_index("section")
    first_section = section_index == 0
    stacked = (
        norm1_gain,
        norm1_shift,
        input_weight,
        input_bias,
        conv_kernel,
        conv_bias,
        gate1_weight,
        gate1_bias,
        gate2_weight,
        gate2_bias,
        gate3_weight,
        gate3_bias,
        output_weight,
        output_bias,
        branch_scale,
        norm2_gain,
        norm2_shift,
        expand_weight,
        expand_bias,
        reduce_weight,
        reduce_bias,
        mlp_scale,
    )
    weights = tuple(
        (
            entry[0] if slot_id in matrix_slots else entry[0].astype(jnp.float32)
            for slot_id, entry in enumerate(stacked)
        )
    )
    micro_count = images.shape[0]
    canvas = images.shape[2]
    places = jnp.arange(canvas, dtype=jnp.int32)
    side_of = jnp.where(crop_class == 0, SIDE_S, jnp.where(crop_class == 1, SIDE_M, canvas))
    inside = (places[None, None, :] < side_of[:, :, None]).astype(jnp.float32)
    regions = (inside[:, :, :, None] * inside[:, :, None, :])[..., None]
    received = jnp.zeros(images.shape[1:], jnp.bfloat16)
    outputs_low = jnp.zeros(images.shape, jnp.bfloat16)
    stash_buffers = None
    for moment in range(micro_count + 1):
        forward_slot = moment - section_index
        slot_now = jnp.clip(forward_slot, 0, micro_count - 1)
        is_valid = (forward_slot >= 0) & (forward_slot < micro_count)
        source = jnp.where(first_section, images[min(moment, micro_count - 1)], received).astype(
            jnp.float32
        )
        region = lax.dynamic_index_in_dim(regions, slot_now, 0, keepdims=False)
        entry_field = source * region
        result, kept_values = block_forward(entry_field, region, weights)
        result_low = result.astype(jnp.bfloat16)
        outputs_low = keep_slot(outputs_low, result_low, slot_now, is_valid)
        if stash_buffers is None:
            stash_buffers = tuple(
                (jnp.zeros((micro_count,) + entry.shape, entry.dtype) for entry in kept_values)
            )
        stash_buffers = tuple(
            (
                keep_slot(buffer, entry, slot_now, is_valid)
                for buffer, entry in zip(stash_buffers, kept_values)
            )
        )
        if moment < micro_count:
            received = shifted(result_low, "section", 1)
    early_totals = tuple((jnp.zeros(entry.shape[1:], jnp.float32) for entry in stacked[:15]))
    late_totals = tuple((jnp.zeros(entry.shape[1:], jnp.float32) for entry in stacked[15:]))
    sent_back = jnp.zeros(images.shape[1:], jnp.bfloat16)
    input_fields = jnp.zeros(images.shape, jnp.float32)
    for moment in range(micro_count + 1):
        back_slot = moment - 1 + section_index
        slot_back = jnp.clip(back_slot, 0, micro_count - 1)
        is_valid = (back_slot >= 0) & (back_slot < micro_count)
        incoming = jnp.where(
            first_section, sent_back, cotangent[min(moment, micro_count - 1)]
        ).astype(jnp.float32)
        incoming = incoming * is_valid.astype(jnp.float32)
        region = lax.dynamic_index_in_dim(regions, slot_back, 0, keepdims=False)
        kept_values = tuple(
            (
                lax.dynamic_index_in_dim(buffer, slot_back, 0, keepdims=False)
                for buffer in stash_buffers
            )
        )
        middle_grad, late_grads = mlp_backward(incoming, region, weights, kept_values)
        late_totals = tuple((total + fresh for total, fresh in zip(late_totals, late_grads)))
        field_grad, early_grads = gn_backward(middle_grad, region, weights, kept_values)
        early_totals = tuple((total + fresh for total, fresh in zip(early_totals, early_grads)))
        input_fields = keep_slot(input_fields, field_grad, slot_back, is_valid)
        if moment < micro_count:
            sent_back = shifted(field_grad.astype(jnp.bfloat16), "section", -1)
    summed = lax.psum(
        (
            early_totals[0],
            early_totals[1],
            early_totals[2],
            early_totals[3],
            early_totals[4],
            early_totals[5],
            early_totals[6],
            early_totals[7],
            early_totals[8],
            early_totals[9],
            early_totals[10],
            early_totals[11],
            early_totals[12],
            early_totals[13],
            early_totals[14],
            late_totals[0],
            late_totals[1],
            late_totals[2],
            late_totals[3],
            late_totals[4],
            late_totals[5],
            late_totals[6],
        ),
        "dp",
    )
    return (outputs_low[None], input_fields[None]) + tuple((entry[None] for entry in summed))


def solution(mesh):
    placed = (
        P(None, "dp", None, None, None),
        P(None, "dp", None, None, None),
        P(None, "dp"),
        P("section", None),
        P("section", None),
        P("section", None, None),
        P("section", None),
        P("section", None, None),
        P("section", None),
        P("section", None, None),
        P("section", None),
        P("section", None, None),
        P("section", None),
        P("section", None, None),
        P("section", None),
        P("section", None, None),
        P("section", None),
        P("section", None),
        P("section", None),
        P("section", None),
        P("section", None, None),
        P("section", None),
        P("section", None, None),
        P("section", None),
        P("section", None),
    )
    return jax.shard_map(
        on_device,
        mesh=mesh,
        in_specs=placed,
        out_specs=(
            P("section", None, "dp", None, None, None),
            P("section", None, "dp", None, None, None),
            P("section", None),
            P("section", None),
            P("section", None, None),
            P("section", None),
            P("section", None, None),
            P("section", None),
            P("section", None, None),
            P("section", None),
            P("section", None, None),
            P("section", None),
            P("section", None, None),
            P("section", None),
            P("section", None, None),
            P("section", None),
            P("section", None),
            P("section", None),
            P("section", None),
            P("section", None, None),
            P("section", None),
            P("section", None, None),
            P("section", None),
            P("section", None),
        ),
        check_vma=False,
    )
```

profile of v0, /device:TPU:0, one launch (start us, length us, event | category | flops | bytes accessed | tf_op | source)
XLA Modules:
  0.0 887.8 jit_solution(13937424760726616775)
XLA Ops:
  29.0 6.6 fusion.123
  40.8 4.8 bitcast_dynamic-update-slice_fusion.5
  45.7 1.5 bitcast_dynamic-update-slice_fusion.41
  47.2 3.3 collective-permute-start
  64.3 1.6 constant_dynamic-slice_fusion.48
  73.2 1.7 reshape.1962
  74.8 1.5 constant_dynamic-slice_fusion.3
  77.0 1.9 bitcast_dynamic-update-slice_fusion.10
  80.1 6.6 fusion.120
  91.5 4.9 bitcast_dynamic-update-slice_fusion.4
  97.3 1.4 collective-permute-start.1
  102.7 1.3 copy-done.9
  110.6 15.8 %fusion.117 = f32[1,16,16,960]{3,0,2,1:T(1,128)S(1)} fusion(bf16[7,7,1,960]{3,2,1,0:T(2,128)(2,1)S(1)} %copy-done.112, f32[1,16,16,960]{3,2,1,0:T(8,128)S(1)} %get-tuple-element.109), kind=kOutput, calls=%fused_computation.239 | convolution fusion | flops 115200000 | bytes 2060160 | tf_op jit(solution)/shard_map/conv_general_dilated | solution.py:64
  128.8 1.9 fusion.130
  132.1 2.4 convert_reduce_fusion.2
  134.4 1.4 fusion.196
  145.0 7.7 fusion.86
  155.2 1.7 collective-permute-start.2
  156.9 2.9 fusion.99
  160.1 1.9 fusion.217
  163.6 38.7 %fusion.135 = f32[7,7,1,960]{3,2,1,0:T(1,128)} fusion(f32[1,16,16,960]{3,0,2,1:T(1,128)S(1)} %squeeze.422, f32[1,16,16,960]{3,2,1,0:T(8,128)S(1)} %copy-done.83), kind=kOutput, calls=%fused_computation.268 | convolution fusion | flops 115200000 | bytes 2154240 | tf_op jit(solution)/shard_map/transpose(jvp())/conv_general_dilated | solution.py:64
  202.3 1.7 squeeze.423
  204.8 2.8 fusion.231
  207.5 5.1 bitcast_dynamic-update-slice_fusion.3
  212.7 2.8 fusion.105
  217.7 1.8 convert_reduce_fusion.1
  222.6 7.5 fusion.85
  231.3 1.9 fusion.216
  233.2 2.7 fusion.229
  236.0 2.8 fusion.103
  239.8 1.7 collective-permute-start.3
  241.5 2.3 fusion.100
  246.3 38.0 %convolution_add_fusion.19 = f32[7,7,1,960]{3,2,1,0:T(1,128)S(1)} fusion(f32[7,7,1,960]{3,2,1,0:T(1,128)S(1)} %copy-done.195, f32[1,16,16,960]{3,0,2,1:T(1,128)S(1)} %copy-done.80, f32[1,16,16,960]{3,2,1,0:T(8,128)S(1)} %get-tuple-element.183), kind=kOutput, calls=%fused_computation.187 | convolution fusion | flops 115247040 | bytes 2342400 | tf_op jit(solution)/shard_map/transpose(jvp())/conv_general_dilated | solution.py:64
  285.9 1.8 convert_reduce_fusion
  294.0 7.9 fusion.84
  302.2 2.3 fusion.101
  307.9 1.9 fusion.26
  309.8 38.6 %convolution_add_fusion.18 = f32[7,7,1,960]{3,2,1,0:T(1,128)} fusion(f32[7,7,1,960]{3,2,1,0:T(1,128)S(1)} %convolution_add_fusion.19, f32[1,16,16,960]{3,0,2,1:T(1,128)S(1)} %squeeze.424, f32[1,16,16,960]{3,2,1,0:T(8,128)S(1)} %get-tuple-element.187), kind=kOutput, calls=%fused_computation.186 | convolution fusion | flops 115247040 | bytes 2342400 | tf_op jit(solution)/shard_map/transpose(jvp())/conv_general_dilated | solution.py:64
  349.5 1.3 copy-done.194
  350.8 5.2 fusion.1
  357.0 2.9 fusion
  372.9 113.5 %all-reduce.5.cloned.1.call-done = (f32[1,512]{1,0:T(1,128)}, f32[1,512]{1,0:T(1,128)}, f32[1,1024]{1,0:T(1,128)}, f32[1,960]{1,0:T(1,128)}, f32[1,64,128]{2,1,0...) async-done(((f32[1,512]{1,0:T(1,128)}, f32[1,512]{1,0:T(1,128)}, ...) | async-done | bytes 68880 | tf_op jit(solution)/shard_map/psum | solution.py:469
  486.4 371.5 %all-reduce.7.cloned.1.call-done = (f32[1,512,1024]{2,1,0:T(8,128)}, f32[1,49,960]{2,0,1:T(1,128)}, f32[1,128,256]{2,1,0:T(8,128)}, f32[1,256,512]{2,1,0:T(8,128...) async-done(((f32[1,512,1024]{2,1,0:T(8,128)}, f32[1,49,960]{2,0,1:T(1,128)}, f32[1,128,256]{2,1,0:T(8,128)}, f32[1,256,512]{2,1,0:T(8,128)}, ...) | async-done | bytes 12377872 | tf_op jit(solution)/shard_map/psum | solution.py:469
  858.0 1.3 copy.274
  860.5 3.3 copy.276
  866.8 1.6 copy.282
  873.6 2.1 copy.291
  877.4 2.0 copy.293
  (665 shorter events, 130.7 us)
Async XLA Ops:
  7.2 38.5 %copy-start = (bf16[1,2048,512]{2,1,0:T(8,128)(2,1)S(1)}, bf16[1,2048,512]{2,1,0:T(8,128)(2,1)}, u32[]{:S(2)}) copy-start(bf16[1,2048,512]{2,1,0:T(8,128)(2,1)} %param.47) | copy-start | bytes 6291460
  7.2 19.5 %copy-start.28 = (bf16[2,1,16,16,512]{4,3,2,1,0:T(8,128)(2,1)S(1)}, bf16[2,1,16,16,512]{4,3,2,1,0:T(8,128)(2,1)}, u32[]{:S(2)}) copy-start(bf16[2,1,16,16,512]{4,3,2,1,0:T(8,128)(2,1)} %param.25) | copy-start | bytes 1572868
  7.2 479.2 %all-reduce.5.cloned.1.call-start = ((), (), s32[]{:S(2)}) async-start(), calls=%async_computation | async-start | bytes 138240 | tf_op jit(solution)/shard_map/psum | solution.py:469
  10.9 24.9 %copy-start.132 = (f32[1,960]{1,0:T(1,128)}, f32[1,960]{1,0:T(1,128)S(1)}, u32[]{:S(2)}) copy-start(f32[1,960]{1,0:T(1,128)S(1)} %convert_element_type.653) | copy-start | bytes 11524
  11.9 17.1 %copy-start.111 = (bf16[7,7,1,960]{3,2,1,0:T(2,128)(2,1)}, bf16[7,7,1,960]{3,2,1,0:T(2,128)(2,1)S(1)}, u32[]{:S(2)}) copy-start(bf16[7,7,1,960]{3,2,1,0:T(2,128)(2,1)S(1)} %reshape.1961) | copy-start | bytes 282244
  12.6 15.6 %copy-start.134 = (f32[1,1024]{1,0:T(1,128)}, f32[1,1024]{1,0:T(1,128)S(1)}, u32[]{:S(2)}) copy-start(f32[1,1024]{1,0:T(1,128)S(1)} %convert_element_type.652) | copy-start | bytes 12292
  13.3 14.9 %copy-start.119 = (f32[1,512]{1,0:T(1,128)}, f32[1,512]{1,0:T(1,128)S(1)}, u32[]{:S(2)}) copy-start(f32[1,512]{1,0:T(1,128)S(1)} %convert_element_type.651) | copy-start | bytes 6148
  15.8 43.1 %copy-start.117 = (f32[16,16]{1,0:T(8,128)}, f32[16,16]{1,0:T(8,128)S(1)}, u32[]{:S(2)}) copy-start(f32[16,16]{1,0:T(8,128)S(1)} %broadcast_multiply_fusion.18) | copy-start | bytes 3076
  17.0 11.3 %copy-start.128 = (f32[16,16]{1,0:T(8,128)}, f32[16,16]{1,0:T(8,128)S(1)}, u32[]{:S(2)}) copy-start(f32[16,16]{1,0:T(8,128)S(1)} %fusion.152) | copy-start | bytes 3076
  17.0 41.9 %copy-start.126 = (f32[16,16]{1,0:T(8,128)}, f32[16,16]{1,0:T(8,128)S(1)}, u32[]{:S(2)}) copy-start(f32[16,16]{1,0:T(8,128)S(1)} %add_rsqrt_fusion.5) | copy-start | bytes 3076
  26.5 30.1 %copy-start.123 = (f32[1,512]{1,0:T(1,128)}, f32[1,512]{1,0:T(1,128)S(1)}, u32[]{:S(2)}) copy-start(f32[1,512]{1,0:T(1,128)S(1)} %convert_element_type.659) | copy-start | bytes 6148
  28.2 25.8 %copy-start.3 = (f32[2,1,16,16,1024]{4,3,2,1,0:T(8,128)}, f32[2,1,16,16,1024]{4,3,2,1,0:T(8,128)S(1)}, u32[]{:S(2)}) copy-start(f32[2,1,16,16,1024]{4,3,2,1,0:T(8,128)S(1)} %get-tuple-element.230) | copy-start | bytes 6291460
  28.9 24.1 %copy-start.5 = (f32[2,1,16,16,960]{4,3,2,1,0:T(8,128)}, f32[2,1,16,16,960]{4,3,2,1,0:T(8,128)S(1)}, u32[]{:S(2)}) copy-start(f32[2,1,16,16,960]{4,3,2,1,0:T(8,128)S(1)} %get-tuple-element.112) | copy-start | bytes 5898244
  36.2 15.8 %copy-start.1 = (f32[2,1,16,16,960]{4,3,2,1,0:T(8,128)}, f32[2,1,16,16,960]{4,3,2,1,0:T(8,128)S(1)}, u32[]{:S(2)}) copy-start(f32[2,1,16,16,960]{4,3,2,1,0:T(8,128)S(1)} %get-tuple-element.157) | copy-start | bytes 5898244
  36.3 36.2 %copy-start.97 = (bf16[2,1,16,16,64]{4,3,2,1,0:T(8,128)(2,1)}, bf16[2,1,16,16,64]{4,3,2,1,0:T(8,128)(2,1)S(1)}, u32[]{:S(2)}) copy-start(bf16[2,1,16,16,64]{4,3,2,1,0:T(8,128)(2,1)S(1)} %get-tuple-element.147) | copy-start | bytes 196612
  36.7 19.1 %copy-start.68 = (bf16[2,1,16,16,128]{4,3,2,1,0:T(8,128)(2,1)}, bf16[2,1,16,16,128]{4,3,2,1,0:T(8,128)(2,1)S(1)}, u32[]{:S(2)}) copy-start(bf16[2,1,16,16,128]{4,3,2,1,0:T(8,128)(2,1)S(1)} %get-tuple-element.106) | copy-start | bytes 393220
  37.0 18.2 %copy-start.86 = (bf16[2,1,16,16,256]{4,3,2,1,0:T(8,128)(2,1)}, bf16[2,1,16,16,256]{4,3,2,1,0:T(8,128)(2,1)S(1)}, u32[]{:S(2)}) copy-start(bf16[2,1,16,16,256]{4,3,2,1,0:T(8,128)(2,1)S(1)} %get-tuple-element.100) | copy-start | bytes 786436
  37.7 13.6 %copy-start.52 = (bf16[2,1,16,16,512]{4,3,2,0,1:T(8,128)(2,1)}, bf16[2,1,16,16,512]{4,3,2,0,1:T(8,128)(2,1)S(1)}, u32[]{:S(2)}) copy-start(bf16[2,1,16,16,512]{4,3,2,0,1:T(8,128)(2,1)S(1)} %get-tuple-element.94) | copy-start | bytes 1572868
  47.2 29.1 %collective-permute-start = (bf16[1,16,16,512]{3,2,1,0:T(8,128)(2,1)}, bf16[1,16,16,512]{3,2,1,0:T(8,128)(2,1)}, u32[]{:S(2)}, u32[]{:S(2)}) collective-permute-start(bf16[1,16,16,512]{3,2,1,0:T(8,128)(2,1)} %bitcast.45), channel_id=1, source_target_pairs={{0,16},{1,17},{2,18},{3,19},{4,20},{5,21},{6,22},{7,23},{8,24},{9,... | collective-permute-start | bytes 786440 | tf_op jit(solution)/shard_map/ppermute | solution.py:19
  97.3 12.0 %collective-permute-start.1 = (bf16[1,16,16,512]{3,2,1,0:T(8,128)(2,1)S(1)}, bf16[1,16,16,512]{3,2,1,0:T(8,128)(2,1)S(1)}, u32[]{:S(2)}, u32[]{:S(2)}) collective-permute-start(bf16[1,16,16,512]{3,2,1,0:T(8,128)(2,1)S(1)} %get-tuple-element.164), channel_id=1, source_target_pairs={{0,16},{1,17},{2,18},{3,19},{4,20},{5,21},{6,22},{7,23},{8,24},{9,... | collective-permute-start | bytes 786440 | tf_op jit(solution)/shard_map/ppermute | solution.py:19
  138.0 167.8 %copy-start.22 = (f32[2,1,16,16,512]{4,3,2,0,1:T(8,128)}, f32[2,1,16,16,512]{4,3,2,0,1:T(8,128)S(1)}, u32[]{:S(2)}) copy-start(f32[2,1,16,16,512]{4,3,2,0,1:T(8,128)S(1)} %get-tuple-element.257) | copy-start | bytes 3145732
  143.8 8.9 %copy-start.43 = (f32[2,1,16,16,128]{4,3,2,1,0:T(8,128)}, f32[2,1,16,16,128]{4,3,2,1,0:T(8,128)S(1)}, u32[]{:S(2)}) copy-start(f32[2,1,16,16,128]{4,3,2,1,0:T(8,128)S(1)} %bitcast_dynamic-update-slice_fusion.49) | copy-start | bytes 786436
  145.0 7.7 copy-start.82
  155.2 61.4 %collective-permute-start.2 = (bf16[1,16,16,512]{3,2,1,0:T(8,128)(2,1)S(1)}, bf16[1,16,16,512]{3,2,1,0:T(8,128)(2,1)}, u32[]{:S(2)}, u32[]{:S(2)}) collective-permute-start(bf16[1,16,16,512]{3,2,1,0:T(8,128)(2,1)S(1)} %get-tuple-element.151), channel_id=1, source_target_pairs={{16,0},{17,1},{18,2},{19,3},{20,4},{21,5},{22,6},{23,7},{24,8},{25... | collective-permute-start | bytes 786440 | tf_op jit(solution)/shard_map/ppermute | solution.py:19
  239.8 45.6 %collective-permute-start.3 = (bf16[1,16,16,512]{3,2,1,0:T(8,128)(2,1)S(1)}, bf16[1,16,16,512]{3,2,1,0:T(8,128)(2,1)S(1)}, u32[]{:S(2)}, u32[]{:S(2)}) collective-permute-start(bf16[1,16,16,512]{3,2,1,0:T(8,128)(2,1)S(1)} %get-tuple-element.149), channel_id=1, source_target_pairs={{16,0},{17,1},{18,2},{19,3},{20,4},{21,5},{22,6},{23,7},{24,8},{25... | collective-permute-start | bytes 786440 | tf_op jit(solution)/shard_map/ppermute | solution.py:19
  246.3 38.0 %copy-start.71 = (bf16[2,1,16,16,128]{4,3,2,1,0:T(8,128)(2,1)S(1)}, bf16[2,1,16,16,128]{4,3,2,1,0:T(8,128)(2,1)}, u32[]{:S(2)}) copy-start(bf16[2,1,16,16,128]{4,3,2,1,0:T(8,128)(2,1)} %copy-done.70) | copy-start | bytes 393220
  246.3 38.9 %copy-start.89 = (bf16[2,1,16,16,256]{4,3,2,1,0:T(8,128)(2,1)S(1)}, bf16[2,1,16,16,256]{4,3,2,1,0:T(8,128)(2,1)}, u32[]{:S(2)}) copy-start(bf16[2,1,16,16,256]{4,3,2,1,0:T(8,128)(2,1)} %copy-done.88) | copy-start | bytes 786436
  309.8 38.6 %copy-start.85 = (bf16[1,16,16,512]{3,2,1,0:T(8,128)(2,1)S(1)}, bf16[1,16,16,512]{3,2,1,0:T(8,128)(2,1)}, u32[]{:S(2)}) copy-start(bf16[1,16,16,512]{3,2,1,0:T(8,128)(2,1)} %copy-done.84) | copy-start | bytes 786436
  356.9 7.6 copy-start.158
  356.9 8.2 copy-start.179
  356.9 8.8 copy-start.178
  356.9 9.3 %copy-start.164 = (f32[2048]{0:T(1024)S(1)}, f32[2048]{0:T(1024)}, u32[]{:S(2)}) copy-start(f32[2048]{0:T(1024)} %get-tuple-element.249) | copy-start | bytes 24580
  356.9 11.2 %copy-start.72 = (bf16[2,1,16,16,128]{4,3,2,1,0:T(8,128)(2,1)S(1)}, bf16[2,1,16,16,128]{4,3,2,1,0:T(8,128)(2,1)}, u32[]{:S(2)}) copy-start(bf16[2,1,16,16,128]{4,3,2,1,0:T(8,128)(2,1)} %copy-done.70) | copy-start | bytes 393220
  356.9 11.2 %copy-start.74 = (bf16[1,16,16,256]{3,2,1,0:T(8,128)(2,1)S(1)}, bf16[1,16,16,256]{3,2,1,0:T(8,128)(2,1)}, u32[]{:S(2)}) copy-start(bf16[1,16,16,256]{3,2,1,0:T(8,128)(2,1)} %copy-done.73) | copy-start | bytes 393220
  357.0 11.2 %copy-start.95 = (f32[128,256]{1,0:T(8,128)S(1)}, f32[128,256]{1,0:T(8,128)}, u32[]{:S(2)}) copy-start(f32[128,256]{1,0:T(8,128)} %convolution_bitcast_fusion.7) | copy-start | bytes 393220
  357.0 11.2 %copy-start.96 = (f32[128,256]{1,0:T(8,128)S(1)}, f32[128,256]{1,0:T(8,128)}, u32[]{:S(2)}) copy-start(f32[128,256]{1,0:T(8,128)} %convolution_bitcast_fusion.6) | copy-start | bytes 393220
  368.1 489.9 %all-reduce.7.cloned.1.call-start = ((), (), s32[]{:S(2)}) async-start(), calls=%async_computation.1 | async-start | bytes 24780800 | tf_op jit(solution)/shard_map/psum | solution.py:469
  857.9 10.4 %copy-start.182 = (f32[1,256]{1,0:T(1,128)S(1)}, f32[1,256]{1,0:T(1,128)}, u32[]{:S(2)}) copy-start(f32[1,256]{1,0:T(1,128)} %get-tuple-element.273) | copy-start | bytes 3076
  857.9 11.0 %copy-start.94 = (f32[1,256,512]{2,1,0:T(8,128)S(1)}, f32[1,256,512]{2,1,0:T(8,128)}, u32[]{:S(2)}) copy-start(f32[1,256,512]{2,1,0:T(8,128)} %get-tuple-element.274) | copy-start | bytes 1572868
  857.9 8.4 copy-start.187
  858.0 7.7 copy-start.144
  860.5 9.3 %copy-start.177 = (f32[1,512]{1,0:T(1,128)S(1)}, f32[1,512]{1,0:T(1,128)}, u32[]{:S(2)}) copy-start(f32[1,512]{1,0:T(1,128)} %get-tuple-element.275) | copy-start | bytes 6148
  860.5 9.9 %copy-start.81 = (f32[1,512,512]{2,1,0:T(8,128)S(1)}, f32[1,512,512]{2,1,0:T(8,128)}, u32[]{:S(2)}) copy-start(f32[1,512,512]{2,1,0:T(8,128)} %get-tuple-element.276) | copy-start | bytes 3145732
  860.5 13.1 %copy-start.37 = (f32[1,512,2048]{2,1,0:T(8,128)S(1)}, f32[1,512,2048]{2,1,0:T(8,128)}, u32[]{:S(2)}) copy-start(f32[1,512,2048]{2,1,0:T(8,128)} %get-tuple-element.281) | copy-start | bytes 12582916
  863.8 7.5 copy-start.176
  863.8 8.1 copy-start.175
  863.8 8.7 copy-start.174
  863.8 9.2 %copy-start.173 = (f32[1,512]{1,0:T(1,128)S(1)}, f32[1,512]{1,0:T(1,128)}, u32[]{:S(2)}) copy-start(f32[1,512]{1,0:T(1,128)} %get-tuple-element.280) | copy-start | bytes 6148
  (154 other events, 368.5 us)
Sparse Core Ops, SparseCore 0:
  368.2 118.1 all-reduce.4
  494.5 363.3 all-reduce.6
where the time goes:
time: 896 us; the launch traced here: 888 us
  waiting for transfers between devices  485 us (54%)
  matrix products  231 us (26%)
  local copies, waits for them, and re-layouts  81.2 us (9%)
  other arithmetic  65.2 us (7%)
  between operations  17.4 us (2%)
    psum x2, waiting for transfers between devices, on_device(): lax.psum((early_totals[0], early_totals[1], early_totals[2], early_totals...  485 us
    conv_general_dilated x9, matrix products, conv_forward(): lax.conv_general_dilated(source, taps, (1, 1), ((3, 3), (3, 3)), dimensio...  167 us
    unnamed x419, local copies, waits for them, and re-layouts  48.8 us
    dot_general x21, matrix products, outer_total(): jnp.einsum('ihwk,ihwn->kn', left, upward, preferred_element_type=jnp.floa...  32.2 us
    dynamic_update_slice x47, other arithmetic, keep_slot(): lax.dynamic_update_index_in_dim(buffer, jnp.where(is_valid, values, curre...  22.4 us
    dynamic_slice x38, local copies, waits for them, and re-layouts, keep_slot(): current = lax.dynamic_index_in_dim(buffer, slot_index, 0, keepdims=False)  19.8 us
  transfers between devices with their start and end apart: 6, of which 2 were waited for; matrix products, arithmetic and copies ran while one was open for 15% of the time, Pallas kernels for 0%

commit v1 on v0

v1 whole, which is shorter than its diff:
```python
import functools

import jax
import jax.numpy as jnp
from jax import lax
from jax.experimental import pallas as pl
from jax.experimental.pallas import tpu as pltpu
from jax.sharding import PartitionSpec as P

SIDE_S = 8
SIDE_M = 12
CANVAS = 16
PIX = CANVAS * CANVAS
C = 512
FF = 2048
LANES = 128
GROUPS = 8
EPS = 1e-06
KS = 7
PAD_ROWS = (CANVAS + 6) * CANVAS
BF = jnp.bfloat16
F32 = jnp.float32
VMEM_BYTES = 56 * 1024 * 1024

V_N1G, V_N1S, V_BIN, V_CB, V_B1, V_B2, V_B3, V_BO, V_BS, V_N2G, V_N2S, V_BE, V_BR, V_MS = range(14)
VEC_ROWS = 16


def nn(a, b):
    return jnp.dot(a, b, preferred_element_type=F32)


def nt(a, b):
    return lax.dot_general(a, b, (((1,), (1,)), ((), ())), preferred_element_type=F32)


def tn(a, b):
    return lax.dot_general(a, b, (((0,), (0,)), ((), ())), preferred_element_type=F32)


def colsum(v):
    return jnp.sum(v, axis=0, keepdims=True)


def wide(m, n):
    return jnp.concatenate([m] * n, axis=1)


def fill_mask(mask_ref, side):
    r = lax.broadcasted_iota(jnp.int32, (PIX, LANES), 0)
    inside = ((r // CANVAS) < side) & ((r % CANVAS) < side)
    mask_ref[...] = inside.astype(F32)


def start_select(sel, pairs, sems):
    for i, (own, other, dst) in enumerate(pairs):

        @pl.when(sel == 0)
        def _():
            pltpu.make_async_copy(own, dst, sems.at[i]).start()

        @pl.when(sel != 0)
        def _():
            pltpu.make_async_copy(other, dst, sems.at[i]).start()


def wait_select(i, pairs, sems):
    own, other, dst = pairs[i]
    pltpu.make_async_copy(own, dst, sems.at[i]).wait()


def conv_rows(src_ref, taps_ref, flip, bias, store):
    def row(h, carry):
        accs = [bias] * CANVAS if bias is not None else [None] * CANVAS
        for a in range(KS):
            ks = []
            for e in range(KS):
                t = (KS - 1 - a) * KS + (KS - 1 - e) if flip else a * KS + e
                ks.append(taps_ref[t * GROUPS : (t + 1) * GROUPS, :])
            for w2 in range(CANVAS):
                x = src_ref[pl.ds(pl.multiple_of(((h + a) * CANVAS + w2) * GROUPS, GROUPS), GROUPS), :]
                for e in range(KS):
                    w = w2 + 3 - e
                    if 0 <= w < CANVAS:
                        term = x * ks[e]
                        accs[w] = term if accs[w] is None else accs[w] + term
        for w in range(CANVAS):
            store(h * CANVAS + w, accs[w])
        return carry

    lax.fori_loop(0, CANVAS, row, 0)


def zero_border(ref):
    zeros = jnp.zeros((3 * CANVAS * GROUPS, LANES), F32)
    ref[0 : 3 * CANVAS * GROUPS, :] = zeros
    ref[(PAD_ROWS - 3 * CANVAS) * GROUPS :, :] = zeros


def lane_group(ref, g, rows=PIX, base=0):
    return ref[pl.ds(base + g, rows, stride=GROUPS), :]


def forward_kernel(
    meta, x_ref, vec_ref, taps_ref, cbias_ref,
    win_a, win_b, w1_a, w1_b, w2_a, w2_b, w3_a, w3_b, wo_a, wo_b, we_a, we_b, wr_a, wr_b,
    n1_ref, cin_ref, mix_ref, p_ref, gl_ref, mid_ref, br_ref, n2_ref, act_ref, slope_ref, out_ref, res_ref,
    mask_ref, mx_ref, win, w1, w2, w3, wo, we, wr, sems,
):
    pairs = [
        (win_a, win_b, win), (w1_a, w1_b, w1.at[0:64]), (w2_a, w2_b, w2), (w3_a, w3_b, w3),
        (wo_a, wo_b, wo), (we_a, we_b, we), (wr_a, wr_b, wr),
    ]
    start_select(meta[0], pairs, sems)
    w1[64:128, :] = jnp.zeros((64, LANES), BF)
    fill_mask(mask_ref, meta[1])
    zero_border(cin_ref)

    def vec(row, lo, n):
        return vec_ref[row : row + 1, lo : lo + n]

    def norm_in(i, carry):
        r = pl.ds(pl.multiple_of(i * 32, 32), 32)
        start = x_ref[r, :].astype(F32) * wide(mask_ref[r, :], 4)
        cen = start - jnp.mean(start, axis=-1, keepdims=True)
        inv = lax.rsqrt(jnp.mean(cen * cen, axis=-1, keepdims=True) + EPS)
        n1_ref[r, :] = (cen * inv * vec(V_N1G, 0, C) + vec(V_N1S, 0, C)).astype(BF)
        return carry

    lax.fori_loop(0, PIX // 32, norm_in, 0)
    wait_select(0, pairs, sems)
    for n in range(4):
        m = nn(n1_ref[...], win[:, n * 256 : (n + 1) * 256]) + vec(V_BIN, n * 256, 256)
        for half in range(2):
            g = 2 * n + half
            v = m[:, half * LANES : (half + 1) * LANES] * mask_ref[...]
            cin_ref[pl.ds(3 * CANVAS * GROUPS + g, PIX, stride=GROUPS), :] = v
            if g == 0:
                p_ref[:, 0:LANES] = v
    bias = cbias_ref[...]

    def keep(pixel, acc):
        mx_ref[pl.ds(pl.multiple_of(pixel * GROUPS, GROUPS), GROUPS), :] = acc * (1.0 / 3.0)

    conv_rows(cin_ref, taps_ref, False, bias, keep)
    for g in range(GROUPS):
        mix_ref[:, g * LANES : (g + 1) * LANES] = lane_group(mx_ref, g)
    for i in (1, 2, 3, 4):
        wait_select(i, pairs, sems)
    gl_ref[:, 0:128] = (p_ref[:, 0:128] * pltpu.roll(mix_ref[:, 0:128], 64, 1)).astype(BF)
    p1 = nn(gl_ref[:, 0:128], w1[...]) + vec(V_B1, 0, 128)
    p_ref[:, 128:256] = p1
    gl_ref[:, 128:256] = (p1 * mix_ref[:, 128:256]).astype(BF)
    p2 = nn(gl_ref[:, 128:256], w2[...]) + vec(V_B2, 0, 256)
    p_ref[:, 256:512] = p2
    gl_ref[:, 256:512] = (p2 * mix_ref[:, 256:512]).astype(BF)
    for n in range(2):
        c = 256 * n
        p3 = nn(gl_ref[:, 256:512], w3[:, c : c + 256]) + vec(V_B3, c, 256)
        p_ref[:, 512 + c : 768 + c] = p3
        gl_ref[:, 512 + c : 768 + c] = (p3 * mix_ref[:, 512 + c : 768 + c]).astype(BF)
    for n in range(2):
        c = 256 * n
        br = nn(gl_ref[:, 512:1024], wo[:, c : c + 256]) + vec(V_BO, c, 256)
        br_ref[:, c : c + 256] = br.astype(BF)
        start = x_ref[:, c : c + 256].astype(F32) * wide(mask_ref[...], 2)
        mid_ref[:, c : c + 256] = start + vec(V_BS, c, 256) * br

    def norm_mid(i, carry):
        r = pl.ds(pl.multiple_of(i * 32, 32), 32)
        mid = mid_ref[r, :]
        cen = mid - jnp.mean(mid, axis=-1, keepdims=True)
        inv = lax.rsqrt(jnp.mean(cen * cen, axis=-1, keepdims=True) + EPS)
        n2_ref[r, :] = (cen * inv * vec(V_N2G, 0, C) + vec(V_N2S, 0, C)).astype(BF)
        return carry

    lax.fori_loop(0, PIX // 32, norm_mid, 0)
    wait_select(5, pairs, sems)
    wait_select(6, pairs, sems)
    for j in range(8):
        c = 256 * j
        pre = nn(n2_ref[...], we[:, c : c + 256]) + vec(V_BE, c, 256)
        cum = 0.5 * (1.0 + lax.erf(pre * 0.7071067811865476))
        act_ref[:, c : c + 256] = (pre * cum).astype(BF)
        slope = cum + pre * jnp.exp(-0.5 * pre * pre) * 0.3989422804014327
        slope_ref[:, c : c + 256] = slope.astype(BF)
    for n in range(2):
        c = 256 * n
        out = nn(act_ref[...], wr[:, c : c + 256]) + vec(V_BR, c, 256)
        out_ref[:, c : c + 256] = out.astype(BF)
        res = wide(mask_ref[...], 2) * (mid_ref[:, c : c + 256] + vec(V_MS, c, 256) * out)
        res_ref[:, c : c + 256] = res.astype(BF)


def piece_rows(meta, p, rows):
    mask = meta[2 + ((p >> 4) & 1)]
    return pl.multiple_of((p ^ mask) * rows, 32)


def mlp_kernel(
    meta, dy_ref, vec_ref, n2_ref, act_ref, slope_ref, out_ref, mid_ref, we_a, we_b, wr_a, wr_b,
    dmid_ref, mvec_ref, keep_ref, send_ref,
    mask_ref, dout_ref, dpre_ref, dn2_ref, bucket, we, wr, sems,
):
    pairs = [(wr_a, wr_b, wr), (we_a, we_b, we)]
    start_select(meta[0], pairs, sems)
    fill_mask(mask_ref, meta[1])
    mvec_ref[...] = jnp.zeros_like(mvec_ref)

    def vec(row, lo, n):
        return vec_ref[row : row + 1, lo : lo + n]

    for n in range(2):
        c = 256 * n
        dyr = dy_ref[:, c : c + 256].astype(F32) * wide(mask_ref[...], 2)
        dmid_ref[:, c : c + 256] = dyr
        dout = (vec(V_MS, c, 256) * dyr).astype(BF)
        dout_ref[:, c : c + 256] = dout
        mvec_ref[3:4, c : c + 256] = colsum(dout.astype(F32))
        mvec_ref[4:5, c : c + 256] = colsum(dyr * out_ref[:, c : c + 256].astype(F32))
    wait_select(0, pairs, sems)
    for j in range(8):
        c = 256 * j
        dw = tn(act_ref[:, c : c + 256], dout_ref[...]).astype(BF)
        for q in range(8):
            p = 8 * j + q
            bucket[pl.ds(piece_rows(meta, p, 64), 32), :] = dw[32 * q : 32 * q + 32, :]
        dact = nt(dout_ref[...], wr[c : c + 256, :])
        dpre = (dact * slope_ref[:, c : c + 256].astype(F32)).astype(BF)
        dpre_ref[:, c : c + 256] = dpre
        mvec_ref[2:3, c : c + 256] = colsum(dpre.astype(F32))
    wait_select(1, pairs, sems)
    for cb in range(4):
        dw = tn(n2_ref[...], dpre_ref[:, 512 * cb : 512 * cb + 512]).astype(BF)
        for q in range(16):
            p = 16 * cb + q
            bucket[pl.ds(pl.multiple_of(piece_rows(meta, p, 64) + 32, 32), 32), :] = dw[32 * q : 32 * q + 32, :]
    keep_copy = pltpu.make_async_copy(bucket.at[0:2048], keep_ref, sems.at[2])
    send_copy = pltpu.make_async_copy(bucket.at[2048:4096], send_ref, sems.at[3])
    send_copy.start()
    keep_copy.start()
    for n in range(2):
        c = 256 * n
        dn2_ref[:, c : c + 256] = nt(dpre_ref[...], we[c : c + 256, :])

    def norm_back(i, carry):
        dgain, dshift = carry
        r = pl.ds(pl.multiple_of(i * 32, 32), 32)
        mid = mid_ref[r, :]
        cen = mid - jnp.mean(mid, axis=-1, keepdims=True)
        inv = lax.rsqrt(jnp.mean(cen * cen, axis=-1, keepdims=True) + EPS)
        xhat = cen * inv
        up = dn2_ref[r, :]
        g = up * vec(V_N2G, 0, C)
        inner = g - jnp.mean(g, axis=-1, keepdims=True) - xhat * jnp.mean(g * xhat, axis=-1, keepdims=True)
        dmid_ref[r, :] = dmid_ref[r, :] + inv * inner
        return dgain + colsum(up * xhat), dshift + colsum(up)

    zero = jnp.zeros((1, C), F32)
    dgain, dshift = lax.fori_loop(0, PIX // 32, norm_back, (zero, zero))
    mvec_ref[0:1, 0:C] = dgain
    mvec_ref[1:2, 0:C] = dshift
    send_copy.wait()
    keep_copy.wait()


def gn_kernel(
    meta, x_ref, dmid_ref, mvec_ref, vec_ref, taps_ref, n1_ref, cin_ref, mix_ref, p_ref, gl_ref, br_ref,
    win_a, win_b, w1_a, w1_b, w2_a, w2_b, w3_a, w3_b, wo_a, wo_b,
    dv_ref, dvb_ref, keep_ref, send_ref,
    mask_ref, dbr_ref, dg_ref, dp_ref, dmix_ref, dcp_ref, ds_ref, dk_ref, dmg_ref, dn1_ref, bucket,
    win, w1, w2, w3, wo, sems,
):
    pairs = [
        (wo_a, wo_b, wo), (w3_a, w3_b, w3), (w2_a, w2_b, w2), (w1_a, w1_b, w1.at[0:64]), (win_a, win_b, win),
    ]
    start_select(meta[0], pairs, sems)
    w1[64:128, :] = jnp.zeros((64, LANES), BF)
    fill_mask(mask_ref, meta[1])
    zero_border(dcp_ref)

    def vec(row, lo, n):
        return vec_ref[row : row + 1, lo : lo + n]

    def put(p, val, sub=0):
        n = val.shape[0]
        bucket[pl.ds(pl.multiple_of(piece_rows(meta, p, 32) + sub, 16), n), :] = val

    tail = {}

    def vec_grad(row, val):
        tail[row] = val

    dbs, dbo = [], []
    for n in range(2):
        c = 256 * n
        dm = dmid_ref[:, c : c + 256]
        dbs.append(colsum(dm * br_ref[:, c : c + 256].astype(F32)))
        dbr = (vec(V_BS, c, 256) * dm).astype(BF)
        dbr_ref[:, c : c + 256] = dbr
        dbo.append(colsum(dbr.astype(F32)))
    wait_select(0, pairs, sems)
    dw = tn(gl_ref[:, 512:1024], dbr_ref[...]).astype(BF)
    for q in range(16):
        put(32 + q, dw[32 * q : 32 * q + 32, :])
    wait_select(1, pairs, sems)
    wait_select(2, pairs, sems)
    wait_select(3, pairs, sems)
    db3 = []
    for n in range(2):
        c = 256 * n
        dg = nt(dbr_ref[...], wo[c : c + 256, :])
        dp = (dg * mix_ref[:, 512 + c : 768 + c]).astype(BF)
        dmix_ref[:, 512 + c : 768 + c] = dg * p_ref[:, 512 + c : 768 + c] * (1.0 / 3.0)
        dp_ref[:, 512 + c : 768 + c] = dp
        db3.append(colsum(dp.astype(F32)))
    dw = tn(gl_ref[:, 256:512], dp_ref[:, 512:1024]).astype(BF)
    for q in range(8):
        put(48 + q, dw[32 * q : 32 * q + 32, :])
    dg = nt(dp_ref[:, 512:1024], w3[...])
    dp = (dg * mix_ref[:, 256:512]).astype(BF)
    dmix_ref[:, 256:512] = dg * p_ref[:, 256:512] * (1.0 / 3.0)
    dp_ref[:, 256:512] = dp
    db2 = colsum(dp.astype(F32))
    dw = tn(gl_ref[:, 128:256], dp_ref[:, 256:512]).astype(BF)
    dw = jnp.concatenate([dw[0:64, :], dw[64:128, :]], axis=1)
    put(56, dw[0:32, :])
    put(57, dw[32:64, :])
    dg = nt(dp_ref[:, 256:512], w2[...])
    dp = (dg * mix_ref[:, 128:256]).astype(BF)
    dmix_ref[:, 128:256] = dg * p_ref[:, 128:256] * (1.0 / 3.0)
    dp_ref[:, 128:256] = dp
    db1 = colsum(dp.astype(F32))
    dw1 = tn(gl_ref[:, 0:128], dp_ref[:, 128:256]).astype(BF)
    put(62, jnp.concatenate([dw1[16 * i : 16 * i + 16, :] for i in range(4)], axis=1))
    put(62, jnp.zeros((16, 512), BF), 16)
    dg = nt(dp_ref[:, 128:256], w1[...])
    dmix_ref[:, 0:128] = pltpu.roll(dg * p_ref[:, 0:128], 64, 1) * (1.0 / 3.0)
    dg_ref[...] = dg * pltpu.roll(mix_ref[:, 0:128], 64, 1)
    for g in range(GROUPS):
        dcp_ref[pl.ds(3 * CANVAS * GROUPS + g, PIX, stride=GROUPS), :] = dmix_ref[:, g * LANES : (g + 1) * LANES]

    def keep(pixel, acc):
        ds_ref[pl.ds(pl.multiple_of(pixel * GROUPS, GROUPS), GROUPS), :] = acc

    conv_rows(dcp_ref, taps_ref, True, None, keep)

    def vreg(ref, index):
        return ref[pl.ds(pl.multiple_of(index * GROUPS, GROUPS), GROUPS), :]

    dk_ref[...] = jnp.zeros_like(dk_ref)
    for taps in ((0, 1), (2, 3), (4, 5), (6,)):

        def row(h, accs):
            accs = list(accs)
            ds = [vreg(dcp_ref, (h + 3) * CANVAS + w) for w in range(CANVAS)]
            for i, a in enumerate(taps):
                for w2 in range(CANVAS):
                    x = vreg(cin_ref, (h + a) * CANVAS + w2)
                    for e in range(KS):
                        w = w2 + 3 - e
                        if 0 <= w < CANVAS:
                            accs[i * KS + e] = accs[i * KS + e] + x * ds[w]
            if len(taps) == 1:
                for w in range(CANVAS):
                    accs[KS] = accs[KS] + ds[w]
            return tuple(accs)

        count = len(taps) * KS + (1 if len(taps) == 1 else 0)
        accs = lax.fori_loop(0, CANVAS, row, tuple(jnp.zeros((GROUPS, LANES), F32) for _ in range(count)))
        for i in range(count):
            t = taps[0] * KS + i
            dk_ref[t * GROUPS : (t + 1) * GROUPS, :] = accs[i]
    for half in range(2):
        dk = jnp.concatenate([lane_group(dk_ref, 4 * half + i, 64) for i in range(4)], axis=1).astype(BF)
        put(58 + 2 * half, dk[0:32, :])
        put(59 + 2 * half, dk[32:64, :])
    dbin = []
    for g in range(GROUPS):
        d = lane_group(ds_ref, g) * mask_ref[...]
        if g == 0:
            d = d + dg_ref[...]
        d = d.astype(BF)
        dmg_ref[:, g * LANES : (g + 1) * LANES] = d
        dbin.append(colsum(d.astype(F32)))
    wait_select(4, pairs, sems)
    for cb in range(2):
        dw = tn(n1_ref[...], dmg_ref[:, 512 * cb : 512 * cb + 512]).astype(BF)
        for q in range(16):
            put(16 * cb + q, dw[32 * q : 32 * q + 32, :])
    for n in range(2):
        c = 256 * n
        dn1_ref[:, c : c + 256] = nt(dmg_ref[...], win[c : c + 256, :])

    def norm_back(i, carry):
        dgain, dshift = carry
        r = pl.ds(pl.multiple_of(i * 32, 32), 32)
        m = wide(mask_ref[r, :], 4)
        start = x_ref[r, :].astype(F32) * m
        cen = start - jnp.mean(start, axis=-1, keepdims=True)
        inv = lax.rsqrt(jnp.mean(cen * cen, axis=-1, keepdims=True) + EPS)
        xhat = cen * inv
        up = dn1_ref[r, :]
        g = up * vec(V_N1G, 0, C)
        inner = g - jnp.mean(g, axis=-1, keepdims=True) - xhat * jnp.mean(g * xhat, axis=-1, keepdims=True)
        dv = m * (dmid_ref[r, :] + inv * inner)
        dv_ref[r, :] = dv
        dvb_ref[r, :] = dv.astype(BF)
        return dgain + colsum(up * xhat), dshift + colsum(up)

    zero = jnp.zeros((1, C), F32)
    dgain, dshift = lax.fori_loop(0, PIX // 32, norm_back, (zero, zero))
    z = jnp.zeros((1, LANES), F32)
    rows = [
        dgain,
        dshift,
        jnp.concatenate(dbin[0:4], axis=1),
        jnp.concatenate(dbin[4:8], axis=1),
        jnp.concatenate([db1, z, z, z], axis=1),
        jnp.concatenate([db2, z, z], axis=1),
        jnp.concatenate(db3, axis=1),
        jnp.concatenate(dbo, axis=1),
        jnp.concatenate(dbs, axis=1),
        mvec_ref[0:1, 0:C],
        mvec_ref[1:2, 0:C],
        mvec_ref[2:3, 0:512],
        mvec_ref[2:3, 512:1024],
        mvec_ref[2:3, 1024:1536],
        mvec_ref[2:3, 1536:2048],
        mvec_ref[3:4, 0:C],
        mvec_ref[4:5, 0:C],
    ]
    rows.append(jnp.zeros((32 - len(rows), C), F32))
    put(63, jnp.concatenate(rows, axis=0).astype(BF))
    send_copy = pltpu.make_async_copy(bucket.at[1024:2048], send_ref, sems.at[5])
    keep_copy = pltpu.make_async_copy(bucket.at[0:1024], keep_ref, sems.at[6])
    send_copy.start()
    keep_copy.start()
    send_copy.wait()
    keep_copy.wait()


def start_pieces(meta, rows, own0, other0, own1, other1, buf, sems):
    for p in range(64):
        mask = meta[2 + ((p >> 4) & 1)]
        rel = p ^ mask
        off = pl.multiple_of((rel & 31) * rows, 32)
        far = rel >> 5
        dst = buf.at[p * rows : (p + 1) * rows]
        sem = sems.at[p // 8]
        for sec, own, other in ((0, own0, other0), (1, own1, other1)):

            @pl.when((meta[4] == sec) & (far == 0))
            def _():
                pltpu.make_async_copy(own.at[pl.ds(off, rows)], dst, sem).start()

            @pl.when((meta[4] == sec) & (far == 1))
            def _():
                pltpu.make_async_copy(other.at[pl.ds(off, rows)], dst, sem).start()


def wait_pieces(i, rows, own0, buf, sems):
    part = pl.ds(i * 8 * rows, 8 * rows)
    pltpu.make_async_copy(own0.at[pl.ds(0, 8 * rows)], buf.at[part], sems.at[i]).wait()


def mlp_finish(meta, own0, other0, own1, other1, wr_ref, we_ref, buf, sems):
    start_pieces(meta, 64, own0, other0, own1, other1, buf, sems)
    for i in range(8):
        wait_pieces(i, 64, own0, buf, sems)
        for q in range(8):
            p = 8 * i + q
            wr_ref[32 * p : 32 * p + 32, :] = buf[64 * p : 64 * p + 32, :].astype(F32)
            cb, r = p // 16, p % 16
            we_ref[32 * r : 32 * r + 32, 512 * cb : 512 * cb + 512] = buf[64 * p + 32 : 64 * p + 64, :].astype(F32)


def gn_finish(
    meta, own0, other0, own1, other1,
    n1g, n1s, win, bin_, conv, w1, b1, w2, b2, w3, b3, wo, bo, bs, n2g, n2s, be, br, ms,
    buf, sems,
):
    start_pieces(meta, 32, own0, other0, own1, other1, buf, sems)
    for i in range(8):
        wait_pieces(i, 32, own0, buf, sems)
    for cb in range(2):
        win[:, 512 * cb : 512 * cb + 512] = buf[512 * cb : 512 * cb + 512, :].astype(F32)
    wo[...] = buf[1024:1536, :].astype(F32)
    w3[...] = buf[1536:1792, :].astype(F32)
    for i in range(2):
        w2[64 * i : 64 * i + 64, :] = buf[1792:1856, 256 * i : 256 * i + 256].astype(F32)
        conv[:, 512 * i : 512 * i + 512] = buf[1856 + 64 * i : 1920 + 64 * i, :].astype(F32)
    for i in range(4):
        w1[16 * i : 16 * i + 16, :] = buf[1984:2000, 128 * i : 128 * i + 128].astype(F32)
    v = buf[2016:2048, :].astype(F32)
    n1g[...] = v[0:1]
    n1s[...] = v[1:2]
    bin_[:, 0:512] = v[2:3]
    bin_[:, 512:1024] = v[3:4]
    b1[...] = v[4:5, 0:128]
    b2[...] = v[5:6, 0:256]
    b3[...] = v[6:7]
    bo[...] = v[7:8]
    bs[...] = v[8:9]
    n2g[...] = v[9:10]
    n2s[...] = v[10:11]
    for i in range(4):
        be[:, 512 * i : 512 * i + 512] = v[11 + i : 12 + i]
    br[...] = v[15:16]
    ms[...] = v[16:17]


SMEM = pl.BlockSpec(memory_space=pltpu.SMEM)
VM = pl.BlockSpec(memory_space=pltpu.VMEM)
ANY = pl.BlockSpec(memory_space=pl.ANY)


def sds(shape, dtype):
    return jax.ShapeDtypeStruct(shape, dtype)


def params():
    return pltpu.CompilerParams(vmem_limit_bytes=VMEM_BYTES)


def cost(flops, bytes_accessed):
    return pl.CostEstimate(flops=flops, bytes_accessed=bytes_accessed, transcendentals=0)


def run_forward(meta, x, vec, taps, cbias, mats):
    outs = [
        sds((PIX, C), BF), sds((PAD_ROWS * GROUPS, LANES), F32), sds((PIX, 1024), F32), sds((PIX, 1024), F32),
        sds((PIX, 1024), BF), sds((PIX, C), F32), sds((PIX, C), BF), sds((PIX, C), BF), sds((PIX, FF), BF),
        sds((PIX, FF), BF), sds((PIX, C), BF), sds((PIX, C), BF),
    ]
    flat = [r for pair in mats for r in pair]
    return pl.pallas_call(
        forward_kernel,
        name="block_forward",
        out_shape=outs,
        in_specs=[SMEM, VM, VM, VM, VM] + [ANY] * 14,
        out_specs=[VM] * len(outs),
        scratch_shapes=[
            pltpu.VMEM((PIX, LANES), F32), pltpu.VMEM((PIX * GROUPS, LANES), F32),
            pltpu.VMEM((C, 1024), BF), pltpu.VMEM((128, 128), BF), pltpu.VMEM((128, 256), BF),
            pltpu.VMEM((256, 512), BF), pltpu.VMEM((512, 512), BF), pltpu.VMEM((C, FF), BF),
            pltpu.VMEM((FF, C), BF), pltpu.SemaphoreType.DMA((7,)),
        ],
        compiler_params=params(),
        cost_estimate=cost(5_000_000_000, 14_000_000),
    )(meta, x, vec, taps, cbias, *flat)


def run_mlp(meta, dy, vec, n2, act, slope, out, mid, mats):
    outs = [sds((PIX, C), F32), sds((8, FF), F32), sds((2048, 512), BF), sds((2048, 512), BF)]
    return pl.pallas_call(
        mlp_kernel,
        name="mlp_backward",
        out_shape=outs,
        in_specs=[SMEM] + [VM] * 7 + [ANY] * 4,
        out_specs=[VM, VM, ANY, ANY],
        scratch_shapes=[
            pltpu.VMEM((PIX, LANES), F32), pltpu.VMEM((PIX, C), BF), pltpu.VMEM((PIX, FF), BF),
            pltpu.VMEM((PIX, C), F32), pltpu.VMEM((4096, 512), BF),
            pltpu.VMEM((C, FF), BF), pltpu.VMEM((FF, C), BF), pltpu.SemaphoreType.DMA((4,)),
        ],
        compiler_params=params(),
        cost_estimate=cost(5_000_000_000, 14_000_000),
    )(meta, dy, vec, n2, act, slope, out, mid, *mats[5], *mats[6])


def run_gn(meta, x, dmid, mvec, vec, taps, n1, cin, mix, p, gl, br, mats):
    outs = [sds((PIX, C), F32), sds((PIX, C), BF), sds((1024, 512), BF), sds((1024, 512), BF)]
    flat = [r for pair in mats[:5] for r in pair]
    return pl.pallas_call(
        gn_kernel,
        name="gnconv_backward",
        out_shape=outs,
        in_specs=[SMEM] + [VM] * 11 + [ANY] * 10,
        out_specs=[VM, VM, ANY, ANY],
        scratch_shapes=[
            pltpu.VMEM((PIX, LANES), F32), pltpu.VMEM((PIX, C), BF), pltpu.VMEM((PIX, LANES), F32),
            pltpu.VMEM((PIX, 1024), BF), pltpu.VMEM((PIX, 1024), F32), pltpu.VMEM((PAD_ROWS * GROUPS, LANES), F32),
            pltpu.VMEM((PIX * GROUPS, LANES), F32), pltpu.VMEM((64 * GROUPS, LANES), F32),
            pltpu.VMEM((PIX, 1024), BF), pltpu.VMEM((PIX, C), F32), pltpu.VMEM((2048, 512), BF),
            pltpu.VMEM((C, 1024), BF), pltpu.VMEM((128, 128), BF), pltpu.VMEM((128, 256), BF),
            pltpu.VMEM((256, 512), BF), pltpu.VMEM((512, 512), BF), pltpu.SemaphoreType.DMA((7,)),
        ],
        compiler_params=params(),
        cost_estimate=cost(5_000_000_000, 14_000_000),
    )(meta, x, dmid, mvec, vec, taps, n1, cin, mix, p, gl, br, *flat)


def run_mlp_finish(meta, halves):
    outs = [sds((FF, C), F32), sds((C, FF), F32)]
    return pl.pallas_call(
        mlp_finish,
        name="mlp_finish",
        out_shape=outs,
        in_specs=[SMEM] + [ANY] * 4,
        out_specs=[VM] * 2,
        scratch_shapes=[pltpu.VMEM((4096, 512), BF), pltpu.SemaphoreType.DMA((8,))],
        compiler_params=params(),
        cost_estimate=cost(1_000_000, 12_000_000),
    )(meta, *halves)


def run_gn_finish(meta, halves):
    widths = [512, 512, (512, 1024), 1024, (64, 1024), (64, 128), 128, (128, 256), 256, (256, 512), 512,
              (512, 512), 512, 512, 512, 512, 2048, 512, 512]
    outs = [sds((1, w) if isinstance(w, int) else w, F32) for w in widths]
    return pl.pallas_call(
        gn_finish,
        name="gn_finish",
        out_shape=outs,
        in_specs=[SMEM] + [ANY] * 4,
        out_specs=[VM] * len(outs),
        scratch_shapes=[pltpu.VMEM((2048, 512), BF), pltpu.SemaphoreType.DMA((8,))],
        compiler_params=params(),
        cost_estimate=cost(1_000_000, 6_000_000),
    )(meta, *halves)


AXES = ("section", "dp")


class Links:
    def __init__(self, count):
        self.count = count

    def to(self, x, section_flip, dp_flip, only=None):
        n = self.count
        pairs = [
            (s * n + d, (s ^ section_flip) * n + (d ^ dp_flip))
            for s in range(2)
            for d in range(n)
            if only is None or s == only
        ]
        return lax.ppermute(x, AXES, pairs)


def reduce_bucket(links, keep, send):
    rows = keep.shape[0] // 32
    shape = (2, 2, 2, 4, rows, 512)
    half = keep.reshape(shape) + links.to(send, 1, 0).reshape(shape)
    got_a = links.to(half[0, 1], 0, 1)
    got_b = links.to(half[1, 1], 0, 2)
    part_a = half[0, 0] + got_a
    part_b = half[1, 0] + got_b
    got_a = links.to(part_a[1], 0, 2)
    got_b = links.to(part_b[1], 0, 1)
    parts = jnp.stack([part_a[0] + got_a, part_b[0] + got_b], axis=1)
    got = [links.to(parts[i], 0, 4 * i) for i in (1, 2, 3)]
    total = parts[0].astype(F32) + got[0].astype(F32) + got[1].astype(F32) + got[2].astype(F32)
    total = total.astype(BF)
    chips = links.count // 16
    if chips > 1:
        groups = [[g * 16 + r for g in range(chips)] for r in range(16)]
        total = lax.psum(total, "dp", axis_index_groups=groups)
    return total


def gather_bucket(links, total):
    got = [links.to(total, 0, 4 * i) for i in (1, 2, 3)]
    whole = jnp.stack([total] + got, axis=1)
    part_a, part_b = whole[0], whole[1]
    got_a = links.to(part_a, 0, 2)
    got_b = links.to(part_b, 0, 1)
    part_a = jnp.stack([part_a, got_a])
    part_b = jnp.stack([part_b, got_b])
    got_a = links.to(part_a, 0, 1)
    got_b = links.to(part_b, 0, 2)
    return jnp.stack([jnp.stack([part_a, got_a]), jnp.stack([part_b, got_b])]).reshape(-1, 512)


MATRIX = (2, 6, 8, 10, 12, 17, 19)
VECTORS = (0, 1, 3, 5, 7, 9, 11, 13, 14, 15, 16, 18, 20, 21)


def on_device(links, images, cotangent, crop_class, *stacked):
    section = lax.axis_index("section")
    place = lax.axis_index("dp") % 16
    x_bit, y_bit, z_at = place & 1, (place >> 1) & 1, place >> 2
    mask_a = section * 32 + x_bit * 8 + y_bit * 4 + z_at
    mask_b = section * 32 + y_bit * 8 + x_bit * 4 + z_at
    kind = lax.dynamic_index_in_dim(crop_class.reshape(-1), section, 0, keepdims=False)
    side = jnp.where(kind == 0, SIDE_S, jnp.where(kind == 1, SIDE_M, CANVAS))

    def meta_for(block):
        sel = section if block == 0 else 1 - section
        return jnp.stack([sel, side, mask_a, mask_b, section, 0, 0, 0]).astype(jnp.int32)

    metas = [meta_for(0), meta_for(1)]
    image = lax.dynamic_index_in_dim(images, section, 0, keepdims=False).reshape(PIX, C)
    cot = lax.dynamic_index_in_dim(cotangent, section, 0, keepdims=False).reshape(PIX, C)

    mats = [stacked[i][0] for i in MATRIX]
    lines = []
    for i in VECTORS:
        v = stacked[i][0]
        if i == 5:
            v = jnp.concatenate([jnp.zeros((64,), BF), v])
        lines.append(jnp.pad(v, (0, FF - v.shape[0])))
    lines += [jnp.zeros((FF,), BF)] * (VEC_ROWS - len(lines))
    vec = jnp.stack(lines)
    taps = jnp.pad(stacked[4][0], ((0, 0), (64, 0)))
    vec_other = links.to(vec, 1, 0)
    taps_other = links.to(taps, 1, 0)
    mats_other = [links.to(m, 1, 0) for m in mats]
    pairs = list(zip(mats, mats_other))
    is_first = section == 0

    def block_vec(block):
        use_own = is_first if block == 0 else jnp.logical_not(is_first)
        v = jnp.where(use_own, vec, vec_other).astype(F32)
        t = jnp.where(use_own, taps, taps_other).astype(F32)
        return v, t.reshape(49 * GROUPS, LANES), v[V_CB, :1024].reshape(GROUPS, LANES)

    small = [block_vec(0), block_vec(1)]
    field = image
    kept = []
    for block in (0, 1):
        v, t, cb = small[block]
        saved = run_forward(metas[block], field, v, t, cb, pairs)
        kept.append((field, saved))
        field = saved[-1]
    hidden, final = kept[0][1][-1], kept[1][1][-1]

    def to_sections(first, second):
        mine = jnp.where(is_first, first, second)
        other = links.to(jnp.where(is_first, second, first), 1, 0)
        low = jnp.where(is_first, mine, other)
        high = jnp.where(is_first, other, mine)
        return jnp.stack([low, high]).reshape(1, 2, 1, CANVAS, CANVAS, C)

    dy = cot
    dvs = [None, None]
    totals = [None, None]
    for block in (1, 0):
        v, t, cb = small[block]
        x, (n1, cin, mix, p, gl, mid, br, n2, act, slope, out, res) = kept[block]
        dmid, mvec, keep_m, send_m = run_mlp(metas[block], dy, v, n2, act, slope, out, mid, pairs)
        total_m = reduce_bucket(links, keep_m, send_m)
        dv, dvb, keep_g, send_g = run_gn(metas[block], x, dmid, mvec, v, t, n1, cin, mix, p, gl, br, pairs)
        total_g = reduce_bucket(links, keep_g, send_g)
        dvs[block] = dv
        dy = dvb
        totals[block] = (total_m, total_g)
    halves_m, halves_g = [None, None], [None, None]
    for block in (1, 0):
        own_m = gather_bucket(links, totals[block][0])
        halves_m[block] = (own_m, links.to(own_m, 1, 0, only=1 - block))
        own_g = gather_bucket(links, totals[block][1])
        halves_g[block] = (own_g, links.to(own_g, 1, 0, only=1 - block))
    wr, we = run_mlp_finish(metas[0], halves_m[0] + halves_m[1])
    (n1g, n1s, win, bin_, conv, w1, b1, w2, b2, w3, b3, wo, bo, bs, n2g, n2s, be, br, ms) = run_gn_finish(
        metas[0], halves_g[0] + halves_g[1]
    )
    block_outputs = to_sections(hidden, final)
    input_grads = to_sections(dvs[0], dvs[1])
    return (
        block_outputs, input_grads, n1g, n1s, win[None], bin_, conv[None, :49, 64:], conv[None, 49, 64:],
        w1[None], b1, w2[None], b2, w3[None], b3, wo[None], bo, bs, n2g, n2s, we[None], be, wr[None], br, ms,
    )


def solution(mesh):
    links = Links(mesh.shape["dp"])
    image = P(None, "dp", None, None, None)
    one, two = P("section", None), P("section", None, None)
    weights = (one, one, two, one, two, one, two, one, two, one, two, one, two, one, one, one, one, two, one, two,
               one, one)
    field = P("section", None, "dp", None, None, None)
    return jax.shard_map(
        functools.partial(on_device, links),
        mesh=mesh,
        in_specs=(image, image, P(None, "dp")) + weights,
        out_specs=(field, field) + weights,
        check_vma=False,
    )
```

time: 896 us -> 313 us (0.35)
  waiting for transfers between devices: 485 us -> 95.8 us
  matrix products: 231 us -> 0 us
  Pallas kernels: 0 us -> 89.7 us
  starting transfers between devices: 8.14 us -> 91.3 us
  local copies, waits for them, and re-layouts: 81.2 us -> 15.5 us
  other arithmetic: 65.2 us -> 16.5 us
  between operations: 17.4 us -> 3.2 us
    psum x2 -> x0, waiting for transfers between devices: 485 us -> none  [on_device(): lax.psum((early_totals[0], early_totals[1], early_totals[2], early_totals...]
    conv_general_dilated x9 -> x0, matrix products: 167 us -> none  [conv_forward(): lax.conv_general_dilated(source, taps, (1, 1), ((3, 3), (3, 3)), dimensio...]
    ppermute x4 -> x75, waiting for transfers between devices: 0.01 us -> 95.8 us  [to(): return lax.ppermute(x, AXES, pairs)]
    pallas_call x0 -> x8, Pallas kernels: none -> 89.7 us  [the longest x2 35.7 us: run_gn(): pl.pallas_call(gn_kernel, name='gnconv_backward', out_shape=outs, in_spec...]
    ppermute x4 -> x75, starting transfers between devices: 8.06 us -> 91.3 us  [to(): return lax.ppermute(x, AXES, pairs)]
    dot_general x63 -> x0, matrix products: 63.3 us -> none  [the longest x21 32.2 us: outer_total(): jnp.einsum('ihwk,ihwn->kn', left, upward, preferred_element_type=jnp.floa...]
    unnamed x419 -> x45, local copies, waits for them, and re-layouts: 48.8 us -> 3.23 us
    dynamic_update_slice x47 -> x0, other arithmetic: 22.4 us -> none  [keep_slot(): lax.dynamic_update_index_in_dim(buffer, jnp.where(is_valid, values, curre...]
  transfers between devices with their start and end apart: 6 -> 75, of which waited for: 2 -> 24; matrix products, arithmetic and copies ran while one was open for 15% -> 10% of each run, Pallas kernels for 0% -> 10%
where the time goes in v1:
time: 313 us; the launch traced here: 312 us
  waiting for transfers between devices  95.8 us (31%)
  starting transfers between devices  91.3 us (29%)
  Pallas kernels  89.7 us (29%)
  other arithmetic  16.5 us (5%)
  local copies, waits for them, and re-layouts  15.5 us (5%)
  between operations  3.2 us (1%)
    ppermute x75, waiting for transfers between devices, to(): return lax.ppermute(x, AXES, pairs)  95.8 us
    ppermute x75, starting transfers between devices, to(): return lax.ppermute(x, AXES, pairs)  91.3 us
    pallas_call x2, Pallas kernels, run_gn(): pl.pallas_call(gn_kernel, name='gnconv_backward', out_shape=outs, in_spec...  35.7 us
    pallas_call x2, Pallas kernels, run_forward(): pl.pallas_call(forward_kernel, name='block_forward', out_shape=outs, in_s...  24.7 us
    pallas_call x2, Pallas kernels, run_mlp(): pl.pallas_call(mlp_kernel, name='mlp_backward', out_shape=outs, in_specs=...  18.3 us
    unnamed x12, other arithmetic  8.44 us
    pallas_call x1, Pallas kernels, run_mlp_finish(): pl.pallas_call(mlp_finish, name='mlp_finish', out_shape=outs, in_specs=[S...  6.59 us
  transfers between devices with their start and end apart: 75, of which 24 were waited for; matrix products, arithmetic and copies ran while one was open for 10% of the time, Pallas kernels for 10%

profile of v1, /device:TPU:0, one launch (start us, length us, event | category | flops | bytes accessed | tf_op | source)
XLA Modules:
  0.0 312.0 jit_solution(3225534452967846623)
XLA Ops:
  25.1 12.3 %block_forward.2 = (bf16[256,512]{1,0:T(8,128)(2,1)}, f32[2816,128]{1,0:T(8,128)}, f32[256,1024]{1,0:T(8,128)}, f32[256,1024]{1,0:T(8,128)}, bf16[256,1024]{1,0:...) custom-call(s32[8]{0:T(128)} %stack.346.meta, ...), custom_call_target="tpu_custom_call" | custom-call | flops 5000000000 | bytes 14000000 | tf_op jit(solution)/shard_map/block_forward/pallas_call | solution.py:537
  37.4 12.4 %block_forward.3 = (bf16[256,512]{1,0:T(8,128)(2,1)}, f32[2816,128]{1,0:T(8,128)}, f32[256,1024]{1,0:T(8,128)}, f32[256,1024]{1,0:T(8,128)}, bf16[256,1024]{1,0:...) custom-call(s32[8]{0:T(128)} %stack.363.meta, ...), custom_call_target="tpu_custom_call" | custom-call | flops 5000000000 | bytes 14000000 | tf_op jit(solution)/shard_map/block_forward/pallas_call | solution.py:537
  49.8 9.2 %mlp_backward.2 = (f32[256,512]{1,0:T(8,128)}, f32[8,2048]{1,0:T(8,128)}, bf16[2048,512]{1,0:T(8,128)(2,1)}, bf16[2048,512]{1,0:T(8,128)(2,1)}) custom-call(s32[8]{0:T(128)} %stack.363.meta, bf16[256,512]{1,0:T(8,128)(2,1)} %bitcast.353, f32[16,2048]{1,0:T(8,128)} %copy-done.17, bf16[256,512]{1,0:T(8,128)(2,1)} %get-tuple-element.86.n2_ref, ...), custom_call_target="tpu_custom_call" | custom-call | flops 5000000000 | bytes 14000000 | tf_op jit(solution)/shard_map/mlp_backward/pallas_call | solution.py:556
  59.0 17.9 %gnconv_backward.2 = (f32[256,512]{1,0:T(8,128)}, bf16[256,512]{1,0:T(8,128)(2,1)}, bf16[1024,512]{1,0:T(8,128)(2,1)}, bf16[1024,512]{1,0:T(8,128)(2,1)}) custom-call(s32[8]{0:T(128)} %stack.363.meta, bf16[256,512]{1,0:T(8,128)(2,1)} %get-tuple-element.84.x_ref, f32[256,512]{1,0:T(8,128)} %get-tuple-element.91.dmid_ref, ...), custom_call_target="tpu_custom_call" | custom-call | flops 5000000000 | bytes 14000000 | tf_op jit(solution)/shard_map/gnconv_backward/pallas_call | solution.py:575
  77.0 9.1 %mlp_backward.3 = (f32[256,512]{1,0:T(8,128)}, f32[8,2048]{1,0:T(8,128)}, bf16[2048,512]{1,0:T(8,128)(2,1)}, bf16[2048,512]{1,0:T(8,128)(2,1)}) custom-call(s32[8]{0:T(128)} %stack.346.meta, bf16[256,512]{1,0:T(8,128)(2,1)} %get-tuple-element.99.dy_ref, f32[16,2048]{1,0:T(8,128)} %copy-done.16, bf16[256,512]{1,0:T(8,128)(2,1)} %get-tuple-element.100.n2_ref, ...), custom_call_target="tpu_custom_call" | custom-call | flops 5000000000 | bytes 14000000 | tf_op jit(solution)/shard_map/mlp_backward/pallas_call | solution.py:556
  86.2 17.8 %gnconv_backward.3 = (f32[256,512]{1,0:T(8,128)}, bf16[256,512]{1,0:T(8,128)(2,1)}, bf16[1024,512]{1,0:T(8,128)(2,1)}, bf16[1024,512]{1,0:T(8,128)(2,1)}) custom-call(s32[8]{0:T(128)} %stack.346.meta, bf16[256,512]{1,0:T(8,128)(2,1)} %bitcast.352, f32[256,512]{1,0:T(8,128)} %get-tuple-element.105.dmid_ref, f32[8,2048]{1,0:T(8,128)} %get-tuple-element.106.mvec_ref, ...), custom_call_target="tpu_custom_call" | custom-call | flops 5000000000 | bytes 14000000 | tf_op jit(solution)/shard_map/gnconv_backward/pallas_call | solution.py:575
  105.4 2.6 collective-permute-start.28
  110.6 4.6 %collective-permute-done.28 = bf16[2,4,32,512]{3,2,1,0:T(8,128)(2,1)S(1)} collective-permute-done((bf16[2,4,32,512]{3,2,1,0:T(8,128)(2,1)S(1)}, bf16[2,4,32,512]{3,2,1,0:T(8,128)(2,1)S(1)}, u32[]{:S(2)}, u32[]{:S(2)}) %collective-permute-start.28) | collective-permute-done | bytes 262176 | tf_op jit(solution)/shard_map/ppermute | solution.py:639
  115.2 2.0 collective-permute-start.14
  118.8 2.0 collective-permute-done.12
  120.8 2.0 collective-permute-start.29
  126.3 1.9 collective-permute-start.32
  128.2 2.6 collective-permute-start.33
  130.9 2.5 collective-permute-start.34
  134.6 2.0 collective-permute-start.17
  137.5 1.9 collective-permute-start.18
  140.5 2.0 collective-permute-start.36
  142.5 1.8 collective-permute-done.18
  150.4 2.6 collective-permute-start.21
  153.1 1.9 collective-permute-start.38
  155.0 1.8 collective-permute-start.40
  158.7 2.0 collective-permute-start.60
  161.5 1.8 collective-permute-start.24
  166.3 7.3 %collective-permute-done.60 = bf16[2,4,64,512]{3,2,1,0:T(8,128)(2,1)S(1)} collective-permute-done((bf16[2,4,64,512]{3,2,1,0:T(8,128)(2,1)S(1)}, bf16[2,4,64,512]{3,2,1,0:T(8,128)(2,1)S(1)}, u32[]{:S(2)}, u32[]{:S(2)}) %collective-permute-start.60) | collective-permute-done | bytes 524320 | tf_op jit(solution)/shard_map/ppermute | solution.py:639
  175.9 16.8 %collective-permute-done.44 = bf16[2,4,64,512]{3,2,1,0:T(8,128)(2,1)S(1)} collective-permute-done((bf16[2,4,64,512]{3,2,1,0:T(8,128)(2,1)S(1)}, bf16[2,4,64,512]{3,2,1,0:T(8,128)(2,1)S(1)}, u32[]{:S(2)}, u32[]{:S(2)}) %collective-permute-start.44) | collective-permute-done | bytes 524320 | tf_op jit(solution)/shard_map/ppermute | solution.py:639
  193.2 1.8 collective-permute-start.47
  196.8 2.3 collective-permute-done.61
  199.2 1.8 collective-permute-start.64
  201.0 1.8 collective-permute-start.65
  202.8 2.0 collective-permute-start.66
  204.9 3.1 %collective-permute-done.64 = bf16[2,64,512]{2,1,0:T(8,128)(2,1)S(1)} collective-permute-done((bf16[2,64,512]{2,1,0:T(8,128)(2,1)S(1)}, bf16[2,64,512]{2,1,0:T(8,128)(2,1)S(1)}, u32[]{:S(2)}, u32[]{:S(2)}) %collective-permute-start.64) | collective-permute-done | bytes 131104 | tf_op jit(solution)/shard_map/ppermute | solution.py:639
  208.1 6.6 %collective-permute-done.65 = bf16[2,64,512]{2,1,0:T(8,128)(2,1)S(1)} collective-permute-done((bf16[2,64,512]{2,1,0:T(8,128)(2,1)S(1)}, bf16[2,64,512]{2,1,0:T(8,128)(2,1)S(1)}, u32[]{:S(2)}, u32[]{:S(2)}) %collective-permute-start.65) | collective-permute-done | bytes 131104 | tf_op jit(solution)/shard_map/ppermute | solution.py:639
  215.7 3.9 %collective-permute-start.67 = (bf16[2,64,512]{2,1,0:T(8,128)(2,1)S(1)}, bf16[2,64,512]{2,1,0:T(8,128)(2,1)S(1)}, u32[]{:S(2)}, u32[]{:S(2)}) collective-permute-start(bf16[2,64,512]{2,1,0:T(8,128)(2,1)S(1)} %fusion.18), channel_id=1, source_target_pairs={{0,4},{1,5},{2,6},{3,7},{4,0},{5,1},{6,2},{7,3},{8,12},{9,13},{10,... | collective-permute-start | bytes 393224 | tf_op jit(solution)/shard_map/ppermute | solution.py:639
  219.6 6.6 %collective-permute-done.49 = bf16[2,64,512]{2,1,0:T(8,128)(2,1)S(1)} collective-permute-done((bf16[2,64,512]{2,1,0:T(8,128)(2,1)S(1)}, bf16[2,64,512]{2,1,0:T(8,128)(2,1)S(1)}, u32[]{:S(2)}, u32[]{:S(2)}) %collective-permute-start.49) | collective-permute-done | bytes 131104 | tf_op jit(solution)/shard_map/ppermute | solution.py:639
  227.9 3.0 collective-permute-start.51
  230.9 3.5 %collective-permute-done.68 = bf16[2,64,512]{2,1,0:T(8,128)(2,1)S(1)} collective-permute-done((bf16[2,64,512]{2,1,0:T(8,128)(2,1)S(1)}, bf16[2,64,512]{2,1,0:T(8,128)(2,1)S(1)}, u32[]{:S(2)}, u32[]{:S(2)}) %collective-permute-start.68) | collective-permute-done | bytes 131104 | tf_op jit(solution)/shard_map/ppermute | solution.py:639
  237.2 4.6 %collective-permute-done.52 = bf16[2,64,512]{2,1,0:T(8,128)(2,1)S(1)} collective-permute-done((bf16[2,64,512]{2,1,0:T(8,128)(2,1)S(1)}, bf16[2,64,512]{2,1,0:T(8,128)(2,1)S(1)}, u32[]{:S(2)}, u32[]{:S(2)}) %collective-permute-start.52) | collective-permute-done | bytes 131104 | tf_op jit(solution)/shard_map/ppermute | solution.py:639
  245.6 4.1 %collective-permute-done.72 = bf16[4,64,512]{2,1,0:T(8,128)(2,1)S(1)} collective-permute-done((bf16[4,64,512]{2,1,0:T(8,128)(2,1)S(1)}, bf16[4,64,512]{2,1,0:T(8,128)(2,1)S(1)}, u32[]{:S(2)}, u32[]{:S(2)}) %collective-permute-start.72) | collective-permute-done | bytes 262176 | tf_op jit(solution)/shard_map/ppermute | solution.py:639
  249.7 1.7 collective-permute-start.71
  254.4 8.4 %collective-permute-done.71 = bf16[2,4,64,512]{3,2,1,0:T(8,128)(2,1)S(1)} collective-permute-done((bf16[2,4,64,512]{3,2,1,0:T(8,128)(2,1)S(1)}, bf16[2,4,64,512]{3,2,1,0:T(8,128)(2,1)S(1)}, u32[]{:S(2)}, u32[]{:S(2)}) %collective-permute-start.71) | collective-permute-done | bytes 524320 | tf_op jit(solution)/shard_map/ppermute | solution.py:639
  262.9 2.9 collective-permute-done.73
  265.8 7.1 %collective-permute-done.55 = bf16[2,4,64,512]{3,2,1,0:T(8,128)(2,1)S(1)} collective-permute-done((bf16[2,4,64,512]{3,2,1,0:T(8,128)(2,1)S(1)}, bf16[2,4,64,512]{3,2,1,0:T(8,128)(2,1)S(1)}, u32[]{:S(2)}, u32[]{:S(2)}) %collective-permute-start.55) | collective-permute-done | bytes 524320 | tf_op jit(solution)/shard_map/ppermute | solution.py:639
  273.6 6.9 %collective-permute-done.57 = bf16[2,4,64,512]{3,2,1,0:T(8,128)(2,1)S(1)} collective-permute-done((bf16[2,4,64,512]{3,2,1,0:T(8,128)(2,1)S(1)}, bf16[2,4,64,512]{3,2,1,0:T(8,128)(2,1)S(1)}, u32[]{:S(2)}, u32[]{:S(2)}) %collective-permute-start.57) | collective-permute-done | bytes 524320 | tf_op jit(solution)/shard_map/ppermute | solution.py:639
  280.4 2.7 collective-permute-start.74
  285.0 4.4 %collective-permute-start.42 = (bf16[1024,512]{1,0:T(8,128)(2,1)S(1)}, bf16[1024,512]{1,0:T(8,128)(2,1)S(1)}, u32[]{:S(2)}, u32[]{:S(2)}) collective-permute-start(bf16[1024,512]{1,0:T(8,128)(2,1)S(1)} %bitcast.335), channel_id=1, source_target_pairs={{0,16},{1,17},{2,18},{3,19},{4,20},{5,21},{6,22},{7,23},{8,24},{9,... | collective-permute-start | bytes 3145736 | tf_op jit(solution)/shard_map/ppermute | solution.py:639
  291.5 2.0 collective-permute-start.10
  297.4 4.4 %gn_finish.1 = (f32[1,512]{1,0:T(1,128)}, f32[1,512]{1,0:T(1,128)}, f32[512,1024]{1,0:T(8,128)}, f32[1,1024]{1,0:T(1,128)}, f32[64,1024]{1,0:T(8,128)}, /*index=...) custom-call(s32[8]{0:T(128)} %stack.346.meta, ...), custom_call_target="tpu_custom_call" | custom-call | flops 1000000 | bytes 6000000 | tf_op jit(solution)/shard_map/gn_finish/pallas_call | solution.py:612
  305.2 6.6 %mlp_finish.1 = (f32[2048,512]{1,0:T(8,128)}, f32[512,2048]{1,0:T(8,128)}) custom-call(s32[8]{0:T(128)} %stack.346.meta, bf16[2048,512]{1,0:T(8,128)(2,1)} %bitcast.330, bf16[2048,512]{1,0:T(8,128)(2,1)} %collective-permute-done.58.other0, bf16[2048,512]{1,0:T(8,128)(2,1)} %bitcast.328, bf16[2048,512]{1,0:T(8,128)(2,1)} %collective-permute-done.74.other1), custom_call_target="tpu_custom_call" | custom-call | flops 1000000 | bytes 12000000 | tf_op jit(solution)/shard_map/mlp_finish/pallas_call | solution.py:596
  (280 shorter events, 75.8 us)
Async XLA Ops:
  0.7 23.1 %collective-permute-start.7 = (bf16[512,2048]{1,0:T(8,128)(2,1)}, bf16[512,2048]{1,0:T(8,128)(2,1)S(1)}, u32[]{:S(2)}, u32[]{:S(2)}) collective-permute-start(bf16[512,2048]{1,0:T(8,128)(2,1)} %bitcast.385), channel_id=1, source_target_pairs={{0,16},{1,17},{2,18},{3,19},{4,20},{5,21},{6,22},{7,23},{8,24},{9,... | collective-permute-start | bytes 6291464 | tf_op jit(solution)/shard_map/ppermute | solution.py:639
  1.2 22.6 %collective-permute-start.8 = (bf16[2048,512]{1,0:T(8,128)(2,1)}, bf16[2048,512]{1,0:T(8,128)(2,1)}, u32[]{:S(2)}, u32[]{:S(2)}) collective-permute-start(bf16[2048,512]{1,0:T(8,128)(2,1)} %bitcast.390), channel_id=1, source_target_pairs={{0,16},{1,17},{2,18},{3,19},{4,20},{5,21},{6,22},{7,23},{8,24},{9,... | collective-permute-start | bytes 6291464 | tf_op jit(solution)/shard_map/ppermute | solution.py:639
  1.3 22.5 %collective-permute-start.2 = (bf16[512,1024]{1,0:T(8,128)(2,1)}, bf16[512,1024]{1,0:T(8,128)(2,1)}, u32[]{:S(2)}, u32[]{:S(2)}) collective-permute-start(bf16[512,1024]{1,0:T(8,128)(2,1)} %bitcast.396), channel_id=1, source_target_pairs={{0,16},{1,17},{2,18},{3,19},{4,20},{5,21},{6,22},{7,23},{8,24},{9,... | collective-permute-start | bytes 3145736 | tf_op jit(solution)/shard_map/ppermute | solution.py:639
  76.9 28.1 %collective-permute-start.27 = (bf16[1024,512]{1,0:T(8,128)(2,1)}, bf16[1024,512]{1,0:T(8,128)(2,1)S(1)}, u32[]{:S(2)}, u32[]{:S(2)}) collective-permute-start(bf16[1024,512]{1,0:T(8,128)(2,1)} %get-tuple-element.118), channel_id=1, source_target_pairs={{0,16},{1,17},{2,18},{3,19},{4,20},{5,21},{6,22},{7,23},{8,24},{9,... | collective-permute-start | bytes 3145736 | tf_op jit(solution)/shard_map/ppermute | solution.py:639
  104.5 53.5 %collective-permute-start.59 = (bf16[2048,512]{1,0:T(8,128)(2,1)}, bf16[2048,512]{1,0:T(8,128)(2,1)S(1)}, u32[]{:S(2)}, u32[]{:S(2)}) collective-permute-start(bf16[2048,512]{1,0:T(8,128)(2,1)} %get-tuple-element.138), channel_id=1, source_target_pairs={{0,16},{1,17},{2,18},{3,19},{4,20},{5,21},{6,22},{7,23},{8,24},{9,... | collective-permute-start | bytes 6291464 | tf_op jit(solution)/shard_map/ppermute | solution.py:639
  104.6 60.0 %collective-permute-start.43 = (bf16[2048,512]{1,0:T(8,128)(2,1)S(1)}, bf16[2048,512]{1,0:T(8,128)(2,1)S(1)}, u32[]{:S(2)}, u32[]{:S(2)}) collective-permute-start(bf16[2048,512]{1,0:T(8,128)(2,1)S(1)} %copy-done.18), channel_id=1, source_target_pairs={{0,16},{1,17},{2,18},{3,19},{4,20},{5,21},{6,22},{7,23},{8,24},{9,... | collective-permute-start | bytes 6291464 | tf_op jit(solution)/shard_map/ppermute | solution.py:639
  105.4 9.8 %collective-permute-start.28 = (bf16[2,4,32,512]{3,2,1,0:T(8,128)(2,1)S(1)}, bf16[2,4,32,512]{3,2,1,0:T(8,128)(2,1)S(1)}, u32[]{:S(2)}, u32[]{:S(2)}) collective-permute-start(bf16[2,4,32,512]{3,2,1,0:T(8,128)(2,1)S(1)} %get-tuple-element.180), channel_id=1, source_target_pairs={{0,1},{1,0},{2,3},{3,2},{4,5},{5,4},{6,7},{7,6},{8,9},{9,8},{10,11... | collective-permute-start | bytes 786440 | tf_op jit(solution)/shard_map/ppermute | solution.py:639
  108.0 9.1 %collective-permute-start.30 = (bf16[2,4,32,512]{3,2,1,0:T(8,128)(2,1)S(1)}, bf16[2,4,32,512]{3,2,1,0:T(8,128)(2,1)S(1)}, u32[]{:S(2)}, u32[]{:S(2)}) collective-permute-start(bf16[2,4,32,512]{3,2,1,0:T(8,128)(2,1)S(1)} %get-tuple-element.181), channel_id=1, source_target_pairs={{0,2},{1,3},{2,0},{3,1},{4,6},{5,7},{6,4},{7,5},{8,10},{9,11},{10,... | collective-permute-start | bytes 786440 | tf_op jit(solution)/shard_map/ppermute | solution.py:639
  110.0 10.8 %collective-permute-start.12 = (bf16[2,4,32,512]{3,2,1,0:T(8,128)(2,1)S(1)}, bf16[2,4,32,512]{3,2,1,0:T(8,128)(2,1)S(1)}, u32[]{:S(2)}, u32[]{:S(2)}) collective-permute-start(bf16[2,4,32,512]{3,2,1,0:T(8,128)(2,1)S(1)} %get-tuple-element.184), channel_id=1, source_target_pairs={{0,1},{1,0},{2,3},{3,2},{4,5},{5,4},{6,7},{7,6},{8,9},{9,8},{10,11... | collective-permute-start | bytes 786440 | tf_op jit(solution)/shard_map/ppermute | solution.py:639
  115.2 7.8 %collective-permute-start.14 = (bf16[2,4,32,512]{3,2,1,0:T(8,128)(2,1)S(1)}, bf16[2,4,32,512]{3,2,1,0:T(8,128)(2,1)S(1)}, u32[]{:S(2)}, u32[]{:S(2)}) collective-permute-start(bf16[2,4,32,512]{3,2,1,0:T(8,128)(2,1)S(1)} %get-tuple-element.185), channel_id=1, source_target_pairs={{0,2},{1,3},{2,0},{3,1},{4,6},{5,7},{6,4},{7,5},{8,10},{9,11},{10,... | collective-permute-start | bytes 786440 | tf_op jit(solution)/shard_map/ppermute | solution.py:639
  117.2 7.4 %collective-permute-start.31 = (bf16[4,32,512]{2,1,0:T(8,128)(2,1)S(1)}, bf16[4,32,512]{2,1,0:T(8,128)(2,1)S(1)}, u32[]{:S(2)}, u32[]{:S(2)}) collective-permute-start(bf16[4,32,512]{2,1,0:T(8,128)(2,1)S(1)} %slice_bitcast_fusion.25), channel_id=1, source_target_pairs={{0,1},{1,0},{2,3},{3,2},{4,5},{5,4},{6,7},{7,6},{8,9},{9,8},{10,11... | collective-permute-start | bytes 393224 | tf_op jit(solution)/shard_map/ppermute | solution.py:639
  139.5 7.6 %collective-permute-start.35 = (bf16[2,32,512]{2,1,0:T(8,128)(2,1)S(1)}, bf16[2,32,512]{2,1,0:T(8,128)(2,1)S(1)}, u32[]{:S(2)}, u32[]{:S(2)}) collective-permute-start(bf16[2,32,512]{2,1,0:T(8,128)(2,1)S(1)} %fusion.46), channel_id=1, source_target_pairs={{0,4},{1,5},{2,6},{3,7},{4,0},{5,1},{6,2},{7,3},{8,12},{9,13},{10,... | collective-permute-start | bytes 196616 | tf_op jit(solution)/shard_map/ppermute | solution.py:639
  153.1 7.6 %collective-permute-start.38 = (bf16[4,32,512]{2,1,0:T(8,128)(2,1)S(1)}, bf16[4,32,512]{2,1,0:T(8,128)(2,1)S(1)}, u32[]{:S(2)}, u32[]{:S(2)}) collective-permute-start(bf16[4,32,512]{2,1,0:T(8,128)(2,1)S(1)} %get-tuple-element.213), channel_id=1, source_target_pairs={{0,2},{1,3},{2,0},{3,1},{4,6},{5,7},{6,4},{7,5},{8,10},{9,11},{10,... | collective-permute-start | bytes 393224 | tf_op jit(solution)/shard_map/ppermute | solution.py:639
  158.7 14.9 %collective-permute-start.60 = (bf16[2,4,64,512]{3,2,1,0:T(8,128)(2,1)S(1)}, bf16[2,4,64,512]{3,2,1,0:T(8,128)(2,1)S(1)}, u32[]{:S(2)}, u32[]{:S(2)}) collective-permute-start(bf16[2,4,64,512]{3,2,1,0:T(8,128)(2,1)S(1)} %get-tuple-element.170), channel_id=1, source_target_pairs={{0,1},{1,0},{2,3},{3,2},{4,5},{5,4},{6,7},{7,6},{8,9},{9,8},{10,11... | collective-permute-start | bytes 1572872 | tf_op jit(solution)/shard_map/ppermute | solution.py:639
  160.7 14.9 %collective-permute-start.62 = (bf16[2,4,64,512]{3,2,1,0:T(8,128)(2,1)S(1)}, bf16[2,4,64,512]{3,2,1,0:T(8,128)(2,1)S(1)}, u32[]{:S(2)}, u32[]{:S(2)}) collective-permute-start(bf16[2,4,64,512]{3,2,1,0:T(8,128)(2,1)S(1)} %get-tuple-element.171), channel_id=1, source_target_pairs={{0,2},{1,3},{2,0},{3,1},{4,6},{5,7},{6,4},{7,5},{8,10},{9,11},{10,... | collective-permute-start | bytes 1572872 | tf_op jit(solution)/shard_map/ppermute | solution.py:639
  161.5 90.0 %collective-permute-start.24 = (bf16[4,32,512]{2,1,0:T(8,128)(2,1)S(1)}, bf16[4,32,512]{2,1,0:T(8,128)(2,1)S(1)}, u32[]{:S(2)}, u32[]{:S(2)}) collective-permute-start(bf16[4,32,512]{2,1,0:T(8,128)(2,1)S(1)} %get-tuple-element.225), channel_id=1, source_target_pairs={{0,1},{1,0},{2,3},{3,2},{4,5},{5,4},{6,7},{7,6},{8,9},{9,8},{10,11... | collective-permute-start | bytes 393224 | tf_op jit(solution)/shard_map/ppermute | solution.py:639
  163.4 88.4 %collective-permute-start.39 = (bf16[2,4,32,512]{3,2,1,0:T(8,128)(2,1)S(1)}, bf16[2,4,32,512]{3,2,1,0:T(8,128)(2,1)S(1)}, u32[]{:S(2)}, u32[]{:S(2)}) collective-permute-start(bf16[2,4,32,512]{3,2,1,0:T(8,128)(2,1)S(1)} %get-tuple-element.211), channel_id=1, source_target_pairs={{0,1},{1,0},{2,3},{3,2},{4,5},{5,4},{6,7},{7,6},{8,9},{9,8},{10,11... | collective-permute-start | bytes 786440 | tf_op jit(solution)/shard_map/ppermute | solution.py:639
  165.2 27.5 %collective-permute-start.44 = (bf16[2,4,64,512]{3,2,1,0:T(8,128)(2,1)S(1)}, bf16[2,4,64,512]{3,2,1,0:T(8,128)(2,1)S(1)}, u32[]{:S(2)}, u32[]{:S(2)}) collective-permute-start(bf16[2,4,64,512]{3,2,1,0:T(8,128)(2,1)S(1)} %get-tuple-element.174), channel_id=1, source_target_pairs={{0,1},{1,0},{2,3},{3,2},{4,5},{5,4},{6,7},{7,6},{8,9},{9,8},{10,11... | collective-permute-start | bytes 1572872 | tf_op jit(solution)/shard_map/ppermute | solution.py:639
  173.6 19.4 %collective-permute-start.46 = (bf16[2,4,64,512]{3,2,1,0:T(8,128)(2,1)S(1)}, bf16[2,4,64,512]{3,2,1,0:T(8,128)(2,1)S(1)}, u32[]{:S(2)}, u32[]{:S(2)}) collective-permute-start(bf16[2,4,64,512]{3,2,1,0:T(8,128)(2,1)S(1)} %get-tuple-element.175), channel_id=1, source_target_pairs={{0,2},{1,3},{2,0},{3,1},{4,6},{5,7},{6,4},{7,5},{8,10},{9,11},{10,... | collective-permute-start | bytes 1572872 | tf_op jit(solution)/shard_map/ppermute | solution.py:639
  175.7 19.8 %collective-permute-start.63 = (bf16[4,64,512]{2,1,0:T(8,128)(2,1)S(1)}, bf16[4,64,512]{2,1,0:T(8,128)(2,1)S(1)}, u32[]{:S(2)}, u32[]{:S(2)}) collective-permute-start(bf16[4,64,512]{2,1,0:T(8,128)(2,1)S(1)} %slice_bitcast_fusion.8), channel_id=1, source_target_pairs={{0,1},{1,0},{2,3},{3,2},{4,5},{5,4},{6,7},{7,6},{8,9},{9,8},{10,11... | collective-permute-start | bytes 786440 | tf_op jit(solution)/shard_map/ppermute | solution.py:639
  193.2 7.8 %collective-permute-start.47 = (bf16[4,64,512]{2,1,0:T(8,128)(2,1)S(1)}, bf16[4,64,512]{2,1,0:T(8,128)(2,1)S(1)}, u32[]{:S(2)}, u32[]{:S(2)}) collective-permute-start(bf16[4,64,512]{2,1,0:T(8,128)(2,1)S(1)} %slice_bitcast_fusion.12), channel_id=1, source_target_pairs={{0,1},{1,0},{2,3},{3,2},{4,5},{5,4},{6,7},{7,6},{8,9},{9,8},{10,11... | collective-permute-start | bytes 786440 | tf_op jit(solution)/shard_map/ppermute | solution.py:639
  199.2 8.9 %collective-permute-start.64 = (bf16[2,64,512]{2,1,0:T(8,128)(2,1)S(1)}, bf16[2,64,512]{2,1,0:T(8,128)(2,1)S(1)}, u32[]{:S(2)}, u32[]{:S(2)}) collective-permute-start(bf16[2,64,512]{2,1,0:T(8,128)(2,1)S(1)} %get-tuple-element.196), channel_id=1, source_target_pairs={{0,4},{1,5},{2,6},{3,7},{4,0},{5,1},{6,2},{7,3},{8,12},{9,13},{10,... | collective-permute-start | bytes 393224 | tf_op jit(solution)/shard_map/ppermute | solution.py:639
  201.0 13.8 %collective-permute-start.65 = (bf16[2,64,512]{2,1,0:T(8,128)(2,1)S(1)}, bf16[2,64,512]{2,1,0:T(8,128)(2,1)S(1)}, u32[]{:S(2)}, u32[]{:S(2)}) collective-permute-start(bf16[2,64,512]{2,1,0:T(8,128)(2,1)S(1)} %get-tuple-element.198), channel_id=1, source_target_pairs={{0,8},{1,9},{2,10},{3,11},{4,12},{5,13},{6,14},{7,15},{8,0},{9,1},... | collective-permute-start | bytes 393224 | tf_op jit(solution)/shard_map/ppermute | solution.py:639
  202.8 11.9 %collective-permute-start.66 = (bf16[2,64,512]{2,1,0:T(8,128)(2,1)S(1)}, bf16[2,64,512]{2,1,0:T(8,128)(2,1)S(1)}, u32[]{:S(2)}, u32[]{:S(2)}) collective-permute-start(bf16[2,64,512]{2,1,0:T(8,128)(2,1)S(1)} %get-tuple-element.197), channel_id=1, source_target_pairs={{0,12},{1,13},{2,14},{3,15},{4,8},{5,9},{6,10},{7,11},{8,4},{9,5},... | collective-permute-start | bytes 393224 | tf_op jit(solution)/shard_map/ppermute | solution.py:639
  208.1 7.7 %collective-permute-start.48 = (bf16[2,64,512]{2,1,0:T(8,128)(2,1)S(1)}, bf16[2,64,512]{2,1,0:T(8,128)(2,1)S(1)}, u32[]{:S(2)}, u32[]{:S(2)}) collective-permute-start(bf16[2,64,512]{2,1,0:T(8,128)(2,1)S(1)} %get-tuple-element.207), channel_id=1, source_target_pairs={{0,4},{1,5},{2,6},{3,7},{4,0},{5,1},{6,2},{7,3},{8,12},{9,13},{10,... | collective-permute-start | bytes 393224 | tf_op jit(solution)/shard_map/ppermute | solution.py:639
  214.7 11.5 %collective-permute-start.49 = (bf16[2,64,512]{2,1,0:T(8,128)(2,1)S(1)}, bf16[2,64,512]{2,1,0:T(8,128)(2,1)S(1)}, u32[]{:S(2)}, u32[]{:S(2)}) collective-permute-start(bf16[2,64,512]{2,1,0:T(8,128)(2,1)S(1)} %get-tuple-element.209), channel_id=1, source_target_pairs={{0,8},{1,9},{2,10},{3,11},{4,12},{5,13},{6,14},{7,15},{8,0},{9,1},... | collective-permute-start | bytes 393224 | tf_op jit(solution)/shard_map/ppermute | solution.py:639
  214.7 11.5 %collective-permute-start.50 = (bf16[2,64,512]{2,1,0:T(8,128)(2,1)S(1)}, bf16[2,64,512]{2,1,0:T(8,128)(2,1)S(1)}, u32[]{:S(2)}, u32[]{:S(2)}) collective-permute-start(bf16[2,64,512]{2,1,0:T(8,128)(2,1)S(1)} %get-tuple-element.208), channel_id=1, source_target_pairs={{0,12},{1,13},{2,14},{3,15},{4,8},{5,9},{6,10},{7,11},{8,4},{9,5},... | collective-permute-start | bytes 393224 | tf_op jit(solution)/shard_map/ppermute | solution.py:639
  215.7 12.1 %collective-permute-start.67 = (bf16[2,64,512]{2,1,0:T(8,128)(2,1)S(1)}, bf16[2,64,512]{2,1,0:T(8,128)(2,1)S(1)}, u32[]{:S(2)}, u32[]{:S(2)}) collective-permute-start(bf16[2,64,512]{2,1,0:T(8,128)(2,1)S(1)} %fusion.18), channel_id=1, source_target_pairs={{0,4},{1,5},{2,6},{3,7},{4,0},{5,1},{6,2},{7,3},{8,12},{9,13},{10,... | collective-permute-start | bytes 393224 | tf_op jit(solution)/shard_map/ppermute | solution.py:639
  226.3 8.1 %collective-permute-start.68 = (bf16[2,64,512]{2,1,0:T(8,128)(2,1)S(1)}, bf16[2,64,512]{2,1,0:T(8,128)(2,1)S(1)}, u32[]{:S(2)}, u32[]{:S(2)}) collective-permute-start(bf16[2,64,512]{2,1,0:T(8,128)(2,1)S(1)} %fusion.18), channel_id=1, source_target_pairs={{0,8},{1,9},{2,10},{3,11},{4,12},{5,13},{6,14},{7,15},{8,0},{9,1},... | collective-permute-start | bytes 393224 | tf_op jit(solution)/shard_map/ppermute | solution.py:639
  226.3 8.1 %collective-permute-start.69 = (bf16[2,64,512]{2,1,0:T(8,128)(2,1)S(1)}, bf16[2,64,512]{2,1,0:T(8,128)(2,1)S(1)}, u32[]{:S(2)}, u32[]{:S(2)}) collective-permute-start(bf16[2,64,512]{2,1,0:T(8,128)(2,1)S(1)} %fusion.18), channel_id=1, source_target_pairs={{0,12},{1,13},{2,14},{3,15},{4,8},{5,9},{6,10},{7,11},{8,4},{9,5},... | collective-permute-start | bytes 393224 | tf_op jit(solution)/shard_map/ppermute | solution.py:639
  227.9 8.4 %collective-permute-start.51 = (bf16[2,64,512]{2,1,0:T(8,128)(2,1)S(1)}, bf16[2,64,512]{2,1,0:T(8,128)(2,1)S(1)}, u32[]{:S(2)}, u32[]{:S(2)}) collective-permute-start(bf16[2,64,512]{2,1,0:T(8,128)(2,1)S(1)} %fusion.21), channel_id=1, source_target_pairs={{0,4},{1,5},{2,6},{3,7},{4,0},{5,1},{6,2},{7,3},{8,12},{9,13},{10,... | collective-permute-start | bytes 393224 | tf_op jit(solution)/shard_map/ppermute | solution.py:639
  234.4 7.4 %collective-permute-start.52 = (bf16[2,64,512]{2,1,0:T(8,128)(2,1)S(1)}, bf16[2,64,512]{2,1,0:T(8,128)(2,1)S(1)}, u32[]{:S(2)}, u32[]{:S(2)}) collective-permute-start(bf16[2,64,512]{2,1,0:T(8,128)(2,1)S(1)} %fusion.21), channel_id=1, source_target_pairs={{0,8},{1,9},{2,10},{3,11},{4,12},{5,13},{6,14},{7,15},{8,0},{9,1},... | collective-permute-start | bytes 393224 | tf_op jit(solution)/shard_map/ppermute | solution.py:639
  234.4 9.2 %collective-permute-start.53 = (bf16[2,64,512]{2,1,0:T(8,128)(2,1)S(1)}, bf16[2,64,512]{2,1,0:T(8,128)(2,1)S(1)}, u32[]{:S(2)}, u32[]{:S(2)}) collective-permute-start(bf16[2,64,512]{2,1,0:T(8,128)(2,1)S(1)} %fusion.21), channel_id=1, source_target_pairs={{0,12},{1,13},{2,14},{3,15},{4,8},{5,9},{6,10},{7,11},{8,4},{9,5},... | collective-permute-start | bytes 393224 | tf_op jit(solution)/shard_map/ppermute | solution.py:639
  236.3 8.4 %collective-permute-start.70 = (bf16[4,64,512]{2,1,0:T(8,128)(2,1)S(1)}, bf16[4,64,512]{2,1,0:T(8,128)(2,1)S(1)}, u32[]{:S(2)}, u32[]{:S(2)}) collective-permute-start(bf16[4,64,512]{2,1,0:T(8,128)(2,1)S(1)} %get-tuple-element.191), channel_id=1, source_target_pairs={{0,2},{1,3},{2,0},{3,1},{4,6},{5,7},{6,4},{7,5},{8,10},{9,11},{10,... | collective-permute-start | bytes 786440 | tf_op jit(solution)/shard_map/ppermute | solution.py:639
  241.8 7.9 %collective-permute-start.72 = (bf16[4,64,512]{2,1,0:T(8,128)(2,1)S(1)}, bf16[4,64,512]{2,1,0:T(8,128)(2,1)S(1)}, u32[]{:S(2)}, u32[]{:S(2)}) collective-permute-start(bf16[4,64,512]{2,1,0:T(8,128)(2,1)S(1)} %get-tuple-element.192), channel_id=1, source_target_pairs={{0,1},{1,0},{2,3},{3,2},{4,5},{5,4},{6,7},{7,6},{8,9},{9,8},{10,11... | collective-permute-start | bytes 786440 | tf_op jit(solution)/shard_map/ppermute | solution.py:639
  243.7 7.9 %collective-permute-start.54 = (bf16[4,64,512]{2,1,0:T(8,128)(2,1)S(1)}, bf16[4,64,512]{2,1,0:T(8,128)(2,1)S(1)}, u32[]{:S(2)}, u32[]{:S(2)}) collective-permute-start(bf16[4,64,512]{2,1,0:T(8,128)(2,1)S(1)} %get-tuple-element.202), channel_id=1, source_target_pairs={{0,2},{1,3},{2,0},{3,1},{4,6},{5,7},{6,4},{7,5},{8,10},{9,11},{10,... | collective-permute-start | bytes 786440 | tf_op jit(solution)/shard_map/ppermute | solution.py:639
  244.7 8.3 %collective-permute-start.56 = (bf16[4,64,512]{2,1,0:T(8,128)(2,1)S(1)}, bf16[4,64,512]{2,1,0:T(8,128)(2,1)S(1)}, u32[]{:S(2)}, u32[]{:S(2)}) collective-permute-start(bf16[4,64,512]{2,1,0:T(8,128)(2,1)S(1)} %get-tuple-element.203), channel_id=1, source_target_pairs={{0,1},{1,0},{2,3},{3,2},{4,5},{5,4},{6,7},{7,6},{8,9},{9,8},{10,11... | collective-permute-start | bytes 786440 | tf_op jit(solution)/shard_map/ppermute | solution.py:639
  249.7 13.0 %collective-permute-start.71 = (bf16[2,4,64,512]{3,2,1,0:T(8,128)(2,1)S(1)}, bf16[2,4,64,512]{3,2,1,0:T(8,128)(2,1)S(1)}, u32[]{:S(2)}, u32[]{:S(2)}) collective-permute-start(bf16[2,4,64,512]{3,2,1,0:T(8,128)(2,1)S(1)} %get-tuple-element.189), channel_id=1, source_target_pairs={{0,1},{1,0},{2,3},{3,2},{4,5},{5,4},{6,7},{7,6},{8,9},{9,8},{10,11... | collective-permute-start | bytes 1572872 | tf_op jit(solution)/shard_map/ppermute | solution.py:639
  251.5 14.2 %collective-permute-start.73 = (bf16[2,4,64,512]{3,2,1,0:T(8,128)(2,1)S(1)}, bf16[2,4,64,512]{3,2,1,0:T(8,128)(2,1)S(1)}, u32[]{:S(2)}, u32[]{:S(2)}) collective-permute-start(bf16[2,4,64,512]{3,2,1,0:T(8,128)(2,1)S(1)} %get-tuple-element.195), channel_id=1, source_target_pairs={{0,2},{1,3},{2,0},{3,1},{4,6},{5,7},{6,4},{7,5},{8,10},{9,11},{10,... | collective-permute-start | bytes 1572872 | tf_op jit(solution)/shard_map/ppermute | solution.py:639
  251.7 39.8 %collective-permute-start.9 = (bf16[256,512]{1,0:T(8,128)(2,1)S(1)}, bf16[256,512]{1,0:T(8,128)(2,1)S(1)}, u32[]{:S(2)}, u32[]{:S(2)}) collective-permute-start(bf16[256,512]{1,0:T(8,128)(2,1)S(1)} %broadcast_select_fusion.6), channel_id=1, source_target_pairs={{0,16},{1,17},{2,18},{3,19},{4,20},{5,21},{6,22},{7,23},{8,24},{9,... | collective-permute-start | bytes 786440 | tf_op jit(solution)/shard_map/ppermute | solution.py:639
  251.8 21.1 %collective-permute-start.55 = (bf16[2,4,64,512]{3,2,1,0:T(8,128)(2,1)S(1)}, bf16[2,4,64,512]{3,2,1,0:T(8,128)(2,1)S(1)}, u32[]{:S(2)}, u32[]{:S(2)}) collective-permute-start(bf16[2,4,64,512]{3,2,1,0:T(8,128)(2,1)S(1)} %get-tuple-element.200), channel_id=1, source_target_pairs={{0,1},{1,0},{2,3},{3,2},{4,5},{5,4},{6,7},{7,6},{8,9},{9,8},{10,11... | collective-permute-start | bytes 1572872 | tf_op jit(solution)/shard_map/ppermute | solution.py:639
  253.0 30.5 %collective-permute-start.41 = (bf16[2,4,32,512]{3,2,1,0:T(8,128)(2,1)S(1)}, bf16[2,4,32,512]{3,2,1,0:T(8,128)(2,1)S(1)}, u32[]{:S(2)}, u32[]{:S(2)}) collective-permute-start(bf16[2,4,32,512]{3,2,1,0:T(8,128)(2,1)S(1)} %get-tuple-element.217), channel_id=1, source_target_pairs={{0,2},{1,3},{2,0},{3,1},{4,6},{5,7},{6,4},{7,5},{8,10},{9,11},{10,... | collective-permute-start | bytes 786440 | tf_op jit(solution)/shard_map/ppermute | solution.py:639
  262.8 17.7 %collective-permute-start.57 = (bf16[2,4,64,512]{3,2,1,0:T(8,128)(2,1)S(1)}, bf16[2,4,64,512]{3,2,1,0:T(8,128)(2,1)S(1)}, u32[]{:S(2)}, u32[]{:S(2)}) collective-permute-start(bf16[2,4,64,512]{3,2,1,0:T(8,128)(2,1)S(1)} %get-tuple-element.206), channel_id=1, source_target_pairs={{0,2},{1,3},{2,0},{3,1},{4,6},{5,7},{6,4},{7,5},{8,10},{9,11},{10,... | collective-permute-start | bytes 1572872 | tf_op jit(solution)/shard_map/ppermute | solution.py:639
  265.7 19.2 %collective-permute-start.23 = (bf16[2,4,32,512]{3,2,1,0:T(8,128)(2,1)S(1)}, bf16[2,4,32,512]{3,2,1,0:T(8,128)(2,1)S(1)}, u32[]{:S(2)}, u32[]{:S(2)}) collective-permute-start(bf16[2,4,32,512]{3,2,1,0:T(8,128)(2,1)S(1)} %get-tuple-element.222), channel_id=1, source_target_pairs={{0,1},{1,0},{2,3},{3,2},{4,5},{5,4},{6,7},{7,6},{8,9},{9,8},{10,11... | collective-permute-start | bytes 786440 | tf_op jit(solution)/shard_map/ppermute | solution.py:639
  272.9 16.6 %collective-permute-start.25 = (bf16[2,4,32,512]{3,2,1,0:T(8,128)(2,1)S(1)}, bf16[2,4,32,512]{3,2,1,0:T(8,128)(2,1)S(1)}, u32[]{:S(2)}, u32[]{:S(2)}) collective-permute-start(bf16[2,4,32,512]{3,2,1,0:T(8,128)(2,1)S(1)} %get-tuple-element.228), channel_id=1, source_target_pairs={{0,2},{1,3},{2,0},{3,1},{4,6},{5,7},{6,4},{7,5},{8,10},{9,11},{10,... | collective-permute-start | bytes 786440 | tf_op jit(solution)/shard_map/ppermute | solution.py:639
  280.4 24.7 %collective-permute-start.74 = (bf16[2048,512]{1,0:T(8,128)(2,1)S(1)}, bf16[2048,512]{1,0:T(8,128)(2,1)}, u32[]{:S(2)}, u32[]{:S(2)}) collective-permute-start(bf16[2048,512]{1,0:T(8,128)(2,1)S(1)} %bitcast.327), channel_id=1, source_target_pairs={{0,16},{1,17},{2,18},{3,19},{4,20},{5,21},{6,22},{7,23},{8,24},{9,... | collective-permute-start | bytes 6291464 | tf_op jit(solution)/shard_map/ppermute | solution.py:639
  283.5 21.7 %collective-permute-start.58 = (bf16[2048,512]{1,0:T(8,128)(2,1)S(1)}, bf16[2048,512]{1,0:T(8,128)(2,1)}, u32[]{:S(2)}, u32[]{:S(2)}) collective-permute-start(bf16[2048,512]{1,0:T(8,128)(2,1)S(1)} %bitcast.329), channel_id=1, source_target_pairs={{16,0},{17,1},{18,2},{19,3},{20,4},{21,5},{22,6},{23,7},{24,8},{25... | collective-permute-start | bytes 6291464 | tf_op jit(solution)/shard_map/ppermute | solution.py:639
  285.0 11.4 %collective-permute-start.42 = (bf16[1024,512]{1,0:T(8,128)(2,1)S(1)}, bf16[1024,512]{1,0:T(8,128)(2,1)S(1)}, u32[]{:S(2)}, u32[]{:S(2)}) collective-permute-start(bf16[1024,512]{1,0:T(8,128)(2,1)S(1)} %bitcast.335), channel_id=1, source_target_pairs={{0,16},{1,17},{2,18},{3,19},{4,20},{5,21},{6,22},{7,23},{8,24},{9,... | collective-permute-start | bytes 3145736 | tf_op jit(solution)/shard_map/ppermute | solution.py:639
  (49 other events, 336.8 us)

commit v2 on v1

v2 whole, which is shorter than its diff:
```python
import functools

import jax
import jax.numpy as jnp
from jax import lax
from jax.experimental import pallas as pl
from jax.experimental.pallas import tpu as pltpu
from jax.sharding import PartitionSpec as P

SIDE_S = 8
SIDE_M = 12
CANVAS = 16
PIX = CANVAS * CANVAS
C = 512
FF = 2048
LANES = 128
GROUPS = 8
EPS = 1e-06
KS = 7
PAD_ROWS = (CANVAS + 6) * CANVAS
BF = jnp.bfloat16
F32 = jnp.float32
VMEM_BYTES = 56 * 1024 * 1024

V_N1G, V_N1S, V_BIN, V_CB, V_B1, V_B2, V_B3, V_BO, V_BS, V_N2G, V_N2S, V_BE, V_BR, V_MS = range(14)
VEC_ROWS = 16


def nn(a, b):
    return jnp.dot(a, b, preferred_element_type=F32)


def nt(a, b):
    return lax.dot_general(a, b, (((1,), (1,)), ((), ())), preferred_element_type=F32)


def tn(a, b):
    return lax.dot_general(a, b, (((0,), (0,)), ((), ())), preferred_element_type=F32)


def colsum(v):
    return jnp.sum(v, axis=0, keepdims=True)


def wide(m, n):
    return jnp.concatenate([m] * n, axis=1)


def place_of(block):
    section = lax.axis_index("section")
    place = lax.axis_index("dp") % 16
    x_bit, y_bit, z_at = place & 1, (place >> 1) & 1, place >> 2
    mask_a = section * 16 + x_bit * 8 + y_bit * 4 + z_at
    mask_b = section * 16 + y_bit * 8 + x_bit * 4 + z_at
    return section ^ block, section, (mask_a, mask_b)


def fill_mask(mask_ref, crop_ref, section):
    kind = crop_ref[section, 0]
    side = jnp.where(kind == 0, SIDE_S, jnp.where(kind == 1, SIDE_M, CANVAS))
    r = lax.broadcasted_iota(jnp.int32, (PIX, LANES), 0)
    inside = ((r // CANVAS) < side) & ((r % CANVAS) < side)
    mask_ref[...] = inside.astype(F32)


def start_select(sel, pairs, sems):
    for i, (own, other, dst) in enumerate(pairs):

        @pl.when(sel == 0)
        def _():
            pltpu.make_async_copy(own, dst, sems.at[i]).start()

        @pl.when(sel != 0)
        def _():
            pltpu.make_async_copy(other, dst, sems.at[i]).start()


def wait_select(i, pairs, sems):
    own, other, dst = pairs[i]
    pltpu.make_async_copy(own, dst, sems.at[i]).wait()


def conv_rows(src_ref, taps_ref, flip, bias, store):
    def row(h, carry):
        accs = [bias] * CANVAS if bias is not None else [None] * CANVAS
        for a in range(KS):
            ks = []
            for e in range(KS):
                t = (KS - 1 - a) * KS + (KS - 1 - e) if flip else a * KS + e
                ks.append(taps_ref[t * GROUPS : (t + 1) * GROUPS, :])
            for w2 in range(CANVAS):
                x = src_ref[pl.ds(pl.multiple_of(((h + a) * CANVAS + w2) * GROUPS, GROUPS), GROUPS), :]
                for e in range(KS):
                    w = w2 + 3 - e
                    if 0 <= w < CANVAS:
                        term = x * ks[e]
                        accs[w] = term if accs[w] is None else accs[w] + term
        for w in range(CANVAS):
            store(h * CANVAS + w, accs[w])
        return carry

    lax.fori_loop(0, CANVAS, row, 0)


def zero_border(ref):
    zeros = jnp.zeros((3 * CANVAS * GROUPS, LANES), F32)
    ref[0 : 3 * CANVAS * GROUPS, :] = zeros
    ref[(PAD_ROWS - 3 * CANVAS) * GROUPS :, :] = zeros


def lane_group(ref, g, rows=PIX, base=0):
    return ref[pl.ds(base + g, rows, stride=GROUPS), :]


def pack_kernel(*refs):
    vectors, taps_in, w1, w2, w3 = refs[:14], refs[14], refs[15], refs[16], refs[17]
    vec_ref, taps_ref, gates_ref = refs[18:]
    gates_ref[0:256, :] = w3[...]
    gates_ref[256:384, 0:256] = w2[...]
    gates_ref[256:384, 256:384] = jnp.concatenate([w1[...], jnp.zeros((64, 128), BF)], axis=0)
    gates_ref[256:384, 384:512] = jnp.zeros((128, 128), BF)
    vec_ref[...] = jnp.zeros_like(vec_ref)
    for row, ref in enumerate(vectors):
        n = ref.shape[1]
        vec_ref[row : row + 1, 0:n] = ref[...].astype(F32)
    taps = taps_in[...].astype(F32)
    bias = vectors[V_CB][...].astype(F32)
    for g in range(GROUPS):
        if g == 0:
            t = jnp.concatenate([jnp.zeros((49, 64), F32), taps[:, 0:64]], axis=1)
            b = jnp.concatenate([jnp.zeros((1, 64), F32), bias[:, 0:64]], axis=1)
        else:
            t = taps[:, g * LANES - 64 : g * LANES + 64]
            b = bias[:, g * LANES - 64 : g * LANES + 64]
        taps_ref[pl.ds(g, 49, stride=GROUPS), :] = t
        taps_ref[49 * GROUPS + g : 49 * GROUPS + g + 1, :] = b


def gn_forward_kernel(
    block, crop_ref, x_any, vec_a, vec_b, taps_a, taps_b,
    gates_a, gates_b, win_a, win_b, wo_a, wo_b,
    n1_ref, cin_ref, mix_ref, p_ref, gl_ref, mid_ref, br_ref,
    mask_ref, x_ref, vec_ref, taps_ref, mx_ref, gates, win, wo, sems,
):
    sel, section, _ = place_of(block)
    pairs = [
        (vec_a, vec_b, vec_ref), (win_a, win_b, win), (taps_a, taps_b, taps_ref), (gates_a, gates_b, gates),
        (wo_a, wo_b, wo),
    ]
    x_copy = pltpu.make_async_copy(x_any.at[section if block == 0 else 0], x_ref, sems.at[7])
    x_copy.start()
    start_select(sel, pairs, sems)
    fill_mask(mask_ref, crop_ref, section)
    zero_border(cin_ref)
    x_copy.wait()
    wait_select(0, pairs, sems)

    def vec(row, lo, n):
        return vec_ref[row : row + 1, lo : lo + n]

    def norm_in(i, carry):
        r = pl.ds(pl.multiple_of(i * 32, 32), 32)
        start = x_ref[r, :].astype(F32) * wide(mask_ref[r, :], 4)
        cen = start - jnp.mean(start, axis=-1, keepdims=True)
        inv = lax.rsqrt(jnp.mean(cen * cen, axis=-1, keepdims=True) + EPS)
        n1_ref[r, :] = (cen * inv * vec(V_N1G, 0, C) + vec(V_N1S, 0, C)).astype(BF)
        return carry

    lax.fori_loop(0, PIX // 32, norm_in, 0)
    wait_select(1, pairs, sems)
    for n in range(4):
        m = nn(n1_ref[...], win[:, n * 256 : (n + 1) * 256]) + vec(V_BIN, n * 256, 256)
        for half in range(2):
            g = 2 * n + half
            v = m[:, half * LANES : (half + 1) * LANES] * mask_ref[...]
            cin_ref[pl.ds(3 * CANVAS * GROUPS + g, PIX, stride=GROUPS), :] = v
            if g == 0:
                p_ref[:, 0:LANES] = v
    wait_select(2, pairs, sems)
    bias = taps_ref[49 * GROUPS : 50 * GROUPS, :]

    def keep(pixel, acc):
        mx_ref[pl.ds(pl.multiple_of(pixel * GROUPS, GROUPS), GROUPS), :] = acc * (1.0 / 3.0)

    conv_rows(cin_ref, taps_ref, False, bias, keep)
    for g in range(GROUPS):
        mix_ref[:, g * LANES : (g + 1) * LANES] = lane_group(mx_ref, g)
    wait_select(3, pairs, sems)
    wait_select(4, pairs, sems)
    gl_ref[:, 0:128] = (p_ref[:, 0:128] * pltpu.roll(mix_ref[:, 0:128], 64, 1)).astype(BF)
    p1 = nn(gl_ref[:, 0:128], gates[256:384, 256:384]) + vec(V_B1, 0, 128)
    p_ref[:, 128:256] = p1
    gl_ref[:, 128:256] = (p1 * mix_ref[:, 128:256]).astype(BF)
    p2 = nn(gl_ref[:, 128:256], gates[256:384, 0:256]) + vec(V_B2, 0, 256)
    p_ref[:, 256:512] = p2
    gl_ref[:, 256:512] = (p2 * mix_ref[:, 256:512]).astype(BF)
    for n in range(2):
        c = 256 * n
        p3 = nn(gl_ref[:, 256:512], gates[0:256, c : c + 256]) + vec(V_B3, c, 256)
        p_ref[:, 512 + c : 768 + c] = p3
        gl_ref[:, 512 + c : 768 + c] = (p3 * mix_ref[:, 512 + c : 768 + c]).astype(BF)
    for n in range(2):
        c = 256 * n
        br = nn(gl_ref[:, 512:1024], wo[:, c : c + 256]) + vec(V_BO, c, 256)
        br_ref[:, c : c + 256] = br.astype(BF)
        start = x_ref[:, c : c + 256].astype(F32) * wide(mask_ref[...], 2)
        mid_ref[:, c : c + 256] = start + vec(V_BS, c, 256) * br


def mlp_forward_kernel(
    block, crop_ref, field_ref, mid_ref, vec_a, vec_b, we_a, we_b, wr_a, wr_b,
    n2_ref, act_ref, slope_ref, out_ref, res_ref, swap_ref,
    mask_ref, vec_ref, we, wr, sems,
):
    sel, section, _ = place_of(block)
    pairs = [(vec_a, vec_b, vec_ref), (we_a, we_b, we), (wr_a, wr_b, wr)]
    start_select(sel, pairs, sems)
    fill_mask(mask_ref, crop_ref, section)
    wait_select(0, pairs, sems)

    def vec(row, lo, n):
        return vec_ref[row : row + 1, lo : lo + n]

    def norm_mid(i, carry):
        r = pl.ds(pl.multiple_of(i * 32, 32), 32)
        mid = mid_ref[r, :]
        cen = mid - jnp.mean(mid, axis=-1, keepdims=True)
        inv = lax.rsqrt(jnp.mean(cen * cen, axis=-1, keepdims=True) + EPS)
        n2_ref[r, :] = (cen * inv * vec(V_N2G, 0, C) + vec(V_N2S, 0, C)).astype(BF)
        return carry

    lax.fori_loop(0, PIX // 32, norm_mid, 0)
    wait_select(1, pairs, sems)
    for j in range(8):
        c = 256 * j
        pre = nn(n2_ref[...], we[:, c : c + 256]) + vec(V_BE, c, 256)
        cum = 0.5 * (1.0 + lax.erf(pre * 0.7071067811865476))
        act_ref[:, c : c + 256] = (pre * cum).astype(BF)
        slope = cum + pre * jnp.exp(-0.5 * pre * pre) * 0.3989422804014327
        slope_ref[:, c : c + 256] = slope.astype(BF)
    wait_select(2, pairs, sems)
    for n in range(2):
        c = 256 * n
        out = nn(act_ref[...], wr[:, c : c + 256]) + vec(V_BR, c, 256)
        out_ref[:, c : c + 256] = out.astype(BF)
        res = wide(mask_ref[...], 2) * (mid_ref[:, c : c + 256] + vec(V_MS, c, 256) * out)
        res_ref[:, c : c + 256] = res.astype(BF)
        if block == 1:
            swap_ref[:, c : c + 256] = jnp.where(section == 0, res.astype(BF), field_ref[0, :, c : c + 256])


def piece_rows(masks, p, rows):
    return pl.multiple_of((p ^ masks[p >> 4]) * rows, 64)


def mlp_kernel(
    block, crop_ref, dy_any, vec_a, vec_b, n2_ref, act_ref, slope_ref, out_ref, mid_ref, we_a, we_b, wr_a, wr_b, *rest,
):
    (dmid_ref, mvec_ref, keep_ref, send_ref,
     mask_ref, dy_ref, vec_ref, dout_ref, dpre_ref, dn2_ref, bucket, we, wr, sems) = rest[-14:]
    sel, section, masks = place_of(block)
    pairs = [(vec_a, vec_b, vec_ref), (wr_a, wr_b, wr), (we_a, we_b, we)]
    dy_copy = pltpu.make_async_copy(dy_any.at[section if block == 1 else 0], dy_ref, sems.at[3])
    dy_copy.start()
    start_select(sel, pairs, sems)
    fill_mask(mask_ref, crop_ref, section)
    mvec_ref[...] = jnp.zeros_like(mvec_ref)
    dy_copy.wait()
    wait_select(0, pairs, sems)

    def vec(row, lo, n):
        return vec_ref[row : row + 1, lo : lo + n]

    for n in range(2):
        c = 256 * n
        dyr = dy_ref[:, c : c + 256].astype(F32) * wide(mask_ref[...], 2)
        dmid_ref[:, c : c + 256] = dyr
        dout = (vec(V_MS, c, 256) * dyr).astype(BF)
        dout_ref[:, c : c + 256] = dout
        mvec_ref[3:4, c : c + 256] = colsum(dout.astype(F32))
        mvec_ref[4:5, c : c + 256] = colsum(dyr * out_ref[:, c : c + 256].astype(F32))
    wait_select(1, pairs, sems)
    for j in range(8):
        c = 256 * j
        dw = tn(act_ref[:, c : c + 256], dout_ref[...]).astype(BF)
        for q in range(4):
            bucket[pl.ds(piece_rows(masks, 4 * j + q, 128), 64), :] = dw[64 * q : 64 * q + 64, :]
        dact = nt(dout_ref[...], wr[c : c + 256, :])
        dpre = (dact * slope_ref[:, c : c + 256].astype(F32)).astype(BF)
        dpre_ref[:, c : c + 256] = dpre
        mvec_ref[2:3, c : c + 256] = colsum(dpre.astype(F32))
    wait_select(2, pairs, sems)
    for cb in range(4):
        dw = tn(n2_ref[...], dpre_ref[:, 512 * cb : 512 * cb + 512]).astype(BF)
        for q in range(8):
            rows = pl.multiple_of(piece_rows(masks, 8 * cb + q, 128) + 64, 64)
            bucket[pl.ds(rows, 64), :] = dw[64 * q : 64 * q + 64, :]
    keep_copy = pltpu.make_async_copy(bucket.at[0:2048], keep_ref, sems.at[4])
    send_copy = pltpu.make_async_copy(bucket.at[2048:4096], send_ref, sems.at[5])
    send_copy.start()
    keep_copy.start()
    for n in range(2):
        c = 256 * n
        dn2_ref[:, c : c + 256] = nt(dpre_ref[...], we[c : c + 256, :])

    def norm_back(i, carry):
        dgain, dshift = carry
        r = pl.ds(pl.multiple_of(i * 32, 32), 32)
        mid = mid_ref[r, :]
        cen = mid - jnp.mean(mid, axis=-1, keepdims=True)
        inv = lax.rsqrt(jnp.mean(cen * cen, axis=-1, keepdims=True) + EPS)
        xhat = cen * inv
        up = dn2_ref[r, :]
        g = up * vec(V_N2G, 0, C)
        inner = g - jnp.mean(g, axis=-1, keepdims=True) - xhat * jnp.mean(g * xhat, axis=-1, keepdims=True)
        dmid_ref[r, :] = dmid_ref[r, :] + inv * inner
        return dgain + colsum(up * xhat), dshift + colsum(up)

    zero = jnp.zeros((1, C), F32)
    dgain, dshift = lax.fori_loop(0, PIX // 32, norm_back, (zero, zero))
    mvec_ref[0:1, 0:C] = dgain
    mvec_ref[1:2, 0:C] = dshift
    send_copy.wait()
    keep_copy.wait()


def gn_back_kernel(
    block, crop_ref, x_any, next_any, dmid_ref, mvec_ref, vec_a, vec_b, taps_a, taps_b, gates_a, gates_b,
    mix_ref, p_ref, gl_ref, br_ref, win_a, win_b, wo_a, wo_b, *rest,
):
    (dv_ref, dvb_ref, dbr_ref, dp_ref, dmg_ref, dcp_ref, gvec_ref, swap_ref,
     mask_ref, x_ref, next_ref, vec_ref, taps_ref, dg_ref, dmix_ref, ds_ref, dn1_ref, gates, win, wo, sems) = rest[-21:]
    sel, section, _ = place_of(block)
    pairs = [
        (vec_a, vec_b, vec_ref), (wo_a, wo_b, wo), (gates_a, gates_b, gates), (taps_a, taps_b, taps_ref),
        (win_a, win_b, win),
    ]
    x_copy = pltpu.make_async_copy(x_any.at[section if block == 0 else 0], x_ref, sems.at[7])
    start_select(sel, pairs, sems)
    x_copy.start()
    if block == 0:
        next_copy = pltpu.make_async_copy(next_any, next_ref, sems.at[5])
        next_copy.start()
    fill_mask(mask_ref, crop_ref, section)
    zero_border(dcp_ref)
    wait_select(0, pairs, sems)

    def vec(row, lo, n):
        return vec_ref[row : row + 1, lo : lo + n]

    dbs, dbo = [], []
    for n in range(2):
        c = 256 * n
        dm = dmid_ref[:, c : c + 256]
        dbs.append(colsum(dm * br_ref[:, c : c + 256].astype(F32)))
        dbr = (vec(V_BS, c, 256) * dm).astype(BF)
        dbr_ref[:, c : c + 256] = dbr
        dbo.append(colsum(dbr.astype(F32)))
    wait_select(1, pairs, sems)
    wait_select(2, pairs, sems)
    db3 = []
    for n in range(2):
        c = 256 * n
        dg = nt(dbr_ref[...], wo[c : c + 256, :])
        dp = (dg * mix_ref[:, 512 + c : 768 + c]).astype(BF)
        dmix_ref[:, 512 + c : 768 + c] = dg * p_ref[:, 512 + c : 768 + c] * (1.0 / 3.0)
        dp_ref[:, 512 + c : 768 + c] = dp
        db3.append(colsum(dp.astype(F32)))
    dg = nt(dp_ref[:, 512:1024], gates[0:256, :])
    dp = (dg * mix_ref[:, 256:512]).astype(BF)
    dmix_ref[:, 256:512] = dg * p_ref[:, 256:512] * (1.0 / 3.0)
    dp_ref[:, 256:512] = dp
    db2 = colsum(dp.astype(F32))
    dg = nt(dp_ref[:, 256:512], gates[256:384, 0:256])
    dp = (dg * mix_ref[:, 128:256]).astype(BF)
    dmix_ref[:, 128:256] = dg * p_ref[:, 128:256] * (1.0 / 3.0)
    dp_ref[:, 128:256] = dp
    db1 = colsum(dp.astype(F32))
    dg = nt(dp_ref[:, 128:256], gates[256:384, 256:384])
    dmix_ref[:, 0:128] = pltpu.roll(dg * p_ref[:, 0:128], 64, 1) * (1.0 / 3.0)
    dg_ref[...] = dg * pltpu.roll(mix_ref[:, 0:128], 64, 1)
    dp_ref[:, 0:128] = jnp.zeros((PIX, LANES), BF)
    for g in range(GROUPS):
        dcp_ref[pl.ds(3 * CANVAS * GROUPS + g, PIX, stride=GROUPS), :] = dmix_ref[:, g * LANES : (g + 1) * LANES]
    wait_select(3, pairs, sems)

    def keep(pixel, acc):
        ds_ref[pl.ds(pl.multiple_of(pixel * GROUPS, GROUPS), GROUPS), :] = acc

    conv_rows(dcp_ref, taps_ref, True, None, keep)
    dbin = []
    for g in range(GROUPS):
        d = lane_group(ds_ref, g) * mask_ref[...]
        if g == 0:
            d = d + dg_ref[...]
        d = d.astype(BF)
        dmg_ref[:, g * LANES : (g + 1) * LANES] = d
        dbin.append(colsum(d.astype(F32)))
    wait_select(4, pairs, sems)
    x_copy.wait()
    if block == 0:
        next_copy.wait()
    for n in range(2):
        c = 256 * n
        dn1_ref[:, c : c + 256] = nt(dmg_ref[...], win[c : c + 256, :])

    def norm_back(i, carry):
        dgain, dshift = carry
        r = pl.ds(pl.multiple_of(i * 32, 32), 32)
        m = wide(mask_ref[r, :], 4)
        start = x_ref[r, :].astype(F32) * m
        cen = start - jnp.mean(start, axis=-1, keepdims=True)
        inv = lax.rsqrt(jnp.mean(cen * cen, axis=-1, keepdims=True) + EPS)
        xhat = cen * inv
        up = dn1_ref[r, :]
        g = up * vec(V_N1G, 0, C)
        inner = g - jnp.mean(g, axis=-1, keepdims=True) - xhat * jnp.mean(g * xhat, axis=-1, keepdims=True)
        dv = m * (dmid_ref[r, :] + inv * inner)
        dv_ref[r, :] = dv
        dvb_ref[r, :] = dv.astype(BF)
        if block == 0:
            swap_ref[r, :] = jnp.where(section == 0, next_ref[r, :], dv)
        return dgain + colsum(up * xhat), dshift + colsum(up)

    zero = jnp.zeros((1, C), F32)
    dgain, dshift = lax.fori_loop(0, PIX // 32, norm_back, (zero, zero))
    z = jnp.zeros((1, LANES), F32)
    rows = [
        dgain,
        dshift,
        jnp.concatenate(dbin[0:4], axis=1),
        jnp.concatenate(dbin[4:8], axis=1),
        jnp.concatenate([db1, z, z, z], axis=1),
        jnp.concatenate([db2, z, z], axis=1),
        jnp.concatenate(db3, axis=1),
        jnp.concatenate(dbo, axis=1),
        jnp.concatenate(dbs, axis=1),
        mvec_ref[0:1, 0:C],
        mvec_ref[1:2, 0:C],
        mvec_ref[2:3, 0:512],
        mvec_ref[2:3, 512:1024],
        mvec_ref[2:3, 1024:1536],
        mvec_ref[2:3, 1536:2048],
        mvec_ref[3:4, 0:C],
        mvec_ref[4:5, 0:C],
    ]
    rows.append(jnp.zeros((32 - len(rows), C), F32))
    gvec_ref[...] = jnp.concatenate(rows, axis=0).astype(BF)


def gn_weights_kernel(block, n1_ref, gl_ref, dbr_ref, dp_ref, dmg_ref, gvec_ref, cin_any, dcp_any, *rest):
    keep_ref, send_ref, dk_ref, cin_ref, dcp_ref, bucket, sems = rest[-7:]
    _, _, masks = place_of(block)
    cin_copy = pltpu.make_async_copy(cin_any, cin_ref, sems.at[0])
    dcp_copy = pltpu.make_async_copy(dcp_any, dcp_ref, sems.at[1])
    cin_copy.start()
    dcp_copy.start()

    def put(p, val, sub=0):
        n = val.shape[0]
        bucket[pl.ds(pl.multiple_of(piece_rows(masks, p, 64) + sub, 16), n), :] = val

    for cb in range(2):
        dw = tn(n1_ref[...], dmg_ref[:, 512 * cb : 512 * cb + 512]).astype(BF)
        for q in range(8):
            put(8 * cb + q, dw[64 * q : 64 * q + 64, :])
    dw = tn(gl_ref[:, 512:1024], dbr_ref[...]).astype(BF)
    for q in range(8):
        put(16 + q, dw[64 * q : 64 * q + 64, :])
    dw = tn(gl_ref[:, 256:512], dp_ref[:, 512:1024]).astype(BF)
    for q in range(4):
        put(24 + q, dw[64 * q : 64 * q + 64, :])
    dw = tn(gl_ref[:, 128:256], dp_ref[:, 256:512]).astype(BF)
    put(28, jnp.concatenate([dw[0:64, :], dw[64:128, :]], axis=1))
    dw1 = tn(gl_ref[:, 0:128], dp_ref[:, 128:256]).astype(BF)
    put(31, jnp.concatenate([dw1[16 * i : 16 * i + 16, :] for i in range(4)], axis=1))
    put(31, jnp.zeros((16, 512), BF), 16)
    put(31, gvec_ref[...], 32)
    cin_copy.wait()
    dcp_copy.wait()

    def vreg(ref, index):
        return ref[pl.ds(pl.multiple_of(index * GROUPS, GROUPS), GROUPS), :]

    dk_ref[...] = jnp.zeros_like(dk_ref)
    for taps in ((0, 1), (2, 3), (4, 5), (6,)):

        def row(h, accs):
            accs = list(accs)
            ds = [vreg(dcp_ref, (h + 3) * CANVAS + w) for w in range(CANVAS)]
            for i, a in enumerate(taps):
                for w2 in range(CANVAS):
                    x = vreg(cin_ref, (h + a) * CANVAS + w2)
                    for e in range(KS):
                        w = w2 + 3 - e
                        if 0 <= w < CANVAS:
                            accs[i * KS + e] = accs[i * KS + e] + x * ds[w]
            if len(taps) == 1:
                for w in range(CANVAS):
                    accs[KS] = accs[KS] + ds[w]
            return tuple(accs)

        count = len(taps) * KS + (1 if len(taps) == 1 else 0)
        accs = lax.fori_loop(0, CANVAS, row, tuple(jnp.zeros((GROUPS, LANES), F32) for _ in range(count)))
        for i in range(count):
            t = taps[0] * KS + i
            dk_ref[t * GROUPS : (t + 1) * GROUPS, :] = accs[i]
    for half in range(2):
        dk = jnp.concatenate([lane_group(dk_ref, 4 * half + i, 64) for i in range(4)], axis=1).astype(BF)
        put(29 + half, dk)
    send_copy = pltpu.make_async_copy(bucket.at[1024:2048], send_ref, sems.at[2])
    keep_copy = pltpu.make_async_copy(bucket.at[0:1024], keep_ref, sems.at[3])
    send_copy.start()
    keep_copy.start()
    send_copy.wait()
    keep_copy.wait()


def start_pieces(layout, rows, halves, buf, sems):
    _, section, masks = place_of(0)
    for p in range(32):
        rel = p ^ masks[p >> 4]
        far = rel >> 4
        dst = buf.at[p * rows : (p + 1) * rows]
        sem = sems.at[p // 4]
        for sec in range(2):
            stride, first = layout[sec]
            off = pl.multiple_of((rel & 15) * stride + first, 64)
            for side in range(2):

                @pl.when((section == sec) & (far == side))
                def _():
                    pltpu.make_async_copy(halves[2 * sec + side].at[pl.ds(off, rows)], dst, sem).start()


def wait_pieces(i, rows, halves, buf, sems):
    part = buf.at[pl.ds(i * 4 * rows, 4 * rows)]
    pltpu.make_async_copy(halves[0].at[pl.ds(0, 4 * rows)], part, sems.at[i]).wait()


def mlp_finish_kernel(layout, *refs):
    halves = refs[:4]
    wr_any, we_any, buf, wr_ref, we_ref, sems, out_sems = refs[-7:]
    start_pieces(layout, 128, halves, buf, sems)
    copies = []
    for i in range(8):
        wait_pieces(i, 128, halves, buf, sems)
        cb = i // 2
        for q in range(4):
            p = 4 * i + q
            r = p % 8
            wr_ref[64 * p : 64 * p + 64, :] = buf[128 * p : 128 * p + 64, :].astype(F32)
            we_ref[64 * r : 64 * r + 64, 512 * cb : 512 * cb + 512] = buf[128 * p + 64 : 128 * p + 128, :].astype(F32)
        rows = slice(256 * i, 256 * i + 256)
        copies.append(pltpu.make_async_copy(wr_ref.at[rows], wr_any.at[rows], out_sems.at[i]))
        half = slice(256 * (i % 2), 256 * (i % 2) + 256)
        cols = slice(512 * cb, 512 * cb + 512)
        copies.append(pltpu.make_async_copy(we_ref.at[half, cols], we_any.at[half, cols], out_sems.at[8 + i]))
        copies[-2].start()
        copies[-1].start()
    for copy in copies:
        copy.wait()


def gn_finish_kernel(layout, *refs):
    halves = refs[:4]
    (n1g, n1s, win, bin_, conv, cbias, w1, b1, w2, b2, w3, b3, wo, bo, bs, n2g, n2s, be, br, ms, buf, sems) = refs[-22:]
    start_pieces(layout, 64, halves, buf, sems)
    for i in range(8):
        wait_pieces(i, 64, halves, buf, sems)
    for cb in range(2):
        win[:, 512 * cb : 512 * cb + 512] = buf[512 * cb : 512 * cb + 512, :].astype(F32)
    wo[...] = buf[1024:1536, :].astype(F32)
    w3[...] = buf[1536:1792, :].astype(F32)
    for i in range(2):
        w2[64 * i : 64 * i + 64, :] = buf[1792:1856, 256 * i : 256 * i + 256].astype(F32)
    for i in range(4):
        w1[16 * i : 16 * i + 16, :] = buf[1984:2000, 128 * i : 128 * i + 128].astype(F32)
    taps = jnp.concatenate([buf[1856:1920, :], buf[1920:1984, :]], axis=1).astype(F32)
    conv[...] = taps[0:49, 64:1024]
    cbias[...] = taps[49:50, 64:1024]
    v = buf[2016:2048, :].astype(F32)
    n1g[...] = v[0:1]
    n1s[...] = v[1:2]
    bin_[:, 0:512] = v[2:3]
    bin_[:, 512:1024] = v[3:4]
    b1[...] = v[4:5, 0:128]
    b2[...] = v[5:6, 0:256]
    b3[...] = v[6:7]
    bo[...] = v[7:8]
    bs[...] = v[8:9]
    n2g[...] = v[9:10]
    n2s[...] = v[10:11]
    for i in range(4):
        be[:, 512 * i : 512 * i + 512] = v[11 + i : 12 + i]
    br[...] = v[15:16]
    ms[...] = v[16:17]


def place_kernel(first, second, got, out):
    section = lax.axis_index("section")

    @pl.when(section == 0)
    def _():
        out[0] = first[...]
        out[1] = got[...]

    @pl.when(section != 0)
    def _():
        out[0] = got[...]
        out[1] = second[...]


SMEM = pl.BlockSpec(memory_space=pltpu.SMEM)
VM = pl.BlockSpec(memory_space=pltpu.VMEM)
ANY = pl.BlockSpec(memory_space=pl.ANY)


def sds(shape, dtype):
    return jax.ShapeDtypeStruct(shape, dtype)


def vmem(rows, cols, dtype):
    return pltpu.VMEM((rows, cols), dtype)


def call(kernel, name, operands, outs, scratch, micros):
    return pl.pallas_call(
        kernel,
        name=name,
        out_shape=[shape for _, shape in outs],
        in_specs=[spec for spec, _ in operands],
        out_specs=[spec for spec, _ in outs],
        scratch_shapes=scratch,
        compiler_params=pltpu.CompilerParams(vmem_limit_bytes=VMEM_BYTES),
        cost_estimate=pl.CostEstimate(flops=int(micros * 1e9), bytes_accessed=int(micros * 3e6), transcendentals=0),
    )(*[array for _, array in operands])


def on(spec, *arrays):
    return [(spec, a) for a in arrays]


SMALL = [vmem(VEC_ROWS, FF, F32)]
TAPS = [vmem(50 * GROUPS, LANES, F32)]
GN_MATS = [vmem(384, 512, BF), vmem(C, 1024, BF), vmem(512, 512, BF)]
FIELD_F32, FIELD_BF = sds((PIX, C), F32), sds((PIX, C), BF)
CONV_F32 = sds((PAD_ROWS * GROUPS, LANES), F32)
WIDE_F32, WIDE_BF = sds((PIX, 1024), F32), sds((PIX, 1024), BF)


def run_pack(vectors, taps, gates):
    outs = on(VM, sds((VEC_ROWS, FF), F32), sds((50 * GROUPS, LANES), F32), sds((384, 512), BF))
    return call(pack_kernel, "pack", on(VM, *vectors, taps, *gates), outs, [], 2)


def run_gn_forward(block, crop, x, small, mats):
    flat = [r for pair in mats[:2] for r in pair]
    outs = on(VM, FIELD_BF, CONV_F32, WIDE_F32, WIDE_F32, WIDE_BF, FIELD_F32, FIELD_BF)
    scratch = [vmem(PIX, LANES, F32), vmem(PIX, C, BF)] + SMALL + TAPS + [vmem(PIX * GROUPS, LANES, F32)] + GN_MATS
    scratch += [pltpu.SemaphoreType.DMA((8,))]
    return call(functools.partial(gn_forward_kernel, block), "gnconv_forward",
                on(SMEM, crop) + on(ANY, x, *small, *flat), outs, scratch, 8)


def run_mlp_forward(block, crop, field, mid, small, mats):
    outs = on(VM, FIELD_BF, sds((PIX, FF), BF), sds((PIX, FF), BF), FIELD_BF, FIELD_BF)
    outs += on(VM, FIELD_BF) if block == 1 else on(ANY, FIELD_BF)
    scratch = [vmem(PIX, LANES, F32)] + SMALL + [vmem(C, FF, BF), vmem(FF, C, BF), pltpu.SemaphoreType.DMA((3,))]
    return call(functools.partial(mlp_forward_kernel, block), "mlp_forward",
                on(SMEM, crop) + on(VM if block == 1 else ANY, field) + on(VM, mid) + on(ANY, *small[:2], *mats[2], *mats[3]),
                outs, scratch, 5)


def run_mlp_back(block, crop, dy, small, n2, act, slope, out, mid, mats):
    outs = on(VM, FIELD_F32, sds((8, FF), F32)) + on(ANY, sds((2048, 512), BF), sds((2048, 512), BF))
    scratch = [vmem(PIX, LANES, F32), vmem(PIX, C, BF)] + SMALL + [
        vmem(PIX, C, BF), vmem(PIX, FF, BF), vmem(PIX, C, F32), vmem(4096, 512, BF), vmem(C, FF, BF), vmem(FF, C, BF),
        pltpu.SemaphoreType.DMA((6,)),
    ]
    operands = on(SMEM, crop) + on(ANY, dy, *small[:2]) + on(VM, n2, act, slope, out, mid)
    operands += on(ANY, *mats[2], *mats[3])
    return call(functools.partial(mlp_kernel, block), "mlp_backward", operands, outs, scratch, 2)


def run_gn_back(block, crop, x, following, dmid, mvec, small, mix, p, gl, br, mats):
    flat = [r for pair in mats[:2] for r in pair]
    outs = on(VM, FIELD_F32, FIELD_BF, FIELD_BF, WIDE_BF, WIDE_BF, CONV_F32, sds((32, 512), BF))
    outs += on(VM if block == 0 else ANY, FIELD_F32)
    scratch = [vmem(PIX, LANES, F32), vmem(PIX, C, BF), vmem(PIX, C, F32)] + SMALL + TAPS + [
        vmem(PIX, LANES, F32), vmem(PIX, 1024, F32), vmem(PIX * GROUPS, LANES, F32), vmem(PIX, C, F32),
    ] + GN_MATS + [pltpu.SemaphoreType.DMA((8,))]
    operands = on(SMEM, crop) + on(ANY, x, following) + on(VM, dmid, mvec) + on(ANY, *small) + on(VM, mix, p, gl, br)
    operands += on(ANY, *flat)
    return call(functools.partial(gn_back_kernel, block), "gnconv_backward", operands, outs, scratch, 2)


def run_gn_weights(block, n1, gl, dbr, dp, dmg, gvec, cin, dcp):
    outs = on(ANY, sds((1024, 512), BF), sds((1024, 512), BF))
    scratch = [vmem(64 * GROUPS, LANES, F32), vmem(PAD_ROWS * GROUPS, LANES, F32), vmem(PAD_ROWS * GROUPS, LANES, F32),
               vmem(2048, 512, BF), pltpu.SemaphoreType.DMA((4,))]
    operands = on(VM, n1, gl, dbr, dp, dmg, gvec) + on(ANY, cin, dcp)
    return call(functools.partial(gn_weights_kernel, block), "gnconv_weights", operands, outs, scratch, 2)


def turn_kernel(token, out):
    out[...] = jnp.zeros_like(out)


def run_turn(token):
    return call(turn_kernel, "turn", on(ANY, token), on(VM, sds((8, LANES), F32)), [], 0.1)[0]


def run_mlp_finish(layout, halves):
    outs = on(ANY, sds((FF, C), F32), sds((C, FF), F32))
    scratch = [vmem(4096, 512, BF), vmem(FF, C, F32), vmem(C, FF, F32), pltpu.SemaphoreType.DMA((8,)),
               pltpu.SemaphoreType.DMA((16,))]
    return call(functools.partial(mlp_finish_kernel, layout), "mlp_finish", on(ANY, *halves), outs, scratch, 20)


def run_gn_finish(layout, halves):
    widths = [512, 512, (512, 1024), 1024, (49, 960), 960, (64, 128), 128, (128, 256), 256, (256, 512), 512,
              (512, 512), 512, 512, 512, 512, 2048, 512, 512]
    outs = on(VM, *[sds((1, w) if isinstance(w, int) else w, F32) for w in widths])
    scratch = [vmem(2048, 512, BF), pltpu.SemaphoreType.DMA((8,))]
    return call(functools.partial(gn_finish_kernel, layout), "gn_finish", on(ANY, *halves), outs, scratch, 3)


def run_place(first, second, got):
    outs = on(VM, sds((2, PIX, C), first.dtype))
    return call(place_kernel, "place", on(VM, first, second, got), outs, [], 0.1)[0]


AXES = ("section", "dp")
X_BIT, Y_BIT, Z_LOW, Z_HIGH = 1, 2, 4, 8


def after(x, *others):
    return lax.optimization_barrier((x,) + others)[0]


class Links:
    def __init__(self, count):
        self.count = count
        self.token = None

    def send(self, x, section_flip, flips, only=None):
        n = self.count
        pairs = [
            (s * n + d, (s ^ section_flip) * n + (d ^ flips[s]))
            for s in range(2)
            for d in range(n)
            if only is None or s == only
        ]
        got = lax.ppermute(x, AXES, pairs)
        return got if self.token is None else after(got, self.token)

    def core(self, x, only=None):
        return self.send(x, 1, (0, 0), only)

    def first(self, x):
        return self.send(x, 0, (X_BIT, Y_BIT))

    def second(self, x):
        return self.send(x, 0, (Y_BIT, X_BIT))

    def low(self, x):
        return self.send(x, 0, (Z_LOW, Z_LOW))

    def high(self, x):
        return self.send(x, 0, (Z_HIGH, Z_HIGH))


def sum_core(links, keep, send):
    return (keep + links.core(send)).reshape(2, 2, 2, 2, keep.shape[0] // 16, 512)


def sum_first(links, parts):
    return parts[0] + links.first(parts[1])


def sum_second(links, parts):
    return parts[0] + links.second(parts[1])


def sum_low(links, parts):
    return parts[:, 0] + links.low(parts[:, 1])


def sum_high(links, parts):
    total = parts[0] + links.high(parts[1])
    chips = links.count // 16
    if chips > 1:
        groups = [[g * 16 + r for g in range(chips)] for r in range(16)]
        total = lax.psum(total, "dp", axis_index_groups=groups)
    return total


def gather_high(links, total):
    return jnp.stack([total, links.high(total)])


def gather_low(links, whole):
    return jnp.stack([whole, links.low(whole)], axis=1)


def gather_second(links, parts):
    return jnp.stack([parts, links.second(parts)])


def gather_first(links, parts):
    return jnp.stack([parts, links.first(parts)]).reshape(-1, 512)


VECTORS = (0, 1, 3, 5, 7, 9, 11, 13, 14, 15, 16, 18, 20, 21)


def on_device(links, images, cotangent, crop, *stacked):
    images = images.reshape(2, PIX, C)
    cotangent = cotangent.reshape(2, PIX, C)
    win, wo, we, wr = [stacked[i][0] for i in (2, 12, 17, 19)]
    vec, taps, gates = run_pack([stacked[i] for i in VECTORS], stacked[4][0], [stacked[i][0] for i in (6, 8, 10)])
    win_other, wo_other = links.core(win), links.core(wo)
    taps_other, vec_other, gates_other = links.core(taps), links.core(vec), links.core(gates)
    we, wr = after((we, wr), win_other, wo_other, taps_other, vec_other, gates_other)
    we_other, wr_other = links.core(we), links.core(wr)
    pairs = [(win, win_other), (wo, wo_other), (we, we_other), (wr, wr_other)]
    small = (vec, vec_other, taps, taps_other, gates, gates_other)

    field = images
    kept = []
    for block in (0, 1):
        gn = run_gn_forward(block, crop, field, small, pairs)
        mlp = run_mlp_forward(block, crop, field, gn[5], small, pairs)
        kept.append((field, gn, mlp))
        field = mlp[4].reshape(1, PIX, C)
    hidden, final, field_swap = kept[0][2][4], kept[1][2][4], kept[1][2][5]

    def mlp_back(block, dy):
        _, gn, (n2, act, slope, out, _, _) = kept[block]
        return run_mlp_back(block, crop, dy, small, n2, act, slope, out, gn[5], pairs)

    def gn_back(block, following, dmid, mvec):
        x, (_, _, mix, p, gl, _, br), _ = kept[block]
        return run_gn_back(block, crop, x, following, dmid, mvec, small, mix, p, gl, br, pairs)

    def gn_weights(block, back, gvec):
        _, (n1, cin, _, _, gl, _, _), _ = kept[block]
        _, _, dbr, dp, dmg, dcp, _, _ = back
        return run_gn_weights(block, n1, gl, dbr, dp, dmg, gvec, cin, dcp)

    together = lax.optimization_barrier
    dmid, mvec, keep_m, send_m = mlp_back(1, cotangent)

    keep_m, send_m, dmid = together((keep_m, send_m, dmid))
    back1 = gn_back(1, mvec, dmid, mvec)
    links.token = back1[6]
    m1 = sum_core(links, keep_m, send_m)

    m1, gvec = together((m1, back1[6]))
    keep_g, send_g = gn_weights(1, back1, gvec)
    links.token = keep_g
    m1 = sum_first(links, m1)

    m1, keep_g, send_g, dvb = together((m1, keep_g, send_g, back1[1]))
    dmid, mvec, keep_m, send_m = mlp_back(0, dvb.reshape(1, PIX, C))
    links.token = mvec
    m1 = sum_second(links, m1)
    g1 = sum_core(links, keep_g, send_g)

    m1, g1, keep_m, send_m, dmid = together((m1, g1, keep_m, send_m, dmid))
    back0 = gn_back(0, back1[0], dmid, mvec)
    links.token = back0[6]
    m1 = sum_low(links, m1)
    g1 = sum_first(links, g1)
    m0 = sum_core(links, keep_m, send_m)

    m1, g1, m0, gvec = together((m1, g1, m0, back0[6]))
    keep_g, send_g = gn_weights(0, back0, gvec)
    links.token = keep_g
    m1 = sum_high(links, m1)
    g1 = sum_second(links, g1)
    m0 = sum_first(links, m0)

    def turn(*values):
        *values, token = together(values + (links.token,))
        links.token = run_turn(token)
        return values

    m1, g1, m0, keep_g, send_g = turn(m1, g1, m0, keep_g, send_g)
    g0 = sum_core(links, keep_g, send_g)
    m0 = sum_second(links, m0)
    g1 = sum_low(links, g1)
    m1 = gather_high(links, m1)

    m1, g1, m0, g0, field_swap, grad_swap = turn(m1, g1, m0, g0, field_swap, back0[7])
    g0 = sum_first(links, g0)
    m1 = gather_low(links, m1)
    g1 = sum_high(links, g1)
    m0 = sum_low(links, m0)
    field_got, grad_got = links.core(field_swap), links.core(grad_swap)

    m1, g1, m0, g0, field_got, grad_got = together((m1, g1, m0, g0, field_got, grad_got))
    links.token = block_outputs = run_place(hidden, final, field_got)
    g0 = sum_second(links, g0)
    m1 = gather_second(links, m1)
    m0 = sum_high(links, m0)

    m1, m0, g0, grad_got, block_outputs = together((m1, m0, g0, grad_got, block_outputs))
    links.token = input_grads = run_place(back0[0], back1[0], grad_got)
    g0 = sum_low(links, g0)
    gm = gather_high(links, jnp.concatenate([m0, g1], axis=0))

    gm, g0, input_grads = turn(gm, g0, input_grads)
    all_m1 = gather_first(links, m1)
    g0 = sum_high(links, g0)
    gm = gather_low(links, gm)

    gm, g0, all_m1 = turn(gm, g0, all_m1)
    g0 = gather_high(links, g0)
    gm = gather_second(links, gm)
    got_m1 = links.core(all_m1, only=0)

    gm, g0, got_m1 = turn(gm, g0, got_m1)
    g0 = gather_low(links, g0)

    (g0,) = turn(g0)
    g0 = gather_second(links, g0)
    all_gm = gather_first(links, gm)

    all_gm, g0 = turn(all_gm, g0)
    all_g0 = gather_first(links, g0)
    got_gm = links.core(all_gm)

    got_gm, all_g0 = together((got_gm, all_g0))
    wr, we = run_mlp_finish(((192, 0), (128, 0)), (all_gm, got_gm, all_m1, got_m1))
    links.token = wr
    got_g0 = links.core(all_g0, only=1)
    (n1g, n1s, win, bin_, conv, cbias, w1, b1, w2, b2, w3, b3, wo, bo, bs, n2g, n2s, be, br, ms) = run_gn_finish(
        ((64, 0), (192, 128)), (all_g0, got_g0, all_gm, got_gm)
    )
    shape = (1, 2, 1, CANVAS, CANVAS, C)
    return (
        block_outputs.reshape(shape), input_grads.reshape(shape), n1g, n1s, win[None], bin_, conv[None], cbias,
        w1[None], b1, w2[None], b2, w3[None], b3, wo[None], bo, bs, n2g, n2s, we[None], be, wr[None], br, ms,
    )


def solution(mesh):
    links = Links(mesh.shape["dp"])
    image = P(None, "dp", None, None, None)
    one, two = P("section", None), P("section", None, None)
    weights = (one, one, two, one, two, one, two, one, two, one, two, one, two, one, one, one, one, two, one, two,
               one, one)
    field = P("section", None, "dp", None, None, None)
    return jax.shard_map(
        functools.partial(on_device, links),
        mesh=mesh,
        in_specs=(image, image, P(None, "dp")) + weights,
        out_specs=(field, field) + weights,
        check_vma=False,
    )
```

time: 313 us -> 253 us (0.81)
  starting transfers between devices: 91.3 us -> 47.2 us
  Pallas kernels: 89.7 us -> 109 us
  waiting for transfers between devices: 95.8 us -> 82.6 us
  other arithmetic: 16.5 us -> 4.12 us
  local copies, waits for them, and re-layouts: 15.5 us -> 6.71 us
    ppermute x75 -> x44, starting transfers between devices: 91.3 us -> 47.2 us  [send(): got = lax.ppermute(x, AXES, pairs)]
    pallas_call x8 -> x15, Pallas kernels: 89.7 us -> 109 us  [call(): pl.pallas_call(kernel, name=name, out_shape=[shape for _, shape in outs],...]
    ppermute x75 -> x44, waiting for transfers between devices: 95.8 us -> 82.6 us  [send(): got = lax.ppermute(x, AXES, pairs)]
    unnamed x12 -> x0, other arithmetic: 8.44 us -> none
    unnamed x45 -> x49, local copies, waits for them, and re-layouts: 3.23 us -> 6.3 us
  transfers between devices with their start and end apart: 75 -> 44, of which waited for: 24 -> 16; matrix products, arithmetic and copies ran while one was open for 10% -> 1% of each run, Pallas kernels for 10% -> 29%
where the time goes in v2:
time: 253 us; the launch traced here: 251 us
  Pallas kernels  109 us (43%)
  waiting for transfers between devices  82.6 us (33%)
  starting transfers between devices  47.2 us (19%)
  local copies, waits for them, and re-layouts  6.71 us (3%)
  other arithmetic  4.12 us (2%)
    pallas_call x15, Pallas kernels, call(): pl.pallas_call(kernel, name=name, out_shape=[shape for _, shape in outs],...  109 us
    ppermute x44, waiting for transfers between devices, send(): got = lax.ppermute(x, AXES, pairs)  82.6 us
    ppermute x44, starting transfers between devices, send(): got = lax.ppermute(x, AXES, pairs)  47.2 us
    unnamed x49, local copies, waits for them, and re-layouts  6.3 us
  transfers between devices with their start and end apart: 44, of which 16 were waited for; matrix products, arithmetic and copies ran while one was open for 1% of the time, Pallas kernels for 29%

profile of v2, /device:TPU:0, one launch (start us, length us, event | category | flops | bytes accessed | tf_op | source)
XLA Modules:
  0.0 250.8 jit_solution(12689178616959991586)
XLA Ops:
  1.3 2.3 pack.1
  4.5 1.5 collective-permute-done.vec_b
  8.0 9.8 %gnconv_forward.2 = (bf16[256,512]{1,0:T(8,128)(2,1)}, f32[2816,128]{1,0:T(8,128)}, f32[256,1024]{1,0:T(8,128)}, f32[256,1024]{1,0:T(8,128)}, bf16[256,1024]{1,0...) custom-call(s32[2,1]{1,0:T(2,128)} %copy.53.crop_ref, bf16[2,256,512]{2,1,0:T(8,128)(2,1)} %bitcast.182, ...), custom_call_target="tpu_custom_call" | custom-call | flops 8000000000 | bytes 24000000 | tf_op jit(solution)/shard_map/gnconv_forward/pallas_call | solution.py:628
  17.8 6.4 %mlp_forward.2 = (bf16[256,512]{1,0:T(8,128)(2,1)}, bf16[256,2048]{1,0:T(8,128)(2,1)}, bf16[256,2048]{1,0:T(8,128)(2,1)}, bf16[256,512]{1,0:T(8,128)(2,1)}, bf16...) custom-call(s32[2,1]{1,0:T(2,128)} %copy.53.crop_ref, bf16[2,256,512]{2,1,0:T(8,128)(2,1)} %bitcast.183, ...), custom_call_target="tpu_custom_call" | custom-call | flops 5000000000 | bytes 15000000 | tf_op jit(solution)/shard_map/mlp_forward/pallas_call | solution.py:628
  24.2 9.8 %gnconv_forward.3 = (bf16[256,512]{1,0:T(8,128)(2,1)}, f32[2816,128]{1,0:T(8,128)}, f32[256,1024]{1,0:T(8,128)}, f32[256,1024]{1,0:T(8,128)}, bf16[256,1024]{1,0...) custom-call(s32[2,1]{1,0:T(2,128)} %copy.53.crop_ref, bf16[1,256,512]{2,1,0:T(8,128)(2,1)} %bitcast.170, ...), custom_call_target="tpu_custom_call" | custom-call | flops 8000000000 | bytes 24000000 | tf_op jit(solution)/shard_map/gnconv_forward/pallas_call | solution.py:628
  34.0 6.6 %mlp_forward.3 = (bf16[256,512]{1,0:T(8,128)(2,1)}, bf16[256,2048]{1,0:T(8,128)(2,1)}, bf16[256,2048]{1,0:T(8,128)(2,1)}, bf16[256,512]{1,0:T(8,128)(2,1)}, bf16...) custom-call(s32[2,1]{1,0:T(2,128)} %copy.53.crop_ref, bf16[1,256,512]{2,1,0:T(8,128)(2,1)} %bitcast.171, ...), custom_call_target="tpu_custom_call" | custom-call | flops 5000000000 | bytes 15000000 | tf_op jit(solution)/shard_map/mlp_forward/pallas_call | solution.py:628
  40.6 9.2 %mlp_backward.2 = (f32[256,512]{1,0:T(8,128)}, f32[8,2048]{1,0:T(8,128)}, bf16[2048,512]{1,0:T(8,128)(2,1)}, bf16[2048,512]{1,0:T(8,128)(2,1)}) custom-call(s32[2,1]{1,0:T(2,128)} %copy.53.crop_ref, bf16[2,256,512]{2,1,0:T(8,128)(2,1)} %bitcast.181, f32[16,2048]{1,0:T(8,128)} %get-tuple-element.200.vec_a, f32[16,2048]{1,0:T(8,128)} %copy-done.3, ...), custom_call_target="tpu_custom_call" | custom-call | flops 2000000000 | bytes 6000000 | tf_op jit(solution)/shard_map/mlp_backward/pallas_call | solution.py:628
  50.0 12.5 %gnconv_backward.2 = (f32[256,512]{1,0:T(8,128)}, bf16[256,512]{1,0:T(8,128)(2,1)}, bf16[256,512]{1,0:T(8,128)(2,1)}, bf16[256,1024]{1,0:T(8,128)(2,1)}, bf16[25...) custom-call(s32[2,1]{1,0:T(2,128)} %copy.53.crop_ref, ...), custom_call_target="tpu_custom_call" | custom-call | flops 2000000000 | bytes 6000000 | tf_op jit(solution)/shard_map/gnconv_backward/pallas_call | solution.py:628
  63.2 2.9 %collective-permute-start.8 = (bf16[2,2,2,128,512]{4,3,1,2,0:T(8,128)(2,1)S(1)}, bf16[2,2,2,128,512]{4,3,1,2,0:T(8,128)(2,1)S(1)}, u32[]{:S(2)}, u32[]{:S(2)}) collective-permute-start(bf16[2,2,2,128,512]{4,3,1,2,0:T(8,128)(2,1)S(1)} %slice_bitcast_fusion.2), channel_id=1, source_target_pairs={{0,1},{1,0},{2,3},{3,2},{4,5},{5,4},{6,7},{7,6},{8,9},{9,8},{10,11... | collective-permute-start | bytes 3145736 | tf_op jit(solution)/shard_map/ppermute | solution.py:755
  66.1 8.9 %gnconv_weights.2 = (bf16[1024,512]{1,0:T(8,128)(2,1)}, bf16[1024,512]{1,0:T(8,128)(2,1)}) custom-call(bf16[256,512]{1,0:T(8,128)(2,1)} %get-tuple-element.226.n1_ref, bf16[256,1024]{1,0:T(8,128)(2,1)} %get-tuple-element.221.gl_ref, bf16[256,512]{1,0:T(8,128)(2,1)} %get-tuple-element.227.dbr_ref, bf16[256,1024]{1,0:T(8,128)(2,1)} %get-tuple-element.228.dp_ref, ...), custom_call_target="tpu_custom_call" | custom-call | flops 2000000000 | bytes 6000000 | tf_op jit(solution)/shard_map/gnconv_weights/pallas_call | solution.py:628
  75.1 3.8 %collective-permute-done.8 = bf16[2,2,2,128,512]{4,3,1,2,0:T(8,128)(2,1)S(1)} collective-permute-done((bf16[2,2,2,128,512]{4,3,1,2,0:T(8,128)(2,1)S(1)}, bf16[2,2,2,128,512]{4,3,1,2,0:T(8,128)(2,1)S(1)}, u32[]{:S(2)}, u32[]{:S(2)}) %collective-permute-start.8) | collective-permute-done | bytes 1048608 | tf_op jit(solution)/shard_map/ppermute | solution.py:755
  79.3 2.1 collective-permute-start.9
  81.5 9.2 %mlp_backward.3 = (f32[256,512]{1,0:T(8,128)}, f32[8,2048]{1,0:T(8,128)}, bf16[2048,512]{1,0:T(8,128)(2,1)}, bf16[2048,512]{1,0:T(8,128)(2,1)}) custom-call(s32[2,1]{1,0:T(2,128)} %copy.53.crop_ref, bf16[1,256,512]{2,1,0:T(8,128)(2,1)} %bitcast.191, f32[16,2048]{1,0:T(8,128)} %get-tuple-element.200.vec_a, f32[16,2048]{1,0:T(8,128)} %copy-done.3, ...), custom_call_target="tpu_custom_call" | custom-call | flops 2000000000 | bytes 6000000 | tf_op jit(solution)/shard_map/mlp_backward/pallas_call | solution.py:628
  94.2 1.6 collective-permute-start.11
  95.8 12.6 %gnconv_backward.3 = (f32[256,512]{1,0:T(8,128)}, bf16[256,512]{1,0:T(8,128)(2,1)}, bf16[256,512]{1,0:T(8,128)(2,1)}, bf16[256,1024]{1,0:T(8,128)(2,1)}, bf16[25...) custom-call(s32[2,1]{1,0:T(2,128)} %copy.53.crop_ref, ...), custom_call_target="tpu_custom_call" | custom-call | flops 2000000000 | bytes 6000000 | tf_op jit(solution)/shard_map/gnconv_backward/pallas_call | solution.py:628
  111.5 2.7 %collective-permute-start.14 = (bf16[128,512]{1,0:T(8,128)(2,1)S(1)}, bf16[128,512]{1,0:T(8,128)(2,1)S(1)}, u32[]{:S(2)}, u32[]{:S(2)}) collective-permute-start(bf16[128,512]{1,0:T(8,128)(2,1)S(1)} %slice_bitcast_fusion.17), channel_id=1, source_target_pairs={{0,8},{1,9},{2,10},{3,11},{4,12},{5,13},{6,14},{7,15},{8,0},{9,1},... | collective-permute-start | bytes 393224 | tf_op jit(solution)/shard_map/ppermute | solution.py:755
  114.1 1.6 collective-permute-start.15
  115.7 8.7 %gnconv_weights.3 = (bf16[1024,512]{1,0:T(8,128)(2,1)}, bf16[1024,512]{1,0:T(8,128)(2,1)}) custom-call(bf16[256,512]{1,0:T(8,128)(2,1)} %get-tuple-element.266.n1_ref, bf16[256,1024]{1,0:T(8,128)(2,1)} %get-tuple-element.256.gl_ref, bf16[256,512]{1,0:T(8,128)(2,1)} %get-tuple-element.267.dbr_ref, bf16[256,1024]{1,0:T(8,128)(2,1)} %get-tuple-element.268.dp_ref, ...), custom_call_target="tpu_custom_call" | custom-call | flops 2000000000 | bytes 6000000 | tf_op jit(solution)/shard_map/gnconv_weights/pallas_call | solution.py:628
  124.6 3.8 %collective-permute-done.16 = bf16[2,2,2,128,512]{4,3,1,2,0:T(8,128)(2,1)S(1)} collective-permute-done((bf16[2,2,2,128,512]{4,3,1,2,0:T(8,128)(2,1)S(1)}, bf16[2,2,2,128,512]{4,3,1,2,0:T(8,128)(2,1)S(1)}, u32[]{:S(2)}, u32[]{:S(2)}) %collective-permute-start.16) | collective-permute-done | bytes 1048608 | tf_op jit(solution)/shard_map/ppermute | solution.py:755
  130.1 2.5 collective-permute-start.17
  132.6 5.5 %collective-permute-done.18 = bf16[2,64,512]{2,1,0:T(8,128)(2,1)S(1)} collective-permute-done((bf16[2,64,512]{2,1,0:T(8,128)(2,1)S(1)}, bf16[2,64,512]{2,1,0:T(8,128)(2,1)S(1)}, u32[]{:S(2)}, u32[]{:S(2)}) %collective-permute-start.18) | collective-permute-done | bytes 131104 | tf_op jit(solution)/shard_map/ppermute | solution.py:755
  138.6 2.0 collective-permute-start.22
  140.6 3.3 %collective-permute-start.23 = (bf16[2,128,512]{2,1,0:T(8,128)(2,1)S(1)}, bf16[2,128,512]{2,1,0:T(8,128)(2,1)S(1)}, u32[]{:S(2)}, u32[]{:S(2)}) collective-permute-start(bf16[2,128,512]{2,1,0:T(8,128)(2,1)S(1)} %slice_bitcast_fusion.11), channel_id=1, source_target_pairs={{0,4},{1,5},{2,6},{3,7},{4,0},{5,1},{6,2},{7,3},{8,12},{9,13},{10,... | collective-permute-start | bytes 786440 | tf_op jit(solution)/shard_map/ppermute | solution.py:755
  145.1 10.3 %collective-permute-done.21 = bf16[2,128,512]{2,1,0:T(8,128)(2,1)S(1)} collective-permute-done((bf16[2,128,512]{2,1,0:T(8,128)(2,1)S(1)}, bf16[2,128,512]{2,1,0:T(8,128)(2,1)S(1)}, u32[]{:S(2)}, u32[]{:S(2)}) %collective-permute-start.21) | collective-permute-done | bytes 262176 | tf_op jit(solution)/shard_map/ppermute | solution.py:755
  155.7 1.7 collective-permute-start.28
  157.9 1.6 collective-permute-start.29
  159.5 1.9 place.2
  161.4 2.2 collective-permute-done.28
  163.6 5.7 %collective-permute-done.29 = bf16[2,2,64,512]{3,2,0,1:T(8,128)(2,1)S(1)} collective-permute-done((bf16[2,2,64,512]{3,2,0,1:T(8,128)(2,1)S(1)}, bf16[2,2,64,512]{3,2,0,1:T(8,128)(2,1)S(1)}, u32[]{:S(2)}, u32[]{:S(2)}) %collective-permute-start.29) | collective-permute-done | bytes 262176 | tf_op jit(solution)/shard_map/ppermute | solution.py:755
  169.5 1.9 collective-permute-start.31
  173.5 2.4 place.3
  175.9 4.8 %collective-permute-done.30 = bf16[192,512]{1,0:T(8,128)(2,1)S(1)} collective-permute-done((bf16[192,512]{1,0:T(8,128)(2,1)S(1)}, bf16[192,512]{1,0:T(8,128)(2,1)S(1)}, u32[]{:S(2)}, u32[]{:S(2)}) %collective-permute-start.30) | collective-permute-done | bytes 196640 | tf_op jit(solution)/shard_map/ppermute | solution.py:755
  180.9 2.6 %collective-permute-start.33 = (bf16[64,512]{1,0:T(8,128)(2,1)S(1)}, bf16[64,512]{1,0:T(8,128)(2,1)S(1)}, u32[]{:S(2)}, u32[]{:S(2)}) collective-permute-start(bf16[64,512]{1,0:T(8,128)(2,1)S(1)} %slice_bitcast_fusion.18), channel_id=1, source_target_pairs={{0,8},{1,9},{2,10},{3,11},{4,12},{5,13},{6,14},{7,15},{8,0},{9,1},... | collective-permute-start | bytes 196616 | tf_op jit(solution)/shard_map/ppermute | solution.py:755
  183.5 5.6 %collective-permute-done.33 = bf16[64,512]{1,0:T(8,128)(2,1)S(1)} collective-permute-done((bf16[64,512]{1,0:T(8,128)(2,1)S(1)}, bf16[64,512]{1,0:T(8,128)(2,1)S(1)}, u32[]{:S(2)}, u32[]{:S(2)}) %collective-permute-start.33) | collective-permute-done | bytes 65568 | tf_op jit(solution)/shard_map/ppermute | solution.py:755
  189.1 2.2 collective-permute-done.32
  191.6 1.6 collective-permute-start.37
  193.3 2.3 collective-permute-start.35
  196.8 4.0 %collective-permute-done.36 = bf16[64,512]{1,0:T(8,128)(2,1)S(1)} collective-permute-done((bf16[64,512]{1,0:T(8,128)(2,1)S(1)}, bf16[64,512]{1,0:T(8,128)(2,1)S(1)}, u32[]{:S(2)}, u32[]{:S(2)}) %collective-permute-start.36) | collective-permute-done | bytes 65568 | tf_op jit(solution)/shard_map/ppermute | solution.py:755
  200.8 4.8 %collective-permute-done.35 = bf16[2,2,192,512]{3,2,1,0:T(8,128)(2,1)S(1)} collective-permute-done((bf16[2,2,192,512]{3,2,1,0:T(8,128)(2,1)S(1)}, bf16[2,2,192,512]{3,2,1,0:T(8,128)(2,1)S(1)}, u32[]{:S(2)}, u32[]{:S(2)}) %collective-permute-start.35) | collective-permute-done | bytes 786464 | tf_op jit(solution)/shard_map/ppermute | solution.py:755
  205.7 1.4 collective-permute-start.38
  207.6 4.6 %collective-permute-done.39 = bf16[2,64,512]{2,1,0:T(8,128)(2,1)S(1)} collective-permute-done((bf16[2,64,512]{2,1,0:T(8,128)(2,1)S(1)}, bf16[2,64,512]{2,1,0:T(8,128)(2,1)S(1)}, u32[]{:S(2)}, u32[]{:S(2)}) %collective-permute-start.39) | collective-permute-done | bytes 131104 | tf_op jit(solution)/shard_map/ppermute | solution.py:755
  213.0 8.5 %collective-permute-done.40 = bf16[2,2,64,512]{3,2,1,0:T(8,128)(2,1)S(1)} collective-permute-done((bf16[2,2,64,512]{3,2,1,0:T(8,128)(2,1)S(1)}, bf16[2,2,64,512]{3,2,1,0:T(8,128)(2,1)S(1)}, u32[]{:S(2)}, u32[]{:S(2)}) %collective-permute-start.40) | collective-permute-done | bytes 262176 | tf_op jit(solution)/shard_map/ppermute | solution.py:755
  221.5 7.5 %collective-permute-done.38 = bf16[2,2,2,192,512]{4,3,2,1,0:T(8,128)(2,1)S(1)} collective-permute-done((bf16[2,2,2,192,512]{4,3,2,1,0:T(8,128)(2,1)S(1)}, bf16[2,2,2,192,512]{4,3,2,1,0:T(8,128)(2,1)S(1)}, u32[]{:S(2)}, u32[]{:S(2)}) %collective-permute-start.38) | collective-permute-done | bytes 1572896 | tf_op jit(solution)/shard_map/ppermute | solution.py:755
  229.4 1.4 collective-permute-start.42
  230.9 7.8 %collective-permute-done.42 = bf16[2,2,2,64,512]{4,3,2,1,0:T(8,128)(2,1)S(1)} collective-permute-done((bf16[2,2,2,64,512]{4,3,2,1,0:T(8,128)(2,1)S(1)}, bf16[2,2,2,64,512]{4,3,2,1,0:T(8,128)(2,1)S(1)}, u32[]{:S(2)}, u32[]{:S(2)}) %collective-permute-start.42) | collective-permute-done | bytes 524320 | tf_op jit(solution)/shard_map/ppermute | solution.py:755
  240.5 4.6 %mlp_finish.1 = (f32[2048,512]{1,0:T(8,128)}, f32[512,2048]{1,0:T(8,128)}) custom-call(bf16[3072,512]{1,0:T(8,128)(2,1)} %bitcast.156, bf16[3072,512]{1,0:T(8,128)(2,1)} %copy-done.15, bf16[2048,512]{1,0:T(8,128)(2,1)} %bitcast.165, bf16[2048,512]{1,0:T(8,128)(2,1)} %copy-done.16), custom_call_target="tpu_custom_call" | custom-call | flops 20000000000 | bytes 60000000 | tf_op jit(solution)/shard_map/mlp_finish/pallas_call | solution.py:628
  245.1 3.8 %gn_finish.1 = (f32[1,512]{1,0:T(1,128)}, f32[1,512]{1,0:T(1,128)}, f32[512,1024]{1,0:T(8,128)}, f32[1,1024]{1,0:T(1,128)}, f32[49,960]{1,0:T(8,128)}, /*index=5...) custom-call(bf16[1024,512]{1,0:T(8,128)(2,1)} %bitcast.175, ...), custom_call_target="tpu_custom_call" | custom-call | flops 3000000000 | bytes 9000000 | tf_op jit(solution)/shard_map/gn_finish/pallas_call | solution.py:628
  249.0 1.8 copy.70
  (153 shorter events, 22.9 us)
Async XLA Ops:
  0.7 5.4 %collective-permute-start.3 = (bf16[512,1024]{1,0:T(8,128)(2,1)}, bf16[512,1024]{1,0:T(8,128)(2,1)S(1)}, u32[]{:S(2)}, u32[]{:S(2)}) collective-permute-start(bf16[512,1024]{1,0:T(8,128)(2,1)} %bitcast.145), channel_id=1, source_target_pairs={{0,16},{1,17},{2,18},{3,19},{4,20},{5,21},{6,22},{7,23},{8,24},{9,... | collective-permute-start | bytes 3145736 | tf_op jit(solution)/shard_map/ppermute | solution.py:755
  1.2 4.8 %collective-permute-start.4 = (bf16[512,512]{1,0:T(8,128)(2,1)}, bf16[512,512]{1,0:T(8,128)(2,1)S(1)}, u32[]{:S(2)}, u32[]{:S(2)}) collective-permute-start(bf16[512,512]{1,0:T(8,128)(2,1)} %bitcast.159), channel_id=1, source_target_pairs={{0,16},{1,17},{2,18},{3,19},{4,20},{5,21},{6,22},{7,23},{8,24},{9,... | collective-permute-start | bytes 1572872 | tf_op jit(solution)/shard_map/ppermute | solution.py:755
  3.5 2.5 collective-permute-start.2
  4.0 2.0 collective-permute-start.1
  4.0 2.0 collective-permute-start
  6.1 11.7 %collective-permute-start.5 = (bf16[512,2048]{1,0:T(8,128)(2,1)S(1)}, bf16[512,2048]{1,0:T(8,128)(2,1)}, u32[]{:S(2)}, u32[]{:S(2)}) collective-permute-start(bf16[512,2048]{1,0:T(8,128)(2,1)S(1)} %bitcast.143), channel_id=1, source_target_pairs={{0,16},{1,17},{2,18},{3,19},{4,20},{5,21},{6,22},{7,23},{8,24},{9,... | collective-permute-start | bytes 6291464 | tf_op jit(solution)/shard_map/ppermute | solution.py:755
  7.0 10.9 %collective-permute-start.6 = (bf16[2048,512]{1,0:T(8,128)(2,1)}, bf16[2048,512]{1,0:T(8,128)(2,1)}, u32[]{:S(2)}, u32[]{:S(2)}) collective-permute-start(bf16[2048,512]{1,0:T(8,128)(2,1)} %bitcast.9.wr_a), channel_id=1, source_target_pairs={{0,16},{1,17},{2,18},{3,19},{4,20},{5,21},{6,22},{7,23},{8,24},{9,... | collective-permute-start | bytes 6291464 | tf_op jit(solution)/shard_map/ppermute | solution.py:755
  49.8 12.7 %collective-permute-start.7 = (bf16[2048,512]{1,0:T(8,128)(2,1)}, bf16[2048,512]{1,0:T(8,128)(2,1)S(1)}, u32[]{:S(2)}, u32[]{:S(2)}) collective-permute-start(bf16[2048,512]{1,0:T(8,128)(2,1)} %get-tuple-element.216), channel_id=1, source_target_pairs={{0,16},{1,17},{2,18},{3,19},{4,20},{5,21},{6,22},{7,23},{8,24},{9,... | collective-permute-start | bytes 6291464 | tf_op jit(solution)/shard_map/ppermute | solution.py:755
  50.0 12.5 %copy-start.5 = (bf16[2048,512]{1,0:T(8,128)(2,1)S(1)}, bf16[2048,512]{1,0:T(8,128)(2,1)}, u32[]{:S(2)}) copy-start(bf16[2048,512]{1,0:T(8,128)(2,1)} %get-tuple-element.215) | copy-start | bytes 6291460
  63.2 15.7 %collective-permute-start.8 = (bf16[2,2,2,128,512]{4,3,1,2,0:T(8,128)(2,1)S(1)}, bf16[2,2,2,128,512]{4,3,1,2,0:T(8,128)(2,1)S(1)}, u32[]{:S(2)}, u32[]{:S(2)}) collective-permute-start(bf16[2,2,2,128,512]{4,3,1,2,0:T(8,128)(2,1)S(1)} %slice_bitcast_fusion.2), channel_id=1, source_target_pairs={{0,1},{1,0},{2,3},{3,2},{4,5},{5,4},{6,7},{7,6},{8,9},{9,8},{10,11... | collective-permute-start | bytes 3145736 | tf_op jit(solution)/shard_map/ppermute | solution.py:755
  79.2 11.5 %collective-permute-start.10 = (bf16[1024,512]{1,0:T(8,128)(2,1)S(1)}, bf16[1024,512]{1,0:T(8,128)(2,1)S(1)}, u32[]{:S(2)}, u32[]{:S(2)}) collective-permute-start(bf16[1024,512]{1,0:T(8,128)(2,1)S(1)} %copy-done.19), channel_id=1, source_target_pairs={{0,16},{1,17},{2,18},{3,19},{4,20},{5,21},{6,22},{7,23},{8,24},{9,... | collective-permute-start | bytes 3145736 | tf_op jit(solution)/shard_map/ppermute | solution.py:755
  79.3 11.3 %collective-permute-start.9 = (bf16[2,2,128,512]{3,2,0,1:T(8,128)(2,1)S(1)}, bf16[2,2,128,512]{3,2,0,1:T(8,128)(2,1)S(1)}, u32[]{:S(2)}, u32[]{:S(2)}) collective-permute-start(bf16[2,2,128,512]{3,2,0,1:T(8,128)(2,1)S(1)} %slice_bitcast_fusion.9), channel_id=1, source_target_pairs={{0,2},{1,3},{2,0},{3,1},{4,6},{5,7},{6,4},{7,5},{8,10},{9,11},{10,... | collective-permute-start | bytes 1572872 | tf_op jit(solution)/shard_map/ppermute | solution.py:755
  92.6 16.0 %collective-permute-start.13 = (bf16[2048,512]{1,0:T(8,128)(2,1)S(1)}, bf16[2048,512]{1,0:T(8,128)(2,1)S(1)}, u32[]{:S(2)}, u32[]{:S(2)}) collective-permute-start(bf16[2048,512]{1,0:T(8,128)(2,1)S(1)} %copy-done.17), channel_id=1, source_target_pairs={{0,16},{1,17},{2,18},{3,19},{4,20},{5,21},{6,22},{7,23},{8,24},{9,... | collective-permute-start | bytes 6291464 | tf_op jit(solution)/shard_map/ppermute | solution.py:755
  92.8 15.7 %collective-permute-start.12 = (bf16[2,2,2,64,512]{4,3,1,2,0:T(8,128)(2,1)S(1)}, bf16[2,2,2,64,512]{4,3,1,2,0:T(8,128)(2,1)S(1)}, u32[]{:S(2)}, u32[]{:S(2)}) collective-permute-start(bf16[2,2,2,64,512]{4,3,1,2,0:T(8,128)(2,1)S(1)} %slice_bitcast_fusion.6), channel_id=1, source_target_pairs={{0,1},{1,0},{2,3},{3,2},{4,5},{5,4},{6,7},{7,6},{8,9},{9,8},{10,11... | collective-permute-start | bytes 1572872 | tf_op jit(solution)/shard_map/ppermute | solution.py:755
  94.2 14.2 %collective-permute-start.11 = (bf16[2,128,512]{2,1,0:T(8,128)(2,1)S(1)}, bf16[2,128,512]{2,1,0:T(8,128)(2,1)S(1)}, u32[]{:S(2)}, u32[]{:S(2)}) collective-permute-start(bf16[2,128,512]{2,1,0:T(8,128)(2,1)S(1)} %slice_bitcast_fusion.13), channel_id=1, source_target_pairs={{0,4},{1,5},{2,6},{3,7},{4,0},{5,1},{6,2},{7,3},{8,12},{9,13},{10,... | collective-permute-start | bytes 786440 | tf_op jit(solution)/shard_map/ppermute | solution.py:755
  110.7 17.7 %collective-permute-start.16 = (bf16[2,2,2,128,512]{4,3,1,2,0:T(8,128)(2,1)S(1)}, bf16[2,2,2,128,512]{4,3,1,2,0:T(8,128)(2,1)S(1)}, u32[]{:S(2)}, u32[]{:S(2)}) collective-permute-start(bf16[2,2,2,128,512]{4,3,1,2,0:T(8,128)(2,1)S(1)} %slice_bitcast_fusion), channel_id=1, source_target_pairs={{0,1},{1,0},{2,3},{3,2},{4,5},{5,4},{6,7},{7,6},{8,9},{9,8},{10,11... | collective-permute-start | bytes 3145736 | tf_op jit(solution)/shard_map/ppermute | solution.py:755
  111.5 13.0 %collective-permute-start.14 = (bf16[128,512]{1,0:T(8,128)(2,1)S(1)}, bf16[128,512]{1,0:T(8,128)(2,1)S(1)}, u32[]{:S(2)}, u32[]{:S(2)}) collective-permute-start(bf16[128,512]{1,0:T(8,128)(2,1)S(1)} %slice_bitcast_fusion.17), channel_id=1, source_target_pairs={{0,8},{1,9},{2,10},{3,11},{4,12},{5,13},{6,14},{7,15},{8,0},{9,1},... | collective-permute-start | bytes 393224 | tf_op jit(solution)/shard_map/ppermute | solution.py:755
  114.1 10.4 %collective-permute-start.15 = (bf16[2,2,64,512]{3,2,0,1:T(8,128)(2,1)S(1)}, bf16[2,2,64,512]{3,2,0,1:T(8,128)(2,1)S(1)}, u32[]{:S(2)}, u32[]{:S(2)}) collective-permute-start(bf16[2,2,64,512]{3,2,0,1:T(8,128)(2,1)S(1)} %slice_bitcast_fusion.12), channel_id=1, source_target_pairs={{0,2},{1,3},{2,0},{3,1},{4,6},{5,7},{6,4},{7,5},{8,10},{9,11},{10,... | collective-permute-start | bytes 786440 | tf_op jit(solution)/shard_map/ppermute | solution.py:755
  128.6 9.6 %collective-permute-start.20 = (bf16[1024,512]{1,0:T(8,128)(2,1)S(1)}, bf16[1024,512]{1,0:T(8,128)(2,1)S(1)}, u32[]{:S(2)}, u32[]{:S(2)}) collective-permute-start(bf16[1024,512]{1,0:T(8,128)(2,1)S(1)} %copy-done.18), channel_id=1, source_target_pairs={{0,16},{1,17},{2,18},{3,19},{4,20},{5,21},{6,22},{7,23},{8,24},{9,... | collective-permute-start | bytes 3145736 | tf_op jit(solution)/shard_map/ppermute | solution.py:755
  128.8 9.3 %collective-permute-start.19 = (bf16[2,2,128,512]{3,2,0,1:T(8,128)(2,1)S(1)}, bf16[2,2,128,512]{3,2,0,1:T(8,128)(2,1)S(1)}, u32[]{:S(2)}, u32[]{:S(2)}) collective-permute-start(bf16[2,2,128,512]{3,2,0,1:T(8,128)(2,1)S(1)} %slice_bitcast_fusion.8), channel_id=1, source_target_pairs={{0,2},{1,3},{2,0},{3,1},{4,6},{5,7},{6,4},{7,5},{8,10},{9,11},{10,... | collective-permute-start | bytes 1572872 | tf_op jit(solution)/shard_map/ppermute | solution.py:755
  129.6 8.5 %collective-permute-start.18 = (bf16[2,64,512]{2,1,0:T(8,128)(2,1)S(1)}, bf16[2,64,512]{2,1,0:T(8,128)(2,1)S(1)}, u32[]{:S(2)}, u32[]{:S(2)}) collective-permute-start(bf16[2,64,512]{2,1,0:T(8,128)(2,1)S(1)} %slice_bitcast_fusion.16), channel_id=1, source_target_pairs={{0,4},{1,5},{2,6},{3,7},{4,0},{5,1},{6,2},{7,3},{8,12},{9,13},{10,... | collective-permute-start | bytes 393224 | tf_op jit(solution)/shard_map/ppermute | solution.py:755
  130.1 8.0 %collective-permute-start.17 = (bf16[128,512]{1,0:T(8,128)(2,1)S(1)}, bf16[128,512]{1,0:T(8,128)(2,1)S(1)}, u32[]{:S(2)}, u32[]{:S(2)}) collective-permute-start(bf16[128,512]{1,0:T(8,128)(2,1)S(1)} %bitcast_add_fusion.9), channel_id=1, source_target_pairs={{0,8},{1,9},{2,10},{3,11},{4,12},{5,13},{6,14},{7,15},{8,0},{9,1},... | collective-permute-start | bytes 393224 | tf_op jit(solution)/shard_map/ppermute | solution.py:755
  138.6 6.4 %collective-permute-start.22 = (bf16[64,512]{1,0:T(8,128)(2,1)S(1)}, bf16[64,512]{1,0:T(8,128)(2,1)S(1)}, u32[]{:S(2)}, u32[]{:S(2)}) collective-permute-start(bf16[64,512]{1,0:T(8,128)(2,1)S(1)} %slice_bitcast_fusion.19), channel_id=1, source_target_pairs={{0,8},{1,9},{2,10},{3,11},{4,12},{5,13},{6,14},{7,15},{8,0},{9,1},... | collective-permute-start | bytes 196616 | tf_op jit(solution)/shard_map/ppermute | solution.py:755
  140.6 14.8 %collective-permute-start.23 = (bf16[2,128,512]{2,1,0:T(8,128)(2,1)S(1)}, bf16[2,128,512]{2,1,0:T(8,128)(2,1)S(1)}, u32[]{:S(2)}, u32[]{:S(2)}) collective-permute-start(bf16[2,128,512]{2,1,0:T(8,128)(2,1)S(1)} %slice_bitcast_fusion.11), channel_id=1, source_target_pairs={{0,4},{1,5},{2,6},{3,7},{4,0},{5,1},{6,2},{7,3},{8,12},{9,13},{10,... | collective-permute-start | bytes 786440 | tf_op jit(solution)/shard_map/ppermute | solution.py:755
  143.9 11.5 %collective-permute-start.25 = (bf16[256,512]{1,0:T(8,128)(2,1)S(1)}, bf16[256,512]{1,0:T(8,128)(2,1)S(1)}, u32[]{:S(2)}, u32[]{:S(2)}) collective-permute-start(bf16[256,512]{1,0:T(8,128)(2,1)S(1)} %copy-done.21), channel_id=1, source_target_pairs={{0,16},{1,17},{2,18},{3,19},{4,20},{5,21},{6,22},{7,23},{8,24},{9,... | collective-permute-start | bytes 786440 | tf_op jit(solution)/shard_map/ppermute | solution.py:755
  144.0 11.4 %collective-permute-start.21 = (bf16[2,128,512]{2,1,0:T(8,128)(2,1)S(1)}, bf16[2,128,512]{2,1,0:T(8,128)(2,1)S(1)}, u32[]{:S(2)}, u32[]{:S(2)}) collective-permute-start(bf16[2,128,512]{2,1,0:T(8,128)(2,1)S(1)} %pad_maximum_fusion.9), channel_id=1, source_target_pairs={{0,4},{1,5},{2,6},{3,7},{4,0},{5,1},{6,2},{7,3},{8,12},{9,13},{10,... | collective-permute-start | bytes 786440 | tf_op jit(solution)/shard_map/ppermute | solution.py:755
  144.2 11.3 %collective-permute-start.24 = (bf16[2,2,2,64,512]{4,3,1,2,0:T(8,128)(2,1)S(1)}, bf16[2,2,2,64,512]{4,3,1,2,0:T(8,128)(2,1)S(1)}, u32[]{:S(2)}, u32[]{:S(2)}) collective-permute-start(bf16[2,2,2,64,512]{4,3,1,2,0:T(8,128)(2,1)S(1)} %slice_bitcast_fusion.4), channel_id=1, source_target_pairs={{0,1},{1,0},{2,3},{3,2},{4,5},{5,4},{6,7},{7,6},{8,9},{9,8},{10,11... | collective-permute-start | bytes 1572872 | tf_op jit(solution)/shard_map/ppermute | solution.py:755
  145.0 10.7 %collective-permute-start.26 = (f32[256,512]{1,0:T(8,128)S(1)}, f32[256,512]{1,0:T(8,128)S(1)}, u32[]{:S(2)}, u32[]{:S(2)}) collective-permute-start(f32[256,512]{1,0:T(8,128)S(1)} %copy-done.20), channel_id=1, source_target_pairs={{0,16},{1,17},{2,18},{3,19},{4,20},{5,21},{6,22},{7,23},{8,24},{9,... | collective-permute-start | bytes 1572872 | tf_op jit(solution)/shard_map/ppermute | solution.py:755
  155.7 13.8 %copy-start.13 = (f32[256,512]{1,0:T(8,128)}, f32[256,512]{1,0:T(8,128)S(1)}, u32[]{:S(2)}) copy-start(f32[256,512]{1,0:T(8,128)S(1)} %collective-permute-done.26.got) | copy-start | bytes 1572868
  155.7 7.9 %collective-permute-start.28 = (bf16[128,512]{1,0:T(8,128)(2,1)S(1)}, bf16[128,512]{1,0:T(8,128)(2,1)S(1)}, u32[]{:S(2)}, u32[]{:S(2)}) collective-permute-start(bf16[128,512]{1,0:T(8,128)(2,1)S(1)} %slice_bitcast_fusion.15), channel_id=1, source_target_pairs={{0,8},{1,9},{2,10},{3,11},{4,12},{5,13},{6,14},{7,15},{8,0},{9,1},... | collective-permute-start | bytes 393224 | tf_op jit(solution)/shard_map/ppermute | solution.py:755
  157.4 12.0 %collective-permute-start.27 = (bf16[2,2,128,512]{3,2,1,0:T(8,128)(2,1)S(1)}, bf16[2,2,128,512]{3,2,1,0:T(8,128)(2,1)S(1)}, u32[]{:S(2)}, u32[]{:S(2)}) collective-permute-start(bf16[2,2,128,512]{3,2,1,0:T(8,128)(2,1)S(1)} %pad_maximum_fusion.6), channel_id=1, source_target_pairs={{0,2},{1,3},{2,0},{3,1},{4,6},{5,7},{6,4},{7,5},{8,10},{9,11},{10,... | collective-permute-start | bytes 1572872 | tf_op jit(solution)/shard_map/ppermute | solution.py:755
  157.9 11.5 %collective-permute-start.29 = (bf16[2,2,64,512]{3,2,0,1:T(8,128)(2,1)S(1)}, bf16[2,2,64,512]{3,2,0,1:T(8,128)(2,1)S(1)}, u32[]{:S(2)}, u32[]{:S(2)}) collective-permute-start(bf16[2,2,64,512]{3,2,0,1:T(8,128)(2,1)S(1)} %slice_bitcast_fusion.10), channel_id=1, source_target_pairs={{0,2},{1,3},{2,0},{3,1},{4,6},{5,7},{6,4},{7,5},{8,10},{9,11},{10,... | collective-permute-start | bytes 786440 | tf_op jit(solution)/shard_map/ppermute | solution.py:755
  169.5 6.4 %collective-permute-start.31 = (bf16[2,64,512]{2,1,0:T(8,128)(2,1)S(1)}, bf16[2,64,512]{2,1,0:T(8,128)(2,1)S(1)}, u32[]{:S(2)}, u32[]{:S(2)}) collective-permute-start(bf16[2,64,512]{2,1,0:T(8,128)(2,1)S(1)} %slice_bitcast_fusion.14), channel_id=1, source_target_pairs={{0,4},{1,5},{2,6},{3,7},{4,0},{5,1},{6,2},{7,3},{8,12},{9,13},{10,... | collective-permute-start | bytes 393224 | tf_op jit(solution)/shard_map/ppermute | solution.py:755
  171.4 20.0 %collective-permute-start.34 = (bf16[2,2,2,128,512]{4,3,2,1,0:T(8,128)(2,1)S(1)}, bf16[2,2,2,128,512]{4,3,2,1,0:T(8,128)(2,1)S(1)}, u32[]{:S(2)}, u32[]{:S(2)}) collective-permute-start(bf16[2,2,2,128,512]{4,3,2,1,0:T(8,128)(2,1)S(1)} %pad_maximum_fusion.3), channel_id=1, source_target_pairs={{0,1},{1,0},{2,3},{3,2},{4,5},{5,4},{6,7},{7,6},{8,9},{9,8},{10,11... | collective-permute-start | bytes 3145736 | tf_op jit(solution)/shard_map/ppermute | solution.py:755
  172.3 8.5 %collective-permute-start.30 = (bf16[192,512]{1,0:T(8,128)(2,1)S(1)}, bf16[192,512]{1,0:T(8,128)(2,1)S(1)}, u32[]{:S(2)}, u32[]{:S(2)}) collective-permute-start(bf16[192,512]{1,0:T(8,128)(2,1)S(1)} %constant_dynamic-update-slice_fusion), channel_id=1, source_target_pairs={{0,8},{1,9},{2,10},{3,11},{4,12},{5,13},{6,14},{7,15},{8,0},{9,1},... | collective-permute-start | bytes 589832 | tf_op jit(solution)/shard_map/ppermute | solution.py:755
  180.8 10.5 %collective-permute-start.32 = (bf16[2,192,512]{2,1,0:T(8,128)(2,1)S(1)}, bf16[2,192,512]{2,1,0:T(8,128)(2,1)S(1)}, u32[]{:S(2)}, u32[]{:S(2)}) collective-permute-start(bf16[2,192,512]{2,1,0:T(8,128)(2,1)S(1)} %pad_maximum_fusion.8), channel_id=1, source_target_pairs={{0,4},{1,5},{2,6},{3,7},{4,0},{5,1},{6,2},{7,3},{8,12},{9,13},{10,... | collective-permute-start | bytes 1179656 | tf_op jit(solution)/shard_map/ppermute | solution.py:755
  180.9 8.2 %collective-permute-start.33 = (bf16[64,512]{1,0:T(8,128)(2,1)S(1)}, bf16[64,512]{1,0:T(8,128)(2,1)S(1)}, u32[]{:S(2)}, u32[]{:S(2)}) collective-permute-start(bf16[64,512]{1,0:T(8,128)(2,1)S(1)} %slice_bitcast_fusion.18), channel_id=1, source_target_pairs={{0,8},{1,9},{2,10},{3,11},{4,12},{5,13},{6,14},{7,15},{8,0},{9,1},... | collective-permute-start | bytes 196616 | tf_op jit(solution)/shard_map/ppermute | solution.py:755
  191.6 29.9 %copy-start.7 = (bf16[2,2,2,2,128,512]{5,4,3,2,1,0:T(8,128)(2,1)}, bf16[2,2,2,2,128,512]{5,4,3,2,1,0:T(8,128)(2,1)S(1)}, u32[]{:S(2)}) copy-start(bf16[2,2,2,2,128,512]{5,4,3,2,1,0:T(8,128)(2,1)S(1)} %pad_maximum_fusion.1) | copy-start | bytes 6291460
  191.6 14.1 %collective-permute-start.37 = (bf16[2048,512]{1,0:T(8,128)(2,1)S(1)}, bf16[2048,512]{1,0:T(8,128)(2,1)S(1)}, u32[]{:S(2)}, u32[]{:S(2)}) collective-permute-start(bf16[2048,512]{1,0:T(8,128)(2,1)S(1)} %bitcast.164), channel_id=1, source_target_pairs={{0,16},{1,17},{2,18},{3,19},{4,20},{5,21},{6,22},{7,23},{8,24},{9,... | collective-permute-start | bytes 6291464 | tf_op jit(solution)/shard_map/ppermute | solution.py:755
  193.3 12.3 %collective-permute-start.35 = (bf16[2,2,192,512]{3,2,1,0:T(8,128)(2,1)S(1)}, bf16[2,2,192,512]{3,2,1,0:T(8,128)(2,1)S(1)}, u32[]{:S(2)}, u32[]{:S(2)}) collective-permute-start(bf16[2,2,192,512]{3,2,1,0:T(8,128)(2,1)S(1)} %pad_maximum_fusion.5), channel_id=1, source_target_pairs={{0,2},{1,3},{2,0},{3,1},{4,6},{5,7},{6,4},{7,5},{8,10},{9,11},{10,... | collective-permute-start | bytes 2359304 | tf_op jit(solution)/shard_map/ppermute | solution.py:755
  195.6 5.2 %collective-permute-start.36 = (bf16[64,512]{1,0:T(8,128)(2,1)S(1)}, bf16[64,512]{1,0:T(8,128)(2,1)S(1)}, u32[]{:S(2)}, u32[]{:S(2)}) collective-permute-start(bf16[64,512]{1,0:T(8,128)(2,1)S(1)} %bitcast_add_fusion.10), channel_id=1, source_target_pairs={{0,8},{1,9},{2,10},{3,11},{4,12},{5,13},{6,14},{7,15},{8,0},{9,1},... | collective-permute-start | bytes 196616 | tf_op jit(solution)/shard_map/ppermute | solution.py:755
  205.7 23.3 %copy-start.16 = (bf16[2048,512]{1,0:T(8,128)(2,1)}, bf16[2048,512]{1,0:T(8,128)(2,1)S(1)}, u32[]{:S(2)}) copy-start(bf16[2048,512]{1,0:T(8,128)(2,1)S(1)} %collective-permute-done.37.refs_3_) | copy-start | bytes 6291460
  205.7 23.3 %collective-permute-start.38 = (bf16[2,2,2,192,512]{4,3,2,1,0:T(8,128)(2,1)S(1)}, bf16[2,2,2,192,512]{4,3,2,1,0:T(8,128)(2,1)S(1)}, u32[]{:S(2)}, u32[]{:S(2)}) collective-permute-start(bf16[2,2,2,192,512]{4,3,2,1,0:T(8,128)(2,1)S(1)} %pad_maximum_fusion.2), channel_id=1, source_target_pairs={{0,1},{1,0},{2,3},{3,2},{4,5},{5,4},{6,7},{7,6},{8,9},{9,8},{10,11... | collective-permute-start | bytes 4718600 | tf_op jit(solution)/shard_map/ppermute | solution.py:755
  207.2 5.0 %collective-permute-start.39 = (bf16[2,64,512]{2,1,0:T(8,128)(2,1)S(1)}, bf16[2,64,512]{2,1,0:T(8,128)(2,1)S(1)}, u32[]{:S(2)}, u32[]{:S(2)}) collective-permute-start(bf16[2,64,512]{2,1,0:T(8,128)(2,1)S(1)} %pad_maximum_fusion.11), channel_id=1, source_target_pairs={{0,4},{1,5},{2,6},{3,7},{4,0},{5,1},{6,2},{7,3},{8,12},{9,13},{10,... | collective-permute-start | bytes 393224 | tf_op jit(solution)/shard_map/ppermute | solution.py:755
  212.2 9.3 %collective-permute-start.40 = (bf16[2,2,64,512]{3,2,1,0:T(8,128)(2,1)S(1)}, bf16[2,2,64,512]{3,2,1,0:T(8,128)(2,1)S(1)}, u32[]{:S(2)}, u32[]{:S(2)}) collective-permute-start(bf16[2,2,64,512]{3,2,1,0:T(8,128)(2,1)S(1)} %pad_maximum_fusion.10), channel_id=1, source_target_pairs={{0,2},{1,3},{2,0},{3,1},{4,6},{5,7},{6,4},{7,5},{8,10},{9,11},{10,... | collective-permute-start | bytes 786440 | tf_op jit(solution)/shard_map/ppermute | solution.py:755
  229.3 9.4 %collective-permute-start.41 = (bf16[3072,512]{1,0:T(8,128)(2,1)S(1)}, bf16[3072,512]{1,0:T(8,128)(2,1)S(1)}, u32[]{:S(2)}, u32[]{:S(2)}) collective-permute-start(bf16[3072,512]{1,0:T(8,128)(2,1)S(1)} %bitcast.155), channel_id=1, source_target_pairs={{0,16},{1,17},{2,18},{3,19},{4,20},{5,21},{6,22},{7,23},{8,24},{9,... | collective-permute-start | bytes 9437192 | tf_op jit(solution)/shard_map/ppermute | solution.py:755
  229.4 9.2 %collective-permute-start.42 = (bf16[2,2,2,64,512]{4,3,2,1,0:T(8,128)(2,1)S(1)}, bf16[2,2,2,64,512]{4,3,2,1,0:T(8,128)(2,1)S(1)}, u32[]{:S(2)}, u32[]{:S(2)}) collective-permute-start(bf16[2,2,2,64,512]{4,3,2,1,0:T(8,128)(2,1)S(1)} %pad_maximum_fusion.7), channel_id=1, source_target_pairs={{0,1},{1,0},{2,3},{3,2},{4,5},{5,4},{6,7},{7,6},{8,9},{9,8},{10,11... | collective-permute-start | bytes 1572872 | tf_op jit(solution)/shard_map/ppermute | solution.py:755
  238.8 6.3 %collective-permute-start.43 = (bf16[1024,512]{1,0:T(8,128)(2,1)S(1)}, bf16[1024,512]{1,0:T(8,128)(2,1)}, u32[]{:S(2)}, u32[]{:S(2)}) collective-permute-start(bf16[1024,512]{1,0:T(8,128)(2,1)S(1)} %bitcast.174), channel_id=1, source_target_pairs={{16,0},{17,1},{18,2},{19,3},{20,4},{21,5},{22,6},{23,7},{24,8},{25... | collective-permute-start | bytes 3145736 | tf_op jit(solution)/shard_map/ppermute | solution.py:755
  (19 other events, 76.6 us)

commit v3 on v2

v3 whole, which is shorter than its diff:
```python
import functools
import math

import jax
import jax.numpy as jnp
from jax import lax
from jax.experimental import pallas as pl
from jax.experimental.pallas import tpu as pltpu
from jax.sharding import PartitionSpec as P

SIDE_S = 8
SIDE_M = 12
CANVAS = 16
PIX = CANVAS * CANVAS
C = 512
FF = 2048
LANES = 128
GROUPS = 8
EPS = 1e-06
KS = 7
PAD_ROWS = (CANVAS + 6) * CANVAS
BF = jnp.bfloat16
F32 = jnp.float32
SPARE_VMEM = 8 * 1024 * 1024
MOST_VMEM = 58 * 1024 * 1024

V_N1G, V_N1S, V_BIN, V_CB, V_B1, V_B2, V_B3, V_BO, V_BS, V_N2G, V_N2S, V_BE, V_BR, V_MS = range(14)
VEC_ROWS = 16


class Slot:
    def __init__(self, ref, copy):
        self.ref, self.copy = ref, copy

    def get(self):
        if self.copy is not None:
            self.copy.wait()
            self.copy = None
        return self.ref


class Ship:
    def __init__(self, ref, copies):
        self.ref, self.copies, self.started = ref, copies, False

    def go(self):
        for copy in self.copies:
            copy.start()
        self.started = True


class Halves:
    def __init__(self, rows):
        self.shape, self.dtype = (rows, 512), BF


def load(array):
    return ("load", array)


def near(array):
    return ("near", array)


def image(array):
    return ("image", array)


def pick(block, pair):
    return (block, pair)


def smem(array):
    return ("smem", array)


def sds(shape, dtype):
    return jax.ShapeDtypeStruct(shape, dtype)


def vmem(rows, cols, dtype):
    return pltpu.VMEM((rows, cols), dtype)


def room(shapes, most):
    if most:
        return pltpu.CompilerParams(vmem_limit_bytes=MOST_VMEM)
    total = 0
    for shape in shapes:
        if len(getattr(shape, "shape", ())) >= 2 and jnp.issubdtype(shape.dtype, jnp.floating):
            total += math.prod(shape.shape) * jnp.dtype(shape.dtype).itemsize
    return pltpu.CompilerParams(vmem_limit_bytes=total + SPARE_VMEM)


SMEM = pl.BlockSpec(memory_space=pltpu.SMEM)
ANY = pl.BlockSpec(memory_space=pl.ANY)
HBM = pl.BlockSpec(memory_space=pltpu.HBM)


def call(kernel, name, operands, outs, scratch, most=False):
    specs, arrays, buffers = [], [], []
    for kind, value in operands:
        if kind == "smem":
            specs.append(SMEM)
            arrays.append(value)
            continue
        sources = value if isinstance(kind, int) else (value,)
        specs += [ANY if kind == "near" else HBM] * len(sources)
        arrays += list(sources)
        shape = value.shape[1:] if kind == "image" else sources[0].shape
        buffers.append(pltpu.VMEM(shape, sources[0].dtype))
    shapes = []
    for out in outs:
        half = sds((out.shape[0] // 2, out.shape[1]), out.dtype) if isinstance(out, Halves) else None
        shapes += [half, half] if half is not None else [out]
    n_in, n_out, n_load, n_ship = len(arrays), len(shapes), len(buffers), len(outs)
    buffers += [pltpu.VMEM(out.shape, out.dtype) for out in outs]

    def body(*refs):
        ins, results = refs[:n_in], refs[n_in : n_in + n_out]
        bufs = refs[n_in + n_out : n_in + n_out + n_load + n_ship]
        rest, sems = refs[n_in + n_out + n_load + n_ship : -1], refs[-1]
        section = lax.axis_index("section")
        slots, at, nth = [], 0, 0
        for kind, value in operands:
            if kind == "smem":
                slots.append(ins[at])
                at += 1
                continue
            dst, sem = bufs[nth], sems.at[nth]
            nth += 1
            if isinstance(kind, int):
                own, other = ins[at], ins[at + 1]
                at += 2

                @pl.when(section == kind)
                def _():
                    pltpu.make_async_copy(own, dst, sem).start()

                @pl.when(section != kind)
                def _():
                    pltpu.make_async_copy(other, dst, sem).start()

                copy = pltpu.make_async_copy(own, dst, sem)
            else:
                src = ins[at]
                at += 1
                if kind == "image":
                    src = src.at[section]
                copy = pltpu.make_async_copy(src, dst, sem)
                copy.start()
            slots.append(Slot(dst, copy))
        ships, at = [], 0
        for i, out in enumerate(outs):
            buf, copies = bufs[n_load + i], []
            if isinstance(out, Halves):
                rows = out.shape[0] // 2
                for half in (1, 0):
                    src = buf.at[half * rows : (half + 1) * rows]
                    copies.append(pltpu.make_async_copy(src, results[at + half], sems.at[n_load + at + half]))
            else:
                copies.append(pltpu.make_async_copy(buf, results[at], sems.at[n_load + at]))
            at += len(copies)
            ships.append(Ship(buf, copies))
        kernel(*slots, *ships, *rest)
        for slot in slots:
            if isinstance(slot, Slot):
                slot.get()
        for ship in ships:
            if not ship.started:
                ship.go()
        for ship in ships:
            for copy in ship.copies:
                copy.wait()

    return pl.pallas_call(
        body,
        name=name,
        out_shape=shapes,
        in_specs=specs,
        out_specs=[ANY] * n_out,
        scratch_shapes=buffers + list(scratch) + [pltpu.SemaphoreType.DMA((n_load + n_out,))],
        compiler_params=room(buffers + list(scratch), most),
        cost_estimate=pl.CostEstimate(flops=0, bytes_accessed=0, transcendentals=0),
    )(*arrays)


def nn(a, b):
    return jnp.dot(a, b, preferred_element_type=F32)


def nt(a, b):
    return lax.dot_general(a, b, (((1,), (1,)), ((), ())), preferred_element_type=F32)


def tn(a, b):
    return lax.dot_general(a, b, (((0,), (0,)), ((), ())), preferred_element_type=F32)


def colsum(v):
    return jnp.sum(v, axis=0, keepdims=True)


def wide(m, n):
    return jnp.concatenate([m] * n, axis=1)


def reader(vec_ref):
    return lambda row, lo, n: vec_ref[row : row + 1, lo : lo + n]


def piece_masks(section):
    place = lax.axis_index("dp") % 16
    x_bit, y_bit, z_at = place & 1, (place >> 1) & 1, place >> 2
    return section * 16 + x_bit * 8 + y_bit * 4 + z_at, section * 16 + y_bit * 8 + x_bit * 4 + z_at


def piece_rows(masks, p, rows):
    return pl.multiple_of((p ^ masks[p >> 4]) * rows, 64)


def fill_mask(mask_ref, crop_ref, section):
    kind = crop_ref[section, 0]
    side = jnp.where(kind == 0, SIDE_S, jnp.where(kind == 1, SIDE_M, CANVAS))
    r = lax.broadcasted_iota(jnp.int32, (PIX, LANES), 0)
    inside = ((r // CANVAS) < side) & ((r % CANVAS) < side)
    mask_ref[...] = inside.astype(F32)


def row_chunks(body, start):
    return lax.fori_loop(0, PIX // 32, lambda i, carry: body(pl.ds(pl.multiple_of(i * 32, 32), 32), carry), start,
                         unroll=True)


def normalized(v):
    cen = v - jnp.mean(v, axis=-1, keepdims=True)
    inv = lax.rsqrt(jnp.mean(cen * cen, axis=-1, keepdims=True) + EPS)
    return cen * inv, inv


def norm_gradient(up, xhat, inv, gain):
    g = up * gain
    return inv * (g - jnp.mean(g, axis=-1, keepdims=True) - xhat * jnp.mean(g * xhat, axis=-1, keepdims=True))


def conv_rows(src_ref, taps_ref, flip, bias, store):
    def row(h, carry):
        accs = [bias] * CANVAS if bias is not None else [None] * CANVAS
        for a in range(KS):
            ks = []
            for e in range(KS):
                t = (KS - 1 - a) * KS + (KS - 1 - e) if flip else a * KS + e
                ks.append(taps_ref[t * GROUPS : (t + 1) * GROUPS, :])
            for w2 in range(CANVAS):
                x = vreg(src_ref, (h + a) * CANVAS + w2)
                for e in range(KS):
                    w = w2 + 3 - e
                    if 0 <= w < CANVAS:
                        term = x * ks[e]
                        accs[w] = term if accs[w] is None else accs[w] + term
        for w in range(CANVAS):
            store(h * CANVAS + w, accs[w])
        return carry

    lax.fori_loop(0, CANVAS, row, 0)


def vreg(ref, index):
    return ref[pl.ds(pl.multiple_of(index * GROUPS, GROUPS), GROUPS), :]


def zero_border(ref):
    zeros = jnp.zeros((3 * CANVAS * GROUPS, LANES), F32)
    ref[0 : 3 * CANVAS * GROUPS, :] = zeros
    ref[(PAD_ROWS - 3 * CANVAS) * GROUPS :, :] = zeros


def lane_group(ref, g, rows=PIX, base=0):
    return ref[pl.ds(base + g, rows, stride=GROUPS), :]


def gn_forward_part(mask, x_ref, vec, taps, gates, win, wo, n1, cin, mix, p, gl, mid, br, mx_ref):
    zero_border(cin.ref)

    def norm_in(r, carry):
        xhat, _ = normalized(x_ref[r, :].astype(F32) * wide(mask[r, :], 4))
        n1.ref[r, :] = (xhat * vec(V_N1G, 0, C) + vec(V_N1S, 0, C)).astype(BF)
        return carry

    row_chunks(norm_in, 0)
    n1.go()
    win_ref = win.get()
    for n in range(4):
        m = nn(n1.ref[...], win_ref[:, n * 256 : (n + 1) * 256]) + vec(V_BIN, n * 256, 256)
        for half in range(2):
            g = 2 * n + half
            v = m[:, half * LANES : (half + 1) * LANES] * mask[...]
            cin.ref[pl.ds(3 * CANVAS * GROUPS + g, PIX, stride=GROUPS), :] = v
            if g == 0:
                p.ref[:, 0:LANES] = v
    cin.go()
    taps_ref = taps.get()
    bias = taps_ref[49 * GROUPS : 50 * GROUPS, :]

    def keep(pixel, acc):
        mx_ref[pl.ds(pl.multiple_of(pixel * GROUPS, GROUPS), GROUPS), :] = acc * (1.0 / 3.0)

    conv_rows(cin.ref, taps_ref, False, bias, keep)
    for g in range(GROUPS):
        mix.ref[:, g * LANES : (g + 1) * LANES] = lane_group(mx_ref, g)
    mix.go()
    gates_ref, wo_ref = gates.get(), wo.get()
    gl.ref[:, 0:128] = (p.ref[:, 0:128] * pltpu.roll(mix.ref[:, 0:128], 64, 1)).astype(BF)
    p1 = nn(gl.ref[:, 0:128], gates_ref[256:384, 256:384]) + vec(V_B1, 0, 128)
    p.ref[:, 128:256] = p1
    gl.ref[:, 128:256] = (p1 * mix.ref[:, 128:256]).astype(BF)
    p2 = nn(gl.ref[:, 128:256], gates_ref[256:384, 0:256]) + vec(V_B2, 0, 256)
    p.ref[:, 256:512] = p2
    gl.ref[:, 256:512] = (p2 * mix.ref[:, 256:512]).astype(BF)
    for n in range(2):
        c = 256 * n
        p3 = nn(gl.ref[:, 256:512], gates_ref[0:256, c : c + 256]) + vec(V_B3, c, 256)
        p.ref[:, 512 + c : 768 + c] = p3
        gl.ref[:, 512 + c : 768 + c] = (p3 * mix.ref[:, 512 + c : 768 + c]).astype(BF)
    p.go()
    gl.go()
    for n in range(2):
        c = 256 * n
        b = nn(gl.ref[:, 512:1024], wo_ref[:, c : c + 256]) + vec(V_BO, c, 256)
        br.ref[:, c : c + 256] = b.astype(BF)
        start = x_ref[:, c : c + 256].astype(F32) * wide(mask[...], 2)
        mid.ref[:, c : c + 256] = start + vec(V_BS, c, 256) * b
    br.go()
    if isinstance(mid, Ship):
        mid.go()


def mlp_forward_part(mask, mid_ref, vec, we, wr, n2_ref, act_ref, slope_ref, out_ref, res_ref):
    def norm_mid(r, carry):
        xhat, _ = normalized(mid_ref[r, :])
        n2_ref[r, :] = (xhat * vec(V_N2G, 0, C) + vec(V_N2S, 0, C)).astype(BF)
        return carry

    row_chunks(norm_mid, 0)
    we_ref = we.get()
    for j in range(8):
        c = 256 * j
        pre = nn(n2_ref[...], we_ref[:, c : c + 256]) + vec(V_BE, c, 256)
        cum = 0.5 * (1.0 + lax.erf(pre * 0.7071067811865476))
        act_ref[:, c : c + 256] = (pre * cum).astype(BF)
        slope = cum + pre * jnp.exp(-0.5 * pre * pre) * 0.3989422804014327
        slope_ref[:, c : c + 256] = slope.astype(BF)
    wr_ref = wr.get()
    for n in range(2):
        c = 256 * n
        out = nn(act_ref[...], wr_ref[:, c : c + 256]) + vec(V_BR, c, 256)
        out_ref[:, c : c + 256] = out.astype(BF)
        res = wide(mask[...], 2) * (mid_ref[:, c : c + 256] + vec(V_MS, c, 256) * out)
        res_ref[:, c : c + 256] = res.astype(BF)


def mlp_back_part(mask, masks, dy_ref, vec, n2_ref, act_ref, slope_ref, out_ref, mid_ref, we, wr,
                  dmid, mvec, bucket, dout_ref, dpre_ref, dn2_ref):
    mvec.ref[...] = jnp.zeros_like(mvec.ref)
    for n in range(2):
        c = 256 * n
        dyr = dy_ref[:, c : c + 256].astype(F32) * wide(mask[...], 2)
        dmid.ref[:, c : c + 256] = dyr
        dout = (vec(V_MS, c, 256) * dyr).astype(BF)
        dout_ref[:, c : c + 256] = dout
        mvec.ref[3:4, c : c + 256] = colsum(dout.astype(F32))
        mvec.ref[4:5, c : c + 256] = colsum(dyr * out_ref[:, c : c + 256].astype(F32))
    wr_ref = wr.get()
    for j in range(8):
        c = 256 * j
        dw = tn(act_ref[:, c : c + 256], dout_ref[...]).astype(BF)
        for q in range(4):
            bucket.ref[pl.ds(piece_rows(masks, 4 * j + q, 128), 64), :] = dw[64 * q : 64 * q + 64, :]
        dact = nt(dout_ref[...], wr_ref[c : c + 256, :])
        dpre = (dact * slope_ref[:, c : c + 256].astype(F32)).astype(BF)
        dpre_ref[:, c : c + 256] = dpre
        mvec.ref[2:3, c : c + 256] = colsum(dpre.astype(F32))
    we_ref = we.get()
    for cb in range(4):
        dw = tn(n2_ref[...], dpre_ref[:, 512 * cb : 512 * cb + 512]).astype(BF)
        for q in range(8):
            rows = pl.multiple_of(piece_rows(masks, 8 * cb + q, 128) + 64, 64)
            bucket.ref[pl.ds(rows, 64), :] = dw[64 * q : 64 * q + 64, :]
    bucket.go()
    for n in range(2):
        c = 256 * n
        dn2_ref[:, c : c + 256] = nt(dpre_ref[...], we_ref[c : c + 256, :])

    def norm_back(r, carry):
        dgain, dshift = carry
        xhat, inv = normalized(mid_ref[r, :])
        up = dn2_ref[r, :]
        dmid.ref[r, :] = dmid.ref[r, :] + norm_gradient(up, xhat, inv, vec(V_N2G, 0, C))
        return dgain + colsum(up * xhat), dshift + colsum(up)

    zero = jnp.zeros((1, C), F32)
    dgain, dshift = row_chunks(norm_back, (zero, zero))
    mvec.ref[0:1, 0:C] = dgain
    mvec.ref[1:2, 0:C] = dshift


def pack_kernel(*refs):
    vectors, taps_in, w1, w2, w3 = refs[:14], refs[14], refs[15], refs[16], refs[17]
    vec_ref, taps_ref, gates_ref = refs[18:]
    gates_ref[0:256, :] = w3[...]
    gates_ref[256:384, 0:256] = w2[...]
    gates_ref[256:384, 256:384] = jnp.concatenate([w1[...], jnp.zeros((64, 128), BF)], axis=0)
    gates_ref[256:384, 384:512] = jnp.zeros((128, 128), BF)
    vec_ref[...] = jnp.zeros_like(vec_ref)
    for row, ref in enumerate(vectors):
        n = ref.shape[1]
        vec_ref[row : row + 1, 0:n] = ref[...].astype(F32)
    taps = taps_in[...].astype(F32)
    bias = vectors[V_CB][...].astype(F32)
    for g in range(GROUPS):
        if g == 0:
            t = jnp.concatenate([jnp.zeros((49, 64), F32), taps[:, 0:64]], axis=1)
            b = jnp.concatenate([jnp.zeros((1, 64), F32), bias[:, 0:64]], axis=1)
        else:
            t = taps[:, g * LANES - 64 : g * LANES + 64]
            b = bias[:, g * LANES - 64 : g * LANES + 64]
        taps_ref[pl.ds(g, 49, stride=GROUPS), :] = t
        taps_ref[49 * GROUPS + g : 49 * GROUPS + g + 1, :] = b


def gn_forward_kernel(crop, x, vec, win, taps, gates, wo, n1, cin, mix, p, gl, mid, br, mask, mx_ref):
    fill_mask(mask, crop, lax.axis_index("section"))
    x_ref = x.get()
    gn_forward_part(mask, x_ref, reader(vec.get()), taps, gates, win, wo, n1, cin, mix, p, gl, mid, br, mx_ref)


def middle_kernel(crop, mid0, vec0, we0, wr0, vec1, win, taps, gates, wo, we1, wr1, dy,
                  hidden, n2, act, slope, out, n1, cin, mix, p, gl, br, final, swap, dmid, mvec, bucket,
                  mask, mx_ref, mid1, n2_1, act1, slope1, out1, dout_ref, dpre_ref, dn2_ref):
    section = lax.axis_index("section")
    masks = piece_masks(section)
    fill_mask(mask, crop, section)
    mid0_ref = mid0.get()
    mlp_forward_part(mask, mid0_ref, reader(vec0.get()), we0, wr0, n2.ref, act.ref, slope.ref, out.ref, hidden.ref)
    for ship in (hidden, n2, act, slope, out):
        ship.go()
    vec = reader(vec1.get())
    gn_forward_part(mask, hidden.ref, vec, taps, gates, win, wo, n1, cin, mix, p, gl, Slot(mid1, None), br, mx_ref)
    mlp_forward_part(mask, mid1, vec, we1, wr1, n2_1, act1, slope1, out1, final.ref)
    final.go()
    swap.ref[...] = jnp.where(section == 0, final.ref[...], hidden.ref[...])
    swap.go()
    mlp_back_part(mask, masks, dy.get(), vec, n2_1, act1, slope1, out1, mid1, we1, wr1,
                  dmid, mvec, bucket, dout_ref, dpre_ref, dn2_ref)


def mlp_back_kernel(crop, dy, vec, n2, act, slope, out, mid, wr, we, dmid, mvec, bucket,
                    mask, dout_ref, dpre_ref, dn2_ref):
    section = lax.axis_index("section")
    fill_mask(mask, crop, section)
    mlp_back_part(mask, piece_masks(section), dy.get(), reader(vec.get()), n2.get(), act.get(), slope.get(), out.get(),
                  mid.get(), we, wr, dmid, mvec, bucket, dout_ref, dpre_ref, dn2_ref)


def gn_back_kernel(block, crop, dmid, br, vec, wo, mix, p, gates, mvec, taps, win, x, *rest):
    if block == 0:
        following, dv, swap, dbr, dp, dmg, dcp, gvec = rest[:8]
    else:
        dv, dvb, dbr, dp, dmg, dcp, gvec = rest[:7]
    mask, dg_ref, dmix_ref, ds_ref, dn1_ref = rest[-5:]
    section = lax.axis_index("section")
    fill_mask(mask, crop, section)
    zero_border(dcp.ref)
    dmid_ref, br_ref = dmid.get(), br.get()
    vec = reader(vec.get())
    dbs, dbo = [], []
    for n in range(2):
        c = 256 * n
        dm = dmid_ref[:, c : c + 256]
        dbs.append(colsum(dm * br_ref[:, c : c + 256].astype(F32)))
        d = (vec(V_BS, c, 256) * dm).astype(BF)
        dbr.ref[:, c : c + 256] = d
        dbo.append(colsum(d.astype(F32)))
    dbr.go()
    wo_ref, mix_ref, p_ref = wo.get(), mix.get(), p.get()
    db3 = []
    for n in range(2):
        c = 256 * n
        dg = nt(dbr.ref[...], wo_ref[c : c + 256, :])
        d = (dg * mix_ref[:, 512 + c : 768 + c]).astype(BF)
        dmix_ref[:, 512 + c : 768 + c] = dg * p_ref[:, 512 + c : 768 + c] * (1.0 / 3.0)
        dp.ref[:, 512 + c : 768 + c] = d
        db3.append(colsum(d.astype(F32)))
    gates_ref = gates.get()
    dg = nt(dp.ref[:, 512:1024], gates_ref[0:256, :])
    d = (dg * mix_ref[:, 256:512]).astype(BF)
    dmix_ref[:, 256:512] = dg * p_ref[:, 256:512] * (1.0 / 3.0)
    dp.ref[:, 256:512] = d
    db2 = colsum(d.astype(F32))
    dg = nt(dp.ref[:, 256:512], gates_ref[256:384, 0:256])
    d = (dg * mix_ref[:, 128:256]).astype(BF)
    dmix_ref[:, 128:256] = dg * p_ref[:, 128:256] * (1.0 / 3.0)
    dp.ref[:, 128:256] = d
    db1 = colsum(d.astype(F32))
    dg = nt(dp.ref[:, 128:256], gates_ref[256:384, 256:384])
    dmix_ref[:, 0:128] = pltpu.roll(dg * p_ref[:, 0:128], 64, 1) * (1.0 / 3.0)
    dg_ref[...] = dg * pltpu.roll(mix_ref[:, 0:128], 64, 1)
    dp.ref[:, 0:128] = jnp.zeros((PIX, LANES), BF)
    dp.go()
    for g in range(GROUPS):
        dcp.ref[pl.ds(3 * CANVAS * GROUPS + g, PIX, stride=GROUPS), :] = dmix_ref[:, g * LANES : (g + 1) * LANES]
    dcp.go()

    def keep(pixel, acc):
        ds_ref[pl.ds(pl.multiple_of(pixel * GROUPS, GROUPS), GROUPS), :] = acc

    conv_rows(dcp.ref, taps.get(), True, None, keep)
    dbin = []
    for g in range(GROUPS):
        d = lane_group(ds_ref, g) * mask[...]
        if g == 0:
            d = d + dg_ref[...]
        d = d.astype(BF)
        dmg.ref[:, g * LANES : (g + 1) * LANES] = d
        dbin.append(colsum(d.astype(F32)))
    dmg.go()
    win_ref, x_ref = win.get(), x.get()
    next_ref = following.get() if block == 0 else None
    for n in range(2):
        c = 256 * n
        dn1_ref[:, c : c + 256] = nt(dmg.ref[...], win_ref[c : c + 256, :])

    def norm_back(r, carry):
        dgain, dshift = carry
        m = wide(mask[r, :], 4)
        xhat, inv = normalized(x_ref[r, :].astype(F32) * m)
        up = dn1_ref[r, :]
        d = m * (dmid_ref[r, :] + norm_gradient(up, xhat, inv, vec(V_N1G, 0, C)))
        dv.ref[r, :] = d
        if block == 0:
            swap.ref[r, :] = jnp.where(section == 0, next_ref[r, :], d)
        else:
            dvb.ref[r, :] = d.astype(BF)
        return dgain + colsum(up * xhat), dshift + colsum(up)

    zero = jnp.zeros((1, C), F32)
    dgain, dshift = row_chunks(norm_back, (zero, zero))
    z = jnp.zeros((1, LANES), F32)
    mvec_ref = mvec.get()
    rows = [
        dgain,
        dshift,
        jnp.concatenate(dbin[0:4], axis=1),
        jnp.concatenate(dbin[4:8], axis=1),
        jnp.concatenate([db1, z, z, z], axis=1),
        jnp.concatenate([db2, z, z], axis=1),
        jnp.concatenate(db3, axis=1),
        jnp.concatenate(dbo, axis=1),
        jnp.concatenate(dbs, axis=1),
        mvec_ref[0:1, 0:C],
        mvec_ref[1:2, 0:C],
        mvec_ref[2:3, 0:512],
        mvec_ref[2:3, 512:1024],
        mvec_ref[2:3, 1024:1536],
        mvec_ref[2:3, 1536:2048],
        mvec_ref[3:4, 0:C],
        mvec_ref[4:5, 0:C],
    ]
    rows.append(jnp.zeros((32 - len(rows), C), F32))
    gvec.ref[...] = jnp.concatenate(rows, axis=0).astype(BF)


def gn_weights_kernel(n1, dmg, gl, dbr, dp, gvec, cin, dcp, bucket, dk_ref):
    masks = piece_masks(lax.axis_index("section"))

    def put(p, val, sub=0):
        n = val.shape[0]
        bucket.ref[pl.ds(pl.multiple_of(piece_rows(masks, p, 64) + sub, 16), n), :] = val

    n1_ref, dmg_ref = n1.get(), dmg.get()
    for cb in range(2):
        dw = tn(n1_ref[...], dmg_ref[:, 512 * cb : 512 * cb + 512]).astype(BF)
        for q in range(8):
            put(8 * cb + q, dw[64 * q : 64 * q + 64, :])
    gl_ref, dbr_ref, dp_ref = gl.get(), dbr.get(), dp.get()
    dw = tn(gl_ref[:, 512:1024], dbr_ref[...]).astype(BF)
    for q in range(8):
        put(16 + q, dw[64 * q : 64 * q + 64, :])
    dw = tn(gl_ref[:, 256:512], dp_ref[:, 512:1024]).astype(BF)
    for q in range(4):
        put(24 + q, dw[64 * q : 64 * q + 64, :])
    dw = tn(gl_ref[:, 128:256], dp_ref[:, 256:512]).astype(BF)
    put(28, jnp.concatenate([dw[0:64, :], dw[64:128, :]], axis=1))
    dw1 = tn(gl_ref[:, 0:128], dp_ref[:, 128:256]).astype(BF)
    put(31, jnp.concatenate([dw1[16 * i : 16 * i + 16, :] for i in range(4)], axis=1))
    put(31, jnp.zeros((16, 512), BF), 16)
    put(31, gvec.get()[...], 32)
    cin_ref, dcp_ref = cin.get(), dcp.get()
    dk_ref[...] = jnp.zeros_like(dk_ref)
    for taps in ((0, 1), (2, 3), (4, 5), (6,)):

        def row(h, accs):
            accs = list(accs)
            ds = [vreg(dcp_ref, (h + 3) * CANVAS + w) for w in range(CANVAS)]
            for i, a in enumerate(taps):
                for w2 in range(CANVAS):
                    x = vreg(cin_ref, (h + a) * CANVAS + w2)
                    for e in range(KS):
                        w = w2 + 3 - e
                        if 0 <= w < CANVAS:
                            accs[i * KS + e] = accs[i * KS + e] + x * ds[w]
            if len(taps) == 1:
                for w in range(CANVAS):
                    accs[KS] = accs[KS] + ds[w]
            return tuple(accs)

        count = len(taps) * KS + (1 if len(taps) == 1 else 0)
        accs = lax.fori_loop(0, CANVAS, row, tuple(jnp.zeros((GROUPS, LANES), F32) for _ in range(count)))
        for i in range(count):
            t = taps[0] * KS + i
            dk_ref[t * GROUPS : (t + 1) * GROUPS, :] = accs[i]
    for half in range(2):
        put(29 + half, jnp.concatenate([lane_group(dk_ref, 4 * half + i, 64) for i in range(4)], axis=1).astype(BF))


def start_pieces(layout, rows, halves, buf, sems):
    section = lax.axis_index("section")
    masks = piece_masks(section)
    for p in range(32):
        rel = p ^ masks[p >> 4]
        far = rel >> 4
        dst = buf.at[p * rows : (p + 1) * rows]
        sem = sems.at[p // 4]
        for sec in range(2):
            stride, first = layout[sec]
            off = pl.multiple_of((rel & 15) * stride + first, 64)
            for side in range(2):

                @pl.when((section == sec) & (far == side))
                def _():
                    pltpu.make_async_copy(halves[2 * sec + side].at[pl.ds(off, rows)], dst, sem).start()


def wait_pieces(i, rows, halves, buf, sems):
    part = buf.at[pl.ds(i * 4 * rows, 4 * rows)]
    pltpu.make_async_copy(halves[0].at[pl.ds(0, 4 * rows)], part, sems.at[i]).wait()


def mlp_finish_kernel(layout, *refs):
    halves = refs[:4]
    wr_any, we_any, buf, wr_ref, we_ref, sems, out_sems = refs[-7:]
    start_pieces(layout, 128, halves, buf, sems)
    copies = []
    for i in range(8):
        wait_pieces(i, 128, halves, buf, sems)
        cb = i // 2
        for q in range(4):
            p = 4 * i + q
            r = p % 8
            wr_ref[64 * p : 64 * p + 64, :] = buf[128 * p : 128 * p + 64, :].astype(F32)
            we_ref[64 * r : 64 * r + 64, 512 * cb : 512 * cb + 512] = buf[128 * p + 64 : 128 * p + 128, :].astype(F32)
        rows = slice(256 * i, 256 * i + 256)
        copies.append(pltpu.make_async_copy(wr_ref.at[rows], wr_any.at[rows], out_sems.at[i]))
        half = slice(256 * (i % 2), 256 * (i % 2) + 256)
        cols = slice(512 * cb, 512 * cb + 512)
        copies.append(pltpu.make_async_copy(we_ref.at[half, cols], we_any.at[half, cols], out_sems.at[8 + i]))
        copies[-2].start()
        copies[-1].start()
    for copy in copies:
        copy.wait()


def gn_finish_kernel(layout, *refs):
    halves = refs[:4]
    (n1g, n1s, win_any, bin_, conv, cbias, w1, b1, w2, b2, w3, b3, wo_any, bo, bs, n2g, n2s, be, br, ms,
     buf, win, wo, sems, out_sems) = refs[-25:]
    start_pieces(layout, 64, halves, buf, sems)
    copies = []
    for cb in range(2):
        cols = slice(512 * cb, 512 * cb + 512)
        for i in range(2):
            wait_pieces(2 * cb + i, 64, halves, buf, sems)
        win[:, cols] = buf[cols, :].astype(F32)
        copies.append(pltpu.make_async_copy(win.at[:, cols], win_any.at[:, cols], out_sems.at[cb]))
        copies[-1].start()
    for i in (4, 5):
        wait_pieces(i, 64, halves, buf, sems)
    wo[...] = buf[1024:1536, :].astype(F32)
    copies.append(pltpu.make_async_copy(wo, wo_any, out_sems.at[2]))
    copies[-1].start()
    for i in (6, 7):
        wait_pieces(i, 64, halves, buf, sems)
    w3[...] = buf[1536:1792, :].astype(F32)
    for i in range(2):
        w2[64 * i : 64 * i + 64, :] = buf[1792:1856, 256 * i : 256 * i + 256].astype(F32)
    for i in range(4):
        w1[16 * i : 16 * i + 16, :] = buf[1984:2000, 128 * i : 128 * i + 128].astype(F32)
    taps = jnp.concatenate([buf[1856:1920, :], buf[1920:1984, :]], axis=1).astype(F32)
    for i in range(49):
        conv[i] = taps[i : i + 1, 64:1024]
    cbias[...] = taps[49:50, 64:1024]
    v = buf[2016:2048, :].astype(F32)
    n1g[...] = v[0:1]
    n1s[...] = v[1:2]
    bin_[:, 0:512] = v[2:3]
    bin_[:, 512:1024] = v[3:4]
    b1[...] = v[4:5, 0:128]
    b2[...] = v[5:6, 0:256]
    b3[...] = v[6:7]
    bo[...] = v[7:8]
    bs[...] = v[8:9]
    n2g[...] = v[9:10]
    n2s[...] = v[10:11]
    for i in range(4):
        be[:, 512 * i : 512 * i + 512] = v[11 + i : 12 + i]
    br[...] = v[15:16]
    ms[...] = v[16:17]
    for copy in copies:
        copy.wait()


def place_kernel(first, second, got, out):
    section = lax.axis_index("section")

    @pl.when(section == 0)
    def _():
        out[0] = first[...]
        out[1] = got[...]

    @pl.when(section != 0)
    def _():
        out[0] = got[...]
        out[1] = second[...]


VM = pl.BlockSpec(memory_space=pltpu.VMEM)


def plain_call(kernel, name, operands, outs, scratch, most=False):
    return pl.pallas_call(
        kernel,
        name=name,
        out_shape=[shape for _, shape in outs],
        in_specs=[spec for spec, _ in operands],
        out_specs=[spec for spec, _ in outs],
        scratch_shapes=scratch,
        compiler_params=room([a for spec, a in operands + outs if spec is VM] + scratch, most),
        cost_estimate=pl.CostEstimate(flops=0, bytes_accessed=0, transcendentals=0),
    )(*[array for _, array in operands])


def on(spec, *arrays):
    return [(spec, a) for a in arrays]


MASK = vmem(PIX, LANES, F32)
PIXEL_CHANNELS = vmem(PIX * GROUPS, LANES, F32)
FIELD_F32, FIELD_BF = sds((PIX, C), F32), sds((PIX, C), BF)
CONV_F32 = sds((PAD_ROWS * GROUPS, LANES), F32)
WIDE_F32, WIDE_BF = sds((PIX, 1024), F32), sds((PIX, 1024), BF)
HIDE_BF = sds((PIX, FF), BF)
GN_SAVED = [FIELD_BF, CONV_F32, WIDE_F32, WIDE_F32, WIDE_BF]


def run_pack(vectors, taps, gates):
    outs = on(VM, sds((VEC_ROWS, FF), F32), sds((50 * GROUPS, LANES), F32), sds((384, 512), BF))
    return plain_call(pack_kernel, "pack", on(VM, *vectors, taps, *gates), outs, [], True)


def run_gn_forward(crop, images, w):
    operands = [smem(crop), image(images)] + [pick(0, w[k]) for k in ("vec", "win", "taps", "gates", "wo")]
    return call(gn_forward_kernel, "gnconv_forward", operands, GN_SAVED + [FIELD_F32, FIELD_BF],
                [MASK, PIXEL_CHANNELS], True)


def run_middle(crop, mid, cotangent, w):
    operands = [smem(crop), load(mid)] + [pick(0, w[k]) for k in ("vec", "we", "wr")]
    operands += [pick(1, w[k]) for k in ("vec", "win", "taps", "gates", "wo", "we", "wr")] + [image(cotangent)]
    outs = [FIELD_BF, FIELD_BF, HIDE_BF, HIDE_BF, FIELD_BF] + GN_SAVED + [FIELD_BF, FIELD_BF, FIELD_BF, FIELD_F32]
    outs += [sds((8, FF), F32), Halves(4096)]
    scratch = [MASK, PIXEL_CHANNELS, vmem(PIX, C, F32), vmem(PIX, C, BF), vmem(PIX, FF, BF), vmem(PIX, FF, BF),
               vmem(PIX, C, BF), vmem(PIX, C, BF), vmem(PIX, FF, BF), vmem(PIX, C, F32)]
    return call(middle_kernel, "middle", operands, outs, scratch, True)


def run_mlp_back(crop, dy, n2, act, slope, out, mid, w):
    operands = [smem(crop), near(dy), pick(0, w["vec"]), load(n2), load(act), load(slope), load(out), load(mid),
                pick(0, w["wr"]), pick(0, w["we"])]
    outs = [FIELD_F32, sds((8, FF), F32), Halves(4096)]
    scratch = [MASK, vmem(PIX, C, BF), vmem(PIX, FF, BF), vmem(PIX, C, F32)]
    return call(mlp_back_kernel, "mlp_backward", operands, outs, scratch, True)


def run_gn_back(block, crop, x, following, dmid, mvec, mix, p, br, w):
    far = load if block == 1 else near
    operands = [smem(crop), far(dmid), load(br), pick(block, w["vec"]), pick(block, w["wo"]), load(mix), load(p),
                pick(block, w["gates"]), far(mvec), pick(block, w["taps"]), pick(block, w["win"])]
    operands += [image(x), near(following)] if block == 0 else [load(x)]
    outs = [FIELD_F32, FIELD_F32 if block == 0 else FIELD_BF, FIELD_BF, WIDE_BF, WIDE_BF, CONV_F32, sds((32, 512), BF)]
    scratch = [MASK, vmem(PIX, LANES, F32), vmem(PIX, 1024, F32), PIXEL_CHANNELS, vmem(PIX, C, F32)]
    return call(functools.partial(gn_back_kernel, block), "gnconv_backward", operands, outs, scratch, block == 1)


def run_gn_weights(block, n1, dmg, gl, dbr, dp, gvec, cin, dcp):
    operands = [load(n1), near(dmg), load(gl), near(dbr), near(dp), near(gvec), load(cin), near(dcp)]
    return call(gn_weights_kernel, "gnconv_weights", operands, [Halves(2048)], [vmem(64 * GROUPS, LANES, F32)],
                block == 1)


def turn_kernel(token, out):
    out[...] = jnp.zeros_like(out)


def run_turn(token):
    return plain_call(turn_kernel, "turn", on(ANY, token), on(VM, sds((8, LANES), F32)), [])[0]


def run_mlp_finish(layout, halves):
    outs = on(ANY, sds((FF, C), F32), sds((C, FF), F32))
    scratch = [vmem(4096, 512, BF), vmem(FF, C, F32), vmem(C, FF, F32), pltpu.SemaphoreType.DMA((8,)),
               pltpu.SemaphoreType.DMA((16,))]
    return plain_call(functools.partial(mlp_finish_kernel, layout), "mlp_finish", on(ANY, *halves), outs, scratch, True)


def run_gn_finish(layout, halves):
    widths = [512, 512, (512, 1024), 1024, (49, 1, 960), 960, (64, 128), 128, (128, 256), 256, (256, 512), 512,
              (512, 512), 512, 512, 512, 512, 2048, 512, 512]
    large = ((512, 1024), (512, 512))
    outs = [(ANY if w in large else VM, sds((1, w) if isinstance(w, int) else w, F32)) for w in widths]
    scratch = [vmem(2048, 512, BF), vmem(512, 1024, F32), vmem(512, 512, F32), pltpu.SemaphoreType.DMA((8,)),
               pltpu.SemaphoreType.DMA((3,))]
    return plain_call(functools.partial(gn_finish_kernel, layout), "gn_finish", on(ANY, *halves), outs, scratch, True)


def run_place(first, second, got):
    outs = on(VM, sds((2, PIX, C), first.dtype))
    return plain_call(place_kernel, "place", on(VM, first, second, got), outs, [])[0]


AXES = ("section", "dp")
X_BIT, Y_BIT, Z_LOW, Z_HIGH = 1, 2, 4, 8

FIRST, SECOND, LOW, HIGH = (X_BIT, Y_BIT), (Y_BIT, X_BIT), (Z_LOW, Z_LOW), (Z_HIGH, Z_HIGH)

ORDER = (
    "+m1.core", "K1", "-m1.core", "+m1.x1", "K2", "+g1.core", "K3", "-g1.core", "+g1.x1", "-m1.x1", "+m1.x2",
    "+m0.core", "K4", "-g1.x1", "+g1.x2", "-m1.x2", "+m1.zl", "-m0.core", "+m0.x1", "-g1.x2", "+g1.zl", "-m1.zl",
    "+m1.zh", "-g1.zl", "+g1.zh", "K5", "-m0.x1", "+m0.x2", "-m1.zh", "-g1.zh", "+b1.ZH", "+g0.core", "-m0.x2",
    "+m0.zl", "-g0.core", "+g0.x1", "-b1.ZH", "+b1.ZL", "-m0.zl", "+m0.zh", "-g0.x1", "+g0.x2", "-b1.ZL", "+b1.X2",
    "+go", "-go", "-g0.x2", "+g0.zl", "-m0.zh", "+m0.ZH", "-b1.X2", "+b1.X1", "-g0.zl", "+g0.zh", "-m0.ZH", "+m0.ZL",
    "P2", "-g0.zh", "+g0.ZH", "-m0.ZL", "+m0.X2", "-g0.ZH", "+g0.ZL", "-g0.ZL", "+g0.X2", "-m0.X2", "+m0.X1",
    "-b1.X1", "+fo", "-fo", "P1", "-g0.X2", "+g0.X1", "+b1.Core", "-b1.Core", "-m0.X1", "+m0.Core", "-m0.Core",
    "-g0.X1", "+g0.Core", "MF", "-g0.Core", "GF",
)


def after(x, *others):
    return lax.optimization_barrier((x,) + others)[0]


class Flow:
    def __init__(self, count):
        self.count = count
        self.token = None
        self.flying = {}

    def exchange(self, x, flips=None, only=None):
        n = self.count
        other, bits = (1, (0, 0)) if flips is None else (0, flips)
        pairs = [
            (s * n + d, (s ^ other) * n + (d ^ bits[s])) for s in range(2) for d in range(n) if only is None or s == only
        ]
        return lax.ppermute(x, AXES, pairs)

    def start(self, name, x, flips=None, only=None):
        self.flying[name] = self.exchange(after(x, self.token), flips, only)

    def end(self, name):
        got, token = lax.optimization_barrier((self.flying.pop(name), self.token))
        self.token = run_turn(token)
        return got

    def tie(self, x):
        return after(x, self.token)


VECTORS = (0, 1, 3, 5, 7, 9, 11, 13, 14, 15, 16, 18, 20, 21)


def on_device(flow, images, cotangent, crop, *stacked):
    images = images.reshape(2, PIX, C)
    cotangent = cotangent.reshape(2, PIX, C)
    win, wo, we, wr = [stacked[i][0] for i in (2, 12, 17, 19)]
    vec, taps, gates = run_pack([stacked[i] for i in VECTORS], stacked[4][0], [stacked[i][0] for i in (6, 8, 10)])
    swap = flow.exchange
    win_other, wo_other = swap(win), swap(wo)
    taps_other, vec_other, gates_other = swap(taps), swap(vec), swap(gates)
    we, wr = after((we, wr), win_other, wo_other, taps_other, vec_other, gates_other)
    we_other, wr_other = swap(we), swap(wr)
    w = {
        "win": (win, win_other), "wo": (wo, wo_other), "we": (we, we_other), "wr": (wr, wr_other),
        "vec": (vec, vec_other), "taps": (taps, taps_other), "gates": (gates, gates_other),
    }

    n1_0, cin_0, mix_0, p_0, gl_0, mid_0, br_0 = run_gn_forward(crop, images, w)
    (hidden, n2_0, act_0, slope_0, out_0, n1_1, cin_1, mix_1, p_1, gl_1, br_1, final, field_swap, dmid_1, mvec_1,
     keep, send) = run_middle(crop, mid_0, cotangent, w)
    flow.token = mvec_1
    value = {"m1.core": (keep, send)}
    chips = flow.count // 16

    def sum_all(total):
        if chips > 1:
            groups = [[g * 16 + r for g in range(chips)] for r in range(16)]
            total = lax.psum(total, "dp", axis_index_groups=groups)
        return total

    def begin(name):
        bucket, step = name.split(".")
        only = {"b1": 0, "m0": 1, "g0": 1}.get(bucket)
        if step == "core":
            flow.start(name, value[name][1])
        elif step == "Core":
            flow.start(name, value[name], None, only)
        elif step in ("x1", "x2", "zh"):
            flow.start(name, value[name][1], {"x1": FIRST, "x2": SECOND, "zh": HIGH}[step])
        elif step == "zl":
            flow.start(name, value[name][:, 1], LOW)
        else:
            flow.start(name, value[name], {"ZH": HIGH, "ZL": LOW, "X2": SECOND, "X1": FIRST}[step])

    def finish(name):
        bucket, step = name.split(".")
        got = flow.end(name)
        mine = value.pop(name)
        if step == "core":
            half = mine[0] + got
            value[bucket + ".x1"] = half.reshape(2, 2, 2, 2, half.shape[0] // 16, 512)
        elif step in ("x1", "x2"):
            value[bucket + (".x2" if step == "x1" else ".zl")] = mine[0] + got
        elif step == "zl":
            value[bucket + ".zh"] = mine[:, 0] + got
        elif step == "zh":
            value[bucket] = sum_all(mine[0] + got)
            if bucket in ("m0", "g0"):
                value[bucket + ".ZH"] = value[bucket]
            elif "m1" in value and "g1" in value:
                value["b1.ZH"] = jnp.concatenate([value["m1"], value["g1"]], axis=0)
        elif step == "ZH":
            value[bucket + ".ZL"] = jnp.stack([mine, got])
        elif step == "ZL":
            value[bucket + ".X2"] = jnp.stack([mine, got], axis=1)
        elif step == "X2":
            value[bucket + ".X1"] = jnp.stack([mine, got])
        elif step == "X1":
            value[bucket + ".Core"] = jnp.stack([mine, got]).reshape(-1, 512)
        else:
            value[bucket] = (mine, got)

    for event in ORDER:
        if event in ("+fo", "+go"):
            flow.start(event[1:], field_swap if event == "+fo" else grad_swap)
        elif event in ("-fo", "-go"):
            value[event[1:]] = flow.end(event[1:])
        elif event[0] == "+":
            begin(event[1:])
        elif event[0] == "-":
            finish(event[1:])
        elif event == "K1":
            back = run_gn_back(1, crop, hidden, None, flow.tie(dmid_1), mvec_1, mix_1, p_1, br_1, w)
            dv_1, dvb, dbr_1, dp_1, dmg_1, dcp_1, gvec_1 = back
            flow.token = gvec_1
        elif event == "K2":
            value["g1.core"] = run_gn_weights(1, n1_1, dmg_1, gl_1, dbr_1, dp_1, flow.tie(gvec_1), cin_1, dcp_1)
            flow.token = value["g1.core"][0]
        elif event == "K3":
            dmid_0, mvec_0, *value["m0.core"] = run_mlp_back(crop, flow.tie(dvb), n2_0, act_0, slope_0, out_0, mid_0, w)
            flow.token = mvec_0
        elif event == "K4":
            back = run_gn_back(0, crop, images, dv_1, flow.tie(dmid_0), mvec_0, mix_0, p_0, br_0, w)
            dv_0, grad_swap, dbr_0, dp_0, dmg_0, dcp_0, gvec_0 = back
            flow.token = gvec_0
        elif event == "K5":
            value["g0.core"] = run_gn_weights(0, n1_0, dmg_0, gl_0, dbr_0, dp_0, flow.tie(gvec_0), cin_0, dcp_0)
            flow.token = value["g0.core"][0]
        elif event == "P1":
            flow.token = block_outputs = run_place(hidden, final, flow.tie(value["fo"]))
        elif event == "P2":
            flow.token = input_grads = run_place(dv_0, dv_1, flow.tie(value["go"]))
        elif event == "MF":
            own, got = value["m0"]
            wr, we = run_mlp_finish(((128, 0), (192, 0)), (flow.tie(own), got) + value["b1"])
            flow.token = wr
        elif event == "GF":
            own, got = value["g0"]
            grads = run_gn_finish(((64, 0), (192, 128)), (flow.tie(own), got) + value["b1"])
    (n1g, n1s, win, bin_, conv, cbias, w1, b1, w2, b2, w3, b3, wo, bo, bs, n2g, n2s, be, br, ms) = grads
    shape = (1, 2, 1, CANVAS, CANVAS, C)
    return (
        block_outputs.reshape(shape), input_grads.reshape(shape), n1g, n1s, win[None], bin_, conv.reshape(1, 49, 960), cbias,
        w1[None], b1, w2[None], b2, w3[None], b3, wo[None], bo, bs, n2g, n2s, we[None], be, wr[None], br, ms,
    )


def solution(mesh):
    count = mesh.shape["dp"]
    image = P(None, "dp", None, None, None)
    one, two = P("section", None), P("section", None, None)
    weights = (one, one, two, one, two, one, two, one, two, one, two, one, two, one, one, one, one, two, one, two,
               one, one)
    field = P("section", None, "dp", None, None, None)
    return jax.shard_map(
        lambda *arrays: on_device(Flow(count), *arrays),
        mesh=mesh,
        in_specs=(image, image, P(None, "dp")) + weights,
        out_specs=(field, field) + weights,
        check_vma=False,
    )
```

time: 253 us -> 227 us (0.90)
  Pallas kernels: 109 us -> 77.2 us
  waiting for transfers between devices: 82.6 us -> 93.8 us
  starting transfers between devices: 47.2 us -> 43.5 us
    pallas_call x15 -> x12, Pallas kernels: 109 us -> 77.2 us  [the longest x7 64.4 us: call(): pl.pallas_call(body, name=name, out_shape=shapes, in_specs=specs, out_spe...]
    ppermute x44, waiting for transfers between devices: 82.6 us -> 93.8 us  [exchange(): return lax.ppermute(x, AXES, pairs)]
    ppermute x44, starting transfers between devices: 47.2 us -> 43.5 us  [exchange(): return lax.ppermute(x, AXES, pairs)]
    unnamed x49 -> x75, local copies, waits for them, and re-layouts: 6.3 us -> 4.03 us
  transfers between devices with their start and end apart: 44 -> 44, of which waited for: 16 -> 24; matrix products, arithmetic and copies ran while one was open for 1% -> 3% of each run, Pallas kernels for 29% -> 22%
where the time goes in v3:
time: 227 us; the launch traced here: 225 us
  waiting for transfers between devices  93.8 us (41%)
  Pallas kernels  77.2 us (34%)
  starting transfers between devices  43.5 us (19%)
  local copies, waits for them, and re-layouts  4.86 us (2%)
  other arithmetic  3.81 us (2%)
    ppermute x44, waiting for transfers between devices, exchange(): return lax.ppermute(x, AXES, pairs)  93.8 us
    pallas_call x7, Pallas kernels, call(): pl.pallas_call(body, name=name, out_shape=shapes, in_specs=specs, out_spe...  64.4 us
    ppermute x44, starting transfers between devices, exchange(): return lax.ppermute(x, AXES, pairs)  43.5 us
    pallas_call x5, Pallas kernels, plain_call(): pl.pallas_call(kernel, name=name, out_shape=[shape for _, shape in outs],...  12.8 us
  transfers between devices with their start and end apart: 44, of which 24 were waited for; matrix products, arithmetic and copies ran while one was open for 3% of the time, Pallas kernels for 22%

profile of v3, /device:TPU:0, one launch (start us, length us, event | category | flops | bytes accessed | tf_op | source)
XLA Modules:
  0.0 224.9 jit_solution(8195175181870027099)
XLA Ops:
  1.3 2.1 pack.1
  4.4 1.5 collective-permute-done.refs_3_.refs_9_.refs_4_
  7.9 8.5 %gnconv_forward.1 = (bf16[256,512]{1,0:T(8,128)(2,1)}, f32[2816,128]{1,0:T(8,128)}, f32[256,1024]{1,0:T(8,128)}, f32[256,1024]{1,0:T(8,128)}, bf16[256,1024]{1,0...) custom-call(s32[2,1]{1,0:T(2,128)} %copy.50.refs_0_, bf16[2,256,512]{2,1,0:T(8,128)(2,1)} %bitcast.157, ...), custom_call_target="tpu_custom_call" | custom-call | tf_op jit(solution)/shard_map/gnconv_forward/pallas_call | solution.py:176
  16.4 16.7 %middle.1 = (bf16[256,512]{1,0:T(8,128)(2,1)}, bf16[256,512]{1,0:T(8,128)(2,1)}, bf16[256,2048]{1,0:T(8,128)(2,1)}, bf16[256,2048]{1,0:T(8,128)(2,1)}, bf16[256,...) custom-call(s32[2,1]{1,0:T(2,128)} %copy.50.refs_0_, ...), custom_call_target="tpu_custom_call" | custom-call | tf_op jit(solution)/shard_map/middle/pallas_call | solution.py:176
  33.6 9.6 %gnconv_backward.2 = (f32[256,512]{1,0:T(8,128)}, bf16[256,512]{1,0:T(8,128)(2,1)}, bf16[256,512]{1,0:T(8,128)(2,1)}, bf16[256,1024]{1,0:T(8,128)(2,1)}, bf16[25...) custom-call(s32[2,1]{1,0:T(2,128)} %copy.50.refs_0_, f32[256,512]{1,0:T(8,128)} %get-tuple-element.227.refs_1_, ...), custom_call_target="tpu_custom_call" | custom-call | tf_op jit(solution)/shard_map/gnconv_backward/pallas_call | solution.py:176
  43.2 7.8 %gnconv_weights.2 = (bf16[1024,512]{1,0:T(8,128)(2,1)}, bf16[1024,512]{1,0:T(8,128)(2,1)}) custom-call(bf16[256,512]{1,0:T(8,128)(2,1)} %get-tuple-element.235.refs_0_, bf16[256,1024]{1,0:T(8,128)(2,1)} %get-tuple-element.236.refs_1_, bf16[256,1024]{1,0:T(8,128)(2,1)} %get-tuple-element.237.refs_2_, bf16[256,512]{1,0:T(8,128)(2,1)} %get-tuple-element.238.refs_3_, ...), custom_call_target="tpu_custom_call" | custom-call | tf_op jit(solution)/shard_map/gnconv_weights/pallas_call | solution.py:176
  52.0 2.9 %collective-permute-start.8 = (bf16[2,2,2,128,512]{4,3,1,2,0:T(8,128)(2,1)S(1)}, bf16[2,2,2,128,512]{4,3,1,2,0:T(8,128)(2,1)S(1)}, u32[]{:S(2)}, u32[]{:S(2)}) collective-permute-start(bf16[2,2,2,128,512]{4,3,1,2,0:T(8,128)(2,1)S(1)} %copy.52), channel_id=1, source_target_pairs={{0,1},{1,0},{2,3},{3,2},{4,5},{5,4},{6,7},{7,6},{8,9},{9,8},{10,11... | collective-permute-start | bytes 3145736 | tf_op jit(solution)/shard_map/ppermute | solution.py:873
  55.0 7.9 %mlp_backward.1 = (f32[256,512]{1,0:T(8,128)}, f32[8,2048]{1,0:T(8,128)}, bf16[2048,512]{1,0:T(8,128)(2,1)}, bf16[2048,512]{1,0:T(8,128)(2,1)}) custom-call(s32[2,1]{1,0:T(2,128)} %copy.50.refs_0_, bf16[256,512]{1,0:T(8,128)(2,1)} %get-tuple-element.247.refs_1_, f32[16,2048]{1,0:T(8,128)} %get-tuple-element.213.refs_2_.refs_8_.refs_3_, ...), custom_call_target="tpu_custom_call" | custom-call | tf_op jit(solution)/shard_map/mlp_backward/pallas_call | solution.py:176
  63.2 4.5 %collective-permute-done.8 = bf16[2,2,2,128,512]{4,3,1,2,0:T(8,128)(2,1)S(1)} collective-permute-done((bf16[2,2,2,128,512]{4,3,1,2,0:T(8,128)(2,1)S(1)}, bf16[2,2,2,128,512]{4,3,1,2,0:T(8,128)(2,1)S(1)}, u32[]{:S(2)}, u32[]{:S(2)}) %collective-permute-start.8) | collective-permute-done | bytes 1048608 | tf_op jit(solution)/shard_map/ppermute | solution.py:873
  67.9 2.1 collective-permute-start.11
  70.2 1.6 collective-permute-start.10
  72.1 8.5 %gnconv_backward.3 = (f32[256,512]{1,0:T(8,128)S(1)}, f32[256,512]{1,0:T(8,128)S(1)}, bf16[256,512]{1,0:T(8,128)(2,1)S(1)}, bf16[256,1024]{1,0:T(8,128)(2,1)S(1)...) custom-call(s32[2,1]{1,0:T(2,128)S(1)} %copy-done.27, ...), custom_call_target="tpu_custom_call" | custom-call | tf_op jit(solution)/shard_map/gnconv_backward/pallas_call | solution.py:176
  81.3 1.4 collective-permute-done.10
  82.8 2.2 collective-permute-start.13
  85.0 1.7 collective-permute-start.12
  87.4 1.9 collective-permute-done.13
  89.5 1.7 collective-permute-start.16
  91.2 1.6 collective-permute-done.12
  92.8 1.6 collective-permute-start.17
  94.4 2.7 %collective-permute-start.15 = (bf16[128,512]{1,0:T(8,128)(2,1)S(1)}, bf16[128,512]{1,0:T(8,128)(2,1)S(1)}, u32[]{:S(2)}, u32[]{:S(2)}) collective-permute-start(bf16[128,512]{1,0:T(8,128)(2,1)S(1)} %slice_bitcast_fusion.18), channel_id=1, source_target_pairs={{0,8},{1,9},{2,10},{3,11},{4,12},{5,13},{6,14},{7,15},{8,0},{9,1},... | collective-permute-start | bytes 393224 | tf_op jit(solution)/shard_map/ppermute | solution.py:873
  97.1 2.2 collective-permute-done.17
  99.4 1.6 collective-permute-start.18
  101.0 5.4 %gnconv_weights.3 = (bf16[1024,512]{1,0:T(8,128)(2,1)S(1)}, bf16[1024,512]{1,0:T(8,128)(2,1)S(1)}) custom-call(bf16[256,512]{1,0:T(8,128)(2,1)S(1)} %copy-done.24, bf16[256,1024]{1,0:T(8,128)(2,1)S(1)} %get-tuple-element.283.refs_1_, bf16[256,1024]{1,0:T(8,128)(2,1)S(1)} %copy-done.21, bf16[256,512]{1,0:T(8,128)(2,1)S(1)} %get-tuple-element.285.refs_3_, ...), custom_call_target="tpu_custom_call" | custom-call | tf_op jit(solution)/shard_map/gnconv_weights/pallas_call | solution.py:176
  106.7 2.1 collective-permute-start.21
  108.9 1.5 collective-permute-start.19
  110.5 5.5 %collective-permute-done.21 = bf16[2,2,128,512]{3,2,0,1:T(8,128)(2,1)S(1)} collective-permute-done((bf16[2,2,128,512]{3,2,0,1:T(8,128)(2,1)S(1)}, bf16[2,2,128,512]{3,2,0,1:T(8,128)(2,1)S(1)}, u32[]{:S(2)}, u32[]{:S(2)}) %collective-permute-start.21) | collective-permute-done | bytes 524320 | tf_op jit(solution)/shard_map/ppermute | solution.py:873
  117.6 1.8 collective-permute-start.24
  119.9 7.0 %collective-permute-done.24 = bf16[2,128,512]{2,1,0:T(8,128)(2,1)S(1)} collective-permute-done((bf16[2,128,512]{2,1,0:T(8,128)(2,1)S(1)}, bf16[2,128,512]{2,1,0:T(8,128)(2,1)S(1)}, u32[]{:S(2)}, u32[]{:S(2)}) %collective-permute-start.24) | collective-permute-done | bytes 262176 | tf_op jit(solution)/shard_map/ppermute | solution.py:873
  126.9 8.2 %collective-permute-done.22 = bf16[2,192,512]{2,1,0:T(8,128)(2,1)S(1)} collective-permute-done((bf16[2,192,512]{2,1,0:T(8,128)(2,1)S(1)}, bf16[2,192,512]{2,1,0:T(8,128)(2,1)S(1)}, u32[]{:S(2)}, u32[]{:S(2)}) %collective-permute-start.22) | collective-permute-done | bytes 393248 | tf_op jit(solution)/shard_map/ppermute | solution.py:873
  138.6 3.1 %collective-permute-done.27 = bf16[2,2,64,512]{3,2,0,1:T(8,128)(2,1)S(1)} collective-permute-done((bf16[2,2,64,512]{3,2,0,1:T(8,128)(2,1)S(1)}, bf16[2,2,64,512]{3,2,0,1:T(8,128)(2,1)S(1)}, u32[]{:S(2)}, u32[]{:S(2)}) %collective-permute-start.27) | collective-permute-done | bytes 262176 | tf_op jit(solution)/shard_map/ppermute | solution.py:873
  141.7 5.0 %collective-permute-done.26 = bf16[128,512]{1,0:T(8,128)(2,1)S(1)} collective-permute-done((bf16[128,512]{1,0:T(8,128)(2,1)S(1)}, bf16[128,512]{1,0:T(8,128)(2,1)S(1)}, u32[]{:S(2)}, u32[]{:S(2)}) %collective-permute-start.26) | collective-permute-done | bytes 131104 | tf_op jit(solution)/shard_map/ppermute | solution.py:873
  146.8 3.3 %collective-permute-done.25 = bf16[2,2,192,512]{3,2,1,0:T(8,128)(2,1)S(1)} collective-permute-done((bf16[2,2,192,512]{3,2,1,0:T(8,128)(2,1)S(1)}, bf16[2,2,192,512]{3,2,1,0:T(8,128)(2,1)S(1)}, u32[]{:S(2)}, u32[]{:S(2)}) %collective-permute-start.25) | collective-permute-done | bytes 786464 | tf_op jit(solution)/shard_map/ppermute | solution.py:873
  151.9 7.8 %collective-permute-done.30 = bf16[128,512]{1,0:T(8,128)(2,1)S(1)} collective-permute-done((bf16[128,512]{1,0:T(8,128)(2,1)S(1)}, bf16[128,512]{1,0:T(8,128)(2,1)S(1)}, u32[]{:S(2)}, u32[]{:S(2)}) %collective-permute-start.30) | collective-permute-done | bytes 131104 | tf_op jit(solution)/shard_map/ppermute | solution.py:873
  159.9 2.0 collective-permute-start.33
  163.0 3.6 %collective-permute-done.33 = bf16[64,512]{1,0:T(8,128)(2,1)S(1)} collective-permute-done((bf16[64,512]{1,0:T(8,128)(2,1)S(1)}, bf16[64,512]{1,0:T(8,128)(2,1)S(1)}, u32[]{:S(2)}, u32[]{:S(2)}) %collective-permute-start.33) | collective-permute-done | bytes 65568 | tf_op jit(solution)/shard_map/ppermute | solution.py:873
  166.5 2.2 collective-permute-done.32
  170.9 4.7 %collective-permute-done.35 = bf16[64,512]{1,0:T(8,128)(2,1)S(1)} collective-permute-done((bf16[64,512]{1,0:T(8,128)(2,1)S(1)}, bf16[64,512]{1,0:T(8,128)(2,1)S(1)}, u32[]{:S(2)}, u32[]{:S(2)}) %collective-permute-start.35) | collective-permute-done | bytes 65568 | tf_op jit(solution)/shard_map/ppermute | solution.py:873
  176.1 4.5 %collective-permute-done.36 = bf16[2,64,512]{2,1,0:T(8,128)(2,1)S(1)} collective-permute-done((bf16[2,64,512]{2,1,0:T(8,128)(2,1)S(1)}, bf16[2,64,512]{2,1,0:T(8,128)(2,1)S(1)}, u32[]{:S(2)}, u32[]{:S(2)}) %collective-permute-start.36) | collective-permute-done | bytes 131104 | tf_op jit(solution)/shard_map/ppermute | solution.py:873
  180.7 1.4 collective-permute-start.38
  184.3 2.9 %collective-permute-done.38 = bf16[2,2,64,512]{3,2,1,0:T(8,128)(2,1)S(1)} collective-permute-done((bf16[2,2,64,512]{3,2,1,0:T(8,128)(2,1)S(1)}, bf16[2,2,64,512]{3,2,1,0:T(8,128)(2,1)S(1)}, u32[]{:S(2)}, u32[]{:S(2)}) %collective-permute-start.38) | collective-permute-done | bytes 262176 | tf_op jit(solution)/shard_map/ppermute | solution.py:873
  187.2 1.7 collective-permute-start.41
  189.4 4.6 %collective-permute-done.41.refs_3_ = bf16[3072,512]{1,0:T(8,128)(2,1)S(1)} collective-permute-done((bf16[3072,512]{1,0:T(8,128)(2,1)S(1)}, bf16[3072,512]{1,0:T(8,128)(2,1)S(1)}, u32[]{:S(2)}, u32[]{:S(2)}) %collective-permute-start.41) | collective-permute-done | bytes 3145760 | tf_op jit(solution)/shard_map/ppermute | solution.py:873
  194.0 1.6 copy-done.29
  195.6 8.3 %collective-permute-done.40 = bf16[2,2,2,128,512]{4,3,2,1,0:T(8,128)(2,1)S(1)} collective-permute-done((bf16[2,2,2,128,512]{4,3,2,1,0:T(8,128)(2,1)S(1)}, bf16[2,2,2,128,512]{4,3,2,1,0:T(8,128)(2,1)S(1)}, u32[]{:S(2)}, u32[]{:S(2)}) %collective-permute-start.40) | collective-permute-done | bytes 1048608 | tf_op jit(solution)/shard_map/ppermute | solution.py:873
  205.9 4.3 %collective-permute-done.42.refs_1_ = bf16[2048,512]{1,0:T(8,128)(2,1)S(1)} collective-permute-done((bf16[2048,512]{1,0:T(8,128)(2,1)S(1)}, bf16[2048,512]{1,0:T(8,128)(2,1)S(1)}, u32[]{:S(2)}, u32[]{:S(2)}) %collective-permute-start.42) | collective-permute-done | bytes 2097184 | tf_op jit(solution)/shard_map/ppermute | solution.py:873
  210.2 4.6 %collective-permute-done.39 = bf16[2,2,2,64,512]{4,3,2,1,0:T(8,128)(2,1)S(1)} collective-permute-done((bf16[2,2,2,64,512]{4,3,2,1,0:T(8,128)(2,1)S(1)}, bf16[2,2,2,64,512]{4,3,2,1,0:T(8,128)(2,1)S(1)}, u32[]{:S(2)}, u32[]{:S(2)}) %collective-permute-start.39) | collective-permute-done | bytes 524320 | tf_op jit(solution)/shard_map/ppermute | solution.py:873
  216.2 4.6 %mlp_finish.1 = (f32[2048,512]{1,0:T(8,128)}, f32[512,2048]{1,0:T(8,128)}) custom-call(bf16[2048,512]{1,0:T(8,128)(2,1)} %bitcast.171, bf16[2048,512]{1,0:T(8,128)(2,1)} %copy-done.34, bf16[3072,512]{1,0:T(8,128)(2,1)} %bitcast.160, bf16[3072,512]{1,0:T(8,128)(2,1)} %copy-done.29), custom_call_target="tpu_custom_call" | custom-call | tf_op jit(solution)/shard_map/mlp_finish/pallas_call | solution.py:740
  220.9 3.9 %gn_finish.1 = (f32[1,512]{1,0:T(1,128)}, f32[1,512]{1,0:T(1,128)}, f32[512,1024]{1,0:T(8,128)}, f32[1,1024]{1,0:T(1,128)}, f32[49,1,960]{2,1,0:T(1,128)}, /*ind...) custom-call(bf16[1024,512]{1,0:T(8,128)(2,1)} %bitcast.177, ...), custom_call_target="tpu_custom_call" | custom-call | tf_op jit(solution)/shard_map/gn_finish/pallas_call | solution.py:740
  (180 shorter events, 25.1 us)
Async XLA Ops:
  0.7 5.3 %collective-permute-start.1 = (bf16[512,1024]{1,0:T(8,128)(2,1)}, bf16[512,1024]{1,0:T(8,128)(2,1)S(1)}, u32[]{:S(2)}, u32[]{:S(2)}) collective-permute-start(bf16[512,1024]{1,0:T(8,128)(2,1)} %bitcast.147), channel_id=1, source_target_pairs={{0,16},{1,17},{2,18},{3,19},{4,20},{5,21},{6,22},{7,23},{8,24},{9,... | collective-permute-start | bytes 3145736 | tf_op jit(solution)/shard_map/ppermute | solution.py:873
  1.2 4.7 %collective-permute-start.4 = (bf16[512,512]{1,0:T(8,128)(2,1)}, bf16[512,512]{1,0:T(8,128)(2,1)S(1)}, u32[]{:S(2)}, u32[]{:S(2)}) collective-permute-start(bf16[512,512]{1,0:T(8,128)(2,1)} %bitcast.152), channel_id=1, source_target_pairs={{0,16},{1,17},{2,18},{3,19},{4,20},{5,21},{6,22},{7,23},{8,24},{9,... | collective-permute-start | bytes 1572872 | tf_op jit(solution)/shard_map/ppermute | solution.py:873
  3.4 2.5 %collective-permute-start.3 = (bf16[384,512]{1,0:T(8,128)(2,1)}, bf16[384,512]{1,0:T(8,128)(2,1)S(1)}, u32[]{:S(2)}, u32[]{:S(2)}) collective-permute-start(bf16[384,512]{1,0:T(8,128)(2,1)} %get-tuple-element.215.refs_8_.refs_14_.refs_9_), channel_id=1, source_target_pairs={{0,16},{1,17},{2,18},{3,19},{4,20},{5,21},{6,22},{7,23},{8,24},{9,... | collective-permute-start | bytes 1179656 | tf_op jit(solution)/shard_map/ppermute | solution.py:873
  3.8 2.0 collective-permute-start.2
  3.9 2.0 collective-permute-start
  6.0 10.5 %collective-permute-start.5 = (bf16[512,2048]{1,0:T(8,128)(2,1)}, bf16[512,2048]{1,0:T(8,128)(2,1)}, u32[]{:S(2)}, u32[]{:S(2)}) collective-permute-start(bf16[512,2048]{1,0:T(8,128)(2,1)} %bitcast.162), channel_id=1, source_target_pairs={{0,16},{1,17},{2,18},{3,19},{4,20},{5,21},{6,22},{7,23},{8,24},{9,... | collective-permute-start | bytes 6291464 | tf_op jit(solution)/shard_map/ppermute | solution.py:873
  6.4 10.0 %collective-permute-start.6 = (bf16[2048,512]{1,0:T(8,128)(2,1)}, bf16[2048,512]{1,0:T(8,128)(2,1)}, u32[]{:S(2)}, u32[]{:S(2)}) collective-permute-start(bf16[2048,512]{1,0:T(8,128)(2,1)} %bitcast.166), channel_id=1, source_target_pairs={{0,16},{1,17},{2,18},{3,19},{4,20},{5,21},{6,22},{7,23},{8,24},{9,... | collective-permute-start | bytes 6291464 | tf_op jit(solution)/shard_map/ppermute | solution.py:873
  33.1 10.0 %collective-permute-start.7 = (bf16[2048,512]{1,0:T(8,128)(2,1)}, bf16[2048,512]{1,0:T(8,128)(2,1)S(1)}, u32[]{:S(2)}, u32[]{:S(2)}) collective-permute-start(bf16[2048,512]{1,0:T(8,128)(2,1)} %get-tuple-element.225), channel_id=1, source_target_pairs={{0,16},{1,17},{2,18},{3,19},{4,20},{5,21},{6,22},{7,23},{8,24},{9,... | collective-permute-start | bytes 6291464 | tf_op jit(solution)/shard_map/ppermute | solution.py:873
  51.0 11.8 %collective-permute-start.9 = (bf16[1024,512]{1,0:T(8,128)(2,1)}, bf16[1024,512]{1,0:T(8,128)(2,1)S(1)}, u32[]{:S(2)}, u32[]{:S(2)}) collective-permute-start(bf16[1024,512]{1,0:T(8,128)(2,1)} %get-tuple-element.245), channel_id=1, source_target_pairs={{0,16},{1,17},{2,18},{3,19},{4,20},{5,21},{6,22},{7,23},{8,24},{9,... | collective-permute-start | bytes 3145736 | tf_op jit(solution)/shard_map/ppermute | solution.py:873
  52.0 15.7 %collective-permute-start.8 = (bf16[2,2,2,128,512]{4,3,1,2,0:T(8,128)(2,1)S(1)}, bf16[2,2,2,128,512]{4,3,1,2,0:T(8,128)(2,1)S(1)}, u32[]{:S(2)}, u32[]{:S(2)}) collective-permute-start(bf16[2,2,2,128,512]{4,3,1,2,0:T(8,128)(2,1)S(1)} %copy.52), channel_id=1, source_target_pairs={{0,1},{1,0},{2,3},{3,2},{4,5},{5,4},{6,7},{7,6},{8,9},{9,8},{10,11... | collective-permute-start | bytes 3145736 | tf_op jit(solution)/shard_map/ppermute | solution.py:873
  67.7 18.9 %collective-permute-start.14 = (bf16[2048,512]{1,0:T(8,128)(2,1)}, bf16[2048,512]{1,0:T(8,128)(2,1)S(1)}, u32[]{:S(2)}, u32[]{:S(2)}) collective-permute-start(bf16[2048,512]{1,0:T(8,128)(2,1)} %get-tuple-element.273), channel_id=1, source_target_pairs={{0,16},{1,17},{2,18},{3,19},{4,20},{5,21},{6,22},{7,23},{8,24},{9,... | collective-permute-start | bytes 6291464 | tf_op jit(solution)/shard_map/ppermute | solution.py:873
  67.9 13.3 %collective-permute-start.11 = (bf16[2,2,2,64,512]{4,3,1,2,0:T(8,128)(2,1)S(1)}, bf16[2,2,2,64,512]{4,3,1,2,0:T(8,128)(2,1)S(1)}, u32[]{:S(2)}, u32[]{:S(2)}) collective-permute-start(bf16[2,2,2,64,512]{4,3,1,2,0:T(8,128)(2,1)S(1)} %copy.55), channel_id=1, source_target_pairs={{0,1},{1,0},{2,3},{3,2},{4,5},{5,4},{6,7},{7,6},{8,9},{9,8},{10,11... | collective-permute-start | bytes 1572872 | tf_op jit(solution)/shard_map/ppermute | solution.py:873
  70.2 12.4 %collective-permute-start.10 = (bf16[2,2,128,512]{3,2,0,1:T(8,128)(2,1)S(1)}, bf16[2,2,128,512]{3,2,0,1:T(8,128)(2,1)S(1)}, u32[]{:S(2)}, u32[]{:S(2)}) collective-permute-start(bf16[2,2,128,512]{3,2,0,1:T(8,128)(2,1)S(1)} %slice_bitcast_fusion.2), channel_id=1, source_target_pairs={{0,2},{1,3},{2,0},{3,1},{4,6},{5,7},{6,4},{7,5},{8,10},{9,11},{10,... | collective-permute-start | bytes 1572872 | tf_op jit(solution)/shard_map/ppermute | solution.py:873
  82.8 6.5 %collective-permute-start.13 = (bf16[2,2,64,512]{3,2,0,1:T(8,128)(2,1)S(1)}, bf16[2,2,64,512]{3,2,0,1:T(8,128)(2,1)S(1)}, u32[]{:S(2)}, u32[]{:S(2)}) collective-permute-start(bf16[2,2,64,512]{3,2,0,1:T(8,128)(2,1)S(1)} %slice_bitcast_fusion.9), channel_id=1, source_target_pairs={{0,2},{1,3},{2,0},{3,1},{4,6},{5,7},{6,4},{7,5},{8,10},{9,11},{10,... | collective-permute-start | bytes 786440 | tf_op jit(solution)/shard_map/ppermute | solution.py:873
  85.0 7.8 %collective-permute-start.12 = (bf16[2,128,512]{2,1,0:T(8,128)(2,1)S(1)}, bf16[2,128,512]{2,1,0:T(8,128)(2,1)S(1)}, u32[]{:S(2)}, u32[]{:S(2)}) collective-permute-start(bf16[2,128,512]{2,1,0:T(8,128)(2,1)S(1)} %slice_bitcast_fusion.10), channel_id=1, source_target_pairs={{0,4},{1,5},{2,6},{3,7},{4,0},{5,1},{6,2},{7,3},{8,12},{9,13},{10,... | collective-permute-start | bytes 786440 | tf_op jit(solution)/shard_map/ppermute | solution.py:873
  89.3 11.6 %copy-start.17 = (f32[2816,128]{1,0:T(8,128)S(1)}, f32[2816,128]{1,0:T(8,128)}, u32[]{:S(2)}) copy-start(f32[2816,128]{1,0:T(8,128)} %get-tuple-element.291.refs_6_) | copy-start | bytes 4325380
  89.4 11.6 %copy-start.21 = (bf16[256,1024]{1,0:T(8,128)(2,1)S(1)}, bf16[256,1024]{1,0:T(8,128)(2,1)}, u32[]{:S(2)}) copy-start(bf16[256,1024]{1,0:T(8,128)(2,1)} %get-tuple-element.284.refs_2_) | copy-start | bytes 1572868
  89.5 16.9 %collective-permute-start.16 = (bf16[2,2,2,128,512]{4,3,1,2,0:T(8,128)(2,1)S(1)}, bf16[2,2,2,128,512]{4,3,1,2,0:T(8,128)(2,1)S(1)}, u32[]{:S(2)}, u32[]{:S(2)}) collective-permute-start(bf16[2,2,2,128,512]{4,3,1,2,0:T(8,128)(2,1)S(1)} %copy.58), channel_id=1, source_target_pairs={{0,1},{1,0},{2,3},{3,2},{4,5},{5,4},{6,7},{7,6},{8,9},{9,8},{10,11... | collective-permute-start | bytes 3145736 | tf_op jit(solution)/shard_map/ppermute | solution.py:873
  92.8 6.5 %collective-permute-start.17 = (bf16[2,64,512]{2,1,0:T(8,128)(2,1)S(1)}, bf16[2,64,512]{2,1,0:T(8,128)(2,1)S(1)}, u32[]{:S(2)}, u32[]{:S(2)}) collective-permute-start(bf16[2,64,512]{2,1,0:T(8,128)(2,1)S(1)} %slice_bitcast_fusion.17), channel_id=1, source_target_pairs={{0,4},{1,5},{2,6},{3,7},{4,0},{5,1},{6,2},{7,3},{8,12},{9,13},{10,... | collective-permute-start | bytes 393224 | tf_op jit(solution)/shard_map/ppermute | solution.py:873
  94.4 12.0 %collective-permute-start.15 = (bf16[128,512]{1,0:T(8,128)(2,1)S(1)}, bf16[128,512]{1,0:T(8,128)(2,1)S(1)}, u32[]{:S(2)}, u32[]{:S(2)}) collective-permute-start(bf16[128,512]{1,0:T(8,128)(2,1)S(1)} %slice_bitcast_fusion.18), channel_id=1, source_target_pairs={{0,8},{1,9},{2,10},{3,11},{4,12},{5,13},{6,14},{7,15},{8,0},{9,1},... | collective-permute-start | bytes 393224 | tf_op jit(solution)/shard_map/ppermute | solution.py:873
  99.4 7.1 %collective-permute-start.18 = (bf16[64,512]{1,0:T(8,128)(2,1)S(1)}, bf16[64,512]{1,0:T(8,128)(2,1)S(1)}, u32[]{:S(2)}, u32[]{:S(2)}) collective-permute-start(bf16[64,512]{1,0:T(8,128)(2,1)S(1)} %slice_bitcast_fusion.22), channel_id=1, source_target_pairs={{0,8},{1,9},{2,10},{3,11},{4,12},{5,13},{6,14},{7,15},{8,0},{9,1},... | collective-permute-start | bytes 196616 | tf_op jit(solution)/shard_map/ppermute | solution.py:873
  106.4 9.6 %collective-permute-start.20 = (bf16[1024,512]{1,0:T(8,128)(2,1)S(1)}, bf16[1024,512]{1,0:T(8,128)(2,1)S(1)}, u32[]{:S(2)}, u32[]{:S(2)}) collective-permute-start(bf16[1024,512]{1,0:T(8,128)(2,1)S(1)} %get-tuple-element.303), channel_id=1, source_target_pairs={{0,16},{1,17},{2,18},{3,19},{4,20},{5,21},{6,22},{7,23},{8,24},{9,... | collective-permute-start | bytes 3145736 | tf_op jit(solution)/shard_map/ppermute | solution.py:873
  106.7 9.3 %collective-permute-start.21 = (bf16[2,2,128,512]{3,2,0,1:T(8,128)(2,1)S(1)}, bf16[2,2,128,512]{3,2,0,1:T(8,128)(2,1)S(1)}, u32[]{:S(2)}, u32[]{:S(2)}) collective-permute-start(bf16[2,2,128,512]{3,2,0,1:T(8,128)(2,1)S(1)} %slice_bitcast_fusion.1), channel_id=1, source_target_pairs={{0,2},{1,3},{2,0},{3,1},{4,6},{5,7},{6,4},{7,5},{8,10},{9,11},{10,... | collective-permute-start | bytes 1572872 | tf_op jit(solution)/shard_map/ppermute | solution.py:873
  108.9 10.8 %collective-permute-start.19 = (bf16[192,512]{1,0:T(8,128)(2,1)S(1)}, bf16[192,512]{1,0:T(8,128)(2,1)S(1)}, u32[]{:S(2)}, u32[]{:S(2)}) collective-permute-start(bf16[192,512]{1,0:T(8,128)(2,1)S(1)} %get-tuple-element.301), channel_id=1, source_target_pairs={{0,8},{1,9},{2,10},{3,11},{4,12},{5,13},{6,14},{7,15},{8,0},{9,1},... | collective-permute-start | bytes 589832 | tf_op jit(solution)/shard_map/ppermute | solution.py:873
  116.5 10.4 %collective-permute-start.23 = (bf16[2,2,2,64,512]{4,3,1,2,0:T(8,128)(2,1)S(1)}, bf16[2,2,2,64,512]{4,3,1,2,0:T(8,128)(2,1)S(1)}, u32[]{:S(2)}, u32[]{:S(2)}) collective-permute-start(bf16[2,2,2,64,512]{4,3,1,2,0:T(8,128)(2,1)S(1)} %copy.60), channel_id=1, source_target_pairs={{0,1},{1,0},{2,3},{3,2},{4,5},{5,4},{6,7},{7,6},{8,9},{9,8},{10,11... | collective-permute-start | bytes 1572872 | tf_op jit(solution)/shard_map/ppermute | solution.py:873
  117.6 9.3 %collective-permute-start.24 = (bf16[2,128,512]{2,1,0:T(8,128)(2,1)S(1)}, bf16[2,128,512]{2,1,0:T(8,128)(2,1)S(1)}, u32[]{:S(2)}, u32[]{:S(2)}) collective-permute-start(bf16[2,128,512]{2,1,0:T(8,128)(2,1)S(1)} %slice_bitcast_fusion.7), channel_id=1, source_target_pairs={{0,4},{1,5},{2,6},{3,7},{4,0},{5,1},{6,2},{7,3},{8,12},{9,13},{10,... | collective-permute-start | bytes 786440 | tf_op jit(solution)/shard_map/ppermute | solution.py:873
  119.8 15.4 %collective-permute-start.22 = (bf16[2,192,512]{2,1,0:T(8,128)(2,1)S(1)}, bf16[2,192,512]{2,1,0:T(8,128)(2,1)S(1)}, u32[]{:S(2)}, u32[]{:S(2)}) collective-permute-start(bf16[2,192,512]{2,1,0:T(8,128)(2,1)S(1)} %get-tuple-element.310), channel_id=1, source_target_pairs={{0,4},{1,5},{2,6},{3,7},{4,0},{5,1},{6,2},{7,3},{8,12},{9,13},{10,... | collective-permute-start | bytes 1179656 | tf_op jit(solution)/shard_map/ppermute | solution.py:873
  135.1 3.4 %collective-permute-start.28 = (f32[256,512]{1,0:T(8,128)S(1)}, f32[256,512]{1,0:T(8,128)S(1)}, u32[]{:S(2)}, u32[]{:S(2)}) collective-permute-start(f32[256,512]{1,0:T(8,128)S(1)} %get-tuple-element.325), channel_id=1, source_target_pairs={{0,16},{1,17},{2,18},{3,19},{4,20},{5,21},{6,22},{7,23},{8,24},{9,... | collective-permute-start | bytes 1572872 | tf_op jit(solution)/shard_map/ppermute | solution.py:873
  135.2 6.4 %collective-permute-start.27 = (bf16[2,2,64,512]{3,2,0,1:T(8,128)(2,1)S(1)}, bf16[2,2,64,512]{3,2,0,1:T(8,128)(2,1)S(1)}, u32[]{:S(2)}, u32[]{:S(2)}) collective-permute-start(bf16[2,2,64,512]{3,2,0,1:T(8,128)(2,1)S(1)} %slice_bitcast_fusion.5), channel_id=1, source_target_pairs={{0,2},{1,3},{2,0},{3,1},{4,6},{5,7},{6,4},{7,5},{8,10},{9,11},{10,... | collective-permute-start | bytes 786440 | tf_op jit(solution)/shard_map/ppermute | solution.py:873
  136.2 13.9 %collective-permute-start.25 = (bf16[2,2,192,512]{3,2,1,0:T(8,128)(2,1)S(1)}, bf16[2,2,192,512]{3,2,1,0:T(8,128)(2,1)S(1)}, u32[]{:S(2)}, u32[]{:S(2)}) collective-permute-start(bf16[2,2,192,512]{3,2,1,0:T(8,128)(2,1)S(1)} %get-tuple-element.319), channel_id=1, source_target_pairs={{0,2},{1,3},{2,0},{3,1},{4,6},{5,7},{6,4},{7,5},{8,10},{9,11},{10,... | collective-permute-start | bytes 2359304 | tf_op jit(solution)/shard_map/ppermute | solution.py:873
  137.5 9.1 %collective-permute-start.26 = (bf16[128,512]{1,0:T(8,128)(2,1)S(1)}, bf16[128,512]{1,0:T(8,128)(2,1)S(1)}, u32[]{:S(2)}, u32[]{:S(2)}) collective-permute-start(bf16[128,512]{1,0:T(8,128)(2,1)S(1)} %slice_bitcast_fusion.15), channel_id=1, source_target_pairs={{0,8},{1,9},{2,10},{3,11},{4,12},{5,13},{6,14},{7,15},{8,0},{9,1},... | collective-permute-start | bytes 393224 | tf_op jit(solution)/shard_map/ppermute | solution.py:873
  146.7 5.2 %collective-permute-start.31 = (bf16[2,64,512]{2,1,0:T(8,128)(2,1)S(1)}, bf16[2,64,512]{2,1,0:T(8,128)(2,1)S(1)}, u32[]{:S(2)}, u32[]{:S(2)}) collective-permute-start(bf16[2,64,512]{2,1,0:T(8,128)(2,1)S(1)} %slice_bitcast_fusion.13), channel_id=1, source_target_pairs={{0,4},{1,5},{2,6},{3,7},{4,0},{5,1},{6,2},{7,3},{8,12},{9,13},{10,... | collective-permute-start | bytes 393224 | tf_op jit(solution)/shard_map/ppermute | solution.py:873
  150.3 30.3 %collective-permute-start.29 = (bf16[2,2,2,192,512]{4,3,2,1,0:T(8,128)(2,1)S(1)}, bf16[2,2,2,192,512]{4,3,2,1,0:T(8,128)(2,1)S(1)}, u32[]{:S(2)}, u32[]{:S(2)}) collective-permute-start(bf16[2,2,2,192,512]{4,3,2,1,0:T(8,128)(2,1)S(1)} %get-tuple-element.331), channel_id=1, source_target_pairs={{0,1},{1,0},{2,3},{3,2},{4,5},{5,4},{6,7},{7,6},{8,9},{9,8},{10,11... | collective-permute-start | bytes 4718600 | tf_op jit(solution)/shard_map/ppermute | solution.py:873
  150.9 8.8 %collective-permute-start.30 = (bf16[128,512]{1,0:T(8,128)(2,1)S(1)}, bf16[128,512]{1,0:T(8,128)(2,1)S(1)}, u32[]{:S(2)}, u32[]{:S(2)}) collective-permute-start(bf16[128,512]{1,0:T(8,128)(2,1)S(1)} %fusion.7), channel_id=1, source_target_pairs={{0,8},{1,9},{2,10},{3,11},{4,12},{5,13},{6,14},{7,15},{8,0},{9,1},... | collective-permute-start | bytes 393224 | tf_op jit(solution)/shard_map/ppermute | solution.py:873
  159.8 8.9 %collective-permute-start.32 = (bf16[2,128,512]{2,1,0:T(8,128)(2,1)S(1)}, bf16[2,128,512]{2,1,0:T(8,128)(2,1)S(1)}, u32[]{:S(2)}, u32[]{:S(2)}) collective-permute-start(bf16[2,128,512]{2,1,0:T(8,128)(2,1)S(1)} %get-tuple-element.339), channel_id=1, source_target_pairs={{0,4},{1,5},{2,6},{3,7},{4,0},{5,1},{6,2},{7,3},{8,12},{9,13},{10,... | collective-permute-start | bytes 786440 | tf_op jit(solution)/shard_map/ppermute | solution.py:873
  159.9 6.6 %collective-permute-start.33 = (bf16[64,512]{1,0:T(8,128)(2,1)S(1)}, bf16[64,512]{1,0:T(8,128)(2,1)S(1)}, u32[]{:S(2)}, u32[]{:S(2)}) collective-permute-start(bf16[64,512]{1,0:T(8,128)(2,1)S(1)} %slice_bitcast_fusion.21), channel_id=1, source_target_pairs={{0,8},{1,9},{2,10},{3,11},{4,12},{5,13},{6,14},{7,15},{8,0},{9,1},... | collective-permute-start | bytes 196616 | tf_op jit(solution)/shard_map/ppermute | solution.py:873
  161.9 18.7 %copy-start.36 = (bf16[256,512]{1,0:T(8,128)(2,1)S(1)}, bf16[256,512]{1,0:T(8,128)(2,1)}, u32[]{:S(2)}) copy-start(bf16[256,512]{1,0:T(8,128)(2,1)} %get-tuple-element.357) | copy-start | bytes 786436
  168.8 11.8 %collective-permute-start.34 = (bf16[2,2,128,512]{3,2,1,0:T(8,128)(2,1)S(1)}, bf16[2,2,128,512]{3,2,1,0:T(8,128)(2,1)S(1)}, u32[]{:S(2)}, u32[]{:S(2)}) collective-permute-start(bf16[2,2,128,512]{3,2,1,0:T(8,128)(2,1)S(1)} %get-tuple-element.348), channel_id=1, source_target_pairs={{0,2},{1,3},{2,0},{3,1},{4,6},{5,7},{6,4},{7,5},{8,10},{9,11},{10,... | collective-permute-start | bytes 1572872 | tf_op jit(solution)/shard_map/ppermute | solution.py:873
  169.6 5.9 %collective-permute-start.35 = (bf16[64,512]{1,0:T(8,128)(2,1)S(1)}, bf16[64,512]{1,0:T(8,128)(2,1)S(1)}, u32[]{:S(2)}, u32[]{:S(2)}) collective-permute-start(bf16[64,512]{1,0:T(8,128)(2,1)S(1)} %fusion.10), channel_id=1, source_target_pairs={{0,8},{1,9},{2,10},{3,11},{4,12},{5,13},{6,14},{7,15},{8,0},{9,1},... | collective-permute-start | bytes 196616 | tf_op jit(solution)/shard_map/ppermute | solution.py:873
  175.6 5.0 %collective-permute-start.36 = (bf16[2,64,512]{2,1,0:T(8,128)(2,1)S(1)}, bf16[2,64,512]{2,1,0:T(8,128)(2,1)S(1)}, u32[]{:S(2)}, u32[]{:S(2)}) collective-permute-start(bf16[2,64,512]{2,1,0:T(8,128)(2,1)S(1)} %get-tuple-element.353), channel_id=1, source_target_pairs={{0,4},{1,5},{2,6},{3,7},{4,0},{5,1},{6,2},{7,3},{8,12},{9,13},{10,... | collective-permute-start | bytes 393224 | tf_op jit(solution)/shard_map/ppermute | solution.py:873
  180.6 1.9 collective-permute-start.37
  180.7 6.4 %collective-permute-start.38 = (bf16[2,2,64,512]{3,2,1,0:T(8,128)(2,1)S(1)}, bf16[2,2,64,512]{3,2,1,0:T(8,128)(2,1)S(1)}, u32[]{:S(2)}, u32[]{:S(2)}) collective-permute-start(bf16[2,2,64,512]{3,2,1,0:T(8,128)(2,1)S(1)} %get-tuple-element.360), channel_id=1, source_target_pairs={{0,2},{1,3},{2,0},{3,1},{4,6},{5,7},{6,4},{7,5},{8,10},{9,11},{10,... | collective-permute-start | bytes 786440 | tf_op jit(solution)/shard_map/ppermute | solution.py:873
  187.2 6.8 %collective-permute-start.41 = (bf16[3072,512]{1,0:T(8,128)(2,1)S(1)}, bf16[3072,512]{1,0:T(8,128)(2,1)S(1)}, u32[]{:S(2)}, u32[]{:S(2)}) collective-permute-start(bf16[3072,512]{1,0:T(8,128)(2,1)S(1)} %bitcast.159), channel_id=1, source_target_pairs={{0,16},{1,17},{2,18},{3,19},{4,20},{5,21},{6,22},{7,23},{8,24},{9,... | collective-permute-start | bytes 9437192 | tf_op jit(solution)/shard_map/ppermute | solution.py:873
  189.1 14.9 %collective-permute-start.40 = (bf16[2,2,2,128,512]{4,3,2,1,0:T(8,128)(2,1)S(1)}, bf16[2,2,2,128,512]{4,3,2,1,0:T(8,128)(2,1)S(1)}, u32[]{:S(2)}, u32[]{:S(2)}) collective-permute-start(bf16[2,2,2,128,512]{4,3,2,1,0:T(8,128)(2,1)S(1)} %get-tuple-element.365), channel_id=1, source_target_pairs={{0,1},{1,0},{2,3},{3,2},{4,5},{5,4},{6,7},{7,6},{8,9},{9,8},{10,11... | collective-permute-start | bytes 3145736 | tf_op jit(solution)/shard_map/ppermute | solution.py:873
  204.1 12.1 %copy-start.30 = (bf16[2,2,2,2,128,512]{5,4,3,2,1,0:T(8,128)(2,1)}, bf16[2,2,2,2,128,512]{5,4,3,2,1,0:T(8,128)(2,1)S(1)}, u32[]{:S(2)}) copy-start(bf16[2,2,2,2,128,512]{5,4,3,2,1,0:T(8,128)(2,1)S(1)} %pad_maximum_fusion.1) | copy-start | bytes 6291460
  204.1 6.1 %collective-permute-start.42 = (bf16[2048,512]{1,0:T(8,128)(2,1)S(1)}, bf16[2048,512]{1,0:T(8,128)(2,1)S(1)}, u32[]{:S(2)}, u32[]{:S(2)}) collective-permute-start(bf16[2048,512]{1,0:T(8,128)(2,1)S(1)} %bitcast.170), channel_id=1, source_target_pairs={{16,0},{17,1},{18,2},{19,3},{20,4},{21,5},{22,6},{23,7},{24,8},{25... | collective-permute-start | bytes 6291464 | tf_op jit(solution)/shard_map/ppermute | solution.py:873
  205.5 9.2 %collective-permute-start.39 = (bf16[2,2,2,64,512]{4,3,2,1,0:T(8,128)(2,1)S(1)}, bf16[2,2,2,64,512]{4,3,2,1,0:T(8,128)(2,1)S(1)}, u32[]{:S(2)}, u32[]{:S(2)}) collective-permute-start(bf16[2,2,2,64,512]{4,3,2,1,0:T(8,128)(2,1)S(1)} %get-tuple-element.363), channel_id=1, source_target_pairs={{0,1},{1,0},{2,3},{3,2},{4,5},{5,4},{6,7},{7,6},{8,9},{9,8},{10,11... | collective-permute-start | bytes 1572872 | tf_op jit(solution)/shard_map/ppermute | solution.py:873
  214.9 6.0 %collective-permute-start.43 = (bf16[1024,512]{1,0:T(8,128)(2,1)S(1)}, bf16[1024,512]{1,0:T(8,128)(2,1)}, u32[]{:S(2)}, u32[]{:S(2)}) collective-permute-start(bf16[1024,512]{1,0:T(8,128)(2,1)S(1)} %bitcast.176), channel_id=1, source_target_pairs={{16,0},{17,1},{18,2},{19,3},{20,4},{21,5},{22,6},{23,7},{24,8},{25... | collective-permute-start | bytes 3145736 | tf_op jit(solution)/shard_map/ppermute | solution.py:873
  (33 other events, 128.8 us)

commit v4 on v3

--- a/solution.py
+++ b/solution.py
@@ -29,10 +29,16 @@
 
 
 class Slot:
-    def __init__(self, ref, copy):
-        self.ref, self.copy = ref, copy
+    def __init__(self, ref, copy, start=None):
+        self.ref, self.copy, self.start = ref, copy, start
+
+    def begin(self):
+        if self.start is not None:
+            self.start()
+            self.start = None
 
     def get(self):
+        self.begin()
         if self.copy is not None:
             self.copy.wait()
             self.copy = None
@@ -97,7 +103,17 @@
 HBM = pl.BlockSpec(memory_space=pltpu.HBM)
 
 
-def call(kernel, name, operands, outs, scratch, most=False):
+def start_pick(is_own, own, other, dst, sem):
+    @pl.when(is_own)
+    def _():
+        pltpu.make_async_copy(own, dst, sem).start()
+
+    @pl.when(jnp.logical_not(is_own))
+    def _():
+        pltpu.make_async_copy(other, dst, sem).start()
+
+
+def call(kernel, name, operands, outs, scratch, most=False, early=99):
     specs, arrays, buffers = [], [], []
     for kind, value in operands:
         if kind == "smem":
@@ -132,24 +148,18 @@
             if isinstance(kind, int):
                 own, other = ins[at], ins[at + 1]
                 at += 2
-
-                @pl.when(section == kind)
-                def _():
-                    pltpu.make_async_copy(own, dst, sem).start()
-
-                @pl.when(section != kind)
-                def _():
-                    pltpu.make_async_copy(other, dst, sem).start()
-
                 copy = pltpu.make_async_copy(own, dst, sem)
+                start = functools.partial(start_pick, section == kind, own, other, dst, sem)
             else:
                 src = ins[at]
                 at += 1
                 if kind == "image":
                     src = src.at[section]
                 copy = pltpu.make_async_copy(src, dst, sem)
-                copy.start()
-            slots.append(Slot(dst, copy))
+                start = copy.start
+            slots.append(Slot(dst, copy, start))
+            if len(slots) <= early:
+                slots[-1].begin()
         ships, at = [], 0
         for i, out in enumerate(outs):
             buf, copies = bufs[n_load + i], []
@@ -209,22 +219,15 @@
     return lambda row, lo, n: vec_ref[row : row + 1, lo : lo + n]
 
 
-def piece_masks(section):
+def piece_masks(section, over_z):
     place = lax.axis_index("dp") % 16
-    x_bit, y_bit, z_at = place & 1, (place >> 1) & 1, place >> 2
-    return section * 16 + x_bit * 8 + y_bit * 4 + z_at, section * 16 + y_bit * 8 + x_bit * 4 + z_at
+    x_bit, y_bit, low, high = place & 1, (place >> 1) & 1, (place >> 2) & 1, place >> 3
+    rest = section * 16 + (low * 2 + high if over_z else 0)
+    return rest + x_bit * 8 + y_bit * 4, rest + y_bit * 8 + x_bit * 4
 
 
 def piece_rows(masks, p, rows):
     return pl.multiple_of((p ^ masks[p >> 4]) * rows, 64)
-
-
-def fill_mask(mask_ref, crop_ref, section):
-    kind = crop_ref[section, 0]
-    side = jnp.where(kind == 0, SIDE_S, jnp.where(kind == 1, SIDE_M, CANVAS))
-    r = lax.broadcasted_iota(jnp.int32, (PIX, LANES), 0)
-    inside = ((r // CANVAS) < side) & ((r % CANVAS) < side)
-    mask_ref[...] = inside.astype(F32)
 
 
 def row_chunks(body, start):
@@ -405,8 +408,14 @@
 
 
 def pack_kernel(*refs):
-    vectors, taps_in, w1, w2, w3 = refs[:14], refs[14], refs[15], refs[16], refs[17]
-    vec_ref, taps_ref, gates_ref = refs[18:]
+    vectors, taps_in, w1, w2, w3, crop_ref = refs[:14], refs[14], refs[15], refs[16], refs[17], refs[18]
+    vec_ref, taps_ref, gates_ref, mask_ref = refs[19:]
+    crops = crop_ref[...]
+    kind = jnp.where(lax.axis_index("section") == 0, crops[:, 0:1], crops[:, 1:2])
+    side = jnp.where(kind == 0, SIDE_S, jnp.where(kind == 1, SIDE_M, CANVAS))
+    r = lax.broadcasted_iota(jnp.int32, (PIX, LANES), 0)
+    inside = ((r // CANVAS) < side) & ((r % CANVAS) < side)
+    mask_ref[...] = inside.astype(F32)
     gates_ref[0:256, :] = w3[...]
     gates_ref[256:384, 0:256] = w2[...]
     gates_ref[256:384, 256:384] = jnp.concatenate([w1[...], jnp.zeros((64, 128), BF)], axis=0)
@@ -428,20 +437,23 @@
         taps_ref[49 * GROUPS + g : 49 * GROUPS + g + 1, :] = b
 
 
-def gn_forward_kernel(crop, x, vec, win, taps, gates, wo, n1, cin, mix, p, gl, mid, br, mask, mx_ref):
-    fill_mask(mask, crop, lax.axis_index("section"))
+def gn_forward_kernel(mask, x, vec, win, taps, gates, wo, n1, cin, mix, p, gl, mid, br, mx_ref):
     x_ref = x.get()
-    gn_forward_part(mask, x_ref, reader(vec.get()), taps, gates, win, wo, n1, cin, mix, p, gl, mid, br, mx_ref)
-
-
-def middle_kernel(crop, mid0, vec0, we0, wr0, vec1, win, taps, gates, wo, we1, wr1, dy,
+    gn_forward_part(mask.get(), x_ref, reader(vec.get()), taps, gates, win, wo, n1, cin, mix, p, gl, mid, br, mx_ref)
+
+
+def middle_kernel(mask, mid0, vec0, we0, wr0, vec1, win, taps, gates, wo, we1, wr1, dy,
                   hidden, n2, act, slope, out, n1, cin, mix, p, gl, br, final, swap, dmid, mvec, bucket,
-                  mask, mx_ref, mid1, n2_1, act1, slope1, out1, dout_ref, dpre_ref, dn2_ref):
+                  mx_ref, mid1, n2_1, act1, slope1, out1, dout_ref, dpre_ref, dn2_ref):
     section = lax.axis_index("section")
-    masks = piece_masks(section)
-    fill_mask(mask, crop, section)
+    masks = piece_masks(section, True)
+    mask = mask.get()
     mid0_ref = mid0.get()
-    mlp_forward_part(mask, mid0_ref, reader(vec0.get()), we0, wr0, n2.ref, act.ref, slope.ref, out.ref, hidden.ref)
+    vec0_ref = vec0.get()
+    wr0.begin()
+    for slot in (vec1, win, taps, gates, wo, we1, wr1, dy):
+        slot.begin()
+    mlp_forward_part(mask, mid0_ref, reader(vec0_ref), we0, wr0, n2.ref, act.ref, slope.ref, out.ref, hidden.ref)
     for ship in (hidden, n2, act, slope, out):
         ship.go()
     vec = reader(vec1.get())
@@ -454,22 +466,20 @@
                   dmid, mvec, bucket, dout_ref, dpre_ref, dn2_ref)
 
 
-def mlp_back_kernel(crop, dy, vec, n2, act, slope, out, mid, wr, we, dmid, mvec, bucket,
-                    mask, dout_ref, dpre_ref, dn2_ref):
-    section = lax.axis_index("section")
-    fill_mask(mask, crop, section)
-    mlp_back_part(mask, piece_masks(section), dy.get(), reader(vec.get()), n2.get(), act.get(), slope.get(), out.get(),
+def mlp_back_kernel(mask, dy, vec, n2, act, slope, out, mid, wr, we, dmid, mvec, bucket,
+                    dout_ref, dpre_ref, dn2_ref):
+    mlp_back_part(mask.get(), piece_masks(lax.axis_index("section"), True), dy.get(), reader(vec.get()), n2.get(), act.get(), slope.get(), out.get(),
                   mid.get(), we, wr, dmid, mvec, bucket, dout_ref, dpre_ref, dn2_ref)
 
 
-def gn_back_kernel(block, crop, dmid, br, vec, wo, mix, p, gates, mvec, taps, win, x, *rest):
+def gn_back_kernel(block, mask, dmid, br, vec, wo, mix, p, gates, mvec, taps, win, x, *rest):
     if block == 0:
         following, dv, swap, dbr, dp, dmg, dcp, gvec = rest[:8]
     else:
         dv, dvb, dbr, dp, dmg, dcp, gvec = rest[:7]
-    mask, dg_ref, dmix_ref, ds_ref, dn1_ref = rest[-5:]
+    dg_ref, dmix_ref, ds_ref, dn1_ref = rest[-4:]
     section = lax.axis_index("section")
-    fill_mask(mask, crop, section)
+    mask = mask.get()
     zero_border(dcp.ref)
     dmid_ref, br_ref = dmid.get(), br.get()
     vec = reader(vec.get())
@@ -571,7 +581,7 @@
 
 
 def gn_weights_kernel(n1, dmg, gl, dbr, dp, gvec, cin, dcp, bucket, dk_ref):
-    masks = piece_masks(lax.axis_index("section"))
+    masks = piece_masks(lax.axis_index("section"), False)
 
     def put(p, val, sub=0):
         n = val.shape[0]
@@ -623,100 +633,107 @@
         put(29 + half, jnp.concatenate([lane_group(dk_ref, 4 * half + i, 64) for i in range(4)], axis=1).astype(BF))
 
 
-def start_pieces(layout, rows, halves, buf, sems):
+def start_half(far, rows, sources, buf, sems, over_z):
     section = lax.axis_index("section")
-    masks = piece_masks(section)
-    for p in range(32):
-        rel = p ^ masks[p >> 4]
-        far = rel >> 4
+    half = 1 - section if far else section
+    masks = piece_masks(section, over_z)
+    mask = jnp.where(half == 0, masks[0], masks[1]) & 15
+    for p in range(16):
+        off = pl.multiple_of((p ^ mask) * rows, 64)
         dst = buf.at[p * rows : (p + 1) * rows]
-        sem = sems.at[p // 4]
         for sec in range(2):
-            stride, first = layout[sec]
-            off = pl.multiple_of((rel & 15) * stride + first, 64)
-            for side in range(2):
-
-                @pl.when((section == sec) & (far == side))
-                def _():
-                    pltpu.make_async_copy(halves[2 * sec + side].at[pl.ds(off, rows)], dst, sem).start()
-
-
-def wait_pieces(i, rows, halves, buf, sems):
+
+            @pl.when(section == sec)
+            def _():
+                pltpu.make_async_copy(sources[sec].at[pl.ds(off, rows)], dst, sems.at[p // 4]).start()
+
+    return half
+
+
+def wait_quarter(i, rows, sources, buf, sems):
     part = buf.at[pl.ds(i * 4 * rows, 4 * rows)]
-    pltpu.make_async_copy(halves[0].at[pl.ds(0, 4 * rows)], part, sems.at[i]).wait()
-
-
-def mlp_finish_kernel(layout, *refs):
-    halves = refs[:4]
+    pltpu.make_async_copy(sources[0].at[pl.ds(0, 4 * rows)], part, sems.at[i]).wait()
+
+
+def mlp_finish_kernel(far, *refs):
+    sources = refs[:2]
     wr_any, we_any, buf, wr_ref, we_ref, sems, out_sems = refs[-7:]
-    start_pieces(layout, 128, halves, buf, sems)
+    half = start_half(far, 128, sources, buf, sems, True)
     copies = []
-    for i in range(8):
-        wait_pieces(i, 128, halves, buf, sems)
+    for i in range(4):
+        wait_quarter(i, 128, sources, buf, sems)
         cb = i // 2
         for q in range(4):
             p = 4 * i + q
             r = p % 8
             wr_ref[64 * p : 64 * p + 64, :] = buf[128 * p : 128 * p + 64, :].astype(F32)
             we_ref[64 * r : 64 * r + 64, 512 * cb : 512 * cb + 512] = buf[128 * p + 64 : 128 * p + 128, :].astype(F32)
-        rows = slice(256 * i, 256 * i + 256)
-        copies.append(pltpu.make_async_copy(wr_ref.at[rows], wr_any.at[rows], out_sems.at[i]))
-        half = slice(256 * (i % 2), 256 * (i % 2) + 256)
-        cols = slice(512 * cb, 512 * cb + 512)
-        copies.append(pltpu.make_async_copy(we_ref.at[half, cols], we_any.at[half, cols], out_sems.at[8 + i]))
+        rows = pl.ds(pl.multiple_of(half * 1024 + 256 * i, 256), 256)
+        copies.append(pltpu.make_async_copy(wr_ref.at[256 * i : 256 * i + 256], wr_any.at[rows], out_sems.at[i]))
+        part = slice(256 * (i % 2), 256 * (i % 2) + 256)
+        cols = pl.ds(pl.multiple_of(half * 1024 + 512 * cb, 512), 512)
+        src = we_ref.at[part, 512 * cb : 512 * cb + 512]
+        copies.append(pltpu.make_async_copy(src, we_any.at[part, cols], out_sems.at[4 + i]))
         copies[-2].start()
         copies[-1].start()
     for copy in copies:
         copy.wait()
 
 
-def gn_finish_kernel(layout, *refs):
-    halves = refs[:4]
-    (n1g, n1s, win_any, bin_, conv, cbias, w1, b1, w2, b2, w3, b3, wo_any, bo, bs, n2g, n2s, be, br, ms,
-     buf, win, wo, sems, out_sems) = refs[-25:]
-    start_pieces(layout, 64, halves, buf, sems)
-    copies = []
-    for cb in range(2):
-        cols = slice(512 * cb, 512 * cb + 512)
+def gn_finish_kernel(far, *refs):
+    sources = refs[:2]
+    count = len(GN_OUTS)
+    results, buf, vals, sems, out_sems = refs[-2 * count - 3 : -count - 3], refs[-count - 3], refs[-count - 2 : -2], refs[-2], refs[-1]
+    (n1g, n1s, win, bin_, conv, cbias, w1, b1, w2, b2, w3, b3, wo, bo, bs, n2g, n2s, be, br, ms) = vals
+    half = start_half(far, 64, sources, buf, sems, False)
+    for i in range(4):
+        wait_quarter(i, 64, sources, buf, sems)
+
+    def out(i):
+        return pltpu.make_async_copy(vals[i], results[i], out_sems.at[i])
+
+    @pl.when(half == 0)
+    def _():
+        for cb in range(2):
+            win[:, 512 * cb : 512 * cb + 512] = buf[512 * cb : 512 * cb + 512, :].astype(F32)
+        out(2).start()
+        out(2).wait()
+
+    @pl.when(half == 1)
+    def _():
+        wo[...] = buf[0:512, :].astype(F32)
+        out(12).start()
+        w3[...] = buf[512:768, :].astype(F32)
+        out(10).start()
         for i in range(2):
-            wait_pieces(2 * cb + i, 64, halves, buf, sems)
-        win[:, cols] = buf[cols, :].astype(F32)
-        copies.append(pltpu.make_async_copy(win.at[:, cols], win_any.at[:, cols], out_sems.at[cb]))
-        copies[-1].start()
-    for i in (4, 5):
-        wait_pieces(i, 64, halves, buf, sems)
-    wo[...] = buf[1024:1536, :].astype(F32)
-    copies.append(pltpu.make_async_copy(wo, wo_any, out_sems.at[2]))
-    copies[-1].start()
-    for i in (6, 7):
-        wait_pieces(i, 64, halves, buf, sems)
-    w3[...] = buf[1536:1792, :].astype(F32)
-    for i in range(2):
-        w2[64 * i : 64 * i + 64, :] = buf[1792:1856, 256 * i : 256 * i + 256].astype(F32)
-    for i in range(4):
-        w1[16 * i : 16 * i + 16, :] = buf[1984:2000, 128 * i : 128 * i + 128].astype(F32)
-    taps = jnp.concatenate([buf[1856:1920, :], buf[1920:1984, :]], axis=1).astype(F32)
-    for i in range(49):
-        conv[i] = taps[i : i + 1, 64:1024]
-    cbias[...] = taps[49:50, 64:1024]
-    v = buf[2016:2048, :].astype(F32)
-    n1g[...] = v[0:1]
-    n1s[...] = v[1:2]
-    bin_[:, 0:512] = v[2:3]
-    bin_[:, 512:1024] = v[3:4]
-    b1[...] = v[4:5, 0:128]
-    b2[...] = v[5:6, 0:256]
-    b3[...] = v[6:7]
-    bo[...] = v[7:8]
-    bs[...] = v[8:9]
-    n2g[...] = v[9:10]
-    n2s[...] = v[10:11]
-    for i in range(4):
-        be[:, 512 * i : 512 * i + 512] = v[11 + i : 12 + i]
-    br[...] = v[15:16]
-    ms[...] = v[16:17]
-    for copy in copies:
-        copy.wait()
+            w2[64 * i : 64 * i + 64, :] = buf[768:832, 256 * i : 256 * i + 256].astype(F32)
+        for i in range(4):
+            w1[16 * i : 16 * i + 16, :] = buf[960:976, 128 * i : 128 * i + 128].astype(F32)
+        taps = jnp.concatenate([buf[832:896, :], buf[896:960, :]], axis=1).astype(F32)
+        for i in range(49):
+            conv[i] = taps[i : i + 1, 64:1024]
+        cbias[...] = taps[49:50, 64:1024]
+        v = buf[992:1024, :].astype(F32)
+        n1g[...] = v[0:1]
+        n1s[...] = v[1:2]
+        bin_[:, 0:512] = v[2:3]
+        bin_[:, 512:1024] = v[3:4]
+        b1[...] = v[4:5, 0:128]
+        b2[...] = v[5:6, 0:256]
+        b3[...] = v[6:7]
+        bo[...] = v[7:8]
+        bs[...] = v[8:9]
+        n2g[...] = v[9:10]
+        n2s[...] = v[10:11]
+        for i in range(4):
+            be[:, 512 * i : 512 * i + 512] = v[11 + i : 12 + i]
+        br[...] = v[15:16]
+        ms[...] = v[16:17]
+        rest = [i for i in range(count) if i not in (2, 10, 12)]
+        for i in rest:
+            out(i).start()
+        for i in rest + [10, 12]:
+            out(i).wait()
 
 
 def place_kernel(first, second, got, out):
@@ -736,7 +753,7 @@
 VM = pl.BlockSpec(memory_space=pltpu.VMEM)
 
 
-def plain_call(kernel, name, operands, outs, scratch, most=False):
+def plain_call(kernel, name, operands, outs, scratch, most=False, aliases={}):
     return pl.pallas_call(
         kernel,
         name=name,
@@ -745,6 +762,7 @@
         out_specs=[spec for spec, _ in outs],
         scratch_shapes=scratch,
         compiler_params=room([a for spec, a in operands + outs if spec is VM] + scratch, most),
+        input_output_aliases=aliases,
         cost_estimate=pl.CostEstimate(flops=0, bytes_accessed=0, transcendentals=0),
     )(*[array for _, array in operands])
 
@@ -753,7 +771,6 @@
     return [(spec, a) for a in arrays]
 
 
-MASK = vmem(PIX, LANES, F32)
 PIXEL_CHANNELS = vmem(PIX * GROUPS, LANES, F32)
 FIELD_F32, FIELD_BF = sds((PIX, C), F32), sds((PIX, C), BF)
 CONV_F32 = sds((PAD_ROWS * GROUPS, LANES), F32)
@@ -762,42 +779,42 @@
 GN_SAVED = [FIELD_BF, CONV_F32, WIDE_F32, WIDE_F32, WIDE_BF]
 
 
-def run_pack(vectors, taps, gates):
-    outs = on(VM, sds((VEC_ROWS, FF), F32), sds((50 * GROUPS, LANES), F32), sds((384, 512), BF))
-    return plain_call(pack_kernel, "pack", on(VM, *vectors, taps, *gates), outs, [], True)
-
-
-def run_gn_forward(crop, images, w):
-    operands = [smem(crop), image(images)] + [pick(0, w[k]) for k in ("vec", "win", "taps", "gates", "wo")]
+def run_pack(vectors, taps, gates, crop):
+    outs = on(VM, sds((VEC_ROWS, FF), F32), sds((50 * GROUPS, LANES), F32), sds((384, 512), BF), sds((PIX, LANES), F32))
+    return plain_call(pack_kernel, "pack", on(VM, *vectors, taps, *gates, crop), outs, [], True)
+
+
+def run_gn_forward(mask, images, w):
+    operands = [load(mask), image(images)] + [pick(0, w[k]) for k in ("vec", "win", "taps", "gates", "wo")]
     return call(gn_forward_kernel, "gnconv_forward", operands, GN_SAVED + [FIELD_F32, FIELD_BF],
-                [MASK, PIXEL_CHANNELS], True)
-
-
-def run_middle(crop, mid, cotangent, w):
-    operands = [smem(crop), load(mid)] + [pick(0, w[k]) for k in ("vec", "we", "wr")]
+                [PIXEL_CHANNELS], True)
+
+
+def run_middle(mask, mid, cotangent, w):
+    operands = [load(mask), load(mid)] + [pick(0, w[k]) for k in ("vec", "we", "wr")]
     operands += [pick(1, w[k]) for k in ("vec", "win", "taps", "gates", "wo", "we", "wr")] + [image(cotangent)]
     outs = [FIELD_BF, FIELD_BF, HIDE_BF, HIDE_BF, FIELD_BF] + GN_SAVED + [FIELD_BF, FIELD_BF, FIELD_BF, FIELD_F32]
     outs += [sds((8, FF), F32), Halves(4096)]
-    scratch = [MASK, PIXEL_CHANNELS, vmem(PIX, C, F32), vmem(PIX, C, BF), vmem(PIX, FF, BF), vmem(PIX, FF, BF),
+    scratch = [PIXEL_CHANNELS, vmem(PIX, C, F32), vmem(PIX, C, BF), vmem(PIX, FF, BF), vmem(PIX, FF, BF),
                vmem(PIX, C, BF), vmem(PIX, C, BF), vmem(PIX, FF, BF), vmem(PIX, C, F32)]
-    return call(middle_kernel, "middle", operands, outs, scratch, True)
-
-
-def run_mlp_back(crop, dy, n2, act, slope, out, mid, w):
-    operands = [smem(crop), near(dy), pick(0, w["vec"]), load(n2), load(act), load(slope), load(out), load(mid),
+    return call(middle_kernel, "middle", operands, outs, scratch, True, 4)
+
+
+def run_mlp_back(mask, dy, n2, act, slope, out, mid, w):
+    operands = [load(mask), near(dy), pick(0, w["vec"]), load(n2), load(act), load(slope), load(out), load(mid),
                 pick(0, w["wr"]), pick(0, w["we"])]
     outs = [FIELD_F32, sds((8, FF), F32), Halves(4096)]
-    scratch = [MASK, vmem(PIX, C, BF), vmem(PIX, FF, BF), vmem(PIX, C, F32)]
+    scratch = [vmem(PIX, C, BF), vmem(PIX, FF, BF), vmem(PIX, C, F32)]
     return call(mlp_back_kernel, "mlp_backward", operands, outs, scratch, True)
 
 
-def run_gn_back(block, crop, x, following, dmid, mvec, mix, p, br, w):
+def run_gn_back(block, mask, x, following, dmid, mvec, mix, p, br, w):
     far = load if block == 1 else near
-    operands = [smem(crop), far(dmid), load(br), pick(block, w["vec"]), pick(block, w["wo"]), load(mix), load(p),
+    operands = [load(mask), far(dmid), load(br), pick(block, w["vec"]), pick(block, w["wo"]), load(mix), load(p),
                 pick(block, w["gates"]), far(mvec), pick(block, w["taps"]), pick(block, w["win"])]
     operands += [image(x), near(following)] if block == 0 else [load(x)]
     outs = [FIELD_F32, FIELD_F32 if block == 0 else FIELD_BF, FIELD_BF, WIDE_BF, WIDE_BF, CONV_F32, sds((32, 512), BF)]
-    scratch = [MASK, vmem(PIX, LANES, F32), vmem(PIX, 1024, F32), PIXEL_CHANNELS, vmem(PIX, C, F32)]
+    scratch = [vmem(PIX, LANES, F32), vmem(PIX, 1024, F32), PIXEL_CHANNELS, vmem(PIX, C, F32)]
     return call(functools.partial(gn_back_kernel, block), "gnconv_backward", operands, outs, scratch, block == 1)
 
 
@@ -815,21 +832,24 @@
     return plain_call(turn_kernel, "turn", on(ANY, token), on(VM, sds((8, LANES), F32)), [])[0]
 
 
-def run_mlp_finish(layout, halves):
+def run_mlp_finish(far, sources, earlier=()):
     outs = on(ANY, sds((FF, C), F32), sds((C, FF), F32))
-    scratch = [vmem(4096, 512, BF), vmem(FF, C, F32), vmem(C, FF, F32), pltpu.SemaphoreType.DMA((8,)),
-               pltpu.SemaphoreType.DMA((16,))]
-    return plain_call(functools.partial(mlp_finish_kernel, layout), "mlp_finish", on(ANY, *halves), outs, scratch, True)
-
-
-def run_gn_finish(layout, halves):
-    widths = [512, 512, (512, 1024), 1024, (49, 1, 960), 960, (64, 128), 128, (128, 256), 256, (256, 512), 512,
-              (512, 512), 512, 512, 512, 512, 2048, 512, 512]
-    large = ((512, 1024), (512, 512))
-    outs = [(ANY if w in large else VM, sds((1, w) if isinstance(w, int) else w, F32)) for w in widths]
-    scratch = [vmem(2048, 512, BF), vmem(512, 1024, F32), vmem(512, 512, F32), pltpu.SemaphoreType.DMA((8,)),
-               pltpu.SemaphoreType.DMA((3,))]
-    return plain_call(functools.partial(gn_finish_kernel, layout), "gn_finish", on(ANY, *halves), outs, scratch, True)
+    scratch = [vmem(2048, 512, BF), vmem(1024, C, F32), vmem(C, 1024, F32), pltpu.SemaphoreType.DMA((4,)),
+               pltpu.SemaphoreType.DMA((8,))]
+    return plain_call(functools.partial(mlp_finish_kernel, far), "mlp_finish", on(ANY, *sources, *earlier), outs, scratch,
+                      True, {2: 0, 3: 1} if far else {})
+
+
+GN_OUTS = [sds((1, w) if isinstance(w, int) else w, F32) for w in (
+    512, 512, (512, 1024), 1024, (49, 1, 960), 960, (64, 128), 128, (128, 256), 256, (256, 512), 512, (512, 512), 512,
+    512, 512, 512, 2048, 512, 512)]
+
+
+def run_gn_finish(far, sources, earlier=()):
+    scratch = [vmem(1024, 512, BF)] + [pltpu.VMEM(o.shape, F32) for o in GN_OUTS]
+    scratch += [pltpu.SemaphoreType.DMA((4,)), pltpu.SemaphoreType.DMA((len(GN_OUTS),))]
+    return plain_call(functools.partial(gn_finish_kernel, far), "gn_finish", on(ANY, *sources, *earlier),
+                      on(ANY, *GN_OUTS), scratch, True, {2 + i: i for i in range(len(GN_OUTS))} if far else {})
 
 
 def run_place(first, second, got):
@@ -842,16 +862,28 @@
 
 FIRST, SECOND, LOW, HIGH = (X_BIT, Y_BIT), (Y_BIT, X_BIT), (Z_LOW, Z_LOW), (Z_HIGH, Z_HIGH)
 
+BUCKETS = ("m1", "g1", "m0", "g0")
+STEPS = ("core", "x1", "x2", "zl", "zh", "fl", "fh", "ZH", "ZL", "X2", "X1", "Core")
+OTHERS = ("fo", "go")
+KERNELS = ("K1", "K2", "K3", "K4", "K5", "MF1", "MF2", "GF1", "GF2", "P1", "P2")
+
 ORDER = (
-    "+m1.core", "K1", "-m1.core", "+m1.x1", "K2", "+g1.core", "K3", "-g1.core", "+g1.x1", "-m1.x1", "+m1.x2",
-    "+m0.core", "K4", "-g1.x1", "+g1.x2", "-m1.x2", "+m1.zl", "-m0.core", "+m0.x1", "-g1.x2", "+g1.zl", "-m1.zl",
-    "+m1.zh", "-g1.zl", "+g1.zh", "K5", "-m0.x1", "+m0.x2", "-m1.zh", "-g1.zh", "+b1.ZH", "+g0.core", "-m0.x2",
-    "+m0.zl", "-g0.core", "+g0.x1", "-b1.ZH", "+b1.ZL", "-m0.zl", "+m0.zh", "-g0.x1", "+g0.x2", "-b1.ZL", "+b1.X2",
-    "+go", "-go", "-g0.x2", "+g0.zl", "-m0.zh", "+m0.ZH", "-b1.X2", "+b1.X1", "-g0.zl", "+g0.zh", "-m0.ZH", "+m0.ZL",
-    "P2", "-g0.zh", "+g0.ZH", "-m0.ZL", "+m0.X2", "-g0.ZH", "+g0.ZL", "-g0.ZL", "+g0.X2", "-m0.X2", "+m0.X1",
-    "-b1.X1", "+fo", "-fo", "P1", "-g0.X2", "+g0.X1", "+b1.Core", "-b1.Core", "-m0.X1", "+m0.Core", "-m0.Core",
-    "-g0.X1", "+g0.Core", "MF", "-g0.Core", "GF",
+    1, 60, 49, -1, 2, 62, 61, 13, -2, 3, 25, -25, 26, 63, -3, 4, 50, -13, 14, 64, -4, 5, -26, 27, 37, -37, 38, -27,
+    28, -5, 8, -28, 29, -8, 9, -49, 69, -14, 15, -29, 32, -38, 39, -9, 10, -15, 18, -39, 42, -32, 33, -33, 34, -18,
+    19, -10, 11, -42, 43, -34, 35, -50, 70, -19, 22, -43, 46, -22, 23, -11, 12, -35, 36, 65, -12, -46, 47, -23, 24,
+    -36, 66, -47, 48, 67, -24, -48, 68,
 )
+
+
+def event_name(number):
+    at = abs(number) - 1
+    if at >= 59:
+        return KERNELS[at - 59]
+    sign = "+" if number > 0 else "-"
+    return sign + (OTHERS[at - 48] if at >= 48 else BUCKETS[at // 12] + "." + STEPS[at % 12])
+
+
+GROUPED = (("m1", ("m1",)), ("m0", ("m0",)), ("g1", ("g1",)), ("g0", ("g0",)))
 
 
 def after(x, *others):
@@ -873,7 +905,8 @@
         return lax.ppermute(x, AXES, pairs)
 
     def start(self, name, x, flips=None, only=None):
-        self.flying[name] = self.exchange(after(x, self.token), flips, only)
+        with jax.named_scope("transfer_" + name.replace(".", "_")):
+            self.flying[name] = self.exchange(after(x, self.token), flips, only)
 
     def end(self, name):
         got, token = lax.optimization_barrier((self.flying.pop(name), self.token))
@@ -891,7 +924,9 @@
     images = images.reshape(2, PIX, C)
     cotangent = cotangent.reshape(2, PIX, C)
     win, wo, we, wr = [stacked[i][0] for i in (2, 12, 17, 19)]
-    vec, taps, gates = run_pack([stacked[i] for i in VECTORS], stacked[4][0], [stacked[i][0] for i in (6, 8, 10)])
+    vec, taps, gates, mask = run_pack(
+        [stacked[i] for i in VECTORS], stacked[4][0], [stacked[i][0] for i in (6, 8, 10)], crop.reshape(1, 2)
+    )
     swap = flow.exchange
     win_other, wo_other = swap(win), swap(wo)
     taps_other, vec_other, gates_other = swap(taps), swap(vec), swap(gates)
@@ -902,9 +937,9 @@
         "vec": (vec, vec_other), "taps": (taps, taps_other), "gates": (gates, gates_other),
     }
 
-    n1_0, cin_0, mix_0, p_0, gl_0, mid_0, br_0 = run_gn_forward(crop, images, w)
+    n1_0, cin_0, mix_0, p_0, gl_0, mid_0, br_0 = run_gn_forward(mask, images, w)
     (hidden, n2_0, act_0, slope_0, out_0, n1_1, cin_1, mix_1, p_1, gl_1, br_1, final, field_swap, dmid_1, mvec_1,
-     keep, send) = run_middle(crop, mid_0, cotangent, w)
+     keep, send) = run_middle(mask, mid_0, cotangent, w)
     flow.token = mvec_1
     value = {"m1.core": (keep, send)}
     chips = flow.count // 16
@@ -917,47 +952,49 @@
 
     def begin(name):
         bucket, step = name.split(".")
-        only = {"b1": 0, "m0": 1, "g0": 1}.get(bucket)
-        if step == "core":
-            flow.start(name, value[name][1])
-        elif step == "Core":
-            flow.start(name, value[name], None, only)
-        elif step in ("x1", "x2", "zh"):
-            flow.start(name, value[name][1], {"x1": FIRST, "x2": SECOND, "zh": HIGH}[step])
-        elif step == "zl":
-            flow.start(name, value[name][:, 1], LOW)
-        else:
-            flow.start(name, value[name], {"ZH": HIGH, "ZL": LOW, "X2": SECOND, "X1": FIRST}[step])
+        only = {"m1": 0, "g1": 0, "m0": 1, "g0": 1}.get(bucket)
+        flips = {"x1": FIRST, "x2": SECOND, "zl": LOW, "zh": HIGH, "fl": LOW, "fh": HIGH}.get(step.lower())
+        whole = step.isupper() or step in ("Core", "fl", "fh")
+        flow.start(name, value[name] if whole else value[name][1], flips, only if step == "Core" else None)
 
     def finish(name):
         bucket, step = name.split(".")
         got = flow.end(name)
-        mine = value.pop(name)
-        if step == "core":
-            half = mine[0] + got
-            value[bucket + ".x1"] = half.reshape(2, 2, 2, 2, half.shape[0] // 16, 512)
-        elif step in ("x1", "x2"):
-            value[bucket + (".x2" if step == "x1" else ".zl")] = mine[0] + got
-        elif step == "zl":
-            value[bucket + ".zh"] = mine[:, 0] + got
-        elif step == "zh":
-            value[bucket] = sum_all(mine[0] + got)
-            if bucket in ("m0", "g0"):
-                value[bucket + ".ZH"] = value[bucket]
-            elif "m1" in value and "g1" in value:
-                value["b1.ZH"] = jnp.concatenate([value["m1"], value["g1"]], axis=0)
-        elif step == "ZH":
-            value[bucket + ".ZL"] = jnp.stack([mine, got])
-        elif step == "ZL":
-            value[bucket + ".X2"] = jnp.stack([mine, got], axis=1)
-        elif step == "X2":
-            value[bucket + ".X1"] = jnp.stack([mine, got])
-        elif step == "X1":
-            value[bucket + ".Core"] = jnp.stack([mine, got]).reshape(-1, 512)
+        mine = value[name]
+        after_step = {"core": "x1", "x1": "x2", "x2": "zl" if bucket[0] == "m" else "fl", "zl": "zh", "fl": "fh",
+                      "ZH": "ZL", "ZL": "X2", "X2": "X1", "X1": "Core"}
+        if step == "Core":
+            value[bucket] = (mine, got)
+            return
+        if step.isupper():
+            total = jnp.stack([mine, got])
+            value[bucket + "." + after_step[step]] = total.reshape(-1, 512) if step == "X1" else total
+            return
+        if step in ("fl", "fh"):
+            total = mine + got
         else:
-            value[bucket] = (mine, got)
-
-    for event in ORDER:
+            mine = mine[0]
+            if step == "core":
+                shape = (2, 2, 2, 2, mine.shape[0] // 16, 512)
+                mine, got = mine.reshape(shape), got.reshape(shape)
+            if step in ("core", "x1", "zl"):
+                total = (mine[0] + got[0], mine[1] + got[1])
+            else:
+                total = mine + got
+        if step == "x2" and bucket[0] == "m":
+            total = (total[0], total[1])
+        if step in ("zh", "fh"):
+            total = sum_all(total)
+            for group, members in GROUPED:
+                if bucket in members:
+                    value["sum of " + bucket] = total
+                    sums = [value.get("sum of " + m) for m in members]
+                    if all(v is not None for v in sums):
+                        value[group + (".ZH" if step == "zh" else ".X2")] = jnp.concatenate(sums, axis=-2)
+        else:
+            value[bucket + "." + after_step[step]] = total
+
+    for event in map(event_name, ORDER):
         if event in ("+fo", "+go"):
             flow.start(event[1:], field_swap if event == "+fo" else grad_swap)
         elif event in ("-fo", "-go"):
@@ -967,17 +1004,17 @@
         elif event[0] == "-":
             finish(event[1:])
         elif event == "K1":
-            back = run_gn_back(1, crop, hidden, None, flow.tie(dmid_1), mvec_1, mix_1, p_1, br_1, w)
+            back = run_gn_back(1, mask, hidden, None, flow.tie(dmid_1), mvec_1, mix_1, p_1, br_1, w)
             dv_1, dvb, dbr_1, dp_1, dmg_1, dcp_1, gvec_1 = back
             flow.token = gvec_1
         elif event == "K2":
             value["g1.core"] = run_gn_weights(1, n1_1, dmg_1, gl_1, dbr_1, dp_1, flow.tie(gvec_1), cin_1, dcp_1)
             flow.token = value["g1.core"][0]
         elif event == "K3":
-            dmid_0, mvec_0, *value["m0.core"] = run_mlp_back(crop, flow.tie(dvb), n2_0, act_0, slope_0, out_0, mid_0, w)
+            dmid_0, mvec_0, *value["m0.core"] = run_mlp_back(mask, flow.tie(dvb), n2_0, act_0, slope_0, out_0, mid_0, w)
             flow.token = mvec_0
         elif event == "K4":
-            back = run_gn_back(0, crop, images, dv_1, flow.tie(dmid_0), mvec_0, mix_0, p_0, br_0, w)
+            back = run_gn_back(0, mask, images, dv_1, flow.tie(dmid_0), mvec_0, mix_0, p_0, br_0, w)
             dv_0, grad_swap, dbr_0, dp_0, dmg_0, dcp_0, gvec_0 = back
             flow.token = gvec_0
         elif event == "K5":
@@ -987,13 +1024,16 @@
             flow.token = block_outputs = run_place(hidden, final, flow.tie(value["fo"]))
         elif event == "P2":
             flow.token = input_grads = run_place(dv_0, dv_1, flow.tie(value["go"]))
-        elif event == "MF":
-            own, got = value["m0"]
-            wr, we = run_mlp_finish(((128, 0), (192, 0)), (flow.tie(own), got) + value["b1"])
+        elif event in ("MF1", "MF2"):
+            far = event == "MF2"
+            one, two = (value[b][1] if far else value[b + ".Core"] for b in ("m0", "m1"))
+            wr, we = mlp_grads = run_mlp_finish(far, (flow.tie(one), two), mlp_grads if far else ())
             flow.token = wr
-        elif event == "GF":
-            own, got = value["g0"]
-            grads = run_gn_finish(((64, 0), (192, 128)), (flow.tie(own), got) + value["b1"])
+        elif event in ("GF1", "GF2"):
+            far = event == "GF2"
+            one, two = (value[b][1] if far else value[b + ".Core"] for b in ("g0", "g1"))
+            grads = run_gn_finish(far, (flow.tie(one), two), grads if far else ())
+            flow.token = grads[0]
     (n1g, n1s, win, bin_, conv, cbias, w1, b1, w2, b2, w3, b3, wo, bo, bs, n2g, n2s, be, br, ms) = grads
     shape = (1, 2, 1, CANVAS, CANVAS, C)
     return (

time: 227 us -> 205 us (0.903)
  waiting for transfers between devices: 93.8 us -> 48.9 us
  starting transfers between devices: 43.5 us -> 64.2 us
  other arithmetic: 3.81 us -> 6.73 us
    ppermute x44 -> x45, waiting for transfers between devices: 93.8 us -> 48.9 us  [exchange(): return lax.ppermute(x, AXES, pairs)]
    ppermute x44 -> x45, starting transfers between devices: 43.5 us -> 64.2 us  [exchange(): return lax.ppermute(x, AXES, pairs)]
    pallas_call x5 -> x7, Pallas kernels: 12.8 us -> 16.5 us  [plain_call(): pl.pallas_call(kernel, name=name, out_shape=[shape for _, shape in outs],...]
    pallas_call x7, Pallas kernels: 64.4 us -> 61.4 us  [call(): pl.pallas_call(body, name=name, out_shape=shapes, in_specs=specs, out_spe...]
    another operation x13 -> x12, other arithmetic: 1.34 us -> 4.24 us  [finish(): total = jnp.stack([mine, got])]
  transfers between devices with their start and end apart: 44 -> 45, of which waited for: 24 -> 14; matrix products, arithmetic and copies ran while one was open for 3% -> 3% of each run, Pallas kernels for 22% -> 29%
where the time goes in v4:
time: 205 us; the launch traced here: 204 us
  Pallas kernels  77.9 us (38%)
  starting transfers between devices  64.2 us (31%)
  waiting for transfers between devices  48.9 us (24%)
  other arithmetic  6.73 us (3%)
  local copies, waits for them, and re-layouts  4.4 us (2%)
    ppermute x45, starting transfers between devices, exchange(): return lax.ppermute(x, AXES, pairs)  64.2 us
    pallas_call x7, Pallas kernels, call(): pl.pallas_call(body, name=name, out_shape=shapes, in_specs=specs, out_spe...  61.4 us
    ppermute x45, waiting for transfers between devices, exchange(): return lax.ppermute(x, AXES, pairs)  48.9 us
    pallas_call x7, Pallas kernels, plain_call(): pl.pallas_call(kernel, name=name, out_shape=[shape for _, shape in outs],...  16.5 us
    another operation x12, other arithmetic, finish(): total = jnp.stack([mine, got])  4.24 us
    unnamed x78, local copies, waits for them, and re-layouts  4.15 us
  transfers between devices with their start and end apart: 45, of which 14 were waited for; matrix products, arithmetic and copies ran while one was open for 3% of the time, Pallas kernels for 29%

profile of v4, /device:TPU:0, one launch (start us, length us, event | category | flops | bytes accessed | tf_op | source)
XLA Modules:
  0.0 203.6 jit_solution(13477835542519865292)
XLA Ops:
  1.3 2.1 %pack.1 = (f32[16,2048]{1,0:T(8,128)}, f32[400,128]{1,0:T(8,128)}, bf16[384,512]{1,0:T(8,128)(2,1)}, f32[256,128]{1,0:T(8,128)}) custom-call(bf16[1,512]{1,0:T(2,128)(2,1)} %refs_0_.1, bf16[1,512]{1,0:T(2,128)(2,1)} %refs_1_.1, bf16[1,1024]{1,0:T(2,128)(2,1)} %refs_2_.1, bf16[1,960]{1,0:T(2,128)(2,1)} %refs_3_.1, bf16[1,128]{1,0:T(2,128)(2,1)} %refs_4_.1, ...), custom_call_target="tpu_custom_call" | custom-call | tf_op jit(solution)/shard_map/pack/pallas_call | solution.py:757
  4.3 1.5 collective-permute-done.refs_3_.refs_9_.refs_4_
  7.3 7.9 %gnconv_forward.1 = (bf16[256,512]{1,0:T(8,128)(2,1)}, f32[2816,128]{1,0:T(8,128)}, f32[256,1024]{1,0:T(8,128)}, f32[256,1024]{1,0:T(8,128)}, bf16[256,1024]{1,0...) custom-call(f32[256,128]{1,0:T(8,128)} %get-tuple-element.229.refs_0_, bf16[2,256,512]{2,1,0:T(8,128)(2,1)} %bitcast.131, ...), custom_call_target="tpu_custom_call" | custom-call | tf_op jit(solution)/shard_map/gnconv_forward/pallas_call | solution.py:186
  16.5 16.0 %middle.1 = (bf16[256,512]{1,0:T(8,128)(2,1)}, bf16[256,512]{1,0:T(8,128)(2,1)}, bf16[256,2048]{1,0:T(8,128)(2,1)}, bf16[256,2048]{1,0:T(8,128)(2,1)}, bf16[256,...) custom-call(f32[256,128]{1,0:T(8,128)} %get-tuple-element.229.refs_0, ...), custom_call_target="tpu_custom_call" | custom-call | tf_op jit(solution)/shard_map/middle/pallas_call | solution.py:186
  32.9 9.3 %gnconv_backward.2 = (f32[256,512]{1,0:T(8,128)}, bf16[256,512]{1,0:T(8,128)(2,1)}, bf16[256,512]{1,0:T(8,128)(2,1)}, bf16[256,1024]{1,0:T(8,128)(2,1)}, bf16[25...) custom-call(f32[256,128]{1,0:T(8,128)} %get-tuple-element.229.refs_0_, ...), custom_call_target="tpu_custom_call" | custom-call | tf_op jit(solution)/shard_map/gnconv_backward/pallas_call | solution.py:186
  43.4 2.6 %collective-permute-start.9 = (bf16[2,2,2,128,512]{4,3,2,1,0:T(8,128)(2,1)}, bf16[2,2,2,128,512]{4,3,2,1,0:T(8,128)(2,1)S(1)}, u32[]{:S(2)}, u32[]{:S(2)}) collective-permute-start(bf16[2,2,2,128,512]{4,3,2,1,0:T(8,128)(2,1)} %bitcast.12), channel_id=1, source_target_pairs={{0,1},{1,0},{2,3},{3,2},{4,5},{5,4},{6,7},{7,6},{8,9},{9,8},{10,11... | collective-permute-start | bytes 3145736 | tf_op jit(solution)/shard_map/transfer_m1_x1/ppermute | solution.py:905
  46.1 7.1 %mlp_backward.1 = (f32[256,512]{1,0:T(8,128)}, f32[8,2048]{1,0:T(8,128)}, bf16[2048,512]{1,0:T(8,128)(2,1)}, bf16[2048,512]{1,0:T(8,128)(2,1)}) custom-call(f32[256,128]{1,0:T(8,128)} %get-tuple-element.229.refs_0_, bf16[256,512]{1,0:T(8,128)(2,1)} %get-tuple-element.259.refs_1_, f32[16,2048]{1,0:T(8,128)} %get-tuple-element.230.refs_2_.refs_8_.refs_3_, ...), custom_call_target="tpu_custom_call" | custom-call | tf_op jit(solution)/shard_map/mlp_backward/pallas_call | solution.py:186
  53.2 7.5 %gnconv_weights.2 = (bf16[1024,512]{1,0:T(8,128)(2,1)}, bf16[1024,512]{1,0:T(8,128)(2,1)}) custom-call(bf16[256,512]{1,0:T(8,128)(2,1)} %get-tuple-element.253.refs_0_, bf16[256,1024]{1,0:T(8,128)(2,1)} %get-tuple-element.254.refs_1_, bf16[256,1024]{1,0:T(8,128)(2,1)} %get-tuple-element.255.refs_2_, bf16[256,512]{1,0:T(8,128)(2,1)} %get-tuple-element.256.refs_3_, ...), custom_call_target="tpu_custom_call" | custom-call | tf_op jit(solution)/shard_map/gnconv_weights/pallas_call | solution.py:186
  61.5 1.6 collective-permute-start.10
  63.1 2.1 %collective-permute-done.11 = bf16[2048,512]{1,0:T(8,128)(2,1)S(1)} collective-permute-done((bf16[2048,512]{1,0:T(8,128)(2,1)}, bf16[2048,512]{1,0:T(8,128)(2,1)S(1)}, u32[]{:S(2)}, u32[]{:S(2)}) %collective-permute-start.11) | collective-permute-done | bytes 2097184 | tf_op jit(solution)/shard_map/transfer_m0_core/ppermute | solution.py:905
  67.9 8.1 %gnconv_backward.3 = (f32[256,512]{1,0:T(8,128)S(1)}, f32[256,512]{1,0:T(8,128)S(1)}, bf16[256,512]{1,0:T(8,128)(2,1)S(1)}, bf16[256,1024]{1,0:T(8,128)(2,1)S(1)...) custom-call(f32[256,128]{1,0:T(8,128)S(1)} %copy-done.12, ...), custom_call_target="tpu_custom_call" | custom-call | tf_op jit(solution)/shard_map/gnconv_backward/pallas_call | solution.py:186
  76.2 1.6 collective-permute-start.12
  77.9 5.4 %gnconv_weights.3 = (bf16[1024,512]{1,0:T(8,128)(2,1)S(1)}, bf16[1024,512]{1,0:T(8,128)(2,1)S(1)}) custom-call(bf16[256,512]{1,0:T(8,128)(2,1)S(1)} %copy-done.25, bf16[256,1024]{1,0:T(8,128)(2,1)S(1)} %get-tuple-element.286.refs_1_, bf16[256,1024]{1,0:T(8,128)(2,1)S(1)} %copy-done.22, bf16[256,512]{1,0:T(8,128)(2,1)S(1)} %get-tuple-element.288.refs_3_, ...), custom_call_target="tpu_custom_call" | custom-call | tf_op jit(solution)/shard_map/gnconv_weights/pallas_call | solution.py:186
  83.3 1.3 collective-permute-done.12
  84.9 1.6 collective-permute-start.16
  87.1 2.7 %collective-permute-start.14 = (bf16[128,512]{1,0:T(8,128)(2,1)S(1)}, bf16[128,512]{1,0:T(8,128)(2,1)S(1)}, u32[]{:S(2)}, u32[]{:S(2)}) collective-permute-start(bf16[128,512]{1,0:T(8,128)(2,1)S(1)} %fusion.3), channel_id=1, source_target_pairs={{0,8},{1,9},{2,10},{3,11},{4,12},{5,13},{6,14},{7,15},{8,0},{9,1},... | collective-permute-start | bytes 393224 | tf_op jit(solution)/shard_map/transfer_m1_zh/ppermute | solution.py:905
  89.9 9.0 %collective-permute-done.16 = bf16[2,2,128,512]{3,2,1,0:T(8,128)(2,1)S(1)} collective-permute-done((bf16[2,2,128,512]{3,2,1,0:T(8,128)(2,1)S(1)}, bf16[2,2,128,512]{3,2,1,0:T(8,128)(2,1)S(1)}, u32[]{:S(2)}, u32[]{:S(2)}) %collective-permute-start.16) | collective-permute-done | bytes 524320 | tf_op jit(solution)/shard_map/transfer_m0_x2/ppermute | solution.py:905
  99.1 1.6 collective-permute-start.19
  100.7 2.7 %collective-permute-start.18 = (bf16[128,512]{1,0:T(8,128)(2,1)S(1)}, bf16[128,512]{1,0:T(8,128)(2,1)S(1)}, u32[]{:S(2)}, u32[]{:S(2)}) collective-permute-start(bf16[128,512]{1,0:T(8,128)(2,1)S(1)} %fusion.5), channel_id=1, source_target_pairs={{0,8},{1,9},{2,10},{3,11},{4,12},{5,13},{6,14},{7,15},{8,0},{9,1},... | collective-permute-start | bytes 393224 | tf_op jit(solution)/shard_map/transfer_m1_ZH/ppermute | solution.py:905
  103.4 2.2 %collective-permute-start.24 = (bf16[2,2,2,64,512]{4,3,2,1,0:T(8,128)(2,1)S(1)}, bf16[2,2,2,64,512]{4,3,2,1,0:T(8,128)(2,1)S(1)}, u32[]{:S(2)}, u32[]{:S(2)}) collective-permute-start(bf16[2,2,2,64,512]{4,3,2,1,0:T(8,128)(2,1)S(1)} %bitcast.171), channel_id=1, source_target_pairs={{0,1},{1,0},{2,3},{3,2},{4,5},{5,4},{6,7},{7,6},{8,9},{9,8},{10,11... | collective-permute-start | bytes 1572872 | tf_op jit(solution)/shard_map/transfer_g0_x1/ppermute | solution.py:905
  105.6 2.8 %collective-permute-done.19 = bf16[2,128,512]{2,1,0:T(8,128)(2,1)S(1)} collective-permute-done((bf16[2,128,512]{2,1,0:T(8,128)(2,1)S(1)}, bf16[2,128,512]{2,1,0:T(8,128)(2,1)S(1)}, u32[]{:S(2)}, u32[]{:S(2)}) %collective-permute-start.19) | collective-permute-done | bytes 262176 | tf_op jit(solution)/shard_map/transfer_m0_zl/ppermute | solution.py:905
  109.6 2.5 %collective-permute-start.21 = (bf16[128,512]{1,0:T(8,128)(2,1)S(1)}, bf16[128,512]{1,0:T(8,128)(2,1)S(1)}, u32[]{:S(2)}, u32[]{:S(2)}) collective-permute-start(bf16[128,512]{1,0:T(8,128)(2,1)S(1)} %fusion), channel_id=1, source_target_pairs={{0,8},{1,9},{2,10},{3,11},{4,12},{5,13},{6,14},{7,15},{8,0},{9,1},... | collective-permute-start | bytes 393224 | tf_op jit(solution)/shard_map/transfer_m0_zh/ppermute | solution.py:905
  112.2 1.8 collective-permute-start.27
  114.0 2.6 %collective-permute-start.26 = (bf16[2,2,64,512]{3,2,1,0:T(8,128)(2,1)S(1)}, bf16[2,2,64,512]{3,2,1,0:T(8,128)(2,1)S(1)}, u32[]{:S(2)}, u32[]{:S(2)}) collective-permute-start(bf16[2,2,64,512]{3,2,1,0:T(8,128)(2,1)S(1)} %add_bitcast_fusion.2), channel_id=1, source_target_pairs={{0,2},{1,3},{2,0},{3,1},{4,6},{5,7},{6,4},{7,5},{8,10},{9,11},{10,... | collective-permute-start | bytes 786440 | tf_op jit(solution)/shard_map/transfer_g1_x2/ppermute | solution.py:905
  116.6 2.1 %collective-permute-start.25 = (bf16[2,2,64,512]{3,2,1,0:T(8,128)(2,1)S(1)}, bf16[2,2,64,512]{3,2,1,0:T(8,128)(2,1)S(1)}, u32[]{:S(2)}, u32[]{:S(2)}) collective-permute-start(bf16[2,2,64,512]{3,2,1,0:T(8,128)(2,1)S(1)} %add_bitcast_fusion.3), channel_id=1, source_target_pairs={{0,2},{1,3},{2,0},{3,1},{4,6},{5,7},{6,4},{7,5},{8,10},{9,11},{10,... | collective-permute-start | bytes 786440 | tf_op jit(solution)/shard_map/transfer_g0_x2/ppermute | solution.py:905
  118.7 3.4 %collective-permute-start.23 = (bf16[128,512]{1,0:T(8,128)(2,1)S(1)}, bf16[128,512]{1,0:T(8,128)(2,1)S(1)}, u32[]{:S(2)}, u32[]{:S(2)}) collective-permute-start(bf16[128,512]{1,0:T(8,128)(2,1)S(1)} %fusion.2), channel_id=1, source_target_pairs={{0,8},{1,9},{2,10},{3,11},{4,12},{5,13},{6,14},{7,15},{8,0},{9,1},... | collective-permute-start | bytes 393224 | tf_op jit(solution)/shard_map/transfer_m0_ZH/ppermute | solution.py:905
  122.2 3.7 %collective-permute-start.31 = (bf16[2,2,128,512]{3,2,1,0:T(8,128)(2,1)S(1)}, bf16[2,2,128,512]{3,2,1,0:T(8,128)(2,1)S(1)}, u32[]{:S(2)}, u32[]{:S(2)}) collective-permute-start(bf16[2,2,128,512]{3,2,1,0:T(8,128)(2,1)S(1)} %get-tuple-element.350), channel_id=1, source_target_pairs={{0,2},{1,3},{2,0},{3,1},{4,6},{5,7},{6,4},{7,5},{8,10},{9,11},{10,... | collective-permute-start | bytes 1572872 | tf_op jit(solution)/shard_map/transfer_m1_X2/ppermute | solution.py:905
  125.9 3.7 %collective-permute-start.28 = (bf16[2,128,512]{2,1,0:T(8,128)(2,1)S(1)}, bf16[2,128,512]{2,1,0:T(8,128)(2,1)S(1)}, u32[]{:S(2)}, u32[]{:S(2)}) collective-permute-start(bf16[2,128,512]{2,1,0:T(8,128)(2,1)S(1)} %get-tuple-element.343), channel_id=1, source_target_pairs={{0,4},{1,5},{2,6},{3,7},{4,0},{5,1},{6,2},{7,3},{8,12},{9,13},{10,... | collective-permute-start | bytes 786440 | tf_op jit(solution)/shard_map/transfer_m0_ZL/ppermute | solution.py:905
  129.7 4.3 %collective-permute-done.28 = bf16[2,128,512]{2,1,0:T(8,128)(2,1)S(1)} collective-permute-done((bf16[2,128,512]{2,1,0:T(8,128)(2,1)S(1)}, bf16[2,128,512]{2,1,0:T(8,128)(2,1)S(1)}, u32[]{:S(2)}, u32[]{:S(2)}) %collective-permute-start.28) | collective-permute-done | bytes 262176 | tf_op jit(solution)/shard_map/transfer_m0_ZL/ppermute | solution.py:905
  134.0 3.7 %collective-permute-done.32 = bf16[2,2,64,512]{3,2,1,0:T(8,128)(2,1)S(1)} collective-permute-done((bf16[2,2,64,512]{3,2,1,0:T(8,128)(2,1)S(1)}, bf16[2,2,64,512]{3,2,1,0:T(8,128)(2,1)S(1)}, u32[]{:S(2)}, u32[]{:S(2)}) %collective-permute-start.32) | collective-permute-done | bytes 262176 | tf_op jit(solution)/shard_map/transfer_g1_fl/ppermute | solution.py:905
  138.1 1.7 collective-permute-start.36
  139.8 1.7 collective-permute-start.30
  141.6 2.4 %collective-permute-start.34 = (bf16[2,2,64,512]{3,2,1,0:T(8,128)(2,1)S(1)}, bf16[2,2,64,512]{3,2,1,0:T(8,128)(2,1)S(1)}, u32[]{:S(2)}, u32[]{:S(2)}) collective-permute-start(bf16[2,2,64,512]{3,2,1,0:T(8,128)(2,1)S(1)} %add.169), channel_id=1, source_target_pairs={{0,8},{1,9},{2,10},{3,11},{4,12},{5,13},{6,14},{7,15},{8,0},{9,1},... | collective-permute-start | bytes 786440 | tf_op jit(solution)/shard_map/transfer_g1_fh/ppermute | solution.py:905
  144.0 2.9 %collective-permute-done.30 = bf16[2,2,64,512]{3,2,1,0:T(8,128)(2,1)S(1)} collective-permute-done((bf16[2,2,64,512]{3,2,1,0:T(8,128)(2,1)S(1)}, bf16[2,2,64,512]{3,2,1,0:T(8,128)(2,1)S(1)}, u32[]{:S(2)}, u32[]{:S(2)}) %collective-permute-start.30) | collective-permute-done | bytes 262176 | tf_op jit(solution)/shard_map/transfer_g0_fl/ppermute | solution.py:905
  146.9 5.9 %collective-permute-done.29 = bf16[2,2,128,512]{3,2,1,0:T(8,128)(2,1)S(1)} collective-permute-done((bf16[2,2,128,512]{3,2,1,0:T(8,128)(2,1)S(1)}, bf16[2,2,128,512]{3,2,1,0:T(8,128)(2,1)S(1)}, u32[]{:S(2)}, u32[]{:S(2)}) %collective-permute-start.29) | collective-permute-done | bytes 524320 | tf_op jit(solution)/shard_map/transfer_m0_X2/ppermute | solution.py:905
  153.1 2.4 %collective-permute-start.33 = (bf16[2,2,64,512]{3,2,1,0:T(8,128)(2,1)S(1)}, bf16[2,2,64,512]{3,2,1,0:T(8,128)(2,1)S(1)}, u32[]{:S(2)}, u32[]{:S(2)}) collective-permute-start(bf16[2,2,64,512]{3,2,1,0:T(8,128)(2,1)S(1)} %add.168), channel_id=1, source_target_pairs={{0,8},{1,9},{2,10},{3,11},{4,12},{5,13},{6,14},{7,15},{8,0},{9,1},... | collective-permute-start | bytes 786440 | tf_op jit(solution)/shard_map/transfer_g0_fh/ppermute | solution.py:905
  156.5 6.2 %collective-permute-done.34 = bf16[2,2,64,512]{3,2,1,0:T(8,128)(2,1)S(1)} collective-permute-done((bf16[2,2,64,512]{3,2,1,0:T(8,128)(2,1)S(1)}, bf16[2,2,64,512]{3,2,1,0:T(8,128)(2,1)S(1)}, u32[]{:S(2)}, u32[]{:S(2)}) %collective-permute-start.34) | collective-permute-done | bytes 262176 | tf_op jit(solution)/shard_map/transfer_g1_fh/ppermute | solution.py:905
  163.9 4.1 %collective-permute-done.33 = bf16[2,2,64,512]{3,2,1,0:T(8,128)(2,1)S(1)} collective-permute-done((bf16[2,2,64,512]{3,2,1,0:T(8,128)(2,1)S(1)}, bf16[2,2,64,512]{3,2,1,0:T(8,128)(2,1)S(1)}, u32[]{:S(2)}, u32[]{:S(2)}) %collective-permute-start.33) | collective-permute-done | bytes 262176 | tf_op jit(solution)/shard_map/transfer_g0_fh/ppermute | solution.py:905
  169.3 2.6 %collective-permute-start.38 = (bf16[2048,512]{1,0:T(8,128)(2,1)S(1)}, bf16[2048,512]{1,0:T(8,128)(2,1)}, u32[]{:S(2)}, u32[]{:S(2)}) collective-permute-start(bf16[2048,512]{1,0:T(8,128)(2,1)S(1)} %bitcast.143), channel_id=1, source_target_pairs={{0,16},{1,17},{2,18},{3,19},{4,20},{5,21},{6,22},{7,23},{8,24},{9,... | collective-permute-start | bytes 6291464 | tf_op jit(solution)/shard_map/transfer_m1_Core/ppermute | solution.py:905
  173.6 2.0 collective-permute-start.35
  175.6 2.0 collective-permute-start.42
  177.6 3.2 %mlp_finish.2 = (f32[2048,512]{1,0:T(8,128)}, f32[512,2048]{1,0:T(8,128)}) custom-call(bf16[2048,512]{1,0:T(8,128)(2,1)} %bitcast.142, bf16[2048,512]{1,0:T(8,128)(2,1)} %bitcast.144), custom_call_target="tpu_custom_call" | custom-call | tf_op jit(solution)/shard_map/mlp_finish/pallas_call | solution.py:757
  181.9 2.0 collective-permute-start.40
  183.9 3.4 %collective-permute-done.42 = bf16[2,2,2,64,512]{4,3,2,1,0:T(8,128)(2,1)} collective-permute-done((bf16[2,2,2,64,512]{4,3,2,1,0:T(8,128)(2,1)S(1)}, bf16[2,2,2,64,512]{4,3,2,1,0:T(8,128)(2,1)}, u32[]{:S(2)}, u32[]{:S(2)}) %collective-permute-start.42) | collective-permute-done | bytes 524320 | tf_op jit(solution)/shard_map/transfer_g1_X1/ppermute | solution.py:905
  188.4 2.2 %collective-permute-start.44 = (bf16[1024,512]{1,0:T(8,128)(2,1)S(1)}, bf16[1024,512]{1,0:T(8,128)(2,1)S(1)}, u32[]{:S(2)}, u32[]{:S(2)}) collective-permute-start(bf16[1024,512]{1,0:T(8,128)(2,1)S(1)} %bitcast.147), channel_id=1, source_target_pairs={{0,16},{1,17},{2,18},{3,19},{4,20},{5,21},{6,22},{7,23},{8,24},{9,... | collective-permute-start | bytes 3145736 | tf_op jit(solution)/shard_map/transfer_g1_Core/ppermute | solution.py:905
  190.6 3.3 %mlp_finish.3 = (f32[2048,512]{1,0:T(8,128)}, f32[512,2048]{1,0:T(8,128)}) custom-call(bf16[2048,512]{1,0:T(8,128)(2,1)} %collective-permute-done.41.refs_0_, bf16[2048,512]{1,0:T(8,128)(2,1)} %collective-permute-done.38.refs_1_, f32[2048,512]{1,0:T(8,128)} %get-tuple-element.378.refs_2_, ...), custom_call_target="tpu_custom_call", output_to_operand_aliasing={{0}: (2, {}), {1}: (3, {})} | custom-call | tf_op jit(solution)/shard_map/mlp_finish/pallas_call | solution.py:757
  196.4 2.9 %gn_finish.2 = (f32[1,512]{1,0:T(1,128)}, f32[1,512]{1,0:T(1,128)}, f32[512,1024]{1,0:T(8,128)}, f32[1,1024]{1,0:T(1,128)}, f32[49,1,960]{2,1,0:T(1,128)}, /*ind...) custom-call(bf16[1024,512]{1,0:T(8,128)(2,1)} %bitcast.150, ...), custom_call_target="tpu_custom_call" | custom-call | tf_op jit(solution)/shard_map/gn_finish/pallas_call | solution.py:757
  200.6 2.8 %gn_finish.3 = (f32[1,512]{1,0:T(1,128)}, f32[1,512]{1,0:T(1,128)}, f32[512,1024]{1,0:T(8,128)}, f32[1,1024]{1,0:T(1,128)}, f32[49,1,960]{2,1,0:T(1,128)}, /*ind...) custom-call(bf16[1024,512]{1,0:T(8,128)(2,1)} %copy-done.37, ...), custom_call_target="tpu_custom_call", output_to_operand_aliasing={{0}: (2, {}), {1}: (3, {}), {2}: (4, {}), {3}: (5, {}), {4}... | custom-call | tf_op jit(solution)/shard_map/gn_finish/pallas_call | solution.py:757
  (172 shorter events, 23.7 us)
Async XLA Ops:
  0.7 5.3 %collective-permute-start.1 = (bf16[512,1024]{1,0:T(8,128)(2,1)}, bf16[512,1024]{1,0:T(8,128)(2,1)S(1)}, u32[]{:S(2)}, u32[]{:S(2)}) collective-permute-start(bf16[512,1024]{1,0:T(8,128)(2,1)} %bitcast.121), channel_id=1, source_target_pairs={{0,16},{1,17},{2,18},{3,19},{4,20},{5,21},{6,22},{7,23},{8,24},{9,... | collective-permute-start | bytes 3145736 | tf_op jit(solution)/shard_map/ppermute | solution.py:905
  1.2 4.7 %collective-permute-start.4 = (bf16[512,512]{1,0:T(8,128)(2,1)}, bf16[512,512]{1,0:T(8,128)(2,1)S(1)}, u32[]{:S(2)}, u32[]{:S(2)}) collective-permute-start(bf16[512,512]{1,0:T(8,128)(2,1)} %bitcast.126), channel_id=1, source_target_pairs={{0,16},{1,17},{2,18},{3,19},{4,20},{5,21},{6,22},{7,23},{8,24},{9,... | collective-permute-start | bytes 1572872 | tf_op jit(solution)/shard_map/ppermute | solution.py:905
  3.4 2.5 %collective-permute-start.3 = (bf16[384,512]{1,0:T(8,128)(2,1)}, bf16[384,512]{1,0:T(8,128)(2,1)S(1)}, u32[]{:S(2)}, u32[]{:S(2)}) collective-permute-start(bf16[384,512]{1,0:T(8,128)(2,1)} %get-tuple-element.232.refs_8_.refs_14_.refs_9_), channel_id=1, source_target_pairs={{0,16},{1,17},{2,18},{3,19},{4,20},{5,21},{6,22},{7,23},{8,24},{9,... | collective-permute-start | bytes 1179656 | tf_op jit(solution)/shard_map/ppermute | solution.py:905
  3.8 2.0 %collective-permute-start.2 = (f32[400,128]{1,0:T(8,128)}, f32[400,128]{1,0:T(8,128)S(1)}, u32[]{:S(2)}, u32[]{:S(2)}) collective-permute-start(f32[400,128]{1,0:T(8,128)} %get-tuple-element.231.refs_6_.refs_12_), channel_id=1, source_target_pairs={{0,16},{1,17},{2,18},{3,19},{4,20},{5,21},{6,22},{7,23},{8,24},{9,... | collective-permute-start | bytes 614408 | tf_op jit(solution)/shard_map/ppermute | solution.py:905
  3.9 2.0 collective-permute-start
  5.9 9.2 %collective-permute-start.5 = (bf16[512,2048]{1,0:T(8,128)(2,1)}, bf16[512,2048]{1,0:T(8,128)(2,1)S(1)}, u32[]{:S(2)}, u32[]{:S(2)}) collective-permute-start(bf16[512,2048]{1,0:T(8,128)(2,1)} %bitcast.133), channel_id=1, source_target_pairs={{0,16},{1,17},{2,18},{3,19},{4,20},{5,21},{6,22},{7,23},{8,24},{9,... | collective-permute-start | bytes 6291464 | tf_op jit(solution)/shard_map/ppermute | solution.py:905
  6.4 8.8 %collective-permute-start.6 = (bf16[2048,512]{1,0:T(8,128)(2,1)}, bf16[2048,512]{1,0:T(8,128)(2,1)}, u32[]{:S(2)}, u32[]{:S(2)}) collective-permute-start(bf16[2048,512]{1,0:T(8,128)(2,1)} %bitcast.137), channel_id=1, source_target_pairs={{0,16},{1,17},{2,18},{3,19},{4,20},{5,21},{6,22},{7,23},{8,24},{9,... | collective-permute-start | bytes 6291464 | tf_op jit(solution)/shard_map/ppermute | solution.py:905
  32.5 9.7 %collective-permute-start.8 = (bf16[2048,512]{1,0:T(8,128)(2,1)}, bf16[2048,512]{1,0:T(8,128)(2,1)S(1)}, u32[]{:S(2)}, u32[]{:S(2)}) collective-permute-start(bf16[2048,512]{1,0:T(8,128)(2,1)} %get-tuple-element.249), channel_id=1, source_target_pairs={{0,16},{1,17},{2,18},{3,19},{4,20},{5,21},{6,22},{7,23},{8,24},{9,... | collective-permute-start | bytes 6291464 | tf_op jit(solution)/shard_map/transfer_m1_core/ppermute | solution.py:905
  43.4 17.3 %collective-permute-start.9 = (bf16[2,2,2,128,512]{4,3,2,1,0:T(8,128)(2,1)}, bf16[2,2,2,128,512]{4,3,2,1,0:T(8,128)(2,1)S(1)}, u32[]{:S(2)}, u32[]{:S(2)}) collective-permute-start(bf16[2,2,2,128,512]{4,3,2,1,0:T(8,128)(2,1)} %bitcast.12), channel_id=1, source_target_pairs={{0,1},{1,0},{2,3},{3,2},{4,5},{5,4},{6,7},{7,6},{8,9},{9,8},{10,11... | collective-permute-start | bytes 3145736 | tf_op jit(solution)/shard_map/transfer_m1_x1/ppermute | solution.py:905
  53.2 12.0 %copy-start.33 = (bf16[2048,512]{1,0:T(8,128)(2,1)S(1)}, bf16[2048,512]{1,0:T(8,128)(2,1)}, u32[]{:S(2)}) copy-start(bf16[2048,512]{1,0:T(8,128)(2,1)} %get-tuple-element.300) | copy-start | bytes 6291460
  60.8 4.4 %collective-permute-start.11 = (bf16[2048,512]{1,0:T(8,128)(2,1)}, bf16[2048,512]{1,0:T(8,128)(2,1)S(1)}, u32[]{:S(2)}, u32[]{:S(2)}) collective-permute-start(bf16[2048,512]{1,0:T(8,128)(2,1)} %get-tuple-element.274), channel_id=1, source_target_pairs={{0,16},{1,17},{2,18},{3,19},{4,20},{5,21},{6,22},{7,23},{8,24},{9,... | collective-permute-start | bytes 6291464 | tf_op jit(solution)/shard_map/transfer_m0_core/ppermute | solution.py:905
  60.9 16.9 %collective-permute-start.13 = (bf16[1024,512]{1,0:T(8,128)(2,1)}, bf16[1024,512]{1,0:T(8,128)(2,1)S(1)}, u32[]{:S(2)}, u32[]{:S(2)}) collective-permute-start(bf16[1024,512]{1,0:T(8,128)(2,1)} %get-tuple-element.291), channel_id=1, source_target_pairs={{0,16},{1,17},{2,18},{3,19},{4,20},{5,21},{6,22},{7,23},{8,24},{9,... | collective-permute-start | bytes 3145736 | tf_op jit(solution)/shard_map/transfer_g1_core/ppermute | solution.py:905
  61.5 14.6 %collective-permute-start.10 = (bf16[2,2,128,512]{3,2,1,0:T(8,128)(2,1)S(1)}, bf16[2,2,128,512]{3,2,1,0:T(8,128)(2,1)S(1)}, u32[]{:S(2)}, u32[]{:S(2)}) collective-permute-start(bf16[2,2,128,512]{3,2,1,0:T(8,128)(2,1)S(1)} %add_bitcast_fusion.1), channel_id=1, source_target_pairs={{0,2},{1,3},{2,0},{3,1},{4,6},{5,7},{6,4},{7,5},{8,10},{9,11},{10,... | collective-permute-start | bytes 1572872 | tf_op jit(solution)/shard_map/transfer_m1_x2/ppermute | solution.py:905
  65.6 19.0 %collective-permute-start.15 = (bf16[2,2,2,128,512]{4,3,2,1,0:T(8,128)(2,1)S(1)}, bf16[2,2,2,128,512]{4,3,2,1,0:T(8,128)(2,1)S(1)}, u32[]{:S(2)}, u32[]{:S(2)}) collective-permute-start(bf16[2,2,2,128,512]{4,3,2,1,0:T(8,128)(2,1)S(1)} %bitcast.162), channel_id=1, source_target_pairs={{0,1},{1,0},{2,3},{3,2},{4,5},{5,4},{6,7},{7,6},{8,9},{9,8},{10,11... | collective-permute-start | bytes 3145736 | tf_op jit(solution)/shard_map/transfer_m0_x1/ppermute | solution.py:905
  76.2 8.4 %collective-permute-start.12 = (bf16[2,128,512]{2,1,0:T(8,128)(2,1)S(1)}, bf16[2,128,512]{2,1,0:T(8,128)(2,1)S(1)}, u32[]{:S(2)}, u32[]{:S(2)}) collective-permute-start(bf16[2,128,512]{2,1,0:T(8,128)(2,1)S(1)} %slice_bitcast_fusion.1), channel_id=1, source_target_pairs={{0,4},{1,5},{2,6},{3,7},{4,0},{5,1},{6,2},{7,3},{8,12},{9,13},{10,... | collective-permute-start | bytes 786440 | tf_op jit(solution)/shard_map/transfer_m1_zl/ppermute | solution.py:905
  77.8 30.6 %collective-permute-start.7 = (bf16[256,512]{1,0:T(8,128)(2,1)S(1)}, bf16[256,512]{1,0:T(8,128)(2,1)S(1)}, u32[]{:S(2)}, u32[]{:S(2)}) collective-permute-start(bf16[256,512]{1,0:T(8,128)(2,1)S(1)} %copy-done.38), channel_id=1, source_target_pairs={{0,16},{1,17},{2,18},{3,19},{4,20},{5,21},{6,22},{7,23},{8,24},{9,... | collective-permute-start | bytes 786440 | tf_op jit(solution)/shard_map/transfer_fo/ppermute | solution.py:905
  84.6 5.2 %collective-permute-start.17 = (bf16[1024,512]{1,0:T(8,128)(2,1)S(1)}, bf16[1024,512]{1,0:T(8,128)(2,1)S(1)}, u32[]{:S(2)}, u32[]{:S(2)}) collective-permute-start(bf16[1024,512]{1,0:T(8,128)(2,1)S(1)} %get-tuple-element.307), channel_id=1, source_target_pairs={{0,16},{1,17},{2,18},{3,19},{4,20},{5,21},{6,22},{7,23},{8,24},{9,... | collective-permute-start | bytes 3145736 | tf_op jit(solution)/shard_map/transfer_g0_core/ppermute | solution.py:905
  84.9 14.1 %collective-permute-start.16 = (bf16[2,2,128,512]{3,2,1,0:T(8,128)(2,1)S(1)}, bf16[2,2,128,512]{3,2,1,0:T(8,128)(2,1)S(1)}, u32[]{:S(2)}, u32[]{:S(2)}) collective-permute-start(bf16[2,2,128,512]{3,2,1,0:T(8,128)(2,1)S(1)} %add_bitcast_fusion), channel_id=1, source_target_pairs={{0,2},{1,3},{2,0},{3,1},{4,6},{5,7},{6,4},{7,5},{8,10},{9,11},{10,... | collective-permute-start | bytes 1572872 | tf_op jit(solution)/shard_map/transfer_m0_x2/ppermute | solution.py:905
  86.5 23.1 %collective-permute-start.22 = (bf16[2,2,2,64,512]{4,3,2,1,0:T(8,128)(2,1)S(1)}, bf16[2,2,2,64,512]{4,3,2,1,0:T(8,128)(2,1)S(1)}, u32[]{:S(2)}, u32[]{:S(2)}) collective-permute-start(bf16[2,2,2,64,512]{4,3,2,1,0:T(8,128)(2,1)S(1)} %bitcast.170), channel_id=1, source_target_pairs={{0,1},{1,0},{2,3},{3,2},{4,5},{5,4},{6,7},{7,6},{8,9},{9,8},{10,11... | collective-permute-start | bytes 1572872 | tf_op jit(solution)/shard_map/transfer_g1_x1/ppermute | solution.py:905
  87.1 11.9 %collective-permute-start.14 = (bf16[128,512]{1,0:T(8,128)(2,1)S(1)}, bf16[128,512]{1,0:T(8,128)(2,1)S(1)}, u32[]{:S(2)}, u32[]{:S(2)}) collective-permute-start(bf16[128,512]{1,0:T(8,128)(2,1)S(1)} %fusion.3), channel_id=1, source_target_pairs={{0,8},{1,9},{2,10},{3,11},{4,12},{5,13},{6,14},{7,15},{8,0},{9,1},... | collective-permute-start | bytes 393224 | tf_op jit(solution)/shard_map/transfer_m1_zh/ppermute | solution.py:905
  99.0 9.5 %copy-start.21 = (bf16[256,512]{1,0:T(8,128)(2,1)S(1)}, bf16[256,512]{1,0:T(8,128)(2,1)}, u32[]{:S(2)}) copy-start(bf16[256,512]{1,0:T(8,128)(2,1)} %get-tuple-element.236.refs_16_.first) | copy-start | bytes 786436
  99.0 9.5 %copy-start.24 = (bf16[256,512]{1,0:T(8,128)(2,1)S(1)}, bf16[256,512]{1,0:T(8,128)(2,1)}, u32[]{:S(2)}) copy-start(bf16[256,512]{1,0:T(8,128)(2,1)} %get-tuple-element.237.second) | copy-start | bytes 786436
  99.1 9.4 %collective-permute-start.19 = (bf16[2,128,512]{2,1,0:T(8,128)(2,1)S(1)}, bf16[2,128,512]{2,1,0:T(8,128)(2,1)S(1)}, u32[]{:S(2)}, u32[]{:S(2)}) collective-permute-start(bf16[2,128,512]{2,1,0:T(8,128)(2,1)S(1)} %slice_bitcast_fusion), channel_id=1, source_target_pairs={{0,4},{1,5},{2,6},{3,7},{4,0},{5,1},{6,2},{7,3},{8,12},{9,13},{10,... | collective-permute-start | bytes 786440 | tf_op jit(solution)/shard_map/transfer_m0_zl/ppermute | solution.py:905
  100.7 7.8 %collective-permute-start.18 = (bf16[128,512]{1,0:T(8,128)(2,1)S(1)}, bf16[128,512]{1,0:T(8,128)(2,1)S(1)}, u32[]{:S(2)}, u32[]{:S(2)}) collective-permute-start(bf16[128,512]{1,0:T(8,128)(2,1)S(1)} %fusion.5), channel_id=1, source_target_pairs={{0,8},{1,9},{2,10},{3,11},{4,12},{5,13},{6,14},{7,15},{8,0},{9,1},... | collective-permute-start | bytes 393224 | tf_op jit(solution)/shard_map/transfer_m1_ZH/ppermute | solution.py:905
  103.4 13.2 %collective-permute-start.24 = (bf16[2,2,2,64,512]{4,3,2,1,0:T(8,128)(2,1)S(1)}, bf16[2,2,2,64,512]{4,3,2,1,0:T(8,128)(2,1)S(1)}, u32[]{:S(2)}, u32[]{:S(2)}) collective-permute-start(bf16[2,2,2,64,512]{4,3,2,1,0:T(8,128)(2,1)S(1)} %bitcast.171), channel_id=1, source_target_pairs={{0,1},{1,0},{2,3},{3,2},{4,5},{5,4},{6,7},{7,6},{8,9},{9,8},{10,11... | collective-permute-start | bytes 1572872 | tf_op jit(solution)/shard_map/transfer_g0_x1/ppermute | solution.py:905
  109.6 7.0 %collective-permute-start.21 = (bf16[128,512]{1,0:T(8,128)(2,1)S(1)}, bf16[128,512]{1,0:T(8,128)(2,1)S(1)}, u32[]{:S(2)}, u32[]{:S(2)}) collective-permute-start(bf16[128,512]{1,0:T(8,128)(2,1)S(1)} %fusion), channel_id=1, source_target_pairs={{0,8},{1,9},{2,10},{3,11},{4,12},{5,13},{6,14},{7,15},{8,0},{9,1},... | collective-permute-start | bytes 393224 | tf_op jit(solution)/shard_map/transfer_m0_zh/ppermute | solution.py:905
  112.2 9.9 %collective-permute-start.27 = (bf16[2,128,512]{2,1,0:T(8,128)(2,1)S(1)}, bf16[2,128,512]{2,1,0:T(8,128)(2,1)S(1)}, u32[]{:S(2)}, u32[]{:S(2)}) collective-permute-start(bf16[2,128,512]{2,1,0:T(8,128)(2,1)S(1)} %get-tuple-element.337), channel_id=1, source_target_pairs={{0,4},{1,5},{2,6},{3,7},{4,0},{5,1},{6,2},{7,3},{8,12},{9,13},{10,... | collective-permute-start | bytes 786440 | tf_op jit(solution)/shard_map/transfer_m1_ZL/ppermute | solution.py:905
  114.0 8.2 %collective-permute-start.26 = (bf16[2,2,64,512]{3,2,1,0:T(8,128)(2,1)S(1)}, bf16[2,2,64,512]{3,2,1,0:T(8,128)(2,1)S(1)}, u32[]{:S(2)}, u32[]{:S(2)}) collective-permute-start(bf16[2,2,64,512]{3,2,1,0:T(8,128)(2,1)S(1)} %add_bitcast_fusion.2), channel_id=1, source_target_pairs={{0,2},{1,3},{2,0},{3,1},{4,6},{5,7},{6,4},{7,5},{8,10},{9,11},{10,... | collective-permute-start | bytes 786440 | tf_op jit(solution)/shard_map/transfer_g1_x2/ppermute | solution.py:905
  116.6 9.3 %collective-permute-start.25 = (bf16[2,2,64,512]{3,2,1,0:T(8,128)(2,1)S(1)}, bf16[2,2,64,512]{3,2,1,0:T(8,128)(2,1)S(1)}, u32[]{:S(2)}, u32[]{:S(2)}) collective-permute-start(bf16[2,2,64,512]{3,2,1,0:T(8,128)(2,1)S(1)} %add_bitcast_fusion.3), channel_id=1, source_target_pairs={{0,2},{1,3},{2,0},{3,1},{4,6},{5,7},{6,4},{7,5},{8,10},{9,11},{10,... | collective-permute-start | bytes 786440 | tf_op jit(solution)/shard_map/transfer_g0_x2/ppermute | solution.py:905
  118.7 7.2 %collective-permute-start.23 = (bf16[128,512]{1,0:T(8,128)(2,1)S(1)}, bf16[128,512]{1,0:T(8,128)(2,1)S(1)}, u32[]{:S(2)}, u32[]{:S(2)}) collective-permute-start(bf16[128,512]{1,0:T(8,128)(2,1)S(1)} %fusion.2), channel_id=1, source_target_pairs={{0,8},{1,9},{2,10},{3,11},{4,12},{5,13},{6,14},{7,15},{8,0},{9,1},... | collective-permute-start | bytes 393224 | tf_op jit(solution)/shard_map/transfer_m0_ZH/ppermute | solution.py:905
  122.2 15.6 %collective-permute-start.31 = (bf16[2,2,128,512]{3,2,1,0:T(8,128)(2,1)S(1)}, bf16[2,2,128,512]{3,2,1,0:T(8,128)(2,1)S(1)}, u32[]{:S(2)}, u32[]{:S(2)}) collective-permute-start(bf16[2,2,128,512]{3,2,1,0:T(8,128)(2,1)S(1)} %get-tuple-element.350), channel_id=1, source_target_pairs={{0,2},{1,3},{2,0},{3,1},{4,6},{5,7},{6,4},{7,5},{8,10},{9,11},{10,... | collective-permute-start | bytes 1572872 | tf_op jit(solution)/shard_map/transfer_m1_X2/ppermute | solution.py:905
  125.9 8.1 %collective-permute-start.28 = (bf16[2,128,512]{2,1,0:T(8,128)(2,1)S(1)}, bf16[2,128,512]{2,1,0:T(8,128)(2,1)S(1)}, u32[]{:S(2)}, u32[]{:S(2)}) collective-permute-start(bf16[2,128,512]{2,1,0:T(8,128)(2,1)S(1)} %get-tuple-element.343), channel_id=1, source_target_pairs={{0,4},{1,5},{2,6},{3,7},{4,0},{5,1},{6,2},{7,3},{8,12},{9,13},{10,... | collective-permute-start | bytes 786440 | tf_op jit(solution)/shard_map/transfer_m0_ZL/ppermute | solution.py:905
  129.6 8.1 %collective-permute-start.32 = (bf16[2,2,64,512]{3,2,1,0:T(8,128)(2,1)S(1)}, bf16[2,2,64,512]{3,2,1,0:T(8,128)(2,1)S(1)}, u32[]{:S(2)}, u32[]{:S(2)}) collective-permute-start(bf16[2,2,64,512]{3,2,1,0:T(8,128)(2,1)S(1)} %bitcast_add_fusion.2), channel_id=1, source_target_pairs={{0,4},{1,5},{2,6},{3,7},{4,0},{5,1},{6,2},{7,3},{8,12},{9,13},{10,... | collective-permute-start | bytes 786440 | tf_op jit(solution)/shard_map/transfer_g1_fl/ppermute | solution.py:905
  137.8 14.9 %collective-permute-start.29 = (bf16[2,2,128,512]{3,2,1,0:T(8,128)(2,1)S(1)}, bf16[2,2,128,512]{3,2,1,0:T(8,128)(2,1)S(1)}, u32[]{:S(2)}, u32[]{:S(2)}) collective-permute-start(bf16[2,2,128,512]{3,2,1,0:T(8,128)(2,1)S(1)} %get-tuple-element.346), channel_id=1, source_target_pairs={{0,2},{1,3},{2,0},{3,1},{4,6},{5,7},{6,4},{7,5},{8,10},{9,11},{10,... | collective-permute-start | bytes 1572872 | tf_op jit(solution)/shard_map/transfer_m0_X2/ppermute | solution.py:905
  138.1 31.1 %collective-permute-start.36 = (bf16[2,2,2,128,512]{4,3,2,1,0:T(8,128)(2,1)S(1)}, bf16[2,2,2,128,512]{4,3,2,1,0:T(8,128)(2,1)S(1)}, u32[]{:S(2)}, u32[]{:S(2)}) collective-permute-start(bf16[2,2,2,128,512]{4,3,2,1,0:T(8,128)(2,1)S(1)} %get-tuple-element.367), channel_id=1, source_target_pairs={{0,1},{1,0},{2,3},{3,2},{4,5},{5,4},{6,7},{7,6},{8,9},{9,8},{10,11... | collective-permute-start | bytes 3145736 | tf_op jit(solution)/shard_map/transfer_m1_X1/ppermute | solution.py:905
  139.8 7.1 %collective-permute-start.30 = (bf16[2,2,64,512]{3,2,1,0:T(8,128)(2,1)S(1)}, bf16[2,2,64,512]{3,2,1,0:T(8,128)(2,1)S(1)}, u32[]{:S(2)}, u32[]{:S(2)}) collective-permute-start(bf16[2,2,64,512]{3,2,1,0:T(8,128)(2,1)S(1)} %bitcast_add_fusion.3), channel_id=1, source_target_pairs={{0,4},{1,5},{2,6},{3,7},{4,0},{5,1},{6,2},{7,3},{8,12},{9,13},{10,... | collective-permute-start | bytes 786440 | tf_op jit(solution)/shard_map/transfer_g0_fl/ppermute | solution.py:905
  141.5 13.9 %collective-permute-start.20 = (f32[256,512]{1,0:T(8,128)S(1)}, f32[256,512]{1,0:T(8,128)S(1)}, u32[]{:S(2)}, u32[]{:S(2)}) collective-permute-start(f32[256,512]{1,0:T(8,128)S(1)} %get-tuple-element.320), channel_id=1, source_target_pairs={{0,16},{1,17},{2,18},{3,19},{4,20},{5,21},{6,22},{7,23},{8,24},{9,... | collective-permute-start | bytes 1572872 | tf_op jit(solution)/shard_map/transfer_go/ppermute | solution.py:905
  141.6 21.0 %collective-permute-start.34 = (bf16[2,2,64,512]{3,2,1,0:T(8,128)(2,1)S(1)}, bf16[2,2,64,512]{3,2,1,0:T(8,128)(2,1)S(1)}, u32[]{:S(2)}, u32[]{:S(2)}) collective-permute-start(bf16[2,2,64,512]{3,2,1,0:T(8,128)(2,1)S(1)} %add.169), channel_id=1, source_target_pairs={{0,8},{1,9},{2,10},{3,11},{4,12},{5,13},{6,14},{7,15},{8,0},{9,1},... | collective-permute-start | bytes 786440 | tf_op jit(solution)/shard_map/transfer_g1_fh/ppermute | solution.py:905
  152.9 19.1 %collective-permute-start.39 = (bf16[2,2,2,128,512]{4,3,2,1,0:T(8,128)(2,1)S(1)}, bf16[2,2,2,128,512]{4,3,2,1,0:T(8,128)(2,1)S(1)}, u32[]{:S(2)}, u32[]{:S(2)}) collective-permute-start(bf16[2,2,2,128,512]{4,3,2,1,0:T(8,128)(2,1)S(1)} %get-tuple-element.375), channel_id=1, source_target_pairs={{0,1},{1,0},{2,3},{3,2},{4,5},{5,4},{6,7},{7,6},{8,9},{9,8},{10,11... | collective-permute-start | bytes 3145736 | tf_op jit(solution)/shard_map/transfer_m0_X1/ppermute | solution.py:905
  153.1 14.9 %collective-permute-start.33 = (bf16[2,2,64,512]{3,2,1,0:T(8,128)(2,1)S(1)}, bf16[2,2,64,512]{3,2,1,0:T(8,128)(2,1)S(1)}, u32[]{:S(2)}, u32[]{:S(2)}) collective-permute-start(bf16[2,2,64,512]{3,2,1,0:T(8,128)(2,1)S(1)} %add.168), channel_id=1, source_target_pairs={{0,8},{1,9},{2,10},{3,11},{4,12},{5,13},{6,14},{7,15},{8,0},{9,1},... | collective-permute-start | bytes 786440 | tf_op jit(solution)/shard_map/transfer_g0_fh/ppermute | solution.py:905
  162.7 6.4 %collective-permute-start.37 = (bf16[2,2,64,512]{3,2,1,0:T(8,128)(2,1)S(1)}, bf16[2,2,64,512]{3,2,1,0:T(8,128)(2,1)S(1)}, u32[]{:S(2)}, u32[]{:S(2)}) collective-permute-start(bf16[2,2,64,512]{3,2,1,0:T(8,128)(2,1)S(1)} %add.171), channel_id=1, source_target_pairs={{0,2},{1,3},{2,0},{3,1},{4,6},{5,7},{6,4},{7,5},{8,10},{9,11},{10,... | collective-permute-start | bytes 786440 | tf_op jit(solution)/shard_map/transfer_g1_X2/ppermute | solution.py:905
  169.3 11.5 %collective-permute-start.38 = (bf16[2048,512]{1,0:T(8,128)(2,1)S(1)}, bf16[2048,512]{1,0:T(8,128)(2,1)}, u32[]{:S(2)}, u32[]{:S(2)}) collective-permute-start(bf16[2048,512]{1,0:T(8,128)(2,1)S(1)} %bitcast.143), channel_id=1, source_target_pairs={{0,16},{1,17},{2,18},{3,19},{4,20},{5,21},{6,22},{7,23},{8,24},{9,... | collective-permute-start | bytes 6291464 | tf_op jit(solution)/shard_map/transfer_m1_Core/ppermute | solution.py:905
  172.2 18.4 %collective-permute-start.41 = (bf16[2048,512]{1,0:T(8,128)(2,1)S(1)}, bf16[2048,512]{1,0:T(8,128)(2,1)}, u32[]{:S(2)}, u32[]{:S(2)}) collective-permute-start(bf16[2048,512]{1,0:T(8,128)(2,1)S(1)} %bitcast.141), channel_id=1, source_target_pairs={{16,0},{17,1},{18,2},{19,3},{20,4},{21,5},{22,6},{23,7},{24,8},{25... | collective-permute-start | bytes 6291464 | tf_op jit(solution)/shard_map/transfer_m0_Core/ppermute | solution.py:905
  173.6 7.3 %collective-permute-start.35 = (bf16[2,2,64,512]{3,2,1,0:T(8,128)(2,1)S(1)}, bf16[2,2,64,512]{3,2,1,0:T(8,128)(2,1)}, u32[]{:S(2)}, u32[]{:S(2)}) collective-permute-start(bf16[2,2,64,512]{3,2,1,0:T(8,128)(2,1)S(1)} %add.170), channel_id=1, source_target_pairs={{0,2},{1,3},{2,0},{3,1},{4,6},{5,7},{6,4},{7,5},{8,10},{9,11},{10,... | collective-permute-start | bytes 786440 | tf_op jit(solution)/shard_map/transfer_g0_X2/ppermute | solution.py:905
  175.6 11.6 %collective-permute-start.42 = (bf16[2,2,2,64,512]{4,3,2,1,0:T(8,128)(2,1)S(1)}, bf16[2,2,2,64,512]{4,3,2,1,0:T(8,128)(2,1)}, u32[]{:S(2)}, u32[]{:S(2)}) collective-permute-start(bf16[2,2,2,64,512]{4,3,2,1,0:T(8,128)(2,1)S(1)} %get-tuple-element.383), channel_id=1, source_target_pairs={{0,1},{1,0},{2,3},{3,2},{4,5},{5,4},{6,7},{7,6},{8,9},{9,8},{10,11... | collective-permute-start | bytes 1572872 | tf_op jit(solution)/shard_map/transfer_g1_X1/ppermute | solution.py:905
  181.9 12.0 %collective-permute-start.40 = (bf16[2,2,2,64,512]{4,3,2,1,0:T(8,128)(2,1)S(1)}, bf16[2,2,2,64,512]{4,3,2,1,0:T(8,128)(2,1)}, u32[]{:S(2)}, u32[]{:S(2)}) collective-permute-start(bf16[2,2,2,64,512]{4,3,2,1,0:T(8,128)(2,1)S(1)} %get-tuple-element.381), channel_id=1, source_target_pairs={{0,1},{1,0},{2,3},{3,2},{4,5},{5,4},{6,7},{7,6},{8,9},{9,8},{10,11... | collective-permute-start | bytes 1572872 | tf_op jit(solution)/shard_map/transfer_g0_X1/ppermute | solution.py:905
  188.4 10.9 %collective-permute-start.44 = (bf16[1024,512]{1,0:T(8,128)(2,1)S(1)}, bf16[1024,512]{1,0:T(8,128)(2,1)S(1)}, u32[]{:S(2)}, u32[]{:S(2)}) collective-permute-start(bf16[1024,512]{1,0:T(8,128)(2,1)S(1)} %bitcast.147), channel_id=1, source_target_pairs={{0,16},{1,17},{2,18},{3,19},{4,20},{5,21},{6,22},{7,23},{8,24},{9,... | collective-permute-start | bytes 3145736 | tf_op jit(solution)/shard_map/transfer_g1_Core/ppermute | solution.py:905
  195.1 4.6 %collective-permute-start.43 = (bf16[1024,512]{1,0:T(8,128)(2,1)S(1)}, bf16[1024,512]{1,0:T(8,128)(2,1)S(1)}, u32[]{:S(2)}, u32[]{:S(2)}) collective-permute-start(bf16[1024,512]{1,0:T(8,128)(2,1)S(1)} %bitcast.149), channel_id=1, source_target_pairs={{16,0},{17,1},{18,2},{19,3},{20,4},{21,5},{22,6},{23,7},{24,8},{25... | collective-permute-start | bytes 3145736 | tf_op jit(solution)/shard_map/transfer_g0_Core/ppermute | solution.py:905
  (36 other events, 89.1 us)

commit v5 on v4

--- a/solution.py
+++ b/solution.py
@@ -868,10 +868,10 @@
 KERNELS = ("K1", "K2", "K3", "K4", "K5", "MF1", "MF2", "GF1", "GF2", "P1", "P2")
 
 ORDER = (
-    1, 60, 49, -1, 2, 62, 61, 13, -2, 3, 25, -25, 26, 63, -3, 4, 50, -13, 14, 64, -4, 5, -26, 27, 37, -37, 38, -27,
-    28, -5, 8, -28, 29, -8, 9, -49, 69, -14, 15, -29, 32, -38, 39, -9, 10, -15, 18, -39, 42, -32, 33, -33, 34, -18,
-    19, -10, 11, -42, 43, -34, 35, -50, 70, -19, 22, -43, 46, -22, 23, -11, 12, -35, 36, 65, -12, -46, 47, -23, 24,
-    -36, 66, -47, 48, 67, -24, -48, 68,
+    1, -1, 2, 60, 62, -2, 3, 25, 61, -25, 26, -3, 4, 13, 63, 50, -4, 5, -26, 27, 64, -13, 14, -27, 28, -5, 8, 49, 37,
+    -37, 38, -28, 29, -8, 9, -29, 32, -14, 15, -38, 39, -32, 33, -9, 10, -15, 18, -39, 42, -33, 34, -49, 69, -42, 43,
+    -10, 11, -18, 19, -34, 35, -43, 46, -46, 47, -50, 70, -11, 12, -19, 22, -35, -47, 48, -22, 23, 36, -12, 65, -36,
+    66, -48, -23, 24, 67, -24, 68,
 )
 
 

time: 205 us -> 204 us (level)
  starting transfers between devices: 64.2 us -> 53.2 us
  waiting for transfers between devices: 48.9 us -> 59.1 us
    ppermute x45, starting transfers between devices: 64.2 us -> 53.2 us  [exchange(): return lax.ppermute(x, AXES, pairs)]
    ppermute x45, waiting for transfers between devices: 48.9 us -> 59.1 us  [exchange(): return lax.ppermute(x, AXES, pairs)]
  transfers between devices with their start and end apart: 45 -> 45, of which waited for: 14 -> 16; matrix products, arithmetic and copies ran while one was open for 3% -> 3% of each run, Pallas kernels for 29% -> 29%
where the time goes in v5:
time: 204 us
  Pallas kernels  77.6 us (38%)
  waiting for transfers between devices  59.1 us (29%)
  starting transfers between devices  53.2 us (26%)
  other arithmetic  7.85 us (4%)
  local copies, waits for them, and re-layouts  4.36 us (2%)
    pallas_call x7, Pallas kernels, call(): pl.pallas_call(body, name=name, out_shape=shapes, in_specs=specs, out_spe...  61.3 us
    ppermute x45, waiting for transfers between devices, exchange(): return lax.ppermute(x, AXES, pairs)  59.1 us
    ppermute x45, starting transfers between devices, exchange(): return lax.ppermute(x, AXES, pairs)  53.2 us
    pallas_call x7, Pallas kernels, plain_call(): pl.pallas_call(kernel, name=name, out_shape=[shape for _, shape in outs],...  16.3 us
  transfers between devices with their start and end apart: 45, of which 16 were waited for; matrix products, arithmetic and copies ran while one was open for 3% of the time, Pallas kernels for 29%

profile of v5, /device:TPU:0, one launch (start us, length us, event | category | flops | bytes accessed | tf_op | source)
XLA Modules:
  0.0 203.8 jit_solution(9471013127084101331)
XLA Ops:
  1.3 2.1 %pack.1 = (f32[16,2048]{1,0:T(8,128)}, f32[400,128]{1,0:T(8,128)}, bf16[384,512]{1,0:T(8,128)(2,1)}, f32[256,128]{1,0:T(8,128)}) custom-call(bf16[1,512]{1,0:T(2,128)(2,1)} %refs_0_.1, bf16[1,512]{1,0:T(2,128)(2,1)} %refs_1_.1, bf16[1,1024]{1,0:T(2,128)(2,1)} %refs_2_.1, bf16[1,960]{1,0:T(2,128)(2,1)} %refs_3_.1, bf16[1,128]{1,0:T(2,128)(2,1)} %refs_4_.1, ...), custom_call_target="tpu_custom_call" | custom-call | tf_op jit(solution)/shard_map/pack/pallas_call | solution.py:757
  4.3 1.5 collective-permute-done.refs_3_.refs_9_.refs_4_
  7.3 7.9 %gnconv_forward.1 = (bf16[256,512]{1,0:T(8,128)(2,1)}, f32[2816,128]{1,0:T(8,128)}, f32[256,1024]{1,0:T(8,128)}, f32[256,1024]{1,0:T(8,128)}, bf16[256,1024]{1,0...) custom-call(f32[256,128]{1,0:T(8,128)} %get-tuple-element.235.refs_0_, bf16[2,256,512]{2,1,0:T(8,128)(2,1)} %bitcast.131, ...), custom_call_target="tpu_custom_call" | custom-call | tf_op jit(solution)/shard_map/gnconv_forward/pallas_call | solution.py:186
  15.2 1.3 copy-done.28
  16.5 16.0 %middle.1 = (bf16[256,512]{1,0:T(8,128)(2,1)}, bf16[256,512]{1,0:T(8,128)(2,1)}, bf16[256,2048]{1,0:T(8,128)(2,1)}, bf16[256,2048]{1,0:T(8,128)(2,1)}, bf16[256,...) custom-call(f32[256,128]{1,0:T(8,128)} %get-tuple-element.235.refs_0, ...), custom_call_target="tpu_custom_call" | custom-call | tf_op jit(solution)/shard_map/middle/pallas_call | solution.py:186
  32.9 4.0 %collective-permute-done.7 = bf16[2048,512]{1,0:T(8,128)(2,1)S(1)} collective-permute-done((bf16[2048,512]{1,0:T(8,128)(2,1)}, bf16[2048,512]{1,0:T(8,128)(2,1)S(1)}, u32[]{:S(2)}, u32[]{:S(2)}) %collective-permute-start.7) | collective-permute-done | bytes 2097184 | tf_op jit(solution)/shard_map/transfer_m1_core/ppermute | solution.py:905
  36.9 1.9 slice_add_fusion.2
  38.8 2.9 %collective-permute-start.8 = (bf16[2,2,2,128,512]{4,3,2,1,0:T(8,128)(2,1)S(1)}, bf16[2,2,2,128,512]{4,3,2,1,0:T(8,128)(2,1)S(1)}, u32[]{:S(2)}, u32[]{:S(2)}) collective-permute-start(bf16[2,2,2,128,512]{4,3,2,1,0:T(8,128)(2,1)S(1)} %bitcast.165), channel_id=1, source_target_pairs={{0,1},{1,0},{2,3},{3,2},{4,5},{5,4},{6,7},{7,6},{8,9},{9,8},{10,11... | collective-permute-start | bytes 3145736 | tf_op jit(solution)/shard_map/transfer_m1_x1/ppermute | solution.py:905
  41.7 9.2 %gnconv_backward.2 = (f32[256,512]{1,0:T(8,128)}, bf16[256,512]{1,0:T(8,128)(2,1)}, bf16[256,512]{1,0:T(8,128)(2,1)}, bf16[256,1024]{1,0:T(8,128)(2,1)}, bf16[25...) custom-call(f32[256,128]{1,0:T(8,128)} %get-tuple-element.235.refs_0_, ...), custom_call_target="tpu_custom_call" | custom-call | tf_op jit(solution)/shard_map/gnconv_backward/pallas_call | solution.py:186
  50.9 7.1 %mlp_backward.1 = (f32[256,512]{1,0:T(8,128)}, f32[8,2048]{1,0:T(8,128)}, bf16[2048,512]{1,0:T(8,128)(2,1)}, bf16[2048,512]{1,0:T(8,128)(2,1)}) custom-call(f32[256,128]{1,0:T(8,128)} %get-tuple-element.235.refs_0_, bf16[256,512]{1,0:T(8,128)(2,1)} %get-tuple-element.259.refs_1_, f32[16,2048]{1,0:T(8,128)} %get-tuple-element.236.refs_2_.refs_8_.refs_3_, ...), custom_call_target="tpu_custom_call" | custom-call | tf_op jit(solution)/shard_map/mlp_backward/pallas_call | solution.py:186
  59.2 1.6 collective-permute-start.9
  60.8 7.5 %gnconv_weights.2 = (bf16[1024,512]{1,0:T(8,128)(2,1)}, bf16[1024,512]{1,0:T(8,128)(2,1)}) custom-call(bf16[256,512]{1,0:T(8,128)(2,1)} %get-tuple-element.270.refs_0_, bf16[256,1024]{1,0:T(8,128)(2,1)} %get-tuple-element.271.refs_1_, bf16[256,1024]{1,0:T(8,128)(2,1)} %get-tuple-element.272.refs_2_, bf16[256,512]{1,0:T(8,128)(2,1)} %get-tuple-element.273.refs_3_, ...), custom_call_target="tpu_custom_call" | custom-call | tf_op jit(solution)/shard_map/gnconv_weights/pallas_call | solution.py:186
  69.3 1.8 bitcast_add_fusion.1
  71.1 1.6 collective-permute-start.11
  73.0 8.2 %gnconv_backward.3 = (f32[256,512]{1,0:T(8,128)S(1)}, f32[256,512]{1,0:T(8,128)S(1)}, bf16[256,512]{1,0:T(8,128)(2,1)S(1)}, bf16[256,1024]{1,0:T(8,128)(2,1)S(1)...) custom-call(f32[256,128]{1,0:T(8,128)S(1)} %copy-done.12, ...), custom_call_target="tpu_custom_call" | custom-call | tf_op jit(solution)/shard_map/gnconv_backward/pallas_call | solution.py:186
  81.2 2.4 %collective-permute-done.13 = bf16[2,2,2,128,512]{4,3,2,1,0:T(8,128)(2,1)S(1)} collective-permute-done((bf16[2,2,2,128,512]{4,3,2,1,0:T(8,128)(2,1)S(1)}, bf16[2,2,2,128,512]{4,3,2,1,0:T(8,128)(2,1)S(1)}, u32[]{:S(2)}, u32[]{:S(2)}) %collective-permute-start.13) | collective-permute-done | bytes 1048608 | tf_op jit(solution)/shard_map/transfer_m0_x1/ppermute | solution.py:905
  84.3 2.7 %collective-permute-start.12 = (bf16[128,512]{1,0:T(8,128)(2,1)S(1)}, bf16[128,512]{1,0:T(8,128)(2,1)S(1)}, u32[]{:S(2)}, u32[]{:S(2)}) collective-permute-start(bf16[128,512]{1,0:T(8,128)(2,1)S(1)} %fusion.5), channel_id=1, source_target_pairs={{0,8},{1,9},{2,10},{3,11},{4,12},{5,13},{6,14},{7,15},{8,0},{9,1},... | collective-permute-start | bytes 393224 | tf_op jit(solution)/shard_map/transfer_m1_zh/ppermute | solution.py:905
  86.9 5.4 %gnconv_weights.3 = (bf16[1024,512]{1,0:T(8,128)(2,1)S(1)}, bf16[1024,512]{1,0:T(8,128)(2,1)S(1)}) custom-call(bf16[256,512]{1,0:T(8,128)(2,1)S(1)} %copy-done.25, bf16[256,1024]{1,0:T(8,128)(2,1)S(1)} %get-tuple-element.302.refs_1_, bf16[256,1024]{1,0:T(8,128)(2,1)S(1)} %copy-done.22, bf16[256,512]{1,0:T(8,128)(2,1)S(1)} %get-tuple-element.304.refs_3_, ...), custom_call_target="tpu_custom_call" | custom-call | tf_op jit(solution)/shard_map/gnconv_weights/pallas_call | solution.py:186
  93.2 1.6 collective-permute-start.17
  95.7 2.4 %collective-permute-start.20 = (bf16[128,512]{1,0:T(8,128)(2,1)S(1)}, bf16[128,512]{1,0:T(8,128)(2,1)S(1)}, u32[]{:S(2)}, u32[]{:S(2)}) collective-permute-start(bf16[128,512]{1,0:T(8,128)(2,1)S(1)} %fusion.1), channel_id=1, source_target_pairs={{0,8},{1,9},{2,10},{3,11},{4,12},{5,13},{6,14},{7,15},{8,0},{9,1},... | collective-permute-start | bytes 393224 | tf_op jit(solution)/shard_map/transfer_m1_ZH/ppermute | solution.py:905
  98.1 6.6 %collective-permute-done.17 = bf16[2,128,512]{2,1,0:T(8,128)(2,1)S(1)} collective-permute-done((bf16[2,128,512]{2,1,0:T(8,128)(2,1)S(1)}, bf16[2,128,512]{2,1,0:T(8,128)(2,1)S(1)}, u32[]{:S(2)}, u32[]{:S(2)}) %collective-permute-start.17) | collective-permute-done | bytes 262176 | tf_op jit(solution)/shard_map/transfer_m0_zl/ppermute | solution.py:905
  104.8 1.7 collective-permute-start.19
  107.4 2.5 %collective-permute-start.27 = (bf16[2,128,512]{2,1,0:T(8,128)(2,1)S(1)}, bf16[2,128,512]{2,1,0:T(8,128)(2,1)S(1)}, u32[]{:S(2)}, u32[]{:S(2)}) collective-permute-start(bf16[2,128,512]{2,1,0:T(8,128)(2,1)S(1)} %get-tuple-element.342), channel_id=1, source_target_pairs={{0,4},{1,5},{2,6},{3,7},{4,0},{5,1},{6,2},{7,3},{8,12},{9,13},{10,... | collective-permute-start | bytes 786440 | tf_op jit(solution)/shard_map/transfer_m1_ZL/ppermute | solution.py:905
  109.9 3.9 %collective-permute-done.19 = bf16[128,512]{1,0:T(8,128)(2,1)S(1)} collective-permute-done((bf16[128,512]{1,0:T(8,128)(2,1)S(1)}, bf16[128,512]{1,0:T(8,128)(2,1)S(1)}, u32[]{:S(2)}, u32[]{:S(2)}) %collective-permute-start.19) | collective-permute-done | bytes 131104 | tf_op jit(solution)/shard_map/transfer_m0_zh/ppermute | solution.py:905
  115.0 1.6 collective-permute-done.22
  117.1 4.6 %collective-permute-done.21 = bf16[128,512]{1,0:T(8,128)(2,1)S(1)} collective-permute-done((bf16[128,512]{1,0:T(8,128)(2,1)S(1)}, bf16[128,512]{1,0:T(8,128)(2,1)S(1)}, u32[]{:S(2)}, u32[]{:S(2)}) %collective-permute-start.21) | collective-permute-done | bytes 131104 | tf_op jit(solution)/shard_map/transfer_m0_ZH/ppermute | solution.py:905
  122.0 1.4 collective-permute-start.33
  123.4 4.8 %collective-permute-done.24 = bf16[2,128,512]{2,1,0:T(8,128)(2,1)S(1)} collective-permute-done((bf16[2,128,512]{2,1,0:T(8,128)(2,1)S(1)}, bf16[2,128,512]{2,1,0:T(8,128)(2,1)S(1)}, u32[]{:S(2)}, u32[]{:S(2)}) %collective-permute-start.24) | collective-permute-done | bytes 262176 | tf_op jit(solution)/shard_map/transfer_m0_ZL/ppermute | solution.py:905
  128.2 1.4 collective-permute-start.29
  129.6 1.2 collective-permute-start.31
  130.9 1.8 collective-permute-start.32
  133.6 3.8 %collective-permute-done.29 = bf16[2,2,64,512]{3,2,1,0:T(8,128)(2,1)S(1)} collective-permute-done((bf16[2,2,64,512]{3,2,1,0:T(8,128)(2,1)S(1)}, bf16[2,2,64,512]{3,2,1,0:T(8,128)(2,1)S(1)}, u32[]{:S(2)}, u32[]{:S(2)}) %collective-permute-start.29) | collective-permute-done | bytes 262176 | tf_op jit(solution)/shard_map/transfer_g0_fl/ppermute | solution.py:905
  137.6 5.1 %collective-permute-start.38 = (bf16[2,2,2,128,512]{4,3,2,1,0:T(8,128)(2,1)S(1)}, bf16[2,2,2,128,512]{4,3,2,1,0:T(8,128)(2,1)S(1)}, u32[]{:S(2)}, u32[]{:S(2)}) collective-permute-start(bf16[2,2,2,128,512]{4,3,2,1,0:T(8,128)(2,1)S(1)} %get-tuple-element.377), channel_id=1, source_target_pairs={{0,1},{1,0},{2,3},{3,2},{4,5},{5,4},{6,7},{7,6},{8,9},{9,8},{10,11... | collective-permute-start | bytes 3145736 | tf_op jit(solution)/shard_map/transfer_m1_X1/ppermute | solution.py:905
  143.2 2.3 %collective-permute-start.36 = (bf16[2,2,2,128,512]{4,3,2,1,0:T(8,128)(2,1)S(1)}, bf16[2,2,2,128,512]{4,3,2,1,0:T(8,128)(2,1)S(1)}, u32[]{:S(2)}, u32[]{:S(2)}) collective-permute-start(bf16[2,2,2,128,512]{4,3,2,1,0:T(8,128)(2,1)S(1)} %get-tuple-element.373), channel_id=1, source_target_pairs={{0,1},{1,0},{2,3},{3,2},{4,5},{5,4},{6,7},{7,6},{8,9},{9,8},{10,11... | collective-permute-start | bytes 3145736 | tf_op jit(solution)/shard_map/transfer_m0_X1/ppermute | solution.py:905
  145.5 6.4 %collective-permute-done.30 = bf16[2,2,64,512]{3,2,1,0:T(8,128)(2,1)S(1)} collective-permute-done((bf16[2,2,64,512]{3,2,1,0:T(8,128)(2,1)S(1)}, bf16[2,2,64,512]{3,2,1,0:T(8,128)(2,1)S(1)}, u32[]{:S(2)}, u32[]{:S(2)}) %collective-permute-start.30) | collective-permute-done | bytes 262176 | tf_op jit(solution)/shard_map/transfer_g0_fh/ppermute | solution.py:905
  153.2 8.0 %collective-permute-done.34 = bf16[2,2,64,512]{3,2,1,0:T(8,128)(2,1)S(1)} collective-permute-done((bf16[2,2,64,512]{3,2,1,0:T(8,128)(2,1)S(1)}, bf16[2,2,64,512]{3,2,1,0:T(8,128)(2,1)S(1)}, u32[]{:S(2)}, u32[]{:S(2)}) %collective-permute-start.34) | collective-permute-done | bytes 262176 | tf_op jit(solution)/shard_map/transfer_g0_X2/ppermute | solution.py:905
  163.0 3.8 %collective-permute-done.37 = bf16[2,2,64,512]{3,2,1,0:T(8,128)(2,1)S(1)} collective-permute-done((bf16[2,2,64,512]{3,2,1,0:T(8,128)(2,1)S(1)}, bf16[2,2,64,512]{3,2,1,0:T(8,128)(2,1)S(1)}, u32[]{:S(2)}, u32[]{:S(2)}) %collective-permute-start.37) | collective-permute-done | bytes 262176 | tf_op jit(solution)/shard_map/transfer_g1_fh/ppermute | solution.py:905
  166.8 2.0 collective-permute-start.40
  169.0 3.0 %collective-permute-start.42 = (bf16[2048,512]{1,0:T(8,128)(2,1)S(1)}, bf16[2048,512]{1,0:T(8,128)(2,1)}, u32[]{:S(2)}, u32[]{:S(2)}) collective-permute-start(bf16[2048,512]{1,0:T(8,128)(2,1)S(1)} %bitcast.141), channel_id=1, source_target_pairs={{0,16},{1,17},{2,18},{3,19},{4,20},{5,21},{6,22},{7,23},{8,24},{9,... | collective-permute-start | bytes 6291464 | tf_op jit(solution)/shard_map/transfer_m1_Core/ppermute | solution.py:905
  172.0 5.9 %collective-permute-done.35 = bf16[2,2,2,64,512]{4,3,2,1,0:T(8,128)(2,1)S(1)} collective-permute-done((bf16[2,2,2,64,512]{4,3,2,1,0:T(8,128)(2,1)S(1)}, bf16[2,2,2,64,512]{4,3,2,1,0:T(8,128)(2,1)S(1)}, u32[]{:S(2)}, u32[]{:S(2)}) %collective-permute-start.35) | collective-permute-done | bytes 524320 | tf_op jit(solution)/shard_map/transfer_g0_X1/ppermute | solution.py:905
  178.1 1.3 collective-permute-start.41
  179.5 1.3 collective-permute-start.39
  181.7 2.0 collective-permute-start.43
  183.7 3.2 %mlp_finish.2 = (f32[2048,512]{1,0:T(8,128)}, f32[512,2048]{1,0:T(8,128)}) custom-call(bf16[2048,512]{1,0:T(8,128)(2,1)} %bitcast.144, bf16[2048,512]{1,0:T(8,128)(2,1)} %bitcast.142), custom_call_target="tpu_custom_call" | custom-call | tf_op jit(solution)/shard_map/mlp_finish/pallas_call | solution.py:757
  187.0 3.3 %mlp_finish.3 = (f32[2048,512]{1,0:T(8,128)}, f32[512,2048]{1,0:T(8,128)}) custom-call(bf16[2048,512]{1,0:T(8,128)(2,1)} %collective-permute-done.41.refs_0_, bf16[2048,512]{1,0:T(8,128)(2,1)} %collective-permute-done.42.refs_1_, f32[2048,512]{1,0:T(8,128)} %get-tuple-element.390.refs_2_, ...), custom_call_target="tpu_custom_call", output_to_operand_aliasing={{0}: (2, {}), {1}: (3, {})} | custom-call | tf_op jit(solution)/shard_map/mlp_finish/pallas_call | solution.py:757
  192.3 4.5 %collective-permute-start.44 = (bf16[1024,512]{1,0:T(8,128)(2,1)S(1)}, bf16[1024,512]{1,0:T(8,128)(2,1)S(1)}, u32[]{:S(2)}, u32[]{:S(2)}) collective-permute-start(bf16[1024,512]{1,0:T(8,128)(2,1)S(1)} %bitcast.149), channel_id=1, source_target_pairs={{0,16},{1,17},{2,18},{3,19},{4,20},{5,21},{6,22},{7,23},{8,24},{9,... | collective-permute-start | bytes 3145736 | tf_op jit(solution)/shard_map/transfer_g1_Core/ppermute | solution.py:905
  196.9 2.9 %gn_finish.2 = (f32[1,512]{1,0:T(1,128)}, f32[1,512]{1,0:T(1,128)}, f32[512,1024]{1,0:T(8,128)}, f32[1,1024]{1,0:T(1,128)}, f32[49,1,960]{2,1,0:T(1,128)}, /*ind...) custom-call(bf16[1024,512]{1,0:T(8,128)(2,1)} %bitcast.148, ...), custom_call_target="tpu_custom_call" | custom-call | tf_op jit(solution)/shard_map/gn_finish/pallas_call | solution.py:757
  200.8 2.8 %gn_finish.3 = (f32[1,512]{1,0:T(1,128)}, f32[1,512]{1,0:T(1,128)}, f32[512,1024]{1,0:T(8,128)}, f32[1,1024]{1,0:T(1,128)}, f32[49,1,960]{2,1,0:T(1,128)}, /*ind...) custom-call(bf16[1024,512]{1,0:T(8,128)(2,1)} %collective-permute-do, ...), custom_call_target="tpu_custom_call", output_to_operand_aliasing={{0}: (2, {}), {1}: (3, {}), {2}: (4, {}), {3}: (5, {}), {4}... | custom-call | tf_op jit(solution)/shard_map/gn_finish/pallas_call | solution.py:757
  (172 shorter events, 19.8 us)
Async XLA Ops:
  0.7 5.3 %collective-permute-start.1 = (bf16[512,1024]{1,0:T(8,128)(2,1)}, bf16[512,1024]{1,0:T(8,128)(2,1)S(1)}, u32[]{:S(2)}, u32[]{:S(2)}) collective-permute-start(bf16[512,1024]{1,0:T(8,128)(2,1)} %bitcast.121), channel_id=1, source_target_pairs={{0,16},{1,17},{2,18},{3,19},{4,20},{5,21},{6,22},{7,23},{8,24},{9,... | collective-permute-start | bytes 3145736 | tf_op jit(solution)/shard_map/ppermute | solution.py:905
  1.2 4.7 %collective-permute-start.4 = (bf16[512,512]{1,0:T(8,128)(2,1)}, bf16[512,512]{1,0:T(8,128)(2,1)S(1)}, u32[]{:S(2)}, u32[]{:S(2)}) collective-permute-start(bf16[512,512]{1,0:T(8,128)(2,1)} %bitcast.126), channel_id=1, source_target_pairs={{0,16},{1,17},{2,18},{3,19},{4,20},{5,21},{6,22},{7,23},{8,24},{9,... | collective-permute-start | bytes 1572872 | tf_op jit(solution)/shard_map/ppermute | solution.py:905
  3.4 2.5 %collective-permute-start.3 = (bf16[384,512]{1,0:T(8,128)(2,1)}, bf16[384,512]{1,0:T(8,128)(2,1)S(1)}, u32[]{:S(2)}, u32[]{:S(2)}) collective-permute-start(bf16[384,512]{1,0:T(8,128)(2,1)} %get-tuple-element.238.refs_8_.refs_14_.refs_9_), channel_id=1, source_target_pairs={{0,16},{1,17},{2,18},{3,19},{4,20},{5,21},{6,22},{7,23},{8,24},{9,... | collective-permute-start | bytes 1179656 | tf_op jit(solution)/shard_map/ppermute | solution.py:905
  3.8 2.0 %collective-permute-start.2 = (f32[400,128]{1,0:T(8,128)}, f32[400,128]{1,0:T(8,128)S(1)}, u32[]{:S(2)}, u32[]{:S(2)}) collective-permute-start(f32[400,128]{1,0:T(8,128)} %get-tuple-element.237.refs_6_.refs_12_), channel_id=1, source_target_pairs={{0,16},{1,17},{2,18},{3,19},{4,20},{5,21},{6,22},{7,23},{8,24},{9,... | collective-permute-start | bytes 614408 | tf_op jit(solution)/shard_map/ppermute | solution.py:905
  3.9 2.0 collective-permute-start
  5.9 9.2 %collective-permute-start.5 = (bf16[512,2048]{1,0:T(8,128)(2,1)}, bf16[512,2048]{1,0:T(8,128)(2,1)S(1)}, u32[]{:S(2)}, u32[]{:S(2)}) collective-permute-start(bf16[512,2048]{1,0:T(8,128)(2,1)} %bitcast.133), channel_id=1, source_target_pairs={{0,16},{1,17},{2,18},{3,19},{4,20},{5,21},{6,22},{7,23},{8,24},{9,... | collective-permute-start | bytes 6291464 | tf_op jit(solution)/shard_map/ppermute | solution.py:905
  6.4 8.8 %collective-permute-start.6 = (bf16[2048,512]{1,0:T(8,128)(2,1)}, bf16[2048,512]{1,0:T(8,128)(2,1)}, u32[]{:S(2)}, u32[]{:S(2)}) collective-permute-start(bf16[2048,512]{1,0:T(8,128)(2,1)} %bitcast.137), channel_id=1, source_target_pairs={{0,16},{1,17},{2,18},{3,19},{4,20},{5,21},{6,22},{7,23},{8,24},{9,... | collective-permute-start | bytes 6291464 | tf_op jit(solution)/shard_map/ppermute | solution.py:905
  32.5 4.4 %collective-permute-start.7 = (bf16[2048,512]{1,0:T(8,128)(2,1)}, bf16[2048,512]{1,0:T(8,128)(2,1)S(1)}, u32[]{:S(2)}, u32[]{:S(2)}) collective-permute-start(bf16[2048,512]{1,0:T(8,128)(2,1)} %get-tuple-element.248), channel_id=1, source_target_pairs={{0,16},{1,17},{2,18},{3,19},{4,20},{5,21},{6,22},{7,23},{8,24},{9,... | collective-permute-start | bytes 6291464 | tf_op jit(solution)/shard_map/transfer_m1_core/ppermute | solution.py:905
  38.8 19.3 %collective-permute-start.8 = (bf16[2,2,2,128,512]{4,3,2,1,0:T(8,128)(2,1)S(1)}, bf16[2,2,2,128,512]{4,3,2,1,0:T(8,128)(2,1)S(1)}, u32[]{:S(2)}, u32[]{:S(2)}) collective-permute-start(bf16[2,2,2,128,512]{4,3,2,1,0:T(8,128)(2,1)S(1)} %bitcast.165), channel_id=1, source_target_pairs={{0,1},{1,0},{2,3},{3,2},{4,5},{5,4},{6,7},{7,6},{8,9},{9,8},{10,11... | collective-permute-start | bytes 3145736 | tf_op jit(solution)/shard_map/transfer_m1_x1/ppermute | solution.py:905
  58.1 10.2 %collective-permute-start.10 = (bf16[2048,512]{1,0:T(8,128)(2,1)}, bf16[2048,512]{1,0:T(8,128)(2,1)S(1)}, u32[]{:S(2)}, u32[]{:S(2)}) collective-permute-start(bf16[2048,512]{1,0:T(8,128)(2,1)} %get-tuple-element.269), channel_id=1, source_target_pairs={{0,16},{1,17},{2,18},{3,19},{4,20},{5,21},{6,22},{7,23},{8,24},{9,... | collective-permute-start | bytes 6291464 | tf_op jit(solution)/shard_map/transfer_m0_core/ppermute | solution.py:905
  59.2 10.1 %collective-permute-start.9 = (bf16[2,2,128,512]{3,2,1,0:T(8,128)(2,1)S(1)}, bf16[2,2,128,512]{3,2,1,0:T(8,128)(2,1)}, u32[]{:S(2)}, u32[]{:S(2)}) collective-permute-start(bf16[2,2,128,512]{3,2,1,0:T(8,128)(2,1)S(1)} %add_bitcast_fusion.1), channel_id=1, source_target_pairs={{0,2},{1,3},{2,0},{3,1},{4,6},{5,7},{6,4},{7,5},{8,10},{9,11},{10,... | collective-permute-start | bytes 1572872 | tf_op jit(solution)/shard_map/transfer_m1_x2/ppermute | solution.py:905
  68.7 14.9 %collective-permute-start.13 = (bf16[2,2,2,128,512]{4,3,2,1,0:T(8,128)(2,1)S(1)}, bf16[2,2,2,128,512]{4,3,2,1,0:T(8,128)(2,1)S(1)}, u32[]{:S(2)}, u32[]{:S(2)}) collective-permute-start(bf16[2,2,2,128,512]{4,3,2,1,0:T(8,128)(2,1)S(1)} %bitcast.163), channel_id=1, source_target_pairs={{0,1},{1,0},{2,3},{3,2},{4,5},{5,4},{6,7},{7,6},{8,9},{9,8},{10,11... | collective-permute-start | bytes 3145736 | tf_op jit(solution)/shard_map/transfer_m0_x1/ppermute | solution.py:905
  71.1 10.1 %collective-permute-start.11 = (bf16[2,128,512]{2,1,0:T(8,128)(2,1)S(1)}, bf16[2,128,512]{2,1,0:T(8,128)(2,1)S(1)}, u32[]{:S(2)}, u32[]{:S(2)}) collective-permute-start(bf16[2,128,512]{2,1,0:T(8,128)(2,1)S(1)} %slice_bitcast_fusion.1), channel_id=1, source_target_pairs={{0,4},{1,5},{2,6},{3,7},{4,0},{5,1},{6,2},{7,3},{8,12},{9,13},{10,... | collective-permute-start | bytes 786440 | tf_op jit(solution)/shard_map/transfer_m1_zl/ppermute | solution.py:905
  72.8 19.6 %collective-permute-start.15 = (bf16[1024,512]{1,0:T(8,128)(2,1)}, bf16[1024,512]{1,0:T(8,128)(2,1)S(1)}, u32[]{:S(2)}, u32[]{:S(2)}) collective-permute-start(bf16[1024,512]{1,0:T(8,128)(2,1)} %get-tuple-element.300), channel_id=1, source_target_pairs={{0,16},{1,17},{2,18},{3,19},{4,20},{5,21},{6,22},{7,23},{8,24},{9,... | collective-permute-start | bytes 3145736 | tf_op jit(solution)/shard_map/transfer_g1_core/ppermute | solution.py:905
  83.7 9.2 %collective-permute-start.14 = (bf16[2,2,128,512]{3,2,1,0:T(8,128)(2,1)S(1)}, bf16[2,2,128,512]{3,2,1,0:T(8,128)(2,1)S(1)}, u32[]{:S(2)}, u32[]{:S(2)}) collective-permute-start(bf16[2,2,128,512]{3,2,1,0:T(8,128)(2,1)S(1)} %add_bitcast_fusion), channel_id=1, source_target_pairs={{0,2},{1,3},{2,0},{3,1},{4,6},{5,7},{6,4},{7,5},{8,10},{9,11},{10,... | collective-permute-start | bytes 1572872 | tf_op jit(solution)/shard_map/transfer_m0_x2/ppermute | solution.py:905
  84.3 8.7 %collective-permute-start.12 = (bf16[128,512]{1,0:T(8,128)(2,1)S(1)}, bf16[128,512]{1,0:T(8,128)(2,1)S(1)}, u32[]{:S(2)}, u32[]{:S(2)}) collective-permute-start(bf16[128,512]{1,0:T(8,128)(2,1)S(1)} %fusion.5), channel_id=1, source_target_pairs={{0,8},{1,9},{2,10},{3,11},{4,12},{5,13},{6,14},{7,15},{8,0},{9,1},... | collective-permute-start | bytes 393224 | tf_op jit(solution)/shard_map/transfer_m1_zh/ppermute | solution.py:905
  92.9 5.2 %collective-permute-start.18 = (bf16[1024,512]{1,0:T(8,128)(2,1)S(1)}, bf16[1024,512]{1,0:T(8,128)(2,1)S(1)}, u32[]{:S(2)}, u32[]{:S(2)}) collective-permute-start(bf16[1024,512]{1,0:T(8,128)(2,1)S(1)} %get-tuple-element.317), channel_id=1, source_target_pairs={{0,16},{1,17},{2,18},{3,19},{4,20},{5,21},{6,22},{7,23},{8,24},{9,... | collective-permute-start | bytes 3145736 | tf_op jit(solution)/shard_map/transfer_g0_core/ppermute | solution.py:905
  93.2 11.6 %collective-permute-start.17 = (bf16[2,128,512]{2,1,0:T(8,128)(2,1)S(1)}, bf16[2,128,512]{2,1,0:T(8,128)(2,1)S(1)}, u32[]{:S(2)}, u32[]{:S(2)}) collective-permute-start(bf16[2,128,512]{2,1,0:T(8,128)(2,1)S(1)} %slice_bitcast_fusion), channel_id=1, source_target_pairs={{0,4},{1,5},{2,6},{3,7},{4,0},{5,1},{6,2},{7,3},{8,12},{9,13},{10,... | collective-permute-start | bytes 786440 | tf_op jit(solution)/shard_map/transfer_m0_zl/ppermute | solution.py:905
  94.9 18.9 %collective-permute-start.23 = (bf16[2,2,2,64,512]{4,3,2,1,0:T(8,128)(2,1)S(1)}, bf16[2,2,2,64,512]{4,3,2,1,0:T(8,128)(2,1)S(1)}, u32[]{:S(2)}, u32[]{:S(2)}) collective-permute-start(bf16[2,2,2,64,512]{4,3,2,1,0:T(8,128)(2,1)S(1)} %bitcast.171), channel_id=1, source_target_pairs={{0,1},{1,0},{2,3},{3,2},{4,5},{5,4},{6,7},{7,6},{8,9},{9,8},{10,11... | collective-permute-start | bytes 1572872 | tf_op jit(solution)/shard_map/transfer_g1_x1/ppermute | solution.py:905
  95.7 11.0 %collective-permute-start.20 = (bf16[128,512]{1,0:T(8,128)(2,1)S(1)}, bf16[128,512]{1,0:T(8,128)(2,1)S(1)}, u32[]{:S(2)}, u32[]{:S(2)}) collective-permute-start(bf16[128,512]{1,0:T(8,128)(2,1)S(1)} %fusion.1), channel_id=1, source_target_pairs={{0,8},{1,9},{2,10},{3,11},{4,12},{5,13},{6,14},{7,15},{8,0},{9,1},... | collective-permute-start | bytes 393224 | tf_op jit(solution)/shard_map/transfer_m1_ZH/ppermute | solution.py:905
  104.8 9.0 %collective-permute-start.19 = (bf16[128,512]{1,0:T(8,128)(2,1)S(1)}, bf16[128,512]{1,0:T(8,128)(2,1)S(1)}, u32[]{:S(2)}, u32[]{:S(2)}) collective-permute-start(bf16[128,512]{1,0:T(8,128)(2,1)S(1)} %fusion.2), channel_id=1, source_target_pairs={{0,8},{1,9},{2,10},{3,11},{4,12},{5,13},{6,14},{7,15},{8,0},{9,1},... | collective-permute-start | bytes 393224 | tf_op jit(solution)/shard_map/transfer_m0_zh/ppermute | solution.py:905
  106.7 10.4 %copy-start.38 = (bf16[256,512]{1,0:T(8,128)(2,1)S(1)}, bf16[256,512]{1,0:T(8,128)(2,1)}, u32[]{:S(2)}) copy-start(bf16[256,512]{1,0:T(8,128)(2,1)} %get-tuple-element.313) | copy-start | bytes 786436
  106.7 9.9 %collective-permute-start.22 = (bf16[2,2,2,64,512]{4,3,2,1,0:T(8,128)(2,1)S(1)}, bf16[2,2,2,64,512]{4,3,2,1,0:T(8,128)(2,1)S(1)}, u32[]{:S(2)}, u32[]{:S(2)}) collective-permute-start(bf16[2,2,2,64,512]{4,3,2,1,0:T(8,128)(2,1)S(1)} %bitcast.175), channel_id=1, source_target_pairs={{0,1},{1,0},{2,3},{3,2},{4,5},{5,4},{6,7},{7,6},{8,9},{9,8},{10,11... | collective-permute-start | bytes 1572872 | tf_op jit(solution)/shard_map/transfer_g0_x1/ppermute | solution.py:905
  107.4 14.4 %collective-permute-start.27 = (bf16[2,128,512]{2,1,0:T(8,128)(2,1)S(1)}, bf16[2,128,512]{2,1,0:T(8,128)(2,1)S(1)}, u32[]{:S(2)}, u32[]{:S(2)}) collective-permute-start(bf16[2,128,512]{2,1,0:T(8,128)(2,1)S(1)} %get-tuple-element.342), channel_id=1, source_target_pairs={{0,4},{1,5},{2,6},{3,7},{4,0},{5,1},{6,2},{7,3},{8,12},{9,13},{10,... | collective-permute-start | bytes 786440 | tf_op jit(solution)/shard_map/transfer_m1_ZL/ppermute | solution.py:905
  113.9 7.9 %collective-permute-start.21 = (bf16[128,512]{1,0:T(8,128)(2,1)S(1)}, bf16[128,512]{1,0:T(8,128)(2,1)S(1)}, u32[]{:S(2)}, u32[]{:S(2)}) collective-permute-start(bf16[128,512]{1,0:T(8,128)(2,1)S(1)} %fusion.4), channel_id=1, source_target_pairs={{0,8},{1,9},{2,10},{3,11},{4,12},{5,13},{6,14},{7,15},{8,0},{9,1},... | collective-permute-start | bytes 393224 | tf_op jit(solution)/shard_map/transfer_m0_ZH/ppermute | solution.py:905
  113.9 8.0 %collective-permute-start.26 = (bf16[2,2,64,512]{3,2,1,0:T(8,128)(2,1)S(1)}, bf16[2,2,64,512]{3,2,1,0:T(8,128)(2,1)S(1)}, u32[]{:S(2)}, u32[]{:S(2)}) collective-permute-start(bf16[2,2,64,512]{3,2,1,0:T(8,128)(2,1)S(1)} %add_bitcast_fusion.2), channel_id=1, source_target_pairs={{0,2},{1,3},{2,0},{3,1},{4,6},{5,7},{6,4},{7,5},{8,10},{9,11},{10,... | collective-permute-start | bytes 786440 | tf_op jit(solution)/shard_map/transfer_g1_x2/ppermute | solution.py:905
  116.7 6.7 %collective-permute-start.25 = (bf16[2,2,64,512]{3,2,1,0:T(8,128)(2,1)S(1)}, bf16[2,2,64,512]{3,2,1,0:T(8,128)(2,1)S(1)}, u32[]{:S(2)}, u32[]{:S(2)}) collective-permute-start(bf16[2,2,64,512]{3,2,1,0:T(8,128)(2,1)S(1)} %add_bitcast_fusion.3), channel_id=1, source_target_pairs={{0,2},{1,3},{2,0},{3,1},{4,6},{5,7},{6,4},{7,5},{8,10},{9,11},{10,... | collective-permute-start | bytes 786440 | tf_op jit(solution)/shard_map/transfer_g0_x2/ppermute | solution.py:905
  117.1 15.6 %collective-permute-start.16 = (bf16[256,512]{1,0:T(8,128)(2,1)S(1)}, bf16[256,512]{1,0:T(8,128)(2,1)S(1)}, u32[]{:S(2)}, u32[]{:S(2)}) collective-permute-start(bf16[256,512]{1,0:T(8,128)(2,1)S(1)} %copy-done.38), channel_id=1, source_target_pairs={{0,16},{1,17},{2,18},{3,19},{4,20},{5,21},{6,22},{7,23},{8,24},{9,... | collective-permute-start | bytes 786440 | tf_op jit(solution)/shard_map/transfer_fo/ppermute | solution.py:905
  121.8 6.4 %collective-permute-start.24 = (bf16[2,128,512]{2,1,0:T(8,128)(2,1)S(1)}, bf16[2,128,512]{2,1,0:T(8,128)(2,1)S(1)}, u32[]{:S(2)}, u32[]{:S(2)}) collective-permute-start(bf16[2,128,512]{2,1,0:T(8,128)(2,1)S(1)} %get-tuple-element.336), channel_id=1, source_target_pairs={{0,4},{1,5},{2,6},{3,7},{4,0},{5,1},{6,2},{7,3},{8,12},{9,13},{10,... | collective-permute-start | bytes 786440 | tf_op jit(solution)/shard_map/transfer_m0_ZL/ppermute | solution.py:905
  121.9 10.8 %copy-start.21 = (bf16[256,512]{1,0:T(8,128)(2,1)S(1)}, bf16[256,512]{1,0:T(8,128)(2,1)}, u32[]{:S(2)}) copy-start(bf16[256,512]{1,0:T(8,128)(2,1)} %get-tuple-element.242.refs_16_.first) | copy-start | bytes 786436
  121.9 10.8 %copy-start.24 = (bf16[256,512]{1,0:T(8,128)(2,1)S(1)}, bf16[256,512]{1,0:T(8,128)(2,1)}, u32[]{:S(2)}) copy-start(bf16[256,512]{1,0:T(8,128)(2,1)} %get-tuple-element.243.second) | copy-start | bytes 786436
  122.0 15.5 %collective-permute-start.33 = (bf16[2,2,128,512]{3,2,1,0:T(8,128)(2,1)S(1)}, bf16[2,2,128,512]{3,2,1,0:T(8,128)(2,1)S(1)}, u32[]{:S(2)}, u32[]{:S(2)}) collective-permute-start(bf16[2,2,128,512]{3,2,1,0:T(8,128)(2,1)S(1)} %get-tuple-element.361), channel_id=1, source_target_pairs={{0,2},{1,3},{2,0},{3,1},{4,6},{5,7},{6,4},{7,5},{8,10},{9,11},{10,... | collective-permute-start | bytes 1572872 | tf_op jit(solution)/shard_map/transfer_m1_X2/ppermute | solution.py:905
  128.2 9.2 %collective-permute-start.29 = (bf16[2,2,64,512]{3,2,1,0:T(8,128)(2,1)S(1)}, bf16[2,2,64,512]{3,2,1,0:T(8,128)(2,1)S(1)}, u32[]{:S(2)}, u32[]{:S(2)}) collective-permute-start(bf16[2,2,64,512]{3,2,1,0:T(8,128)(2,1)S(1)} %bitcast_add_fusion.3), channel_id=1, source_target_pairs={{0,4},{1,5},{2,6},{3,7},{4,0},{5,1},{6,2},{7,3},{8,12},{9,13},{10,... | collective-permute-start | bytes 786440 | tf_op jit(solution)/shard_map/transfer_g0_fl/ppermute | solution.py:905
  129.6 13.4 %collective-permute-start.31 = (bf16[2,2,128,512]{3,2,1,0:T(8,128)(2,1)S(1)}, bf16[2,2,128,512]{3,2,1,0:T(8,128)(2,1)S(1)}, u32[]{:S(2)}, u32[]{:S(2)}) collective-permute-start(bf16[2,2,128,512]{3,2,1,0:T(8,128)(2,1)S(1)} %get-tuple-element.357), channel_id=1, source_target_pairs={{0,2},{1,3},{2,0},{3,1},{4,6},{5,7},{6,4},{7,5},{8,10},{9,11},{10,... | collective-permute-start | bytes 1572872 | tf_op jit(solution)/shard_map/transfer_m0_X2/ppermute | solution.py:905
  130.9 12.1 %collective-permute-start.32 = (bf16[2,2,64,512]{3,2,1,0:T(8,128)(2,1)S(1)}, bf16[2,2,64,512]{3,2,1,0:T(8,128)(2,1)S(1)}, u32[]{:S(2)}, u32[]{:S(2)}) collective-permute-start(bf16[2,2,64,512]{3,2,1,0:T(8,128)(2,1)S(1)} %bitcast_add_fusion.2), channel_id=1, source_target_pairs={{0,4},{1,5},{2,6},{3,7},{4,0},{5,1},{6,2},{7,3},{8,12},{9,13},{10,... | collective-permute-start | bytes 786440 | tf_op jit(solution)/shard_map/transfer_g1_fl/ppermute | solution.py:905
  137.6 25.4 %collective-permute-start.38 = (bf16[2,2,2,128,512]{4,3,2,1,0:T(8,128)(2,1)S(1)}, bf16[2,2,2,128,512]{4,3,2,1,0:T(8,128)(2,1)S(1)}, u32[]{:S(2)}, u32[]{:S(2)}) collective-permute-start(bf16[2,2,2,128,512]{4,3,2,1,0:T(8,128)(2,1)S(1)} %get-tuple-element.377), channel_id=1, source_target_pairs={{0,1},{1,0},{2,3},{3,2},{4,5},{5,4},{6,7},{7,6},{8,9},{9,8},{10,11... | collective-permute-start | bytes 3145736 | tf_op jit(solution)/shard_map/transfer_m1_X1/ppermute | solution.py:905
  142.7 9.1 %collective-permute-start.30 = (bf16[2,2,64,512]{3,2,1,0:T(8,128)(2,1)S(1)}, bf16[2,2,64,512]{3,2,1,0:T(8,128)(2,1)S(1)}, u32[]{:S(2)}, u32[]{:S(2)}) collective-permute-start(bf16[2,2,64,512]{3,2,1,0:T(8,128)(2,1)S(1)} %add.165), channel_id=1, source_target_pairs={{0,8},{1,9},{2,10},{3,11},{4,12},{5,13},{6,14},{7,15},{8,0},{9,1},... | collective-permute-start | bytes 786440 | tf_op jit(solution)/shard_map/transfer_g0_fh/ppermute | solution.py:905
  143.2 28.8 %collective-permute-start.36 = (bf16[2,2,2,128,512]{4,3,2,1,0:T(8,128)(2,1)S(1)}, bf16[2,2,2,128,512]{4,3,2,1,0:T(8,128)(2,1)S(1)}, u32[]{:S(2)}, u32[]{:S(2)}) collective-permute-start(bf16[2,2,2,128,512]{4,3,2,1,0:T(8,128)(2,1)S(1)} %get-tuple-element.373), channel_id=1, source_target_pairs={{0,1},{1,0},{2,3},{3,2},{4,5},{5,4},{6,7},{7,6},{8,9},{9,8},{10,11... | collective-permute-start | bytes 3145736 | tf_op jit(solution)/shard_map/transfer_m0_X1/ppermute | solution.py:905
  151.9 9.3 %collective-permute-start.34 = (bf16[2,2,64,512]{3,2,1,0:T(8,128)(2,1)S(1)}, bf16[2,2,64,512]{3,2,1,0:T(8,128)(2,1)S(1)}, u32[]{:S(2)}, u32[]{:S(2)}) collective-permute-start(bf16[2,2,64,512]{3,2,1,0:T(8,128)(2,1)S(1)} %add.169), channel_id=1, source_target_pairs={{0,2},{1,3},{2,0},{3,1},{4,6},{5,7},{6,4},{7,5},{8,10},{9,11},{10,... | collective-permute-start | bytes 786440 | tf_op jit(solution)/shard_map/transfer_g0_X2/ppermute | solution.py:905
  153.0 8.9 %collective-permute-start.28 = (f32[256,512]{1,0:T(8,128)S(1)}, f32[256,512]{1,0:T(8,128)S(1)}, u32[]{:S(2)}, u32[]{:S(2)}) collective-permute-start(f32[256,512]{1,0:T(8,128)S(1)} %get-tuple-element.350), channel_id=1, source_target_pairs={{0,16},{1,17},{2,18},{3,19},{4,20},{5,21},{6,22},{7,23},{8,24},{9,... | collective-permute-start | bytes 1572872 | tf_op jit(solution)/shard_map/transfer_go/ppermute | solution.py:905
  153.1 13.6 %collective-permute-start.37 = (bf16[2,2,64,512]{3,2,1,0:T(8,128)(2,1)S(1)}, bf16[2,2,64,512]{3,2,1,0:T(8,128)(2,1)S(1)}, u32[]{:S(2)}, u32[]{:S(2)}) collective-permute-start(bf16[2,2,64,512]{3,2,1,0:T(8,128)(2,1)S(1)} %add.170), channel_id=1, source_target_pairs={{0,8},{1,9},{2,10},{3,11},{4,12},{5,13},{6,14},{7,15},{8,0},{9,1},... | collective-permute-start | bytes 786440 | tf_op jit(solution)/shard_map/transfer_g1_fh/ppermute | solution.py:905
  161.3 16.6 %collective-permute-start.35 = (bf16[2,2,2,64,512]{4,3,2,1,0:T(8,128)(2,1)S(1)}, bf16[2,2,2,64,512]{4,3,2,1,0:T(8,128)(2,1)S(1)}, u32[]{:S(2)}, u32[]{:S(2)}) collective-permute-start(bf16[2,2,2,64,512]{4,3,2,1,0:T(8,128)(2,1)S(1)} %get-tuple-element.371), channel_id=1, source_target_pairs={{0,1},{1,0},{2,3},{3,2},{4,5},{5,4},{6,7},{7,6},{8,9},{9,8},{10,11... | collective-permute-start | bytes 1572872 | tf_op jit(solution)/shard_map/transfer_g0_X1/ppermute | solution.py:905
  166.8 11.1 %collective-permute-start.40 = (bf16[2,2,64,512]{3,2,1,0:T(8,128)(2,1)S(1)}, bf16[2,2,64,512]{3,2,1,0:T(8,128)(2,1)S(1)}, u32[]{:S(2)}, u32[]{:S(2)}) collective-permute-start(bf16[2,2,64,512]{3,2,1,0:T(8,128)(2,1)S(1)} %add.171), channel_id=1, source_target_pairs={{0,2},{1,3},{2,0},{3,1},{4,6},{5,7},{6,4},{7,5},{8,10},{9,11},{10,... | collective-permute-start | bytes 786440 | tf_op jit(solution)/shard_map/transfer_g1_X2/ppermute | solution.py:905
  169.0 18.0 %collective-permute-start.42 = (bf16[2048,512]{1,0:T(8,128)(2,1)S(1)}, bf16[2048,512]{1,0:T(8,128)(2,1)}, u32[]{:S(2)}, u32[]{:S(2)}) collective-permute-start(bf16[2048,512]{1,0:T(8,128)(2,1)S(1)} %bitcast.141), channel_id=1, source_target_pairs={{0,16},{1,17},{2,18},{3,19},{4,20},{5,21},{6,22},{7,23},{8,24},{9,... | collective-permute-start | bytes 6291464 | tf_op jit(solution)/shard_map/transfer_m1_Core/ppermute | solution.py:905
  178.1 8.9 %collective-permute-start.41 = (bf16[2048,512]{1,0:T(8,128)(2,1)S(1)}, bf16[2048,512]{1,0:T(8,128)(2,1)}, u32[]{:S(2)}, u32[]{:S(2)}) collective-permute-start(bf16[2048,512]{1,0:T(8,128)(2,1)S(1)} %bitcast.143), channel_id=1, source_target_pairs={{16,0},{17,1},{18,2},{19,3},{20,4},{21,5},{22,6},{23,7},{24,8},{25... | collective-permute-start | bytes 6291464 | tf_op jit(solution)/shard_map/transfer_m0_Core/ppermute | solution.py:905
  179.5 10.7 %collective-permute-start.39 = (bf16[1024,512]{1,0:T(8,128)(2,1)S(1)}, bf16[1024,512]{1,0:T(8,128)(2,1)}, u32[]{:S(2)}, u32[]{:S(2)}) collective-permute-start(bf16[1024,512]{1,0:T(8,128)(2,1)S(1)} %bitcast.147), channel_id=1, source_target_pairs={{16,0},{17,1},{18,2},{19,3},{20,4},{21,5},{22,6},{23,7},{24,8},{25... | collective-permute-start | bytes 3145736 | tf_op jit(solution)/shard_map/transfer_g0_Core/ppermute | solution.py:905
  181.7 9.5 %collective-permute-start.43 = (bf16[2,2,2,64,512]{4,3,2,1,0:T(8,128)(2,1)}, bf16[2,2,2,64,512]{4,3,2,1,0:T(8,128)(2,1)}, u32[]{:S(2)}, u32[]{:S(2)}) collective-permute-start(bf16[2,2,2,64,512]{4,3,2,1,0:T(8,128)(2,1)} %get-tuple-element.398), channel_id=1, source_target_pairs={{0,1},{1,0},{2,3},{3,2},{4,5},{5,4},{6,7},{7,6},{8,9},{9,8},{10,11... | collective-permute-start | bytes 1572872 | tf_op jit(solution)/shard_map/transfer_g1_X1/ppermute | solution.py:905
  192.3 7.5 %collective-permute-start.44 = (bf16[1024,512]{1,0:T(8,128)(2,1)S(1)}, bf16[1024,512]{1,0:T(8,128)(2,1)S(1)}, u32[]{:S(2)}, u32[]{:S(2)}) collective-permute-start(bf16[1024,512]{1,0:T(8,128)(2,1)S(1)} %bitcast.149), channel_id=1, source_target_pairs={{0,16},{1,17},{2,18},{3,19},{4,20},{5,21},{6,22},{7,23},{8,24},{9,... | collective-permute-start | bytes 3145736 | tf_op jit(solution)/shard_map/transfer_g1_Core/ppermute | solution.py:905
  (36 other events, 155.1 us)
